TPU v7x, 32 devices: a whole 2x2x4 slice. The times are simulated.
32 devices in a mesh: tm: 2 (over core), height: 16 (over z, y, x).
Axes of the slice: x: 2, y: 2, z: 4, core: 2. Of those that a mesh axis runs over, the one named last changes fastest.
Arguments:
- features: bfloat16 [4, 64, 32, 192], P('tm', 'height'), may hold values from -6 to 6
- weight_one: bfloat16 [3, 3, 3, 192, 192], replicated, may hold values from -0.078125 to 0.078125
- bias_one: float32 [192], replicated, may hold values from -3 to 3
- gain_one: float32 [192], replicated, may hold values from 0.1 to 1.9
- weight_two: bfloat16 [3, 3, 3, 192, 192], replicated, may hold values from -0.078125 to 0.078125
- bias_two: float32 [192], replicated, may hold values from -3 to 3
- gain_two: float32 [192], replicated, may hold values from 0.1 to 1.9
- cotangent: bfloat16 [4, 64, 32, 192], P('tm', 'height'), may hold values from -6 to 6
Outputs:
- block_out: bfloat16 [4, 64, 32, 192], P('tm', 'height')
- grad_input: bfloat16 [4, 64, 32, 192], P('tm', 'height')
- grad_weight_one: bfloat16 [3, 3, 3, 192, 192], replicated
- grad_weight_two: bfloat16 [3, 3, 3, 192, 192], replicated
- grad_bias_one: bfloat16 [192], replicated
- grad_bias_two: bfloat16 [192], replicated
- grad_gain_one: bfloat16 [192], replicated
- grad_gain_two: bfloat16 [192], replicated
All inputs are finite; a program needn't handle non-finite values.
Results may differ from a plain program's by a relative error of at most 0.013.
Values may be sent and summed in bfloat16 or wider, within the bound.
No kernel may reach another device: no remote copies, remote signals or barrier semaphores. Data moves between devices by JAX's collectives and lax.ppermute only.
A program may use at most 128 MiB of HBM per device.

v0:
```python
import jax
import jax.numpy as jnp
from jax import lax
from jax.sharding import PartitionSpec as P

epsilon = 1e-06


def from_behind(value, axis, by):
    size = lax.axis_size(axis)
    pairs = [(i, i + by) for i in range(size) if 0 <= i + by < size]
    return lax.ppermute(value, axis, pairs)


def padded_2(value, sides, width):
    for axis, dim in sides:
        size, length = (lax.axis_size(axis), value.shape[dim])
        up = [(i, (i + 1) % size) for i in range(size - 1)]
        down = [(j, i) for i, j in up]
        last = lax.slice_in_dim(value, length - width, length, axis=dim)
        first = lax.slice_in_dim(value, 0, width, axis=dim)
        before = lax.ppermute(last, axis, up)
        after = lax.ppermute(first, axis, down)
        value = jnp.concatenate([before, value, after], axis=dim)
    return value


def norm_silu(values, gain):
    vals = values.astype(jnp.float32)
    scale = lax.rsqrt(jnp.mean(vals * vals, axis=-1, keepdims=True) + epsilon)
    normed = vals * scale
    lifted = normed * gain
    return lifted * jax.nn.sigmoid(lifted)


def norm_silu_back(grad, values, gain):
    vals = values.astype(jnp.float32)
    scale = lax.rsqrt(jnp.mean(vals * vals, axis=-1, keepdims=True) + epsilon)
    normed = vals * scale
    lifted = normed * gain
    sig = jax.nn.sigmoid(lifted)
    d_lift = grad * sig * (1.0 + lifted * (1.0 - sig))
    d_gain = jnp.sum(d_lift * normed, axis=(0, 1, 2))
    d_norm = d_lift * gain
    d_vals = scale * (d_norm - normed * jnp.mean(d_norm * normed, axis=-1, keepdims=True))
    return (d_vals, d_gain)


def column_stack(padded, start_t, start_h, frames, rows, cols, flip):
    pieces = []
    for step_w in range(3):
        offset = 2 - step_w if flip else step_w
        pieces.append(
            padded[start_t : start_t + frames, start_h : start_h + rows, offset : offset + cols]
        )
    return jnp.concatenate(pieces, axis=3).reshape(frames * rows * cols, -1)


def taps_forward(padded, weight):
    frames = padded.shape[0] - 2
    rows = padded.shape[1] - 2
    cols = padded.shape[2] - 2
    chans = padded.shape[3]
    total = jnp.zeros((frames * rows * cols, weight.shape[4]), jnp.float32)
    for step_t in range(3):
        for step_h in range(3):
            stacked = column_stack(padded, step_t, step_h, frames, rows, cols, False)
            folded = weight[step_t, step_h].reshape(3 * chans, weight.shape[4])
            total = total + jnp.dot(stacked, folded, preferred_element_type=jnp.float32)
    return total.reshape(frames, rows, cols, weight.shape[4])


def taps_back(padded, weight):
    frames = padded.shape[0] - 2
    rows = padded.shape[1] - 2
    cols = padded.shape[2] - 2
    chans = padded.shape[3]
    total = jnp.zeros((frames * rows * cols, weight.shape[3]), jnp.float32)
    for step_t in range(3):
        for step_h in range(3):
            stacked = column_stack(padded, 2 - step_t, 2 - step_h, frames, rows, cols, True)
            folded = jnp.transpose(weight[step_t, step_h], (0, 2, 1)).reshape(
                3 * chans, weight.shape[3]
            )
            total = total + jnp.dot(stacked, folded, preferred_element_type=jnp.float32)
    return total.reshape(frames, rows, cols, weight.shape[3])


def weight_grads(padded, grad):
    frames, rows, cols, chans = grad.shape
    flat_grad = grad.reshape(-1, chans)
    results = []
    for step_t in range(3):
        for step_h in range(3):
            stacked = column_stack(padded, step_t, step_h, frames, rows, cols, False)
            product = lax.dot_general(
                stacked, flat_grad, (((0,), (0,)), ((), ())), preferred_element_type=jnp.float32
            )
            results.append(product.reshape(3, padded.shape[3], chans))
    return jnp.stack(results).reshape(3, 3, 3, padded.shape[3], chans)


def widen_cols(values):
    return jnp.pad(values, ((0, 0), (0, 0), (1, 1), (0, 0)))


def ahead_frames(extended):
    earlier = from_behind(extended, "tm", 1)
    return widen_cols(jnp.concatenate([earlier, extended], axis=0))


def behind_frames(extended):
    later = from_behind(extended, "tm", -1)
    return widen_cols(jnp.concatenate([extended, later], axis=0))


def pad_ahead(values):
    extended = padded_2(values, (("height", 1),), 1)
    return ahead_frames(extended)


def pad_behind(values):
    extended = padded_2(values, (("height", 1),), 1)
    return behind_frames(extended)


def body(features, weight_one, bias_one, gain_one, weight_two, bias_two, gain_two, cotangent):
    act_one = norm_silu(features, gain_one).astype(jnp.bfloat16)
    stacked = padded_2(jnp.stack([act_one, cotangent]), (("height", 2),), 1)
    padded_one = ahead_frames(stacked[0])
    padded_cot = behind_frames(stacked[1])
    middle = (taps_forward(padded_one, weight_one) + bias_one).astype(jnp.bfloat16)
    act_two = norm_silu(middle, gain_two).astype(jnp.bfloat16)
    padded_two = pad_ahead(act_two)
    block_out = (
        features.astype(jnp.float32) + taps_forward(padded_two, weight_two) + bias_two
    ).astype(jnp.bfloat16)
    grad_w_two = weight_grads(padded_two, cotangent)
    grad_b_two = jnp.sum(cotangent.astype(jnp.float32), axis=(0, 1, 2))
    grad_act_two = taps_back(padded_cot, weight_two)
    grad_mid, grad_g_two = norm_silu_back(grad_act_two, middle, gain_two)
    grad_mid = grad_mid.astype(jnp.bfloat16)
    grad_b_one = jnp.sum(grad_mid.astype(jnp.float32), axis=(0, 1, 2))
    grad_w_one = weight_grads(padded_one, grad_mid)
    grad_act_one = taps_back(pad_behind(grad_mid), weight_one)
    grad_feat, grad_g_one = norm_silu_back(grad_act_one, features, gain_one)
    grad_input = (grad_feat + cotangent.astype(jnp.float32)).astype(jnp.bfloat16)
    totals = lax.psum(
        (grad_w_one, grad_w_two, grad_b_one, grad_b_two, grad_g_one, grad_g_two), ("tm", "height")
    )
    sum_w_one = totals[0].astype(jnp.bfloat16)
    sum_w_two = totals[1].astype(jnp.bfloat16)
    sum_b_one = totals[2].astype(jnp.bfloat16)
    sum_b_two = totals[3].astype(jnp.bfloat16)
    sum_g_one = totals[4].astype(jnp.bfloat16)
    sum_g_two = totals[5].astype(jnp.bfloat16)
    return (block_out, grad_input, sum_w_one, sum_w_two, sum_b_one, sum_b_two, sum_g_one, sum_g_two)


def solution(mesh):
    return jax.shard_map(
        body,
        mesh=mesh,
        in_specs=(
            P("tm", "height", None, None),
            P(),
            P(),
            P(),
            P(),
            P(),
            P(),
            P("tm", "height", None, None),
        ),
        out_specs=(
            P("tm", "height", None, None),
            P("tm", "height", None, None),
            P(),
            P(),
            P(),
            P(),
            P(),
            P(),
        ),
        check_vma=False,
    )
```

profile of v0, /device:TPU:0, one launch (start us, length us, event | category | flops | bytes accessed | tf_op | source)
XLA Modules:
  0.0 330.7 jit_solution(3233921679666509870)
XLA Ops:
  3.7 4.8 %collective-permute-start = (bf16[2,2,1,32,192]{4,3,2,1,0:T(8,128)(2,1)S(1)}, bf16[2,2,1,32,192]{4,3,2,1,0:T(8,128)(2,1)S(1)}, u32[]{:S(2)}, u32[]{:S(2)}) collective-permute-start(bf16[2,2,1,32,192]{4,3,2,1,0:T(8,128)(2,1)S(1)} %get-tuple-element.147), channel_id=1, source_target_pairs={{0,1},{1,2},{2,3},{3,4},{4,5},{5,6},{6,7},{7,8},{8,9},{9,10},{10,1... | collective-permute-start | bytes 147464 | tf_op jit(solution)/shard_map/ppermute | solution.py:22
  9.9 3.3 slice_bitcast_fusion.11
  13.2 1.6 collective-permute-done.1
  16.2 2.4 slice_bitcast_fusion.2
  26.6 1.9 copy.57
  28.5 1.9 copy.49
  30.3 1.9 copy.50
  32.2 1.9 copy.51
  34.1 1.8 copy.52
  39.5 3.2 collective-permute-start.2
  42.8 1.5 pad_slice_fusion.31
  55.4 1.4 pad_maximum_fusion.14
  58.6 1.4 fusion.88
  68.7 1.4 pad_maximum_fusion.24
  71.9 1.4 pad_maximum_fusion.26
  77.1 1.7 fusion.62
  79.9 1.8 copy.58
  82.9 4.3 %collective-permute-start.7 = (bf16[2,1,32,192]{3,2,1,0:T(8,128)(2,1)S(1)}, bf16[2,1,32,192]{3,2,1,0:T(8,128)(2,1)S(1)}, u32[]{:S(2)}, u32[]{:S(2)}) collective-permute-start(bf16[2,1,32,192]{3,2,1,0:T(8,128)(2,1)S(1)} %get-tuple-element.173), channel_id=1, source_target_pairs={{0,1},{1,2},{2,3},{3,4},{4,5},{5,6},{6,7},{7,8},{8,9},{9,10},{10,1... | collective-permute-start | bytes 73736 | tf_op jit(solution)/shard_map/ppermute | solution.py:22
  88.5 4.5 %collective-permute-start.3 = (bf16[2,1,32,192]{3,2,1,0:T(8,128)(2,1)S(1)}, bf16[2,1,32,192]{3,2,1,0:T(8,128)(2,1)S(1)}, u32[]{:S(2)}, u32[]{:S(2)}) collective-permute-start(bf16[2,1,32,192]{3,2,1,0:T(8,128)(2,1)S(1)} %get-tuple-element.178), channel_id=1, source_target_pairs={{0,1},{1,2},{2,3},{3,4},{4,5},{5,6},{6,7},{7,8},{8,9},{9,10},{10,1... | collective-permute-start | bytes 73736 | tf_op jit(solution)/shard_map/ppermute | solution.py:22
  98.1 2.4 copy-done.1
  100.5 3.4 %collective-permute-start.5 = (bf16[2,6,32,192]{3,2,1,0:T(8,128)(2,1)S(1)}, bf16[2,6,32,192]{3,2,1,0:T(8,128)(2,1)S(1)}, u32[]{:S(2)}, u32[]{:S(2)}) collective-permute-start(bf16[2,6,32,192]{3,2,1,0:T(8,128)(2,1)S(1)} %pad_maximum_fusion.40), channel_id=1, source_target_pairs={{0,16},{1,17},{2,18},{3,19},{4,20},{5,21},{6,22},{7,23},{8,24},{9,... | collective-permute-start | bytes 442376 | tf_op jit(solution)/shard_map/ppermute | solution.py:12
  116.8 1.5 fusion.30
  140.8 2.4 copy-done.2
  143.2 187.5 %all-reduce.6 = (bf16[3,3,3,192,192]{4,3,2,1,0:T(8,128)(2,1)}, bf16[3,3,3,192,192]{4,3,2,1,0:T(8,128)(2,1)}, bf16[192]{0:T(256)(128)(2,1)}, bf16[192]{0:T(256)(1...) all-reduce(f32[3,3,3,192,192]{4,3,2,1,0:T(8,128)} %bitcast.426, ...), channel_id=1, replica_groups=mesh['tm'=2,'height'=16] {'tm','height'}, use_global_device_ids=true, to_apply=%region_4.5 | all-reduce | flops 1991424 | bytes 11948544 | tf_op jit(solution)/shard_map/psum | solution.py:148
  (268 shorter events, 87.6 us)
Async XLA Ops:
  0.6 14.1 %copy-start = (bf16[2,4,32,192]{3,2,1,0:T(8,128)(2,1)S(1)}, bf16[2,4,32,192]{3,2,1,0:T(8,128)(2,1)}, u32[]{:S(2)}) copy-start(bf16[2,4,32,192]{3,2,1,0:T(8,128)(2,1)} %param.15) | copy-start | bytes 294916
  0.6 15.5 %copy-start.3 = (bf16[3,3,3,192,192]{4,3,2,1,0:T(8,128)(2,1)S(1)}, bf16[3,3,3,192,192]{4,3,2,1,0:T(8,128)(2,1)}, u32[]{:S(2)}) copy-start(bf16[3,3,3,192,192]{4,3,2,1,0:T(8,128)(2,1)} %param.12) | copy-start | bytes 5971972
  3.7 9.4 %collective-permute-start = (bf16[2,2,1,32,192]{4,3,2,1,0:T(8,128)(2,1)S(1)}, bf16[2,2,1,32,192]{4,3,2,1,0:T(8,128)(2,1)S(1)}, u32[]{:S(2)}, u32[]{:S(2)}) collective-permute-start(bf16[2,2,1,32,192]{4,3,2,1,0:T(8,128)(2,1)S(1)} %get-tuple-element.147), channel_id=1, source_target_pairs={{0,1},{1,2},{2,3},{3,4},{4,5},{5,6},{6,7},{7,8},{8,9},{9,10},{10,1... | collective-permute-start | bytes 147464 | tf_op jit(solution)/shard_map/ppermute | solution.py:22
  8.6 6.2 %collective-permute-start.1 = (bf16[2,2,1,32,192]{4,3,2,1,0:T(8,128)(2,1)S(1)}, bf16[2,2,1,32,192]{4,3,2,1,0:T(8,128)(2,1)S(1)}, u32[]{:S(2)}, u32[]{:S(2)}) collective-permute-start(bf16[2,2,1,32,192]{4,3,2,1,0:T(8,128)(2,1)S(1)} %get-tuple-element.148), channel_id=1, source_target_pairs={{1,0},{2,1},{3,2},{4,3},{5,4},{6,5},{7,6},{8,7},{9,8},{10,9},{11,1... | collective-permute-start | bytes 147464 | tf_op jit(solution)/shard_map/ppermute | solution.py:23
  14.9 27.9 %collective-permute-start.6 = (bf16[2,6,32,192]{3,2,1,0:T(8,128)(2,1)S(1)}, bf16[2,6,32,192]{3,2,1,0:T(8,128)(2,1)S(1)}, u32[]{:S(2)}, u32[]{:S(2)}) collective-permute-start(bf16[2,6,32,192]{3,2,1,0:T(8,128)(2,1)S(1)} %get-tuple-element.101), channel_id=1, source_target_pairs={{16,0},{17,1},{18,2},{19,3},{20,4},{21,5},{22,6},{23,7},{24,8},{25... | collective-permute-start | bytes 442376 | tf_op jit(solution)/shard_map/ppermute | solution.py:12
  19.5 19.1 %copy-start.6 = (bf16[3,192,192]{1,2,0:T(8,128)(2,1)S(1)}, bf16[3,192,192]{1,2,0:T(8,128)(2,1)}, u32[]{:S(2)}) copy-start(bf16[3,192,192]{1,2,0:T(8,128)(2,1)} %get-tuple-element.49) | copy-start | bytes 663556
  20.4 17.3 %copy-start.7 = (bf16[3,192,192]{1,2,0:T(8,128)(2,1)S(1)}, bf16[3,192,192]{1,2,0:T(8,128)(2,1)}, u32[]{:S(2)}) copy-start(bf16[3,192,192]{1,2,0:T(8,128)(2,1)} %get-tuple-element.48) | copy-start | bytes 663556
  21.3 15.5 %copy-start.8 = (bf16[3,192,192]{1,2,0:T(8,128)(2,1)S(1)}, bf16[3,192,192]{1,2,0:T(8,128)(2,1)}, u32[]{:S(2)}) copy-start(bf16[3,192,192]{1,2,0:T(8,128)(2,1)} %get-tuple-element.47) | copy-start | bytes 663556
  39.5 4.8 %collective-permute-start.2 = (bf16[2,6,32,192]{3,2,1,0:T(8,128)(2,1)S(1)}, bf16[2,6,32,192]{3,2,1,0:T(8,128)(2,1)S(1)}, u32[]{:S(2)}, u32[]{:S(2)}) collective-permute-start(bf16[2,6,32,192]{3,2,1,0:T(8,128)(2,1)S(1)} %get-tuple-element.102), channel_id=1, source_target_pairs={{0,16},{1,17},{2,18},{3,19},{4,20},{5,21},{6,22},{7,23},{8,24},{9,... | collective-permute-start | bytes 442376 | tf_op jit(solution)/shard_map/ppermute | solution.py:12
  74.0 20.4 %copy-start.29 = (bf16[256,576]{0,1:T(8,128)(2,1)S(1)}, bf16[256,576]{0,1:T(8,128)(2,1)}, u32[]{:S(2)}) copy-start(bf16[256,576]{0,1:T(8,128)(2,1)} %copy.69) | copy-start | bytes 884740
  75.3 19.3 %copy-start.28 = (bf16[256,576]{0,1:T(8,128)(2,1)S(1)}, bf16[256,576]{0,1:T(8,128)(2,1)}, u32[]{:S(2)}) copy-start(bf16[256,576]{0,1:T(8,128)(2,1)} %copy.70) | copy-start | bytes 884740
  75.7 19.2 %copy-start.33 = (bf16[256,576]{0,1:T(8,128)(2,1)S(1)}, bf16[256,576]{0,1:T(8,128)(2,1)}, u32[]{:S(2)}) copy-start(bf16[256,576]{0,1:T(8,128)(2,1)} %copy.71) | copy-start | bytes 884740
  76.0 19.1 %copy-start.30 = (bf16[256,576]{0,1:T(8,128)(2,1)S(1)}, bf16[256,576]{0,1:T(8,128)(2,1)}, u32[]{:S(2)}) copy-start(bf16[256,576]{0,1:T(8,128)(2,1)} %copy.72) | copy-start | bytes 884740
  76.1 19.3 %copy-start.35 = (bf16[256,576]{0,1:T(8,128)(2,1)S(1)}, bf16[256,576]{0,1:T(8,128)(2,1)}, u32[]{:S(2)}) copy-start(bf16[256,576]{0,1:T(8,128)(2,1)} %copy.73) | copy-start | bytes 884740
  76.3 19.4 %copy-start.34 = (bf16[256,576]{0,1:T(8,128)(2,1)S(1)}, bf16[256,576]{0,1:T(8,128)(2,1)}, u32[]{:S(2)}) copy-start(bf16[256,576]{0,1:T(8,128)(2,1)} %copy.74) | copy-start | bytes 884740
  76.7 19.3 %copy-start.38 = (bf16[256,576]{0,1:T(8,128)(2,1)S(1)}, bf16[256,576]{0,1:T(8,128)(2,1)}, u32[]{:S(2)}) copy-start(bf16[256,576]{0,1:T(8,128)(2,1)} %copy.75) | copy-start | bytes 884740
  77.1 19.2 %copy-start.36 = (bf16[256,576]{0,1:T(8,128)(2,1)S(1)}, bf16[256,576]{0,1:T(8,128)(2,1)}, u32[]{:S(2)}) copy-start(bf16[256,576]{0,1:T(8,128)(2,1)} %copy.76) | copy-start | bytes 884740
  78.7 19.1 %copy-start.23 = (bf16[256,576]{0,1:T(8,128)(2,1)S(1)}, bf16[256,576]{0,1:T(8,128)(2,1)}, u32[]{:S(2)}) copy-start(bf16[256,576]{0,1:T(8,128)(2,1)} %copy.77) | copy-start | bytes 884740
  82.9 13.6 %collective-permute-start.7 = (bf16[2,1,32,192]{3,2,1,0:T(8,128)(2,1)S(1)}, bf16[2,1,32,192]{3,2,1,0:T(8,128)(2,1)S(1)}, u32[]{:S(2)}, u32[]{:S(2)}) collective-permute-start(bf16[2,1,32,192]{3,2,1,0:T(8,128)(2,1)S(1)} %get-tuple-element.173), channel_id=1, source_target_pairs={{0,1},{1,2},{2,3},{3,4},{4,5},{5,6},{6,7},{7,8},{8,9},{9,10},{10,1... | collective-permute-start | bytes 73736 | tf_op jit(solution)/shard_map/ppermute | solution.py:22
  87.2 9.3 %collective-permute-start.8 = (bf16[2,1,32,192]{3,2,1,0:T(8,128)(2,1)S(1)}, bf16[2,1,32,192]{3,2,1,0:T(8,128)(2,1)S(1)}, u32[]{:S(2)}, u32[]{:S(2)}) collective-permute-start(bf16[2,1,32,192]{3,2,1,0:T(8,128)(2,1)S(1)} %get-tuple-element.174), channel_id=1, source_target_pairs={{1,0},{2,1},{3,2},{4,3},{5,4},{6,5},{7,6},{8,7},{9,8},{10,9},{11,1... | collective-permute-start | bytes 73736 | tf_op jit(solution)/shard_map/ppermute | solution.py:23
  88.5 12.0 %collective-permute-start.3 = (bf16[2,1,32,192]{3,2,1,0:T(8,128)(2,1)S(1)}, bf16[2,1,32,192]{3,2,1,0:T(8,128)(2,1)S(1)}, u32[]{:S(2)}, u32[]{:S(2)}) collective-permute-start(bf16[2,1,32,192]{3,2,1,0:T(8,128)(2,1)S(1)} %get-tuple-element.178), channel_id=1, source_target_pairs={{0,1},{1,2},{2,3},{3,4},{4,5},{5,6},{6,7},{7,8},{8,9},{9,10},{10,1... | collective-permute-start | bytes 73736 | tf_op jit(solution)/shard_map/ppermute | solution.py:22
  93.1 7.4 %collective-permute-start.4 = (bf16[2,1,32,192]{3,2,1,0:T(8,128)(2,1)S(1)}, bf16[2,1,32,192]{3,2,1,0:T(8,128)(2,1)S(1)}, u32[]{:S(2)}, u32[]{:S(2)}) collective-permute-start(bf16[2,1,32,192]{3,2,1,0:T(8,128)(2,1)S(1)} %get-tuple-element.179), channel_id=1, source_target_pairs={{1,0},{2,1},{3,2},{4,3},{5,4},{6,5},{7,6},{8,7},{9,8},{10,9},{11,1... | collective-permute-start | bytes 73736 | tf_op jit(solution)/shard_map/ppermute | solution.py:23
  96.6 7.4 %collective-permute-start.9 = (bf16[2,6,32,192]{3,2,1,0:T(8,128)(2,1)S(1)}, bf16[2,6,32,192]{3,2,1,0:T(8,128)(2,1)S(1)}, u32[]{:S(2)}, u32[]{:S(2)}) collective-permute-start(bf16[2,6,32,192]{3,2,1,0:T(8,128)(2,1)S(1)} %pad_maximum_fusion.41), channel_id=1, source_target_pairs={{16,0},{17,1},{18,2},{19,3},{20,4},{21,5},{22,6},{23,7},{24,8},{25... | collective-permute-start | bytes 442376 | tf_op jit(solution)/shard_map/ppermute | solution.py:12
  100.5 4.2 %collective-permute-start.5 = (bf16[2,6,32,192]{3,2,1,0:T(8,128)(2,1)S(1)}, bf16[2,6,32,192]{3,2,1,0:T(8,128)(2,1)S(1)}, u32[]{:S(2)}, u32[]{:S(2)}) collective-permute-start(bf16[2,6,32,192]{3,2,1,0:T(8,128)(2,1)S(1)} %pad_maximum_fusion.40), channel_id=1, source_target_pairs={{0,16},{1,17},{2,18},{3,19},{4,20},{5,21},{6,22},{7,23},{8,24},{9,... | collective-permute-start | bytes 442376 | tf_op jit(solution)/shard_map/ppermute | solution.py:12
  (45 other events, 293.1 us)
where the time goes:
time: 332 us; the launch traced here: 331 us
  blocking collectives  187 us (56%)
  local copies, waits for them, and re-layouts  55.1 us (17%)
  matrix products  34.1 us (10%)
  starting transfers between devices  26.8 us (8%)
  other arithmetic  23.4 us (7%)
    psum x1, blocking collectives, body(): lax.psum((grad_w_one, grad_w_two, grad_b_one, grad_b_two, grad_g_one, gra...  187 us
    transpose x20, local copies, waits for them, and re-layouts, taps_back(): jnp.transpose(weight[step_t, step_h], (0, 2, 1))  26.6 us
    dot_general x18, matrix products, taps_forward(): total = total + jnp.dot(stacked, folded, preferred_element_type=jnp.float32)  20.5 us
    reshape x18, local copies, waits for them, and re-layouts, column_stack(): return jnp.concatenate(pieces, axis=3).reshape(frames * rows * cols, -1)  15.9 us
    concatenate x24, other arithmetic, column_stack(): return jnp.concatenate(pieces, axis=3).reshape(frames * rows * cols, -1)  14.8 us
    ppermute x3, starting transfers between devices, padded_2(): before = lax.ppermute(last, axis, up)  13.7 us
    ppermute x4, starting transfers between devices, from_behind(): return lax.ppermute(value, axis, pairs)  9.2 us
    dot_general x18, matrix products, taps_back(): total = total + jnp.dot(stacked, folded, preferred_element_type=jnp.float32)  7.35 us
  transfers between devices with their start and end apart: 10, of which 2 were waited for; matrix products, arithmetic and copies ran while one was open for 9% of the time, Pallas kernels for 0%

commit v1 on v0

v1 whole, which is shorter than its diff:
```python
import functools

import jax
import jax.numpy as jnp
from jax import lax
from jax.experimental import pallas as pl
from jax.experimental.pallas import tpu as pltpu
from jax.sharding import PartitionSpec as P

epsilon = 1e-06
bf16 = jnp.bfloat16
f32 = jnp.float32


def shift_cols(value, by):
    zero = jnp.zeros_like(value[:, :1])
    if by == 1:
        return jnp.concatenate([value[:, 1:], zero], axis=1)
    return jnp.concatenate([zero, value[:, :-1]], axis=1)


def norm_parts(vals, gain):
    scale = lax.rsqrt(jnp.mean(vals * vals, axis=-1, keepdims=True) + epsilon)
    normed = vals * scale
    lifted = normed * gain
    return scale, normed, lifted, jax.nn.sigmoid(lifted)


def norm_silu(vals, gain):
    _, _, lifted, sig = norm_parts(vals, gain)
    return lifted * sig


def norm_silu_back(grad, vals, gain):
    scale, normed, lifted, sig = norm_parts(vals, gain)
    d_lift = grad * sig * (1.0 + lifted * (1.0 - sig))
    d_gain = jnp.sum(d_lift * normed, axis=0, keepdims=True)
    d_norm = d_lift * gain
    d_vals = scale * (d_norm - normed * jnp.mean(d_norm * normed, axis=-1, keepdims=True))
    return d_vals, d_gain


def conv(window, weight, frames, rows, back):
    cols, chans = window.shape[2], window.shape[3]
    parts = [None] * 3
    for t in range(3):
        for h in range(3):
            t0, h0 = (2 - t, 2 - h) if back else (t, h)
            piece = window[t0 : t0 + frames, h0 : h0 + rows].reshape(frames * rows * cols, chans)
            for k in range(3):
                dims = (((1,), (1 if back else 0,)), ((), ()))
                prod = lax.dot_general(piece, weight[t, h, k], dims, preferred_element_type=f32)
                parts[k] = prod if parts[k] is None else parts[k] + prod
    parts = [part.reshape(frames * rows, cols, chans) for part in parts]
    sign = -1 if back else 1
    total = parts[1] + shift_cols(parts[0], -sign) + shift_cols(parts[2], sign)
    return total.reshape(frames * rows * cols, chans)


def first_kernel(
    feat_ref, cot_ref, w1_ref, w2_ref, b1_ref, g1_ref, g2_ref, act1_ref, act2_ref, gmid_ref, sums_ref
):
    frames, rows, cols, chans = act2_ref.shape
    for f in range(frames + 2):
        vals = feat_ref[f].astype(f32).reshape(-1, chans)
        act1_ref[f] = norm_silu(vals, g1_ref[...]).astype(bf16).reshape(rows + 2, cols, chans)
    mid = (conv(act1_ref, w1_ref, frames, rows, False) + b1_ref[...]).astype(bf16).astype(f32)
    act2_ref[...] = norm_silu(mid, g2_ref[...]).astype(bf16).reshape(act2_ref.shape)
    grad = conv(cot_ref, w2_ref, frames, rows, True)
    gmid, d_gain = norm_silu_back(grad, mid, g2_ref[...])
    gmid = gmid.astype(bf16)
    gmid_ref[...] = gmid.reshape(gmid_ref.shape)
    cot = cot_ref[:frames, 1 : rows + 1].astype(f32).reshape(-1, chans)
    sums_ref[...] = jnp.concatenate(
        [
            d_gain,
            jnp.sum(gmid.astype(f32), axis=0, keepdims=True),
            jnp.sum(cot, axis=0, keepdims=True),
            jnp.zeros((5, chans), f32),
        ],
        axis=0,
    )


def last_kernel(
    act2_ref, gmid_ref, feat_ref, cot_ref, w1_ref, w2_ref, b2_ref, g1_ref, out_ref, gin_ref, sums_ref
):
    frames, rows, cols, chans = out_ref.shape
    feat = feat_ref[...].astype(f32).reshape(-1, chans)
    out = feat + conv(act2_ref, w2_ref, frames, rows, False) + b2_ref[...]
    out_ref[...] = out.astype(bf16).reshape(out_ref.shape)
    grad = conv(gmid_ref, w1_ref, frames, rows, True)
    d_vals, d_gain = norm_silu_back(grad, feat, g1_ref[...])
    gin = d_vals + cot_ref[...].astype(f32).reshape(-1, chans)
    gin_ref[...] = gin.astype(bf16).reshape(gin_ref.shape)
    sums_ref[...] = jnp.concatenate([d_gain, jnp.zeros((7, chans), f32)], axis=0)


def pack_rows(chans):
    return chans + chans // 2


def wgrad_kernel(x_ref, y_ref, out_ref, xk_ref):
    frames, rows, cols, chans = x_ref.shape
    cells = frames * rows * cols
    values = x_ref[...].astype(f32).reshape(frames * rows, cols, chans)
    xk_ref[0] = shift_cols(values, 1).astype(bf16).reshape(cells, chans)
    xk_ref[1] = x_ref[...].reshape(cells, chans)
    xk_ref[2] = shift_cols(values, -1).astype(bf16).reshape(cells, chans)
    step = pack_rows(chans)
    odd = lax.axis_index("tm") % 2 == 1
    dims = (((0,), (0,)), ((), ()))

    def store(tap, grad):
        grad = grad.astype(bf16)
        base = tap * step
        half = chans // 2
        out_ref[base : base + chans] = grad[:, :128]
        out_ref[base + chans : base + step] = jnp.concatenate(
            [grad[:half, 128:], grad[half:, 128:]], axis=1
        )

    for t in range(3):
        for h in range(3):
            piece = y_ref[t : t + frames, h : h + rows].reshape(cells, chans)

            @pl.when(odd)
            def _():
                for k in range(3):
                    grad = lax.dot_general(piece, xk_ref[k], dims, preferred_element_type=f32)
                    store((t * 3 + h) * 3 + k, grad)

            @pl.when(jnp.logical_not(odd))
            def _():
                for k in range(3):
                    grad = lax.dot_general(xk_ref[k], piece, dims, preferred_element_type=f32)
                    store(((2 - t) * 3 + 2 - h) * 3 + 2 - k, grad)

    used = 27 * step
    out_ref[used:] = jnp.zeros((out_ref.shape[0] - used, 128), bf16)


def unpack_kernel(one_ref, two_ref, out_one_ref, out_two_ref):
    chans = out_one_ref.shape[1]
    half = chans // 2
    for src, dst in ((one_ref, out_one_ref), (two_ref, out_two_ref)):
        low = src[:chans]
        high = src[chans:]
        dst[0, :, :128] = low
        dst[0, :half, 128:] = high[:, : chans - 128]
        dst[0, half:, 128:] = high[:, chans - 128 :]


def params(limit=50 * 2**20, **kw):
    return pltpu.CompilerParams(vmem_limit_bytes=limit, **kw)


vmem = pl.BlockSpec(memory_space=pltpu.VMEM)


def call(kernel, outs, args, flops, scratch=()):
    return pl.pallas_call(
        kernel,
        out_shape=outs,
        in_specs=[vmem] * len(args),
        out_specs=[vmem] * len(outs),
        scratch_shapes=list(scratch),
        compiler_params=params(),
        cost_estimate=pl.CostEstimate(flops=flops, bytes_accessed=8 * 2**20, transcendentals=0),
    )(*args)


def moved(value, axis, by):
    size = lax.axis_size(axis)
    return lax.ppermute(value, axis, [(i, i + by) for i in range(size) if 0 <= i + by < size])


def windows(ahead, behind):
    both = jnp.stack([ahead, behind])
    above = moved(both[:, :, -1:], "height", 1)
    below = moved(both[:, :, :1], "height", -1)
    both = jnp.concatenate([above, both, below], axis=2)
    earlier = moved(both[0, -2:], "tm", 1)
    later = moved(both[1, :2], "tm", -1)
    return jnp.concatenate([earlier, both[0]], axis=0), jnp.concatenate([both[1], later], axis=0)


def total_of(pieces):
    return functools.reduce(lambda a, b: a + b, [p.astype(f32) for p in pieces])


def piece_at(value, index):
    return lax.dynamic_index_in_dim(value, index, 0, keepdims=False)


def body(features, weight_one, bias_one, gain_one, weight_two, bias_two, gain_two, cotangent):
    frames, rows, cols, chans = features.shape
    tm, height = lax.axis_size("tm"), lax.axis_size("height")
    planes = height // 4
    c, me = lax.axis_index("tm"), lax.axis_index("height")
    p, q = me % 4, me // 4
    line = lambda v: v.reshape(1, chans)
    local = jax.ShapeDtypeStruct(features.shape, bf16)
    sums = jax.ShapeDtypeStruct((8, chans), f32)
    flops = 4 * frames * rows * cols * 27 * chans * chans

    feat_win, cot_win = windows(features, cotangent)
    act1_win, act2, gmid, sums_one = call(
        first_kernel,
        (jax.ShapeDtypeStruct(feat_win.shape, bf16), local, local, sums),
        (feat_win, cot_win, weight_one, weight_two, line(bias_one), line(gain_one), line(gain_two)),
        flops,
    )

    odd = c % 2 == 1
    swap = [(i, i ^ 1) for i in range(tm)]
    mine = jnp.where(odd, gmid, act2)
    other = lax.ppermute(jnp.where(odd, act2, gmid), "tm", swap)
    x_pair = jnp.where(odd, jnp.concatenate([other, mine]), jnp.concatenate([mine, other]))
    edge = lax.ppermute(jnp.where(odd, cot_win[-2:], feat_edge(act1_win)), "tm", swap)
    y_pair = jnp.where(
        odd, jnp.concatenate([edge, act1_win]), jnp.concatenate([cot_win, edge])
    )
    unit = 4 * planes * 16
    flat_rows = -(-27 * pack_rows(chans) // unit) * unit
    (flat,) = call(
        wgrad_kernel,
        (jax.ShapeDtypeStruct((flat_rows, 128), bf16),),
        (x_pair, y_pair),
        flops,
        [pltpu.VMEM((3, 2 * frames * rows * cols, chans), bf16)],
    )

    act2_win, gmid_win = windows(act2, gmid)
    block_out, grad_input, sums_two = call(
        last_kernel,
        (local, local, sums),
        (act2_win, gmid_win, features, cotangent, weight_one, weight_two, line(bias_two), line(gain_one)),
        flops,
    )
    small = lax.psum(jnp.concatenate([sums_one, sums_two]), ("tm", "height")).astype(bf16)

    def plane_move(value, d):
        return lax.ppermute(value, "height", [(i, i ^ d) for i in range(height)])

    def column_move(value, d):
        pairs = [(z * 4 + j, (z + d) % planes * 4 + j) for z in range(planes) for j in range(4)]
        return lax.ppermute(value, "height", pairs)

    flat = flat.reshape(4, flat_rows // 4, 128)
    arrived = [plane_move(piece_at(flat, p ^ d), d) for d in (1, 2, 3)]
    part = total_of([piece_at(flat, p), *arrived]).astype(bf16)
    part = part.reshape(planes, -1, 128)
    arrived = [column_move(piece_at(part, (q + d) % planes), d) for d in range(1, planes)]
    part = total_of([piece_at(part, q), *arrived])
    step = 2
    while step < tm:
        part = part + lax.ppermute(part, "tm", [(i, i ^ step) for i in range(tm)])
        step *= 2
    part = part.astype(bf16)

    got = [part] + [column_move(part, d) for d in range(1, planes)]
    stack = jnp.stack(got)
    order = (q - jnp.arange(planes)) % planes
    quarter = jnp.take(stack, order, axis=0).reshape(-1, 128)
    got = [quarter] + [plane_move(quarter, d) for d in (1, 2, 3)]
    other = [lax.ppermute(g, "tm", swap) for g in got]

    def ordered(pieces):
        stack = jnp.stack(pieces)
        return jnp.take(stack, jnp.arange(4) ^ p, axis=0).reshape(-1, 128)

    mine, other = ordered(got), ordered(other)
    flat_one, flat_two = jnp.where(odd, mine, other), jnp.where(odd, other, mine)
    step = pack_rows(chans)
    taps = jax.ShapeDtypeStruct((27, chans, chans), bf16)
    grad_one, grad_two = pl.pallas_call(
        unpack_kernel,
        grid=(27,),
        out_shape=(taps, taps),
        in_specs=[pl.BlockSpec((step, 128), lambda i: (i, 0))] * 2,
        out_specs=[pl.BlockSpec((1, chans, chans), lambda i: (i, 0, 0))] * 2,
        compiler_params=params(),
    )(flat_one, flat_two)
    shape = weight_one.shape
    return (
        block_out,
        grad_input,
        grad_one.reshape(shape),
        grad_two.reshape(shape),
        small[1],
        small[2],
        small[8],
        small[0],
    )


def feat_edge(act1_win):
    return act1_win[:2]


def solution(mesh):
    split = P("tm", "height", None, None)
    return jax.shard_map(
        body,
        mesh=mesh,
        in_specs=(split, P(), P(), P(), P(), P(), P(), split),
        out_specs=(split, split, P(), P(), P(), P(), P(), P()),
        check_vma=False,
    )
```

time: 332 us -> 179 us (0.54)
  blocking collectives: 187 us -> 46.1 us
  local copies, waits for them, and re-layouts: 55.1 us -> 12 us
  matrix products: 34.1 us -> 0 us
  waiting for transfers between devices: 1.82 us -> 34.6 us
  Pallas kernels: 0 us -> 24.1 us
  starting transfers between devices: 26.8 us -> 38.1 us
    psum x1, blocking collectives: 187 us -> 46.1 us  [body(): lax.psum(jnp.concatenate([sums_one, sums_two]), ('tm', 'height'))]
    dot_general x54 -> x0, matrix products: 34.1 us -> none  [the longest x18 20.5 us: taps_forward(): total = total + jnp.dot(stacked, folded, preferred_element_type=jnp.float32)]
    ppermute x10 -> x26, waiting for transfers between devices: 1.82 us -> 34.6 us  [the longest x6 18.1 us: plane_move(): return lax.ppermute(value, 'height', [(i, i ^ d) for i in range(height)])]
    transpose x20 -> x0, local copies, waits for them, and re-layouts: 26.6 us -> none  [taps_back(): jnp.transpose(weight[step_t, step_h], (0, 2, 1))]
    pallas_call x0 -> x4, Pallas kernels: none -> 24.1 us  [the longest x3 13.6 us: call(): pl.pallas_call(kernel, out_shape=outs, in_specs=[vmem] * len(args), out_s...]
    reshape x18 -> x0, local copies, waits for them, and re-layouts: 15.9 us -> none  [column_stack(): return jnp.concatenate(pieces, axis=3).reshape(frames * rows * cols, -1)]
    ppermute x10 -> x26, starting transfers between devices: 26.8 us -> 38.1 us  [the longest x8 19 us: moved(): lax.ppermute(value, axis, [(i, i + by) for i in range(size) if 0 <= i + b...]
    concatenate x33 -> x7, other arithmetic: 16.2 us -> 5.24 us  [the longest x2 2.09 us: windows(): jnp.concatenate([earlier, both[0]], axis=0)]
  transfers between devices with their start and end apart: 10 -> 26, of which waited for: 2 -> 11; matrix products, arithmetic and copies ran while one was open for 9% -> 10% of each run, Pallas kernels for 0% -> 3%
where the time goes in v1:
time: 179 us; the launch traced here: 178 us
  blocking collectives  46.1 us (26%)
  starting transfers between devices  38.1 us (21%)
  waiting for transfers between devices  34.6 us (19%)
  Pallas kernels  24.1 us (13%)
  other arithmetic  22 us (12%)
  local copies, waits for them, and re-layouts  12 us (7%)
    psum x1, blocking collectives, body(): lax.psum(jnp.concatenate([sums_one, sums_two]), ('tm', 'height'))  46.1 us
    ppermute x8, starting transfers between devices, moved(): lax.ppermute(value, axis, [(i, i + by) for i in range(size) if 0 <= i + b...  19 us
    ppermute x6, waiting for transfers between devices, plane_move(): return lax.ppermute(value, 'height', [(i, i ^ d) for i in range(height)])  18.1 us
    pallas_call x3, Pallas kernels, call(): pl.pallas_call(kernel, out_shape=outs, in_specs=[vmem] * len(args), out_s...  13.6 us
    pallas_call x1, Pallas kernels, body(): pl.pallas_call(unpack_kernel, grid=(27,), out_shape=(taps, taps), in_spec...  10.5 us
    ppermute x6, waiting for transfers between devices, column_move(): return lax.ppermute(value, 'height', pairs)  9.32 us
    ppermute x6, starting transfers between devices, column_move(): return lax.ppermute(value, 'height', pairs)  9.24 us
    ppermute x6, starting transfers between devices, plane_move(): return lax.ppermute(value, 'height', [(i, i ^ d) for i in range(height)])  8.3 us
  transfers between devices with their start and end apart: 26, of which 11 were waited for; matrix products, arithmetic and copies ran while one was open for 10% of the time, Pallas kernels for 3%

profile of v1, /device:TPU:0, one launch (start us, length us, event | category | flops | bytes accessed | tf_op | source)
XLA Modules:
  0.0 177.9 jit_solution(16311789334691000847)
XLA Ops:
  1.7 4.8 %collective-permute-start = (bf16[2,2,1,32,192]{4,3,2,1,0:T(8,128)(2,1)S(1)}, bf16[2,2,1,32,192]{4,3,2,1,0:T(8,128)(2,1)S(1)}, u32[]{:S(2)}, u32[]{:S(2)}) collective-permute-start(bf16[2,2,1,32,192]{4,3,2,1,0:T(8,128)(2,1)S(1)} %get-tuple-element.47), channel_id=1, source_target_pairs={{0,1},{1,2},{2,3},{3,4},{4,5},{5,6},{6,7},{7,8},{8,9},{9,10},{10,1... | collective-permute-start | bytes 147464 | tf_op jit(solution)/shard_map/ppermute | solution.py:175
  8.4 4.3 %collective-permute-done.1 = bf16[2,2,1,32,192]{4,3,2,1,0:T(8,128)(2,1)S(1)} collective-permute-done((bf16[2,2,1,32,192]{4,3,2,1,0:T(8,128)(2,1)S(1)}, bf16[2,2,1,32,192]{4,3,2,1,0:T(8,128)(2,1)S(1)}, u32[]{:S(2)}, u32[]{:S(2)}) %collective-permute-start.1) | collective-permute-done | bytes 49184 | tf_op jit(solution)/shard_map/ppermute | solution.py:175
  19.8 4.2 %shard_map.143 = (bf16[4,6,32,192]{3,2,1,0:T(8,128)(2,1)S(1)}, bf16[2,4,32,192]{3,2,1,0:T(8,128)(2,1)S(1)}, bf16[2,4,32,192]{3,2,1,0:T(8,128)(2,1)S(1)}, f32[8,192]{1,0:T(8,128)S(1)}) custom-call(bf16[4,6,32,192]{3,2,1,0:T(8,128)(2,1)S(1)} %pad_maximum_fusion.4.feat_ref, bf16[4,6,32,192]{3,2,1,0:T(8,128)(2,1)S(1)} %pad_maximum_fusion.5.cot_ref, ...), custom_call_target="tpu_custom_call" | custom-call | flops 1019215872 | bytes 8388608 | tf_op jit(solution)/shard_map/pallas_call | solution.py:162
  29.8 4.8 %shard_map.145 = bf16[7936,128]{1,0:T(8,128)(2,1)S(1)} custom-call(bf16[4,4,32,192]{3,2,1,0:T(8,128)(2,1)S(1)} %maximum_select_fusion.1.x_ref, bf16[6,6,32,192]{3,2,1,0:T(8,128)(2,1)S(1)} %maximum_select_fusion.y_ref), custom_call_target="tpu_custom_call" | custom-call | flops 1019215872 | bytes 8388608 | tf_op jit(solution)/shard_map/pallas_call | solution.py:162
  37.1 2.4 %collective-permute-start.10 = (bf16[1984,128]{1,0:T(8,128)(2,1)}, bf16[1984,128]{1,0:T(8,128)(2,1)S(1)}, u32[]{:S(2)}, u32[]{:S(2)}) collective-permute-start(bf16[1984,128]{1,0:T(8,128)(2,1)} %get-tuple-element.33), channel_id=1, source_target_pairs={{0,1},{1,0},{2,3},{3,2},{4,5},{5,4},{6,7},{7,6},{8,9},{9,8},{10,11... | collective-permute-start | bytes 1523720 | tf_op jit(solution)/shard_map/ppermute | solution.py:244
  39.5 1.9 %collective-permute-start.12 = (bf16[1984,128]{1,0:T(8,128)(2,1)}, bf16[1984,128]{1,0:T(8,128)(2,1)}, u32[]{:S(2)}, u32[]{:S(2)}) collective-permute-start(bf16[1984,128]{1,0:T(8,128)(2,1)} %get-tuple-element.34), channel_id=1, source_target_pairs={{0,3},{1,2},{2,1},{3,0},{4,7},{5,6},{6,5},{7,4},{8,11},{9,10},{10,... | collective-permute-start | bytes 1523720 | tf_op jit(solution)/shard_map/ppermute | solution.py:244
  42.7 3.4 %collective-permute-start.4 = (bf16[2,2,1,32,192]{4,3,2,1,0:T(8,128)(2,1)}, bf16[2,2,1,32,192]{4,3,2,1,0:T(8,128)(2,1)S(1)}, u32[]{:S(2)}, u32[]{:S(2)}) collective-permute-start(bf16[2,2,1,32,192]{4,3,2,1,0:T(8,128)(2,1)} %get-tuple-element.45), channel_id=1, source_target_pairs={{0,1},{1,2},{2,3},{3,4},{4,5},{5,6},{6,7},{7,8},{8,9},{9,10},{10,1... | collective-permute-start | bytes 147464 | tf_op jit(solution)/shard_map/ppermute | solution.py:175
  47.4 5.1 %collective-permute-done.10 = bf16[1984,128]{1,0:T(8,128)(2,1)S(1)} collective-permute-done((bf16[1984,128]{1,0:T(8,128)(2,1)}, bf16[1984,128]{1,0:T(8,128)(2,1)S(1)}, u32[]{:S(2)}, u32[]{:S(2)}) %collective-permute-start.10) | collective-permute-done | bytes 507936 | tf_op jit(solution)/shard_map/ppermute | solution.py:244
  52.5 12.2 %collective-permute-done.12 = bf16[1984,128]{1,0:T(8,128)(2,1)} collective-permute-done((bf16[1984,128]{1,0:T(8,128)(2,1)}, bf16[1984,128]{1,0:T(8,128)(2,1)}, u32[]{:S(2)}, u32[]{:S(2)}) %collective-permute-start.12) | collective-permute-done | bytes 507936 | tf_op jit(solution)/shard_map/ppermute | solution.py:244
  65.4 1.8 fusion.2
  68.0 3.0 %collective-permute-start.13 = (bf16[496,128]{1,0:T(8,128)(2,1)}, bf16[496,128]{1,0:T(8,128)(2,1)}, u32[]{:S(2)}, u32[]{:S(2)}) collective-permute-start(bf16[496,128]{1,0:T(8,128)(2,1)} %get-tuple-element.36), channel_id=1, source_target_pairs={{0,4},{1,5},{2,6},{3,7},{4,8},{5,9},{6,10},{7,11},{8,12},{9,13},{1... | collective-permute-start | bytes 380936 | tf_op jit(solution)/shard_map/ppermute | solution.py:248
  71.8 2.2 %collective-permute-start.14 = (bf16[496,128]{1,0:T(8,128)(2,1)}, bf16[496,128]{1,0:T(8,128)(2,1)}, u32[]{:S(2)}, u32[]{:S(2)}) collective-permute-start(bf16[496,128]{1,0:T(8,128)(2,1)} %get-tuple-element.38), channel_id=1, source_target_pairs={{0,8},{1,9},{2,10},{3,11},{4,12},{5,13},{6,14},{7,15},{8,0},{9,1},... | collective-permute-start | bytes 380936 | tf_op jit(solution)/shard_map/ppermute | solution.py:248
  77.6 4.2 %collective-permute-done.14 = bf16[496,128]{1,0:T(8,128)(2,1)} collective-permute-done((bf16[496,128]{1,0:T(8,128)(2,1)}, bf16[496,128]{1,0:T(8,128)(2,1)}, u32[]{:S(2)}, u32[]{:S(2)}) %collective-permute-start.14) | collective-permute-done | bytes 127008 | tf_op jit(solution)/shard_map/ppermute | solution.py:248
  82.9 2.6 %collective-permute-start.18 = (bf16[496,128]{1,0:T(8,128)(2,1)S(1)}, bf16[496,128]{1,0:T(8,128)(2,1)S(1)}, u32[]{:S(2)}, u32[]{:S(2)}) collective-permute-start(bf16[496,128]{1,0:T(8,128)(2,1)S(1)} %fusion.5), channel_id=1, source_target_pairs={{0,12},{1,13},{2,14},{3,15},{4,0},{5,1},{6,2},{7,3},{8,4},{9,5},{1... | collective-permute-start | bytes 380936 | tf_op jit(solution)/shard_map/ppermute | solution.py:248
  88.2 4.4 %collective-permute-start.6 = (bf16[2,6,32,192]{3,2,1,0:T(8,128)(2,1)}, bf16[2,6,32,192]{3,2,1,0:T(8,128)(2,1)}, u32[]{:S(2)}, u32[]{:S(2)}) collective-permute-start(bf16[2,6,32,192]{3,2,1,0:T(8,128)(2,1)} %get-tuple-element.40), channel_id=1, source_target_pairs={{0,16},{1,17},{2,18},{3,19},{4,20},{5,21},{6,22},{7,23},{8,24},{9,... | collective-permute-start | bytes 442376 | tf_op jit(solution)/shard_map/ppermute | solution.py:175
  92.6 2.6 %collective-permute-done.17 = bf16[496,128]{1,0:T(8,128)(2,1)S(1)} collective-permute-done((bf16[496,128]{1,0:T(8,128)(2,1)S(1)}, bf16[496,128]{1,0:T(8,128)(2,1)S(1)}, u32[]{:S(2)}, u32[]{:S(2)}) %collective-permute-start.17) | collective-permute-done | bytes 127008 | tf_op jit(solution)/shard_map/ppermute | solution.py:248
  98.9 1.8 %collective-permute-start.21 = (bf16[1984,128]{1,0:T(8,128)(2,1)}, bf16[1984,128]{1,0:T(8,128)(2,1)}, u32[]{:S(2)}, u32[]{:S(2)}) collective-permute-start(bf16[1984,128]{1,0:T(8,128)(2,1)} %bitcast_select_fusion), channel_id=1, source_target_pairs={{0,3},{1,2},{2,1},{3,0},{4,7},{5,6},{6,5},{7,4},{8,11},{9,10},{10,... | collective-permute-start | bytes 1523720 | tf_op jit(solution)/shard_map/ppermute | solution.py:244
  104.6 4.6 %shard_map.144 = (bf16[2,4,32,192]{3,2,1,0:T(8,128)(2,1)}, bf16[2,4,32,192]{3,2,1,0:T(8,128)(2,1)}, f32[8,192]{1,0:T(8,128)S(1)}) custom-call(bf16[4,6,32,192]{3,2,1,0:T(8,128)(2,1)S(1)} %pad_maximum_fusion.7.act2_ref, bf16[4,6,32,192]{3,2,1,0:T(8,128)(2,1)S(1)} %pad_maximum_fusion.8.gmid_ref, bf16[2,4,32,192]{3,2,1,0:T(8,128)(2,1)S(1)} %copy-done.3, ...), custom_call_target="tpu_custom_call" | custom-call | flops 1019215872 | bytes 8388608 | tf_op jit(solution)/shard_map/pallas_call | solution.py:162
  109.2 46.1 %psum.7 = bf16[16,192]{1,0:T(8,128)(2,1)S(1)} all-reduce(f32[16,192]{1,0:T(8,128)S(1)} %pad_maximum_fusion.13), channel_id=1, replica_groups=mesh['tm'=2,'height'=16] {'tm','height'}, use_global_device_ids=true, to_apply=%region_0.2 | all-reduce | flops 3072 | bytes 18432 | tf_op jit(solution)/shard_map/psum | solution.py:241
  158.8 2.1 %gather_fusion.1 = bf16[4,1984,128]{2,1,0:T(8,128)(2,1)} fusion(bf16[4,1984,128]{2,1,0:T(8,128)(2,1)S(1)} %pad_maximum_fusion, s32[1024]{0:T(1024)S(1)} %pad_clamp_fusion), kind=kCustom, calls=%fused_computation.clone | custom fusion | bytes 4063248 | tf_op jit(solution)/shard_map/jit(_take)/gather | solution.py:271
  161.0 1.8 pad_maximum_fusion.1
  162.7 2.1 %gather_fusion.2 = bf16[4,1984,128]{2,1,0:T(8,128)(2,1)} fusion(bf16[4,1984,128]{2,1,0:T(8,128)(2,1)S(1)} %pad_maximum_fusion.1, s32[1024]{0:T(1024)S(1)} %pad_clamp_fusion), kind=kCustom, calls=%fused_computation.1.clone | custom fusion | bytes 4063248 | tf_op jit(solution)/shard_map/jit(_take)/gather | solution.py:271
  164.8 2.6 %broadcast_select_fusion.2 = (bf16[4,1984,128]{2,1,0:T(8,128)(2,1)S(1)}, bf16[4,1984,128]{2,1,0:T(8,128)(2,1)S(1)}) fusion(pred[]{:T(512)S(6)} %eq.11, bf16[4,1984,128]{2,1,0:T(8,128)(2,1)} %gather_fusion.1, pred[4]{0:T(512)(128)(4,1)S(1)} %compare_and_fusion, bf16[4,1984,128]{2,1,0:T(8,128)(2,1)} %gather_fusion.2), kind=kLoop, calls=%fused_computation.7 | loop fusion | flops 4063232 | bytes 8126469 | tf_op jit(solution)/shard_map/jit(_where)/select_n | solution.py:274
  167.4 10.5 %shard_map.146 = (bf16[27,192,192]{2,1,0:T(8,128)(2,1)}, bf16[27,192,192]{2,1,0:T(8,128)(2,1)}) custom-call(bf16[7936,128]{1,0:T(8,128)(2,1)S(1)} %bitcast.59, bf16[7936,128]{1,0:T(8,128)(2,1)S(1)} %bitcast.58), custom_call_target="tpu_custom_call" | custom-call | tf_op jit(solution)/shard_map/pallas_call | solution.py:277
  (92 shorter events, 41.4 us)
Async XLA Ops:
  1.7 6.7 %collective-permute-start = (bf16[2,2,1,32,192]{4,3,2,1,0:T(8,128)(2,1)S(1)}, bf16[2,2,1,32,192]{4,3,2,1,0:T(8,128)(2,1)S(1)}, u32[]{:S(2)}, u32[]{:S(2)}) collective-permute-start(bf16[2,2,1,32,192]{4,3,2,1,0:T(8,128)(2,1)S(1)} %get-tuple-element.47), channel_id=1, source_target_pairs={{0,1},{1,2},{2,3},{3,4},{4,5},{5,6},{6,7},{7,8},{8,9},{9,10},{10,1... | collective-permute-start | bytes 147464 | tf_op jit(solution)/shard_map/ppermute | solution.py:175
  6.5 6.2 %collective-permute-start.1 = (bf16[2,2,1,32,192]{4,3,2,1,0:T(8,128)(2,1)S(1)}, bf16[2,2,1,32,192]{4,3,2,1,0:T(8,128)(2,1)S(1)}, u32[]{:S(2)}, u32[]{:S(2)}) collective-permute-start(bf16[2,2,1,32,192]{4,3,2,1,0:T(8,128)(2,1)S(1)} %get-tuple-element.48), channel_id=1, source_target_pairs={{1,0},{2,1},{3,2},{4,3},{5,4},{6,5},{7,6},{8,7},{9,8},{10,9},{11,1... | collective-permute-start | bytes 147464 | tf_op jit(solution)/shard_map/ppermute | solution.py:175
  15.7 3.3 %collective-permute-start.3 = (bf16[2,6,32,192]{3,2,1,0:T(8,128)(2,1)S(1)}, bf16[2,6,32,192]{3,2,1,0:T(8,128)(2,1)S(1)}, u32[]{:S(2)}, u32[]{:S(2)}) collective-permute-start(bf16[2,6,32,192]{3,2,1,0:T(8,128)(2,1)S(1)} %get-tuple-element.41), channel_id=1, source_target_pairs={{16,0},{17,1},{18,2},{19,3},{20,4},{21,5},{22,6},{23,7},{24,8},{25... | collective-permute-start | bytes 442376 | tf_op jit(solution)/shard_map/ppermute | solution.py:175
  24.7 3.8 %collective-permute-start.9 = (bf16[2,6,32,192]{3,2,1,0:T(8,128)(2,1)}, bf16[2,6,32,192]{3,2,1,0:T(8,128)(2,1)}, u32[]{:S(2)}, u32[]{:S(2)}) collective-permute-start(bf16[2,6,32,192]{3,2,1,0:T(8,128)(2,1)} %slice_select_fusion), channel_id=1, source_target_pairs={{0,16},{16,0},{1,17},{17,1},{2,18},{18,2},{3,19},{19,3},{4,20},{20... | collective-permute-start | bytes 442376 | tf_op jit(solution)/shard_map/ppermute | solution.py:220
  37.1 15.4 %collective-permute-start.10 = (bf16[1984,128]{1,0:T(8,128)(2,1)}, bf16[1984,128]{1,0:T(8,128)(2,1)S(1)}, u32[]{:S(2)}, u32[]{:S(2)}) collective-permute-start(bf16[1984,128]{1,0:T(8,128)(2,1)} %get-tuple-element.33), channel_id=1, source_target_pairs={{0,1},{1,0},{2,3},{3,2},{4,5},{5,4},{6,7},{7,6},{8,9},{9,8},{10,11... | collective-permute-start | bytes 1523720 | tf_op jit(solution)/shard_map/ppermute | solution.py:244
  39.5 25.3 %collective-permute-start.12 = (bf16[1984,128]{1,0:T(8,128)(2,1)}, bf16[1984,128]{1,0:T(8,128)(2,1)}, u32[]{:S(2)}, u32[]{:S(2)}) collective-permute-start(bf16[1984,128]{1,0:T(8,128)(2,1)} %get-tuple-element.34), channel_id=1, source_target_pairs={{0,3},{1,2},{2,1},{3,0},{4,7},{5,6},{6,5},{7,4},{8,11},{9,10},{10,... | collective-permute-start | bytes 1523720 | tf_op jit(solution)/shard_map/ppermute | solution.py:244
  41.3 24.1 %collective-permute-start.11 = (bf16[1984,128]{1,0:T(8,128)(2,1)}, bf16[1984,128]{1,0:T(8,128)(2,1)}, u32[]{:S(2)}, u32[]{:S(2)}) collective-permute-start(bf16[1984,128]{1,0:T(8,128)(2,1)} %get-tuple-element.35), channel_id=1, source_target_pairs={{0,2},{1,3},{2,0},{3,1},{4,6},{5,7},{6,4},{7,5},{8,10},{9,11},{10,... | collective-permute-start | bytes 1523720 | tf_op jit(solution)/shard_map/ppermute | solution.py:244
  42.7 31.4 %collective-permute-start.4 = (bf16[2,2,1,32,192]{4,3,2,1,0:T(8,128)(2,1)}, bf16[2,2,1,32,192]{4,3,2,1,0:T(8,128)(2,1)S(1)}, u32[]{:S(2)}, u32[]{:S(2)}) collective-permute-start(bf16[2,2,1,32,192]{4,3,2,1,0:T(8,128)(2,1)} %get-tuple-element.45), channel_id=1, source_target_pairs={{0,1},{1,2},{2,3},{3,4},{4,5},{5,6},{6,7},{7,8},{8,9},{9,10},{10,1... | collective-permute-start | bytes 147464 | tf_op jit(solution)/shard_map/ppermute | solution.py:175
  46.1 28.1 %collective-permute-start.5 = (bf16[2,2,1,32,192]{4,3,2,1,0:T(8,128)(2,1)}, bf16[2,2,1,32,192]{4,3,2,1,0:T(8,128)(2,1)}, u32[]{:S(2)}, u32[]{:S(2)}) collective-permute-start(bf16[2,2,1,32,192]{4,3,2,1,0:T(8,128)(2,1)} %get-tuple-element.46), channel_id=1, source_target_pairs={{1,0},{2,1},{3,2},{4,3},{5,4},{6,5},{7,6},{8,7},{9,8},{10,9},{11,1... | collective-permute-start | bytes 147464 | tf_op jit(solution)/shard_map/ppermute | solution.py:175
  68.0 8.3 %collective-permute-start.13 = (bf16[496,128]{1,0:T(8,128)(2,1)}, bf16[496,128]{1,0:T(8,128)(2,1)}, u32[]{:S(2)}, u32[]{:S(2)}) collective-permute-start(bf16[496,128]{1,0:T(8,128)(2,1)} %get-tuple-element.36), channel_id=1, source_target_pairs={{0,4},{1,5},{2,6},{3,7},{4,8},{5,9},{6,10},{7,11},{8,12},{9,13},{1... | collective-permute-start | bytes 380936 | tf_op jit(solution)/shard_map/ppermute | solution.py:248
  70.9 6.6 %collective-permute-start.15 = (bf16[496,128]{1,0:T(8,128)(2,1)}, bf16[496,128]{1,0:T(8,128)(2,1)}, u32[]{:S(2)}, u32[]{:S(2)}) collective-permute-start(bf16[496,128]{1,0:T(8,128)(2,1)} %get-tuple-element.37), channel_id=1, source_target_pairs={{0,12},{1,13},{2,14},{3,15},{4,0},{5,1},{6,2},{7,3},{8,4},{9,5},{1... | collective-permute-start | bytes 380936 | tf_op jit(solution)/shard_map/ppermute | solution.py:248
  71.8 10.0 %collective-permute-start.14 = (bf16[496,128]{1,0:T(8,128)(2,1)}, bf16[496,128]{1,0:T(8,128)(2,1)}, u32[]{:S(2)}, u32[]{:S(2)}) collective-permute-start(bf16[496,128]{1,0:T(8,128)(2,1)} %get-tuple-element.38), channel_id=1, source_target_pairs={{0,8},{1,9},{2,10},{3,11},{4,12},{5,13},{6,14},{7,15},{8,0},{9,1},... | collective-permute-start | bytes 380936 | tf_op jit(solution)/shard_map/ppermute | solution.py:248
  82.9 9.7 %collective-permute-start.18 = (bf16[496,128]{1,0:T(8,128)(2,1)S(1)}, bf16[496,128]{1,0:T(8,128)(2,1)S(1)}, u32[]{:S(2)}, u32[]{:S(2)}) collective-permute-start(bf16[496,128]{1,0:T(8,128)(2,1)S(1)} %fusion.5), channel_id=1, source_target_pairs={{0,12},{1,13},{2,14},{3,15},{4,0},{5,1},{6,2},{7,3},{8,4},{9,5},{1... | collective-permute-start | bytes 380936 | tf_op jit(solution)/shard_map/ppermute | solution.py:248
  85.5 9.7 %collective-permute-start.17 = (bf16[496,128]{1,0:T(8,128)(2,1)S(1)}, bf16[496,128]{1,0:T(8,128)(2,1)S(1)}, u32[]{:S(2)}, u32[]{:S(2)}) collective-permute-start(bf16[496,128]{1,0:T(8,128)(2,1)S(1)} %fusion.5), channel_id=1, source_target_pairs={{0,8},{1,9},{2,10},{3,11},{4,12},{5,13},{6,14},{7,15},{8,0},{9,1},... | collective-permute-start | bytes 380936 | tf_op jit(solution)/shard_map/ppermute | solution.py:248
  85.5 9.7 %collective-permute-start.16 = (bf16[496,128]{1,0:T(8,128)(2,1)S(1)}, bf16[496,128]{1,0:T(8,128)(2,1)S(1)}, u32[]{:S(2)}, u32[]{:S(2)}) collective-permute-start(bf16[496,128]{1,0:T(8,128)(2,1)S(1)} %fusion.5), channel_id=1, source_target_pairs={{0,4},{1,5},{2,6},{3,7},{4,8},{5,9},{6,10},{7,11},{8,12},{9,13},{1... | collective-permute-start | bytes 380936 | tf_op jit(solution)/shard_map/ppermute | solution.py:248
  86.9 15.5 %collective-permute-start.7 = (bf16[2,6,32,192]{3,2,1,0:T(8,128)(2,1)}, bf16[2,6,32,192]{3,2,1,0:T(8,128)(2,1)}, u32[]{:S(2)}, u32[]{:S(2)}) collective-permute-start(bf16[2,6,32,192]{3,2,1,0:T(8,128)(2,1)} %get-tuple-element.39), channel_id=1, source_target_pairs={{16,0},{17,1},{18,2},{19,3},{20,4},{21,5},{22,6},{23,7},{24,8},{25... | collective-permute-start | bytes 442376 | tf_op jit(solution)/shard_map/ppermute | solution.py:175
  88.2 15.3 %collective-permute-start.6 = (bf16[2,6,32,192]{3,2,1,0:T(8,128)(2,1)}, bf16[2,6,32,192]{3,2,1,0:T(8,128)(2,1)}, u32[]{:S(2)}, u32[]{:S(2)}) collective-permute-start(bf16[2,6,32,192]{3,2,1,0:T(8,128)(2,1)} %get-tuple-element.40), channel_id=1, source_target_pairs={{0,16},{1,17},{2,18},{3,19},{4,20},{5,21},{6,22},{7,23},{8,24},{9,... | collective-permute-start | bytes 442376 | tf_op jit(solution)/shard_map/ppermute | solution.py:175
  98.9 57.0 %collective-permute-start.21 = (bf16[1984,128]{1,0:T(8,128)(2,1)}, bf16[1984,128]{1,0:T(8,128)(2,1)}, u32[]{:S(2)}, u32[]{:S(2)}) collective-permute-start(bf16[1984,128]{1,0:T(8,128)(2,1)} %bitcast_select_fusion), channel_id=1, source_target_pairs={{0,3},{1,2},{2,1},{3,0},{4,7},{5,6},{6,5},{7,4},{8,11},{9,10},{10,... | collective-permute-start | bytes 1523720 | tf_op jit(solution)/shard_map/ppermute | solution.py:244
  100.7 55.7 %collective-permute-start.20 = (bf16[1984,128]{1,0:T(8,128)(2,1)}, bf16[1984,128]{1,0:T(8,128)(2,1)}, u32[]{:S(2)}, u32[]{:S(2)}) collective-permute-start(bf16[1984,128]{1,0:T(8,128)(2,1)} %bitcast_select_fusion), channel_id=1, source_target_pairs={{0,2},{1,3},{2,0},{3,1},{4,6},{5,7},{6,4},{7,5},{8,10},{9,11},{10,... | collective-permute-start | bytes 1523720 | tf_op jit(solution)/shard_map/ppermute | solution.py:244
  100.7 55.7 %collective-permute-start.19 = (bf16[1984,128]{1,0:T(8,128)(2,1)}, bf16[1984,128]{1,0:T(8,128)(2,1)}, u32[]{:S(2)}, u32[]{:S(2)}) collective-permute-start(bf16[1984,128]{1,0:T(8,128)(2,1)} %bitcast_select_fusion), channel_id=1, source_target_pairs={{0,1},{1,0},{2,3},{3,2},{4,5},{5,4},{6,7},{7,6},{8,9},{9,8},{10,11... | collective-permute-start | bytes 1523720 | tf_op jit(solution)/shard_map/ppermute | solution.py:244
  155.9 5.1 %collective-permute-start.22 = (bf16[1984,128]{1,0:T(8,128)(2,1)}, bf16[1984,128]{1,0:T(8,128)(2,1)}, u32[]{:S(2)}, u32[]{:S(2)}) collective-permute-start(bf16[1984,128]{1,0:T(8,128)(2,1)} %bitcast_select_fusion), channel_id=1, source_target_pairs={{0,16},{16,0},{1,17},{17,1},{2,18},{18,2},{3,19},{19,3},{4,20},{20... | collective-permute-start | bytes 1523720 | tf_op jit(solution)/shard_map/ppermute | solution.py:267
  155.9 5.1 %collective-permute-start.25 = (bf16[1984,128]{1,0:T(8,128)(2,1)}, bf16[1984,128]{1,0:T(8,128)(2,1)}, u32[]{:S(2)}, u32[]{:S(2)}) collective-permute-start(bf16[1984,128]{1,0:T(8,128)(2,1)} %collective-permute-done.21), channel_id=1, source_target_pairs={{0,16},{16,0},{1,17},{17,1},{2,18},{18,2},{3,19},{19,3},{4,20},{20... | collective-permute-start | bytes 1523720 | tf_op jit(solution)/shard_map/ppermute | solution.py:267
  156.4 4.6 %collective-permute-start.24 = (bf16[1984,128]{1,0:T(8,128)(2,1)}, bf16[1984,128]{1,0:T(8,128)(2,1)}, u32[]{:S(2)}, u32[]{:S(2)}) collective-permute-start(bf16[1984,128]{1,0:T(8,128)(2,1)} %collective-permute-done.20), channel_id=1, source_target_pairs={{0,16},{16,0},{1,17},{17,1},{2,18},{18,2},{3,19},{19,3},{4,20},{20... | collective-permute-start | bytes 1523720 | tf_op jit(solution)/shard_map/ppermute | solution.py:267
  156.5 4.5 %collective-permute-start.23 = (bf16[1984,128]{1,0:T(8,128)(2,1)}, bf16[1984,128]{1,0:T(8,128)(2,1)}, u32[]{:S(2)}, u32[]{:S(2)}) collective-permute-start(bf16[1984,128]{1,0:T(8,128)(2,1)} %collective-permute-done.19), channel_id=1, source_target_pairs={{0,16},{16,0},{1,17},{17,1},{2,18},{18,2},{3,19},{19,3},{4,20},{20... | collective-permute-start | bytes 1523720 | tf_op jit(solution)/shard_map/ppermute | solution.py:267
  (13 other events, 124.9 us)

commit v2 on v1

v2 whole, which is shorter than its diff:
```python
import functools

import jax
import jax.numpy as jnp
from jax import lax
from jax.experimental import pallas as pl
from jax.experimental.pallas import tpu as pltpu
from jax.sharding import PartitionSpec as P

epsilon = 1e-06
bf16 = jnp.bfloat16
f32 = jnp.float32
chunks = ((0, 4), (4, 3))
taps_each = 7
taps_all = 27


def shift_cols(value, by):
    zero = jnp.zeros_like(value[:, :1])
    if by == 1:
        return jnp.concatenate([value[:, 1:], zero], axis=1)
    return jnp.concatenate([zero, value[:, :-1]], axis=1)


def norm_parts(vals, gain):
    scale = lax.rsqrt(jnp.mean(vals * vals, axis=-1, keepdims=True) + epsilon)
    normed = vals * scale
    lifted = normed * gain
    return scale, normed, lifted, jax.nn.sigmoid(lifted)


def norm_silu(vals, gain):
    _, _, lifted, sig = norm_parts(vals, gain)
    return lifted * sig


def norm_silu_back(grad, vals, gain):
    scale, normed, lifted, sig = norm_parts(vals, gain)
    d_lift = grad * sig * (1.0 + lifted * (1.0 - sig))
    d_gain = jnp.sum(d_lift * normed, axis=0, keepdims=True)
    d_norm = d_lift * gain
    d_vals = scale * (d_norm - normed * jnp.mean(d_norm * normed, axis=-1, keepdims=True))
    return d_vals, d_gain


def conv(window, weight, frames, rows, back):
    cols, chans = window.shape[2], window.shape[3]
    parts = [None] * 3
    for t in range(3):
        for h in range(3):
            t0, h0 = (2 - t, 2 - h) if back else (t, h)
            piece = window[t0 : t0 + frames, h0 : h0 + rows].reshape(frames * rows * cols, chans)
            for k in range(3):
                dims = (((1,), (1 if back else 0,)), ((), ()))
                prod = lax.dot_general(piece, weight[t, h, k], dims, preferred_element_type=f32)
                parts[k] = prod if parts[k] is None else parts[k] + prod
    parts = [part.reshape(frames * rows, cols, chans) for part in parts]
    sign = -1 if back else 1
    total = parts[1] + shift_cols(parts[0], -sign) + shift_cols(parts[2], sign)
    return total.reshape(frames * rows * cols, chans)


def fill(window, first, second, above, below):
    count, rows = first.shape[0], first.shape[1]
    window[:count, 1 : rows + 1] = first[...]
    window[count:, 1 : rows + 1] = second[...]
    window[:, :1] = above
    window[:, rows + 1 :] = below


def first_kernel(
    feat_ref, earlier_ref, cot_ref, later_ref, above_ref, below_ref, w1_ref, w2_ref, b1_ref, g1_ref, g2_ref,
    act2_ref, gmid_ref, give_ref, keep_ref, sums_ref, ahead, behind,
):
    frames, rows, cols, chans = act2_ref.shape
    half = frames + 2
    fill(ahead, earlier_ref, feat_ref, above_ref[:half], below_ref[:half])
    fill(behind, cot_ref, later_ref, above_ref[half:], below_ref[half:])
    for f in range(half):
        vals = ahead[f].astype(f32).reshape(-1, chans)
        ahead[f] = norm_silu(vals, g1_ref[...]).astype(bf16).reshape(rows + 2, cols, chans)
    mid = (conv(ahead, w1_ref, frames, rows, False) + b1_ref[...]).astype(bf16).astype(f32)
    act2 = norm_silu(mid, g2_ref[...]).astype(bf16).reshape(act2_ref.shape)
    act2_ref[...] = act2
    grad = conv(behind, w2_ref, frames, rows, True)
    gmid, d_gain = norm_silu_back(grad, mid, g2_ref[...])
    gmid = gmid.astype(bf16)
    cot = cot_ref[...].astype(f32).reshape(-1, chans)
    sums_ref[...] = jnp.concatenate(
        [
            d_gain,
            jnp.sum(gmid.astype(f32), axis=0, keepdims=True),
            jnp.sum(cot, axis=0, keepdims=True),
            jnp.zeros((5, chans), f32),
        ],
        axis=0,
    )
    gmid = gmid.reshape(gmid_ref.shape)
    gmid_ref[...] = gmid
    odd = lax.axis_index("tm") % 2 == 1

    @pl.when(odd)
    def _():
        give_ref[...] = act2
        keep_ref[...] = gmid

    @pl.when(jnp.logical_not(odd))
    def _():
        give_ref[...] = gmid
        keep_ref[...] = act2


def last_kernel(
    act2_ref, earlier_ref, gmid_ref, later_ref, above_ref, below_ref, feat_ref, cot_ref, w1_ref, w2_ref, b2_ref, g1_ref,
    out_ref, gin_ref, sums_ref, ahead, behind,
):
    frames, rows, cols, chans = out_ref.shape
    half = frames + 2
    fill(ahead, earlier_ref, act2_ref, above_ref[:half], below_ref[:half])
    fill(behind, gmid_ref, later_ref, above_ref[half:], below_ref[half:])
    feat = feat_ref[...].astype(f32).reshape(-1, chans)
    out = feat + conv(ahead, w2_ref, frames, rows, False) + b2_ref[...]
    out_ref[...] = out.astype(bf16).reshape(out_ref.shape)
    grad = conv(behind, w1_ref, frames, rows, True)
    d_vals, d_gain = norm_silu_back(grad, feat, g1_ref[...])
    gin = d_vals + cot_ref[...].astype(f32).reshape(-1, chans)
    gin_ref[...] = gin.astype(bf16).reshape(gin_ref.shape)
    sums_ref[...] = jnp.concatenate([d_gain, jnp.zeros((7, chans), f32)], axis=0)


def pack_rows(chans):
    return chans + chans // 2


def wgrad_kernel(blocks, taps, *refs):
    xs, ys = refs[:4], refs[4:8]
    gain_ref, out_ref, plane, xk = refs[8:]
    two, rows, cols, _ = ys[0].shape
    chans = gain_ref.shape[1]
    tall = 4 * rows
    cells = 2 * two * tall * cols
    odd = lax.axis_index("tm") % 2 == 1
    p = lax.axis_index("height") % 4
    single = blocks == 2
    start = jnp.where(odd, 2, 0) if single else 0
    if single:
        plane[pl.ds(jnp.where(odd, 0, 4), 2)] = jnp.zeros((2,) + plane.shape[1:], bf16)

    def put_y(values, row, count):
        for b in range(blocks):
            part = values[..., b * chans : (b + 1) * chans]
            place = (pl.ds(start + 2 * b, 2), pl.ds(row, count))

            @pl.when(odd)
            def _():
                flat = part.astype(f32).reshape(-1, chans)
                plane[place] = norm_silu(flat, gain_ref[...]).astype(bf16).reshape(part.shape)

            @pl.when(jnp.logical_not(odd))
            def _():
                plane[place] = part

    for d in range(4):
        at = p ^ d
        put_y(ys[d][...], 1 + rows * at, rows)
        for b in range(2):
            part = xs[d][:, :rows, :, b * chans : (b + 1) * chans]
            wide = part.astype(f32).reshape(two * rows, cols, chans)
            place = (pl.ds(2 * b, 2), pl.ds(rows * at, rows))
            xk[(0,) + place] = shift_cols(wide, 1).astype(bf16).reshape(part.shape)
            xk[(1,) + place] = part
            xk[(2,) + place] = shift_cols(wide, -1).astype(bf16).reshape(part.shape)

        @pl.when(at == 0)
        def _():
            put_y(xs[d][:, rows:, :, : blocks * chans], 0, 1)

        @pl.when(at == 3)
        def _():
            put_y(xs[d][:, rows:, :, : blocks * chans], tall + 1, 1)

    step = pack_rows(chans)
    dims = (((0,), (0,)), ((), ()))
    first, count = taps
    half = chans // 2

    def store(base, grad):
        grad = grad.astype(bf16)
        out_ref[base : base + chans] = grad[:, :128]
        out_ref[base + chans : base + step] = jnp.concatenate(
            [grad[:half, 128:], grad[half:, 128:]], axis=1
        )

    for j in range(count):
        tap = jnp.minimum(p * taps_each + first + j, taps_all - 1)
        t, h, k = tap // 9, tap // 3 % 3, tap % 3

        @pl.when(odd)
        def _():
            piece = plane[pl.ds(t, 4), pl.ds(h, tall)].reshape(cells, chans)
            x = xk[k].reshape(cells, chans)
            store(j * step, lax.dot_general(piece, x, dims, preferred_element_type=f32))

        @pl.when(jnp.logical_not(odd))
        def _():
            piece = plane[pl.ds(2 - t, 4), pl.ds(2 - h, tall)].reshape(cells, chans)
            x = xk[2 - k].reshape(cells, chans)
            store(j * step, lax.dot_general(x, piece, dims, preferred_element_type=f32))

    used = count * step
    if used < out_ref.shape[0]:
        out_ref[used:] = jnp.zeros((out_ref.shape[0] - used, 128), bf16)


def unpack_kernel(*refs):
    outs = refs[-2:]
    chans = outs[0].shape[1]
    half = chans // 2
    step = pack_rows(chans)
    odd = lax.axis_index("tm") % 2 == 1
    p = lax.axis_index("height") % 4
    at = 0
    for first, count in chunks:
        for own in (True, False):
            for d in range(4):
                src = refs[at]
                at += 1
                for j in range(count):
                    tap = (p ^ d) * taps_each + first + j
                    low = src[j * step : j * step + chans]
                    high = src[j * step + chans : (j + 1) * step]
                    for which in range(2):
                        mine = odd if which == 0 else jnp.logical_not(odd)
                        cond = mine if own else jnp.logical_not(mine)

                        @pl.when(jnp.logical_and(cond, tap < taps_all))
                        def _():
                            dst = outs[which].at[tap]
                            dst[:, :128] = low
                            dst[:half, 128:] = high[:, : chans - 128]
                            dst[half:, 128:] = high[:, chans - 128 :]


vmem = pl.BlockSpec(memory_space=pltpu.VMEM)


def call(kernel, outs, args, flops, scratch=()):
    return pl.pallas_call(
        kernel,
        out_shape=outs,
        in_specs=[vmem] * len(args),
        out_specs=[vmem] * len(outs),
        scratch_shapes=list(scratch),
        compiler_params=pltpu.CompilerParams(vmem_limit_bytes=50 * 2**20),
        cost_estimate=pl.CostEstimate(flops=flops, bytes_accessed=8 * 2**20, transcendentals=0),
    )(*args)


def moved(value, axis, by):
    size = lax.axis_size(axis)
    return lax.ppermute(value, axis, [(i, i + by) for i in range(size) if 0 <= i + by < size])


def frame_parts(ahead, behind):
    return moved(ahead[-2:], "tm", 1), moved(behind[:2], "tm", -1)


def row_parts(ahead, earlier, behind, later):
    all_of = (earlier, ahead, behind, later)
    above = moved(jnp.concatenate([v[:, -1:] for v in all_of]), "height", 1)
    below = moved(jnp.concatenate([v[:, :1] for v in all_of]), "height", -1)
    return above, below


def total_of(pieces):
    return functools.reduce(lambda a, b: a + b, [p.astype(f32) for p in pieces])


def piece_at(value, index):
    return lax.dynamic_index_in_dim(value, index, 0, keepdims=False)


def body(features, weight_one, bias_one, gain_one, weight_two, bias_two, gain_two, cotangent):
    frames, rows, cols, chans = features.shape
    tm, height = lax.axis_size("tm"), lax.axis_size("height")
    planes = height // 4
    c, me = lax.axis_index("tm"), lax.axis_index("height")
    odd = c % 2 == 1
    p, q = me % 4, me // 4
    swap = [(i, i ^ 1) for i in range(tm)]
    line = lambda v: v.reshape(1, chans)
    local = jax.ShapeDtypeStruct(features.shape, bf16)
    sums = jax.ShapeDtypeStruct((8, chans), f32)
    flops = 4 * frames * rows * cols * 27 * chans * chans
    window = pltpu.VMEM((frames + 2, rows + 2, cols, chans), bf16)

    def plane_move(value, d):
        return lax.ppermute(value, "height", [(i, i ^ d) for i in range(height)])

    def column_move(value, d):
        pairs = [(z * 4 + j, (z + d) % planes * 4 + j) for z in range(planes) for j in range(4)]
        return lax.ppermute(value, "height", pairs)

    def lanes(odd_blocks, even_blocks):
        return jnp.where(odd, jnp.concatenate(odd_blocks, -1), jnp.concatenate(even_blocks, -1))

    earlier, later = frame_parts(features, cotangent)
    above, below = row_parts(features, earlier, cotangent, later)

    odd_blocks = [(earlier, above[:2], below[:2]), (features, above[2:4], below[2:4])]
    even_blocks = [(cotangent, above[4:6], below[4:6]), (later, above[6:], below[6:])]
    if tm > 2:
        extra = tuple(
            lax.ppermute(jnp.where(odd, b, a), "tm", swap) for a, b in zip(odd_blocks[0], even_blocks[1])
        )
        odd_blocks, even_blocks = [extra, *odd_blocks], [*even_blocks, extra]
    blocks = len(odd_blocks)
    y_own = lanes([b[0] for b in odd_blocks], [b[0] for b in even_blocks])
    ys = [y_own] + [plane_move(y_own, d) for d in (1, 2, 3)]
    edge_above = lanes([b[1] for b in odd_blocks], [b[1] for b in even_blocks])
    edge_below = lanes([b[2] for b in odd_blocks], [b[2] for b in even_blocks])
    edge = jnp.where(p == 0, edge_above, edge_below)

    act2, gmid, give, keep, sums_one = call(
        first_kernel,
        (local, local, local, local, sums),
        (
            features, earlier, cotangent, later, above, below,
            weight_one, weight_two, line(bias_one), line(gain_one), line(gain_two),
        ),
        flops,
        [window, window],
    )
    other = lax.ppermute(give, "tm", swap)
    x_own = lanes([other, keep], [keep, other])
    if blocks > 2:
        x_own = jnp.pad(x_own, ((0, 0), (0, 0), (0, 0), (0, (blocks - 2) * chans)))
    x_own = jnp.concatenate([x_own, edge], axis=1)
    xs = [x_own] + [plane_move(x_own, d) for d in (1, 2, 3)]

    earlier2, later2 = frame_parts(act2, gmid)
    above2, below2 = row_parts(act2, earlier2, gmid, later2)

    step = pack_rows(chans)
    unit = 16 * planes
    cells = (2 * frames, 4 * rows, cols, chans)
    parts = []
    for taps in chunks:
        packed = -(-taps[1] * step // unit) * unit
        (flat,) = call(
            functools.partial(wgrad_kernel, blocks, taps),
            (jax.ShapeDtypeStruct((packed, 128), bf16),),
            (*xs, *ys, line(gain_one)),
            flops // 2,
            [
                pltpu.VMEM((2 * frames + 2, 4 * rows + 2, cols, chans), bf16),
                pltpu.VMEM((3, *cells), bf16),
            ],
        )
        flat = flat.reshape(planes, packed // planes, 128)
        arrived = [column_move(piece_at(flat, (q + d) % planes), d) for d in range(1, planes)]
        part = total_of([piece_at(flat, q), *arrived])
        hop = 2
        while hop < tm:
            part = part + lax.ppermute(part, "tm", [(i, i ^ hop) for i in range(tm)])
            hop *= 2
        parts.append(part.astype(bf16))

    block_out, grad_input, sums_two = call(
        last_kernel,
        (local, local, sums),
        (
            act2, earlier2, gmid, later2, above2, below2, features, cotangent,
            weight_one, weight_two, line(bias_two), line(gain_one),
        ),
        flops,
        [window, window],
    )

    small = jnp.concatenate([sums_one[:3], sums_two[:1]]).reshape(-1, 128)
    count = small.shape[0]

    def with_small(value, small):
        high = small.astype(bf16)
        low = (small - high.astype(f32)).astype(bf16)
        pad = jnp.zeros((-2 * count % 16, 128), bf16)
        return jnp.concatenate([value, high, low, pad])

    def without_small(pieces, rows):
        total = total_of([v[rows : rows + count].astype(f32) + v[rows + count : rows + 2 * count].astype(f32) for v in pieces])
        return [v[:rows] for v in pieces], total

    hop = 2
    while hop < tm:
        small = small + lax.ppermute(small, "tm", [(i, i ^ hop) for i in range(tm)])
        hop *= 2

    final = []
    for n, part in enumerate(parts):
        last = n == len(parts) - 1
        size = part.shape[0]
        send = with_small(part, small) if last else part
        got = [send] + [column_move(send, d) for d in range(1, planes)]
        if last:
            got, small = without_small(got, size)
        stack = jnp.stack(got)
        quarter = jnp.take(stack, (q - jnp.arange(planes)) % planes, axis=0).reshape(-1, 128)
        size = quarter.shape[0]
        send = with_small(quarter, small) if last else quarter
        got = [send] + [plane_move(send, d) for d in (1, 2, 3)]
        others = [lax.ppermute(g, "tm", swap) for g in got]
        if last:
            _, small = without_small(got + others, size)
        final += [*got, *others]

    gradient = jax.ShapeDtypeStruct((taps_all, chans, chans), bf16)
    grad_one, grad_two = call(unpack_kernel, (gradient, gradient), final, 0)
    shape = weight_one.shape
    small = small.reshape(4, chans).astype(bf16)
    return (
        block_out,
        grad_input,
        grad_one.reshape(shape),
        grad_two.reshape(shape),
        small[1],
        small[2],
        small[3],
        small[0],
    )


def solution(mesh):
    split = P("tm", "height", None, None)
    return jax.shard_map(
        body,
        mesh=mesh,
        in_specs=(split, P(), P(), P(), P(), P(), P(), split),
        out_specs=(split, split, P(), P(), P(), P(), P(), P()),
        check_vma=False,
    )
```

time: 179 us -> 132 us (0.74)
  blocking collectives: 46.1 us -> 0 us
  other arithmetic: 22 us -> 2.24 us
  starting transfers between devices: 38.1 us -> 55.6 us
    psum x1 -> x0, blocking collectives: 46.1 us -> none  [body(): lax.psum(jnp.concatenate([sums_one, sums_two]), ('tm', 'height'))]
    pallas_call x3 -> x5, Pallas kernels: 13.6 us -> 24.6 us  [call(): pl.pallas_call(kernel, out_shape=outs, in_specs=[vmem] * len(args), out_s...]
    ppermute x6 -> x12, starting transfers between devices: 8.3 us -> 19 us  [plane_move(): return lax.ppermute(value, 'height', [(i, i ^ d) for i in range(height)])]
    pallas_call x1 -> x0, Pallas kernels: 10.5 us -> none  [body(): pl.pallas_call(unpack_kernel, grid=(27,), out_shape=(taps, taps), in_spec...]
    unnamed x22 -> x28, local copies, waits for them, and re-layouts: 1.93 us -> 8.86 us
    ppermute x6 -> x12, starting transfers between devices: 9.24 us -> 15.6 us  [column_move(): return lax.ppermute(value, 'height', pairs)]
    select_n x9 -> x6, other arithmetic: 8.03 us -> 1.82 us  [the longest x2 1.29 us: lanes(): jnp.where(odd, jnp.concatenate(odd_blocks, -1), jnp.concatenate(even_bloc...]
    concatenate x7 -> x8, other arithmetic: 5.24 us -> 0.2 us  [the longest x2 0.07 us: row_parts(): below = moved(jnp.concatenate([v[:, :1] for v in all_of]), 'height', -1)]
  transfers between devices with their start and end apart: 26 -> 41, of which waited for: 11 -> 11; matrix products, arithmetic and copies ran while one was open for 10% -> 4% of each run, Pallas kernels for 3% -> 10%
where the time goes in v2:
time: 132 us
  starting transfers between devices  55.6 us (42%)
  waiting for transfers between devices  36.2 us (27%)
  Pallas kernels  24.6 us (19%)
  local copies, waits for them, and re-layouts  12 us (9%)
  other arithmetic  2.24 us (2%)
    pallas_call x5, Pallas kernels, call(): pl.pallas_call(kernel, out_shape=outs, in_specs=[vmem] * len(args), out_s...  24.6 us
    ppermute x12, waiting for transfers between devices, plane_move(): return lax.ppermute(value, 'height', [(i, i ^ d) for i in range(height)])  21.4 us
    ppermute x12, starting transfers between devices, plane_move(): return lax.ppermute(value, 'height', [(i, i ^ d) for i in range(height)])  19 us
    ppermute x8, starting transfers between devices, moved(): lax.ppermute(value, axis, [(i, i + by) for i in range(size) if 0 <= i + b...  18 us
    ppermute x12, starting transfers between devices, column_move(): return lax.ppermute(value, 'height', pairs)  15.6 us
    ppermute x12, waiting for transfers between devices, column_move(): return lax.ppermute(value, 'height', pairs)  9.45 us
    unnamed x28, local copies, waits for them, and re-layouts  8.86 us
    ppermute x8, waiting for transfers between devices, moved(): lax.ppermute(value, axis, [(i, i + by) for i in range(size) if 0 <= i + b...  5.33 us
  transfers between devices with their start and end apart: 41, of which 11 were waited for; matrix products, arithmetic and copies ran while one was open for 4% of the time, Pallas kernels for 10%

profile of v2, /device:TPU:0, one launch (start us, length us, event | category | flops | bytes accessed | tf_op | source)
XLA Modules:
  0.0 131.7 jit_solution(2950834296082848509)
XLA Ops:
  0.6 2.4 %collective-permute-start = (bf16[2,4,32,192]{3,2,1,0:T(8,128)(2,1)}, bf16[2,4,32,192]{3,2,1,0:T(8,128)(2,1)S(1)}, u32[]{:S(2)}, u32[]{:S(2)}) collective-permute-start(bf16[2,4,32,192]{3,2,1,0:T(8,128)(2,1)} %feat_ref.3), channel_id=1, source_target_pairs={{0,16},{1,17},{2,18},{3,19},{4,20},{5,21},{6,22},{7,23},{8,24},{9,... | collective-permute-start | bytes 294920 | tf_op jit(solution)/shard_map/ppermute | solution.py:261
  6.5 4.2 %collective-permute-start.2 = (bf16[8,1,32,192]{3,2,1,0:T(8,128)(2,1)S(1)}, bf16[8,1,32,192]{3,2,1,0:T(8,128)(2,1)S(1)}, u32[]{:S(2)}, u32[]{:S(2)}) collective-permute-start(bf16[8,1,32,192]{3,2,1,0:T(8,128)(2,1)S(1)} %pad_maximum_fusion.4), channel_id=1, source_target_pairs={{0,1},{1,2},{2,3},{3,4},{4,5},{5,6},{6,7},{7,8},{8,9},{9,10},{10,1... | collective-permute-start | bytes 294920 | tf_op jit(solution)/shard_map/ppermute | solution.py:261
  13.2 3.7 %collective-permute-start.14 = (bf16[2,4,32,384]{3,2,1,0:T(8,128)(2,1)S(1)}, bf16[2,4,32,384]{3,2,1,0:T(8,128)(2,1)S(1)}, u32[]{:S(2)}, u32[]{:S(2)}) collective-permute-start(bf16[2,4,32,384]{3,2,1,0:T(8,128)(2,1)S(1)} %maximum_select_fusion.1.refs_4_), channel_id=1, source_target_pairs={{0,3},{1,2},{2,1},{3,0},{4,7},{5,6},{6,5},{7,4},{8,11},{9,10},{10,... | collective-permute-start | bytes 589832 | tf_op jit(solution)/shard_map/ppermute | solution.py:298
  18.7 1.7 %copy-done = bf16[3,3,3,192,192]{4,3,2,1,0:T(8,128)(2,1)S(1)} copy-done((bf16[3,3,3,192,192]{4,3,2,1,0:T(8,128)(2,1)S(1)}, bf16[3,3,3,192,192]{4,3,2,1,0:T(8,128)(2,1)}, u32[]{:S(2)}) %copy-start) | copy-done | bytes 1990680
  24.3 4.2 %shard_map.143 = (bf16[2,4,32,192]{3,2,1,0:T(8,128)(2,1)S(1)}, bf16[2,4,32,192]{3,2,1,0:T(8,128)(2,1)S(1)}, bf16[2,4,32,192]{3,2,1,0:T(8,128)(2,1)S(1)}, bf16[2,4,32,192]{3,2,1,0:T(8,128)(2,1)S(1)}, f32[8,192]{1,0:T(8,128)S(1)}) custom-call(bf16[2,4,32,192]{3,2,1,0:T(8,128)(2,1)S(1)} %copy-done.2, ...), custom_call_target="tpu_custom_call" | custom-call | flops 1019215872 | bytes 8388608 | tf_op jit(solution)/shard_map/pallas_call | solution.py:248
  33.6 4.5 %collective-permute-start.6 = (bf16[8,1,32,192]{3,2,1,0:T(8,128)(2,1)S(1)}, bf16[8,1,32,192]{3,2,1,0:T(8,128)(2,1)S(1)}, u32[]{:S(2)}, u32[]{:S(2)}) collective-permute-start(bf16[8,1,32,192]{3,2,1,0:T(8,128)(2,1)S(1)} %pad_maximum_fusion.6), channel_id=1, source_target_pairs={{0,1},{1,2},{2,3},{3,4},{4,5},{5,6},{6,7},{7,8},{8,9},{9,10},{10,1... | collective-permute-start | bytes 294920 | tf_op jit(solution)/shard_map/ppermute | solution.py:261
  39.7 3.8 %collective-permute-start.11 = (bf16[2,5,32,384]{3,2,1,0:T(8,128)(2,1)S(1)}, bf16[2,5,32,384]{3,2,1,0:T(8,128)(2,1)S(1)}, u32[]{:S(2)}, u32[]{:S(2)}) collective-permute-start(bf16[2,5,32,384]{3,2,1,0:T(8,128)(2,1)S(1)} %pad_maximum_fusion.1.refs_0_), channel_id=1, source_target_pairs={{0,3},{1,2},{2,1},{3,0},{4,7},{5,6},{6,5},{7,4},{8,11},{9,10},{10,... | collective-permute-start | bytes 737288 | tf_op jit(solution)/shard_map/ppermute | solution.py:298
  43.9 2.6 %collective-permute-done.7.below_ref = bf16[8,1,32,192]{3,2,1,0:T(8,128)(2,1)S(1)} collective-permute-done((bf16[8,1,32,192]{3,2,1,0:T(8,128)(2,1)S(1)}, bf16[8,1,32,192]{3,2,1,0:T(8,128)(2,1)S(1)}, u32[]{:S(2)}, u32[]{:S(2)}) %collective-permute-start.7) | collective-permute-done | bytes 98336 | tf_op jit(solution)/shard_map/ppermute | solution.py:261
  46.4 2.0 %collective-permute-start.9 = (bf16[2,5,32,384]{3,2,1,0:T(8,128)(2,1)S(1)}, bf16[2,5,32,384]{3,2,1,0:T(8,128)(2,1)S(1)}, u32[]{:S(2)}, u32[]{:S(2)}) collective-permute-start(bf16[2,5,32,384]{3,2,1,0:T(8,128)(2,1)S(1)} %pad_maximum_fusion.1.refs_0_), channel_id=1, source_target_pairs={{0,1},{1,0},{2,3},{3,2},{4,5},{5,4},{6,7},{7,6},{8,9},{9,8},{10,11... | collective-permute-start | bytes 737288 | tf_op jit(solution)/shard_map/ppermute | solution.py:298
  48.4 4.6 %shard_map.144 = (bf16[2,4,32,192]{3,2,1,0:T(8,128)(2,1)}, bf16[2,4,32,192]{3,2,1,0:T(8,128)(2,1)}, f32[8,192]{1,0:T(8,128)S(1)}) custom-call(bf16[2,4,32,192]{3,2,1,0:T(8,128)(2,1)S(1)} %get-tuple-element.18.act2_ref, bf16[2,4,32,192]{3,2,1,0:T(8,128)(2,1)S(1)} %collective-permute-done.4.earlier_ref, ...), custom_call_target="tpu_custom_call" | custom-call | flops 1019215872 | bytes 8388608 | tf_op jit(solution)/shard_map/pallas_call | solution.py:248
  53.2 6.9 %collective-permute-done.12.refs_5_ = bf16[2,4,32,384]{3,2,1,0:T(8,128)(2,1)S(1)} collective-permute-done((bf16[2,4,32,384]{3,2,1,0:T(8,128)(2,1)S(1)}, bf16[2,4,32,384]{3,2,1,0:T(8,128)(2,1)S(1)}, u32[]{:S(2)}, u32[]{:S(2)}) %collective-permute-start.12) | collective-permute-done | bytes 196640 | tf_op jit(solution)/shard_map/ppermute | solution.py:298
  60.2 3.7 %shard_map.146 = bf16[896,128]{1,0:T(8,128)(2,1)S(1)} custom-call(bf16[2,5,32,384]{3,2,1,0:T(8,128)(2,1)S(1)} %pad_maximum_fusion.1.refs_0_, bf16[2,5,32,384]{3,2,1,0:T(8,128)(2,1)S(1)} %collective-permute-done.9.refs_1_, bf16[2,5,32,384]{3,2,1,0:T(8,128)(2,1)S(1)} %collective-permute-done.10.refs_2_, ...), custom_call_target="tpu_custom_call" | custom-call | flops 509607936 | bytes 8388608 | tf_op jit(solution)/shard_map/pallas_call | solution.py:248
  65.5 2.2 %collective-permute-start.30 = (bf16[224,128]{1,0:T(8,128)(2,1)S(1)}, bf16[224,128]{1,0:T(8,128)(2,1)S(1)}, u32[]{:S(2)}, u32[]{:S(2)}) collective-permute-start(bf16[224,128]{1,0:T(8,128)(2,1)S(1)} %get-tuple-element.38), channel_id=1, source_target_pairs={{0,12},{1,13},{2,14},{3,15},{4,0},{5,1},{6,2},{7,3},{8,4},{9,5},{1... | collective-permute-start | bytes 172040 | tf_op jit(solution)/shard_map/ppermute | solution.py:302
  68.5 4.1 %shard_map.145 = bf16[1152,128]{1,0:T(8,128)(2,1)S(1)} custom-call(bf16[2,5,32,384]{3,2,1,0:T(8,128)(2,1)S(1)} %pad_maximum_fusion.1.refs_0_, bf16[2,5,32,384]{3,2,1,0:T(8,128)(2,1)S(1)} %collective-permute-done.9.refs_1_, bf16[2,5,32,384]{3,2,1,0:T(8,128)(2,1)S(1)} %collective-permute-done.10.refs_2_, ...), custom_call_target="tpu_custom_call" | custom-call | flops 509607936 | bytes 8388608 | tf_op jit(solution)/shard_map/pallas_call | solution.py:248
  74.3 2.2 %collective-permute-start.17 = (bf16[288,128]{1,0:T(8,128)(2,1)S(1)}, bf16[288,128]{1,0:T(8,128)(2,1)S(1)}, u32[]{:S(2)}, u32[]{:S(2)}) collective-permute-start(bf16[288,128]{1,0:T(8,128)(2,1)S(1)} %get-tuple-element.35), channel_id=1, source_target_pairs={{0,12},{1,13},{2,14},{3,15},{4,0},{5,1},{6,2},{7,3},{8,4},{9,5},{1... | collective-permute-start | bytes 221192 | tf_op jit(solution)/shard_map/ppermute | solution.py:302
  76.9 1.9 %collective-permute-start.33 = (bf16[240,128]{1,0:T(8,128)(2,1)S(1)}, bf16[240,128]{1,0:T(8,128)(2,1)S(1)}, u32[]{:S(2)}, u32[]{:S(2)}) collective-permute-start(bf16[240,128]{1,0:T(8,128)(2,1)S(1)} %pad_maximum_fusion.8), channel_id=1, source_target_pairs={{0,12},{1,13},{2,14},{3,15},{4,0},{5,1},{6,2},{7,3},{8,4},{9,5},{1... | collective-permute-start | bytes 184328 | tf_op jit(solution)/shard_map/ppermute | solution.py:302
  79.6 2.0 %collective-permute-start.31 = (bf16[240,128]{1,0:T(8,128)(2,1)S(1)}, bf16[240,128]{1,0:T(8,128)(2,1)S(1)}, u32[]{:S(2)}, u32[]{:S(2)}) collective-permute-start(bf16[240,128]{1,0:T(8,128)(2,1)S(1)} %pad_maximum_fusion.8), channel_id=1, source_target_pairs={{0,4},{1,5},{2,6},{3,7},{4,8},{5,9},{6,10},{7,11},{8,12},{9,13},{1... | collective-permute-start | bytes 184328 | tf_op jit(solution)/shard_map/ppermute | solution.py:302
  81.6 5.3 %collective-permute-done.16 = bf16[288,128]{1,0:T(8,128)(2,1)S(1)} collective-permute-done((bf16[288,128]{1,0:T(8,128)(2,1)S(1)}, bf16[288,128]{1,0:T(8,128)(2,1)S(1)}, u32[]{:S(2)}, u32[]{:S(2)}) %collective-permute-start.16) | collective-permute-done | bytes 73760 | tf_op jit(solution)/shard_map/ppermute | solution.py:302
  90.7 2.3 %collective-permute-start.36 = (bf16[912,128]{1,0:T(8,128)(2,1)S(1)}, bf16[912,128]{1,0:T(8,128)(2,1)S(1)}, u32[]{:S(2)}, u32[]{:S(2)}) collective-permute-start(bf16[912,128]{1,0:T(8,128)(2,1)S(1)} %pad_maximum_fusion.2.refs_8_), channel_id=1, source_target_pairs={{0,3},{1,2},{2,1},{3,0},{4,7},{5,6},{6,5},{7,4},{8,11},{9,10},{10,... | collective-permute-start | bytes 700424 | tf_op jit(solution)/shard_map/ppermute | solution.py:298
  93.0 3.6 %collective-permute-done.19 = bf16[288,128]{1,0:T(8,128)(2,1)S(1)} collective-permute-done((bf16[288,128]{1,0:T(8,128)(2,1)S(1)}, bf16[288,128]{1,0:T(8,128)(2,1)S(1)}, u32[]{:S(2)}, u32[]{:S(2)}) %collective-permute-start.19) | collective-permute-done | bytes 73760 | tf_op jit(solution)/shard_map/ppermute | solution.py:302
  97.5 2.3 %collective-permute-start.23 = (bf16[1152,128]{1,0:T(8,128)(2,1)S(1)}, bf16[1152,128]{1,0:T(8,128)(2,1)S(1)}, u32[]{:S(2)}, u32[]{:S(2)}) collective-permute-start(bf16[1152,128]{1,0:T(8,128)(2,1)S(1)} %bitcast_select_fusion.refs_0_), channel_id=1, source_target_pairs={{0,3},{1,2},{2,1},{3,0},{4,7},{5,6},{6,5},{7,4},{8,11},{9,10},{10,... | collective-permute-start | bytes 884744 | tf_op jit(solution)/shard_map/ppermute | solution.py:298
  103.8 8.7 %collective-permute-done.35.refs_10_ = bf16[912,128]{1,0:T(8,128)(2,1)S(1)} collective-permute-done((bf16[912,128]{1,0:T(8,128)(2,1)S(1)}, bf16[912,128]{1,0:T(8,128)(2,1)S(1)}, u32[]{:S(2)}, u32[]{:S(2)}) %collective-permute-start.35) | collective-permute-done | bytes 233504 | tf_op jit(solution)/shard_map/ppermute | solution.py:298
  113.8 5.0 %collective-permute-done.22.refs_2_ = bf16[1152,128]{1,0:T(8,128)(2,1)S(1)} collective-permute-done((bf16[1152,128]{1,0:T(8,128)(2,1)S(1)}, bf16[1152,128]{1,0:T(8,128)(2,1)S(1)}, u32[]{:S(2)}, u32[]{:S(2)}) %collective-permute-start.22) | collective-permute-done | bytes 294944 | tf_op jit(solution)/shard_map/ppermute | solution.py:298
  123.8 8.0 %shard_map.147 = (bf16[27,192,192]{2,1,0:T(8,128)(2,1)}, bf16[27,192,192]{2,1,0:T(8,128)(2,1)}) custom-call(bf16[1152,128]{1,0:T(8,128)(2,1)S(1)} %bitcast_select_fusion.refs_0_, bf16[1152,128]{1,0:T(8,128)(2,1)S(1)} %collective-permute-done.21.refs_1_, bf16[1152,128]{1,0:T(8,128)(2,1)S(1)} %collective-permute-done.22.refs_2_, ...), custom_call_target="tpu_custom_call" | custom-call | bytes 8388608 | tf_op jit(solution)/shard_map/pallas_call | solution.py:248
  (141 shorter events, 38.7 us)
Async XLA Ops:
  6.5 10.9 %collective-permute-start.2 = (bf16[8,1,32,192]{3,2,1,0:T(8,128)(2,1)S(1)}, bf16[8,1,32,192]{3,2,1,0:T(8,128)(2,1)S(1)}, u32[]{:S(2)}, u32[]{:S(2)}) collective-permute-start(bf16[8,1,32,192]{3,2,1,0:T(8,128)(2,1)S(1)} %pad_maximum_fusion.4), channel_id=1, source_target_pairs={{0,1},{1,2},{2,3},{3,4},{4,5},{5,6},{6,7},{7,8},{8,9},{9,10},{10,1... | collective-permute-start | bytes 294920 | tf_op jit(solution)/shard_map/ppermute | solution.py:261
  13.2 40.0 %collective-permute-start.14 = (bf16[2,4,32,384]{3,2,1,0:T(8,128)(2,1)S(1)}, bf16[2,4,32,384]{3,2,1,0:T(8,128)(2,1)S(1)}, u32[]{:S(2)}, u32[]{:S(2)}) collective-permute-start(bf16[2,4,32,384]{3,2,1,0:T(8,128)(2,1)S(1)} %maximum_select_fusion.1.refs_4_), channel_id=1, source_target_pairs={{0,3},{1,2},{2,1},{3,0},{4,7},{5,6},{6,5},{7,4},{8,11},{9,10},{10,... | collective-permute-start | bytes 589832 | tf_op jit(solution)/shard_map/ppermute | solution.py:298
  16.9 36.4 %collective-permute-start.13 = (bf16[2,4,32,384]{3,2,1,0:T(8,128)(2,1)S(1)}, bf16[2,4,32,384]{3,2,1,0:T(8,128)(2,1)S(1)}, u32[]{:S(2)}, u32[]{:S(2)}) collective-permute-start(bf16[2,4,32,384]{3,2,1,0:T(8,128)(2,1)S(1)} %maximum_select_fusion.1.refs_4_), channel_id=1, source_target_pairs={{0,2},{1,3},{2,0},{3,1},{4,6},{5,7},{6,4},{7,5},{8,10},{9,11},{10,... | collective-permute-start | bytes 589832 | tf_op jit(solution)/shard_map/ppermute | solution.py:298
  33.6 9.9 %collective-permute-start.6 = (bf16[8,1,32,192]{3,2,1,0:T(8,128)(2,1)S(1)}, bf16[8,1,32,192]{3,2,1,0:T(8,128)(2,1)S(1)}, u32[]{:S(2)}, u32[]{:S(2)}) collective-permute-start(bf16[8,1,32,192]{3,2,1,0:T(8,128)(2,1)S(1)} %pad_maximum_fusion.6), channel_id=1, source_target_pairs={{0,1},{1,2},{2,3},{3,4},{4,5},{5,6},{6,7},{7,8},{8,9},{9,10},{10,1... | collective-permute-start | bytes 294920 | tf_op jit(solution)/shard_map/ppermute | solution.py:261
  38.2 8.3 %collective-permute-start.7 = (bf16[8,1,32,192]{3,2,1,0:T(8,128)(2,1)S(1)}, bf16[8,1,32,192]{3,2,1,0:T(8,128)(2,1)S(1)}, u32[]{:S(2)}, u32[]{:S(2)}) collective-permute-start(bf16[8,1,32,192]{3,2,1,0:T(8,128)(2,1)S(1)} %pad_maximum_fusion.7), channel_id=1, source_target_pairs={{1,0},{2,1},{3,2},{4,3},{5,4},{6,5},{7,6},{8,7},{9,8},{10,9},{11,1... | collective-permute-start | bytes 294920 | tf_op jit(solution)/shard_map/ppermute | solution.py:261
  39.7 20.4 %collective-permute-start.11 = (bf16[2,5,32,384]{3,2,1,0:T(8,128)(2,1)S(1)}, bf16[2,5,32,384]{3,2,1,0:T(8,128)(2,1)S(1)}, u32[]{:S(2)}, u32[]{:S(2)}) collective-permute-start(bf16[2,5,32,384]{3,2,1,0:T(8,128)(2,1)S(1)} %pad_maximum_fusion.1.refs_0_), channel_id=1, source_target_pairs={{0,3},{1,2},{2,1},{3,0},{4,7},{5,6},{6,5},{7,4},{8,11},{9,10},{10,... | collective-permute-start | bytes 737288 | tf_op jit(solution)/shard_map/ppermute | solution.py:298
  43.5 16.7 %collective-permute-start.10 = (bf16[2,5,32,384]{3,2,1,0:T(8,128)(2,1)S(1)}, bf16[2,5,32,384]{3,2,1,0:T(8,128)(2,1)S(1)}, u32[]{:S(2)}, u32[]{:S(2)}) collective-permute-start(bf16[2,5,32,384]{3,2,1,0:T(8,128)(2,1)S(1)} %pad_maximum_fusion.1.refs_0_), channel_id=1, source_target_pairs={{0,2},{1,3},{2,0},{3,1},{4,6},{5,7},{6,4},{7,5},{8,10},{9,11},{10,... | collective-permute-start | bytes 737288 | tf_op jit(solution)/shard_map/ppermute | solution.py:298
  46.4 13.7 %collective-permute-start.9 = (bf16[2,5,32,384]{3,2,1,0:T(8,128)(2,1)S(1)}, bf16[2,5,32,384]{3,2,1,0:T(8,128)(2,1)S(1)}, u32[]{:S(2)}, u32[]{:S(2)}) collective-permute-start(bf16[2,5,32,384]{3,2,1,0:T(8,128)(2,1)S(1)} %pad_maximum_fusion.1.refs_0_), channel_id=1, source_target_pairs={{0,1},{1,0},{2,3},{3,2},{4,5},{5,4},{6,7},{7,6},{8,9},{9,8},{10,11... | collective-permute-start | bytes 737288 | tf_op jit(solution)/shard_map/ppermute | solution.py:298
  63.9 12.7 %collective-permute-start.28 = (bf16[224,128]{1,0:T(8,128)(2,1)S(1)}, bf16[224,128]{1,0:T(8,128)(2,1)S(1)}, u32[]{:S(2)}, u32[]{:S(2)}) collective-permute-start(bf16[224,128]{1,0:T(8,128)(2,1)S(1)} %get-tuple-element.37), channel_id=1, source_target_pairs={{0,4},{1,5},{2,6},{3,7},{4,8},{5,9},{6,10},{7,11},{8,12},{9,13},{1... | collective-permute-start | bytes 172040 | tf_op jit(solution)/shard_map/ppermute | solution.py:302
  65.5 11.4 %collective-permute-start.30 = (bf16[224,128]{1,0:T(8,128)(2,1)S(1)}, bf16[224,128]{1,0:T(8,128)(2,1)S(1)}, u32[]{:S(2)}, u32[]{:S(2)}) collective-permute-start(bf16[224,128]{1,0:T(8,128)(2,1)S(1)} %get-tuple-element.38), channel_id=1, source_target_pairs={{0,12},{1,13},{2,14},{3,15},{4,0},{5,1},{6,2},{7,3},{8,4},{9,5},{1... | collective-permute-start | bytes 172040 | tf_op jit(solution)/shard_map/ppermute | solution.py:302
  67.7 9.1 %collective-permute-start.29 = (bf16[224,128]{1,0:T(8,128)(2,1)S(1)}, bf16[224,128]{1,0:T(8,128)(2,1)S(1)}, u32[]{:S(2)}, u32[]{:S(2)}) collective-permute-start(bf16[224,128]{1,0:T(8,128)(2,1)S(1)} %get-tuple-element.39), channel_id=1, source_target_pairs={{0,8},{1,9},{2,10},{3,11},{4,12},{5,13},{6,14},{7,15},{8,0},{9,1},... | collective-permute-start | bytes 172040 | tf_op jit(solution)/shard_map/ppermute | solution.py:302
  76.5 10.4 %collective-permute-start.16 = (bf16[288,128]{1,0:T(8,128)(2,1)S(1)}, bf16[288,128]{1,0:T(8,128)(2,1)S(1)}, u32[]{:S(2)}, u32[]{:S(2)}) collective-permute-start(bf16[288,128]{1,0:T(8,128)(2,1)S(1)} %get-tuple-element.36), channel_id=1, source_target_pairs={{0,8},{1,9},{2,10},{3,11},{4,12},{5,13},{6,14},{7,15},{8,0},{9,1},... | collective-permute-start | bytes 221192 | tf_op jit(solution)/shard_map/ppermute | solution.py:302
  76.9 10.9 %collective-permute-start.33 = (bf16[240,128]{1,0:T(8,128)(2,1)S(1)}, bf16[240,128]{1,0:T(8,128)(2,1)S(1)}, u32[]{:S(2)}, u32[]{:S(2)}) collective-permute-start(bf16[240,128]{1,0:T(8,128)(2,1)S(1)} %pad_maximum_fusion.8), channel_id=1, source_target_pairs={{0,12},{1,13},{2,14},{3,15},{4,0},{5,1},{6,2},{7,3},{8,4},{9,5},{1... | collective-permute-start | bytes 184328 | tf_op jit(solution)/shard_map/ppermute | solution.py:302
  78.8 10.8 %collective-permute-start.32 = (bf16[240,128]{1,0:T(8,128)(2,1)S(1)}, bf16[240,128]{1,0:T(8,128)(2,1)S(1)}, u32[]{:S(2)}, u32[]{:S(2)}) collective-permute-start(bf16[240,128]{1,0:T(8,128)(2,1)S(1)} %pad_maximum_fusion.8), channel_id=1, source_target_pairs={{0,8},{1,9},{2,10},{3,11},{4,12},{5,13},{6,14},{7,15},{8,0},{9,1},... | collective-permute-start | bytes 184328 | tf_op jit(solution)/shard_map/ppermute | solution.py:302
  79.6 9.9 %collective-permute-start.31 = (bf16[240,128]{1,0:T(8,128)(2,1)S(1)}, bf16[240,128]{1,0:T(8,128)(2,1)S(1)}, u32[]{:S(2)}, u32[]{:S(2)}) collective-permute-start(bf16[240,128]{1,0:T(8,128)(2,1)S(1)} %pad_maximum_fusion.8), channel_id=1, source_target_pairs={{0,4},{1,5},{2,6},{3,7},{4,8},{5,9},{6,10},{7,11},{8,12},{9,13},{1... | collective-permute-start | bytes 184328 | tf_op jit(solution)/shard_map/ppermute | solution.py:302
  87.8 8.8 %collective-permute-start.19 = (bf16[288,128]{1,0:T(8,128)(2,1)S(1)}, bf16[288,128]{1,0:T(8,128)(2,1)S(1)}, u32[]{:S(2)}, u32[]{:S(2)}) collective-permute-start(bf16[288,128]{1,0:T(8,128)(2,1)S(1)} %fusion.2), channel_id=1, source_target_pairs={{0,8},{1,9},{2,10},{3,11},{4,12},{5,13},{6,14},{7,15},{8,0},{9,1},... | collective-permute-start | bytes 221192 | tf_op jit(solution)/shard_map/ppermute | solution.py:302
  87.8 8.8 %collective-permute-start.18 = (bf16[288,128]{1,0:T(8,128)(2,1)S(1)}, bf16[288,128]{1,0:T(8,128)(2,1)S(1)}, u32[]{:S(2)}, u32[]{:S(2)}) collective-permute-start(bf16[288,128]{1,0:T(8,128)(2,1)S(1)} %fusion.2), channel_id=1, source_target_pairs={{0,4},{1,5},{2,6},{3,7},{4,8},{5,9},{6,10},{7,11},{8,12},{9,13},{1... | collective-permute-start | bytes 221192 | tf_op jit(solution)/shard_map/ppermute | solution.py:302
  90.5 10.5 %collective-permute-start.37 = (bf16[912,128]{1,0:T(8,128)(2,1)S(1)}, bf16[912,128]{1,0:T(8,128)(2,1)S(1)}, u32[]{:S(2)}, u32[]{:S(2)}) collective-permute-start(bf16[912,128]{1,0:T(8,128)(2,1)S(1)} %pad_maximum_fusion.2.refs_8_), channel_id=1, source_target_pairs={{0,16},{16,0},{1,17},{17,1},{2,18},{18,2},{3,19},{19,3},{4,20},{20... | collective-permute-start | bytes 700424 | tf_op jit(solution)/shard_map/ppermute | solution.py:411
  90.7 11.6 %collective-permute-start.36 = (bf16[912,128]{1,0:T(8,128)(2,1)S(1)}, bf16[912,128]{1,0:T(8,128)(2,1)S(1)}, u32[]{:S(2)}, u32[]{:S(2)}) collective-permute-start(bf16[912,128]{1,0:T(8,128)(2,1)S(1)} %pad_maximum_fusion.2.refs_8_), channel_id=1, source_target_pairs={{0,3},{1,2},{2,1},{3,0},{4,7},{5,6},{6,5},{7,4},{8,11},{9,10},{10,... | collective-permute-start | bytes 700424 | tf_op jit(solution)/shard_map/ppermute | solution.py:298
  97.5 15.8 %collective-permute-start.23 = (bf16[1152,128]{1,0:T(8,128)(2,1)S(1)}, bf16[1152,128]{1,0:T(8,128)(2,1)S(1)}, u32[]{:S(2)}, u32[]{:S(2)}) collective-permute-start(bf16[1152,128]{1,0:T(8,128)(2,1)S(1)} %bitcast_select_fusion.refs_0_), channel_id=1, source_target_pairs={{0,3},{1,2},{2,1},{3,0},{4,7},{5,6},{6,5},{7,4},{8,11},{9,10},{10,... | collective-permute-start | bytes 884744 | tf_op jit(solution)/shard_map/ppermute | solution.py:298
  99.8 12.8 %collective-permute-start.35 = (bf16[912,128]{1,0:T(8,128)(2,1)S(1)}, bf16[912,128]{1,0:T(8,128)(2,1)S(1)}, u32[]{:S(2)}, u32[]{:S(2)}) collective-permute-start(bf16[912,128]{1,0:T(8,128)(2,1)S(1)} %pad_maximum_fusion.2.refs_8_), channel_id=1, source_target_pairs={{0,2},{1,3},{2,0},{3,1},{4,6},{5,7},{6,4},{7,5},{8,10},{9,11},{10,... | collective-permute-start | bytes 700424 | tf_op jit(solution)/shard_map/ppermute | solution.py:298
  100.5 12.7 %collective-permute-start.34 = (bf16[912,128]{1,0:T(8,128)(2,1)S(1)}, bf16[912,128]{1,0:T(8,128)(2,1)S(1)}, u32[]{:S(2)}, u32[]{:S(2)}) collective-permute-start(bf16[912,128]{1,0:T(8,128)(2,1)S(1)} %pad_maximum_fusion.2.refs_8_), channel_id=1, source_target_pairs={{0,1},{1,0},{2,3},{3,2},{4,5},{5,4},{6,7},{7,6},{8,9},{9,8},{10,11... | collective-permute-start | bytes 700424 | tf_op jit(solution)/shard_map/ppermute | solution.py:298
  101.0 17.8 %collective-permute-start.22 = (bf16[1152,128]{1,0:T(8,128)(2,1)S(1)}, bf16[1152,128]{1,0:T(8,128)(2,1)S(1)}, u32[]{:S(2)}, u32[]{:S(2)}) collective-permute-start(bf16[1152,128]{1,0:T(8,128)(2,1)S(1)} %bitcast_select_fusion.refs_0_), channel_id=1, source_target_pairs={{0,2},{1,3},{2,0},{3,1},{4,6},{5,7},{6,4},{7,5},{8,10},{9,11},{10,... | collective-permute-start | bytes 884744 | tf_op jit(solution)/shard_map/ppermute | solution.py:298
  102.3 16.5 %collective-permute-start.21 = (bf16[1152,128]{1,0:T(8,128)(2,1)S(1)}, bf16[1152,128]{1,0:T(8,128)(2,1)S(1)}, u32[]{:S(2)}, u32[]{:S(2)}) collective-permute-start(bf16[1152,128]{1,0:T(8,128)(2,1)S(1)} %bitcast_select_fusion.refs_0_), channel_id=1, source_target_pairs={{0,1},{1,0},{2,3},{3,2},{4,5},{5,4},{6,7},{7,6},{8,9},{9,8},{10,11... | collective-permute-start | bytes 884744 | tf_op jit(solution)/shard_map/ppermute | solution.py:298
  (31 other events, 170.0 us)

commit v3 on v2

v3 whole, which is shorter than its diff:
```python
import functools

import jax
import jax.numpy as jnp
from jax import lax
from jax.experimental import pallas as pl
from jax.experimental.pallas import tpu as pltpu
from jax.sharding import PartitionSpec as P

epsilon = 1e-06
bf16 = jnp.bfloat16
f32 = jnp.float32
chunks = ((0, 3), (3, 4))
taps_each = 7
taps_all = 27


def shift_cols(value, by):
    zero = jnp.zeros_like(value[:, :1])
    if by == 1:
        return jnp.concatenate([value[:, 1:], zero], axis=1)
    return jnp.concatenate([zero, value[:, :-1]], axis=1)


def norm_parts(vals, gain):
    scale = lax.rsqrt(jnp.mean(vals * vals, axis=-1, keepdims=True) + epsilon)
    normed = vals * scale
    lifted = normed * gain
    return scale, normed, lifted, jax.nn.sigmoid(lifted)


def norm_silu(vals, gain):
    _, _, lifted, sig = norm_parts(vals, gain)
    return lifted * sig


def norm_silu_back(grad, vals, gain):
    scale, normed, lifted, sig = norm_parts(vals, gain)
    d_lift = grad * sig * (1.0 + lifted * (1.0 - sig))
    d_gain = jnp.sum(d_lift * normed, axis=0, keepdims=True)
    d_norm = d_lift * gain
    d_vals = scale * (d_norm - normed * jnp.mean(d_norm * normed, axis=-1, keepdims=True))
    return d_vals, d_gain


def conv(window, weight, frames, rows, back):
    cols, chans = window.shape[2], window.shape[3]
    parts = [None] * 3
    for t in range(3):
        for h in range(3):
            t0, h0 = (2 - t, 2 - h) if back else (t, h)
            piece = window[t0 : t0 + frames, h0 : h0 + rows].reshape(frames * rows * cols, chans)
            for k in range(3):
                dims = (((1,), (1 if back else 0,)), ((), ()))
                prod = lax.dot_general(piece, weight[t, h, k], dims, preferred_element_type=f32)
                parts[k] = prod if parts[k] is None else parts[k] + prod
    parts = [part.reshape(frames * rows, cols, chans) for part in parts]
    sign = -1 if back else 1
    total = parts[1] + shift_cols(parts[0], -sign) + shift_cols(parts[2], sign)
    return total.reshape(frames * rows * cols, chans)


def fill_rows(window, at, edges, row):
    chans = window.shape[3]
    for f in range(2):
        window[at + f, row] = edges[:, f * chans : (f + 1) * chans]


def fill_edges(ahead, behind, above, below, passed_ahead, passed_behind):
    last = ahead.shape[1] - 1
    for row, own, i in ((0, above, 0), (last, below, 1)):
        fill_rows(ahead, 2, own[0], row)
        fill_rows(behind, 0, own[1], row)
        fill_rows(ahead, 0, passed_ahead[i], row)
        fill_rows(behind, 2, passed_behind[i], row)


def fill_packed(window, at, packed):
    rows, chans = packed.shape[0], window.shape[3]
    for f in range(2):
        window[at + f, 1 : rows + 1] = packed[..., f * chans : (f + 1) * chans]


def started(copies, sems):
    made = [pltpu.make_async_copy(src, dst, sems.at[i]) for i, (src, dst) in enumerate(copies)]
    for copy in made:
        copy.start()
    return made


def pack_frames(values):
    return jnp.concatenate([values[0], values[1]], axis=-1)


def first_kernel(
    feat_any, earlier_any, cot_any, later_any, above_ref, below_ref, pa_ref, pb_ref, w1_any, w2_any, b1_any, g1_any, g2_any,
    act2_ref, gmid_ref, give_ref, keep_ref, sums_ref, ahead, behind, w1, w2, b1, g1, g2, sems,
):
    frames, rows, cols, chans = feat_any.shape
    own = pl.ds(1, rows)
    copies = started(
        (
            (feat_any, ahead.at[pl.ds(2, 2), own]),
            (earlier_any, ahead.at[pl.ds(0, 2), own]),
            (g1_any, g1),
            (w1_any, w1),
            (b1_any, b1),
            (g2_any, g2),
            (cot_any, behind.at[pl.ds(0, 2), own]),
            (later_any, behind.at[pl.ds(2, 2), own]),
            (w2_any, w2),
        ),
        sems,
    )
    fill_edges(ahead, behind, above_ref, below_ref, pa_ref, pb_ref)
    for copy in copies[:3]:
        copy.wait()
    for f in range(frames + 2):
        vals = ahead[f].astype(f32).reshape(-1, chans)
        ahead[f] = norm_silu(vals, g1[...]).astype(bf16).reshape(rows + 2, cols, chans)
    for copy in copies[3:6]:
        copy.wait()
    mid = (conv(ahead, w1, frames, rows, False) + b1[...]).astype(bf16).astype(f32)
    act2 = norm_silu(mid, g2[...]).astype(bf16).reshape(frames, rows, cols, chans)
    act2 = pack_frames(act2)
    act2_ref[...] = act2
    for copy in copies[6:]:
        copy.wait()
    grad = conv(behind, w2, frames, rows, True)
    gmid, d_gain = norm_silu_back(grad, mid, g2[...])
    gmid = gmid.astype(bf16)
    cot = behind[:2, 1 : rows + 1].astype(f32).reshape(-1, chans)
    sums_ref[...] = jnp.concatenate(
        [
            d_gain,
            jnp.sum(gmid.astype(f32), axis=0, keepdims=True),
            jnp.sum(cot, axis=0, keepdims=True),
            jnp.zeros((5, chans), f32),
        ],
        axis=0,
    )
    gmid = pack_frames(gmid.reshape(frames, rows, cols, chans))
    gmid_ref[...] = gmid
    odd = lax.axis_index("tm") % 2 == 1

    @pl.when(odd)
    def _():
        give_ref[...] = act2
        keep_ref[...] = gmid

    @pl.when(jnp.logical_not(odd))
    def _():
        give_ref[...] = gmid
        keep_ref[...] = act2


def last_kernel(
    act2_ref, earlier_ref, gmid_ref, later_ref, above_ref, below_ref, pa_ref, pb_ref,
    feat_any, cot_any, w1_any, w2_any, b2_any, g1_any,
    out_ref, gin_ref, sums_ref, ahead, behind, feat, cot, w1, w2, b2, g1, sems,
):
    frames, rows, cols, chans = out_ref.shape
    copies = started(
        ((w2_any, w2), (b2_any, b2), (feat_any, feat), (w1_any, w1), (cot_any, cot), (g1_any, g1)), sems
    )
    fill_packed(ahead, 0, earlier_ref)
    fill_packed(ahead, 2, act2_ref)
    fill_packed(behind, 0, gmid_ref)
    fill_packed(behind, 2, later_ref)
    fill_edges(ahead, behind, above_ref, below_ref, pa_ref, pb_ref)
    for copy in copies[:3]:
        copy.wait()
    values = feat[...].astype(f32).reshape(-1, chans)
    out = values + conv(ahead, w2, frames, rows, False) + b2[...]
    out_ref[...] = out.astype(bf16).reshape(out_ref.shape)
    for copy in copies[3:]:
        copy.wait()
    grad = conv(behind, w1, frames, rows, True)
    d_vals, d_gain = norm_silu_back(grad, values, g1[...])
    gin = d_vals + cot[...].astype(f32).reshape(-1, chans)
    gin_ref[...] = gin.astype(bf16).reshape(gin_ref.shape)
    sums_ref[...] = jnp.concatenate([d_gain, jnp.zeros((7, chans), f32)], axis=0)


def pack_rows(chans):
    return chans + chans // 2


def wgrad_kernel(blocks, taps, passes, *refs):
    xs, ys = refs[:4], refs[4:8]
    gain_ref, refs = refs[8], refs[9:]
    if passes:
        (one_ref, two_ref, out_ref, up_ref, down_ref), refs = refs[:5], refs[5:]
        for i, ref in enumerate((one_ref, two_ref)):
            up_ref[i] = ref[ref.shape[0] - 1]
            down_ref[i] = ref[0]
    else:
        out_ref, refs = refs[0], refs[1:]
    plane, xk = refs
    _, rows, cols, _ = ys[0].shape
    chans = gain_ref.shape[1]
    tall = 4 * rows
    cells = 4 * tall * cols
    odd = lax.axis_index("tm") % 2 == 1
    p = lax.axis_index("height") % 4
    single = blocks == 2
    start = jnp.where(odd, 2, 0) if single else 0
    if single:
        plane[pl.ds(jnp.where(odd, 0, 4), 2)] = jnp.zeros((2,) + plane.shape[1:], bf16)

    def put_y(values, row, count):
        for b in range(blocks):
            for f in range(2):
                part = values[b, :, :, f * chans : (f + 1) * chans]
                place = (start + 2 * b + f, pl.ds(row, count))

                @pl.when(odd)
                def _():
                    flat = part.astype(f32).reshape(-1, chans)
                    plane[place] = norm_silu(flat, gain_ref[...]).astype(bf16).reshape(part.shape)

                @pl.when(jnp.logical_not(odd))
                def _():
                    plane[place] = part

    for d in range(4):
        at = p ^ d
        put_y(ys[d][...], 1 + rows * at, rows)
        for b in range(2):
            for f in range(2):
                part = xs[d][b, :rows, :, f * chans : (f + 1) * chans]
                wide = part.astype(f32)
                place = (2 * b + f, pl.ds(rows * at, rows))
                xk[(0,) + place] = shift_cols(wide, 1).astype(bf16)
                xk[(1,) + place] = part
                xk[(2,) + place] = shift_cols(wide, -1).astype(bf16)

        @pl.when(at == 0)
        def _():
            put_y(xs[d][:, rows:], 0, 1)

        @pl.when(at == 3)
        def _():
            put_y(xs[d][:, rows:], tall + 1, 1)

    step = pack_rows(chans)
    dims = (((0,), (0,)), ((), ()))
    first, count = taps
    half = chans // 2

    def store(base, grad):
        grad = grad.astype(bf16)
        out_ref[base : base + chans] = grad[:, :128]
        out_ref[base + chans : base + step] = jnp.concatenate(
            [grad[:half, 128:], grad[half:, 128:]], axis=1
        )

    for j in range(count):
        tap = jnp.minimum(p * taps_each + first + j, taps_all - 1)
        t, h, k = tap // 9, tap // 3 % 3, tap % 3

        @pl.when(odd)
        def _():
            piece = plane[pl.ds(t, 4), pl.ds(h, tall)].reshape(cells, chans)
            x = xk[k].reshape(cells, chans)
            store(j * step, lax.dot_general(piece, x, dims, preferred_element_type=f32))

        @pl.when(jnp.logical_not(odd))
        def _():
            piece = plane[pl.ds(2 - t, 4), pl.ds(2 - h, tall)].reshape(cells, chans)
            x = xk[2 - k].reshape(cells, chans)
            store(j * step, lax.dot_general(x, piece, dims, preferred_element_type=f32))

    used = count * step
    if used < out_ref.shape[0]:
        out_ref[used:] = jnp.zeros((out_ref.shape[0] - used, 128), bf16)


def unpack_kernel(taps, held, *refs):
    pieces = refs[:8]
    outs, stage, sems = refs[8 + 2 * held : 10 + 2 * held], refs[-2], refs[-1]
    first, count = taps
    chans = stage.shape[1]
    half = chans // 2
    step = pack_rows(chans)
    odd = lax.axis_index("tm") % 2 == 1
    p = lax.axis_index("height") % 4
    made = []
    for n, src in enumerate(pieces):
        for j in range(count):
            tap = (p ^ (n % 4)) * taps_each + first + j
            slot = n * count + j
            high = src[j * step + chans : (j + 1) * step]
            stage[slot, :, :128] = src[j * step : j * step + chans]
            stage[slot, :half, 128:] = high[:, : chans - 128]
            stage[slot, half:, 128:] = high[:, chans - 128 :]
            real = tap < taps_all
            tap = jnp.minimum(tap, taps_all - 1)
            for which in range(2):
                good = odd if (which == 0) == (n < 4) else jnp.logical_not(odd)
                good = jnp.logical_and(good, real)
                copy = pltpu.make_async_copy(stage.at[slot], outs[which].at[tap], sems.at[slot])
                pl.when(good)(copy.start)
                made.append((good, copy))
    for good, copy in made:
        pl.when(good)(copy.wait)


vmem = pl.BlockSpec(memory_space=pltpu.VMEM)
anywhere = pl.BlockSpec(memory_space=pl.ANY)


def call(kernel, outs, args, flops, scratch=(), free=(), out_spec=vmem, **kw):
    return pl.pallas_call(
        kernel,
        out_shape=outs,
        in_specs=[anywhere if i in free else vmem for i in range(len(args))],
        out_specs=[out_spec] * len(outs),
        scratch_shapes=list(scratch),
        compiler_params=pltpu.CompilerParams(vmem_limit_bytes=50 * 2**20),
        cost_estimate=pl.CostEstimate(flops=flops, bytes_accessed=8 * 2**20, transcendentals=0),
        **kw,
    )(*args)


def moved(value, axis, by):
    size = lax.axis_size(axis)
    return lax.ppermute(value, axis, [(i, i + by) for i in range(size) if 0 <= i + by < size])


def edge_parts(up, down):
    above = moved(up, "height", 1)
    below = moved(down, "height", -1)
    passed_ahead = moved(jnp.stack([above[0], below[0]]), "tm", 1)
    passed_behind = moved(jnp.stack([above[1], below[1]]), "tm", -1)
    return above, below, passed_ahead, passed_behind


def total_of(pieces):
    return functools.reduce(lambda a, b: a + b, [p.astype(f32) for p in pieces])


def piece_at(value, index):
    return lax.dynamic_index_in_dim(value, index, 0, keepdims=False)


def body(features, weight_one, bias_one, gain_one, weight_two, bias_two, gain_two, cotangent):
    frames, rows, cols, chans = features.shape
    tm, height = lax.axis_size("tm"), lax.axis_size("height")
    planes = height // 4
    c, me = lax.axis_index("tm"), lax.axis_index("height")
    odd = c % 2 == 1
    p, q = me % 4, me // 4
    swap = [(i, i ^ 1) for i in range(tm)]
    line = lambda v: v.reshape(1, chans)
    local = jax.ShapeDtypeStruct(features.shape, bf16)
    sums = jax.ShapeDtypeStruct((8, chans), f32)
    flops = 4 * frames * rows * cols * 27 * chans * chans
    window = pltpu.VMEM((frames + 2, rows + 2, cols, chans), bf16)
    weight = pltpu.VMEM(weight_one.shape, bf16)
    vector = pltpu.VMEM((1, chans), f32)
    packed_shape = jax.ShapeDtypeStruct((rows, cols, 2 * chans), bf16)
    edge_shape = jax.ShapeDtypeStruct((2, cols, 2 * chans), bf16)

    def plane_move(value, d):
        return lax.ppermute(value, "height", [(i, i ^ d) for i in range(height)])

    def column_move(value, d):
        pairs = [(z * 4 + j, (z + d) % planes * 4 + j) for z in range(planes) for j in range(4)]
        return lax.ppermute(value, "height", pairs)

    up = jnp.stack([pack_frames(v[:, -1]) for v in (features, cotangent)])
    down = jnp.stack([pack_frames(v[:, 0]) for v in (features, cotangent)])
    above, below, passed_ahead, passed_behind = edge_parts(up, down)
    earlier, later = moved(features, "tm", 1), moved(cotangent, "tm", -1)

    top = p == 0
    odd_y = [pack_frames(earlier), pack_frames(features)]
    even_y = [pack_frames(cotangent), pack_frames(later)]
    near = jnp.where(top, above, below)
    odd_edge = [jnp.where(top, passed_ahead[0], passed_ahead[1]), near[0]]
    even_edge = [near[1], jnp.where(top, passed_behind[0], passed_behind[1])]
    if tm > 2:
        extra = lax.ppermute(jnp.where(odd, even_y[1], odd_y[0]), "tm", swap)
        odd_y, even_y = [extra, *odd_y], [*even_y, extra]
        extra = lax.ppermute(jnp.where(odd, even_edge[1], odd_edge[0]), "tm", swap)
        odd_edge, even_edge = [extra, *odd_edge], [*even_edge, extra]
    blocks = len(odd_y)
    y_own = jnp.where(odd, jnp.stack(odd_y), jnp.stack(even_y))
    ys = [y_own] + [plane_move(y_own, d) for d in (1, 2, 3)]
    edge = jnp.where(odd, jnp.stack(odd_edge), jnp.stack(even_edge))[:, None]

    act2, gmid, give, keep, sums_one = call(
        first_kernel,
        (packed_shape,) * 4 + (sums,),
        (
            features, earlier, cotangent, later, above, below, passed_ahead, passed_behind,
            weight_one, weight_two, line(bias_one), line(gain_one), line(gain_two),
        ),
        flops,
        [window, window, weight, weight, vector, vector, vector, pltpu.SemaphoreType.DMA((9,))],
        free=(0, 1, 2, 3, 8, 9, 10, 11, 12),
    )
    other = lax.ppermute(give, "tm", swap)
    x_own = jnp.where(odd, jnp.stack([other, keep]), jnp.stack([keep, other]))
    if blocks > 2:
        x_own = jnp.concatenate([x_own, jnp.zeros((blocks - 2, *x_own.shape[1:]), bf16)])
    x_own = jnp.concatenate([x_own, edge], axis=1)
    xs = [x_own] + [plane_move(x_own, d) for d in (1, 2, 3)]

    earlier2, later2 = moved(act2, "tm", 1), moved(gmid, "tm", -1)

    step = pack_rows(chans)
    unit = 16 * planes
    cells = (2 * frames, 4 * rows, cols, chans)
    parts = []
    for n, taps in enumerate(chunks):
        packed = -(-taps[1] * step // unit) * unit
        passes = n == 0
        flat, *ends = call(
            functools.partial(wgrad_kernel, blocks, taps, passes),
            (jax.ShapeDtypeStruct((packed, 128), bf16),) + (edge_shape,) * (2 * passes),
            (*xs, *ys, line(gain_one)) + (act2, gmid) * passes,
            flops // 2,
            [
                pltpu.VMEM((2 * frames + 2, 4 * rows + 2, cols, chans), bf16),
                pltpu.VMEM((3, *cells), bf16),
            ],
        )
        if passes:
            edges2 = edge_parts(*ends)
        flat = flat.reshape(planes, packed // planes, 128)
        arrived = [column_move(piece_at(flat, (q + d) % planes), d) for d in range(1, planes)]
        part = total_of([piece_at(flat, q), *arrived])
        hop = 2
        while hop < tm:
            part = part + lax.ppermute(part, "tm", [(i, i ^ hop) for i in range(tm)])
            hop *= 2
        parts.append(part.astype(bf16))

    local_scratch = pltpu.VMEM(features.shape, bf16)
    block_out, grad_input, sums_two = call(
        last_kernel,
        (local, local, sums),
        (
            act2, earlier2, gmid, later2, *edges2, features, cotangent,
            weight_one, weight_two, line(bias_two), line(gain_one),
        ),
        flops,
        [
            window, window, local_scratch, local_scratch, weight, weight, vector, vector,
            pltpu.SemaphoreType.DMA((6,)),
        ],
        free=(8, 9, 10, 11, 12, 13),
    )

    small = jnp.concatenate([sums_one[:3], sums_two[:1]]).reshape(-1, 128)
    count = small.shape[0]

    def with_small(value, small):
        high = small.astype(bf16)
        low = (small - high.astype(f32)).astype(bf16)
        pad = jnp.zeros((-2 * count % 16, 128), bf16)
        return jnp.concatenate([value, high, low, pad])

    def without_small(pieces, rows):
        total = total_of([v[rows : rows + count].astype(f32) + v[rows + count : rows + 2 * count].astype(f32) for v in pieces])
        return [v[:rows] for v in pieces], total

    hop = 2
    while hop < tm:
        small = small + lax.ppermute(small, "tm", [(i, i ^ hop) for i in range(tm)])
        hop *= 2

    gradient = jax.ShapeDtypeStruct((taps_all, chans, chans), bf16)
    grads = ()
    for n, (part, taps) in enumerate(zip(parts, chunks)):
        last = n == len(parts) - 1
        size = part.shape[0]
        send = with_small(part, small) if last else part
        got = [send] + [column_move(send, d) for d in range(1, planes)]
        if last:
            got, small = without_small(got, size)
        stack = jnp.stack(got)
        quarter = jnp.take(stack, (q - jnp.arange(planes)) % planes, axis=0).reshape(-1, 128)
        size = quarter.shape[0]
        send = with_small(quarter, small) if last else quarter
        got = [send] + [plane_move(send, d) for d in (1, 2, 3)]
        others = [lax.ppermute(g, "tm", swap) for g in got]
        if last:
            _, small = without_small(got + others, size)
        held = len(grads) > 0
        grads = call(
            functools.partial(unpack_kernel, taps, held),
            (gradient, gradient),
            (*got, *others, *grads),
            0,
            [pltpu.VMEM((8 * taps[1], chans, chans), bf16), pltpu.SemaphoreType.DMA((8 * taps[1],))],
            free=(8, 9),
            out_spec=anywhere,
            input_output_aliases={8: 0, 9: 1} if held else {},
        )
    grad_one, grad_two = grads
    shape = weight_one.shape
    small = small.reshape(4, chans).astype(bf16)
    return (
        block_out,
        grad_input,
        grad_one.reshape(shape),
        grad_two.reshape(shape),
        small[1],
        small[2],
        small[3],
        small[0],
    )


def solution(mesh):
    split = P("tm", "height", None, None)
    return jax.shard_map(
        body,
        mesh=mesh,
        in_specs=(split, P(), P(), P(), P(), P(), P(), split),
        out_specs=(split, split, P(), P(), P(), P(), P(), P()),
        check_vma=False,
    )
```

time: 132 us -> 146 us (1.11)
  waiting for transfers between devices: 36.2 us -> 44 us
  starting transfers between devices: 55.6 us -> 63 us
    ppermute x8 -> x12, starting transfers between devices: 18 us -> 27.5 us  [moved(): lax.ppermute(value, axis, [(i, i + by) for i in range(size) if 0 <= i + b...]
    ppermute x12, waiting for transfers between devices: 21.4 us -> 30.2 us  [plane_move(): return lax.ppermute(value, 'height', [(i, i ^ d) for i in range(height)])]
    ppermute x12, starting transfers between devices: 19 us -> 14 us  [plane_move(): return lax.ppermute(value, 'height', [(i, i ^ d) for i in range(height)])]
    ppermute x12, starting transfers between devices: 15.6 us -> 20.2 us  [column_move(): return lax.ppermute(value, 'height', pairs)]
    squeeze x0 -> x6, local copies, waits for them, and re-layouts: none -> 3.34 us  [pack_frames(): return jnp.concatenate([values[0], values[1]], axis=-1)]
    unnamed x28 -> x22, local copies, waits for them, and re-layouts: 8.86 us -> 5.62 us
    ppermute x12, waiting for transfers between devices: 9.45 us -> 7.11 us  [column_move(): return lax.ppermute(value, 'height', pairs)]
    ppermute x8, waiting for transfers between devices: 0.02 us -> 1.77 us  [body(): others = [lax.ppermute(g, 'tm', swap) for g in got]]
  transfers between devices with their start and end apart: 41 -> 45, of which waited for: 11 -> 14; matrix products, arithmetic and copies ran while one was open for 4% -> 5% of each run, Pallas kernels for 10% -> 12%
where the time goes in v3:
time: 146 us; the launch traced here: 145 us
  starting transfers between devices  63 us (43%)
  waiting for transfers between devices  44 us (30%)
  Pallas kernels  23.9 us (16%)
  local copies, waits for them, and re-layouts  11.6 us (8%)
  between operations  1.55 us (1%)
    ppermute x12, waiting for transfers between devices, plane_move(): return lax.ppermute(value, 'height', [(i, i ^ d) for i in range(height)])  30.2 us
    ppermute x12, starting transfers between devices, moved(): lax.ppermute(value, axis, [(i, i + by) for i in range(size) if 0 <= i + b...  27.5 us
    pallas_call x6, Pallas kernels, call(): pl.pallas_call(kernel, out_shape=outs, in_specs=[anywhere if i in free el...  23.9 us
    ppermute x12, starting transfers between devices, column_move(): return lax.ppermute(value, 'height', pairs)  20.2 us
    ppermute x12, starting transfers between devices, plane_move(): return lax.ppermute(value, 'height', [(i, i ^ d) for i in range(height)])  14 us
    ppermute x12, waiting for transfers between devices, column_move(): return lax.ppermute(value, 'height', pairs)  7.11 us
    unnamed x22, local copies, waits for them, and re-layouts  5.62 us
    ppermute x12, waiting for transfers between devices, moved(): lax.ppermute(value, axis, [(i, i + by) for i in range(size) if 0 <= i + b...  4.95 us
  transfers between devices with their start and end apart: 45, of which 14 were waited for; matrix products, arithmetic and copies ran while one was open for 5% of the time, Pallas kernels for 12%

profile of v3, /device:TPU:0, one launch (start us, length us, event | category | flops | bytes accessed | tf_op | source)
XLA Modules:
  0.0 145.3 jit_solution(4062661360560619735)
XLA Ops:
  0.6 2.4 %collective-permute-start = (bf16[2,4,32,192]{3,2,1,0:T(8,128)(2,1)}, bf16[2,4,32,192]{3,2,1,0:T(8,128)(2,1)S(1)}, u32[]{:S(2)}, u32[]{:S(2)}) collective-permute-start(bf16[2,4,32,192]{3,2,1,0:T(8,128)(2,1)} %feat_any.3), channel_id=1, source_target_pairs={{0,16},{1,17},{2,18},{3,19},{4,20},{5,21},{6,22},{7,23},{8,24},{9,... | collective-permute-start | bytes 294920 | tf_op jit(solution)/shard_map/ppermute | solution.py:328
  6.0 4.2 %collective-permute-start.2 = (bf16[2,32,384]{2,1,0:T(8,128)(2,1)S(1)}, bf16[2,32,384]{2,1,0:T(8,128)(2,1)S(1)}, u32[]{:S(2)}, u32[]{:S(2)}) collective-permute-start(bf16[2,32,384]{2,1,0:T(8,128)(2,1)S(1)} %pad_maximum_fusion.4), channel_id=1, source_target_pairs={{0,1},{1,2},{2,3},{3,4},{4,5},{5,6},{6,7},{7,8},{8,9},{9,10},{10,1... | collective-permute-start | bytes 147464 | tf_op jit(solution)/shard_map/ppermute | solution.py:328
  13.5 3.1 %collective-permute-done.3.below_ref = bf16[2,32,384]{2,1,0:T(8,128)(2,1)S(1)} collective-permute-done((bf16[2,32,384]{2,1,0:T(8,128)(2,1)S(1)}, bf16[2,32,384]{2,1,0:T(8,128)(2,1)S(1)}, u32[]{:S(2)}, u32[]{:S(2)}) %collective-permute-start.3) | collective-permute-done | bytes 49184 | tf_op jit(solution)/shard_map/ppermute | solution.py:328
  16.7 1.9 %collective-permute-start.4 = (bf16[2,32,384]{2,1,0:T(8,128)(2,1)S(1)}, bf16[2,32,384]{2,1,0:T(8,128)(2,1)S(1)}, u32[]{:S(2)}, u32[]{:S(2)}) collective-permute-start(bf16[2,32,384]{2,1,0:T(8,128)(2,1)S(1)} %pad_maximum_fusion.6), channel_id=1, source_target_pairs={{0,16},{1,17},{2,18},{3,19},{4,20},{5,21},{6,22},{7,23},{8,24},{9,... | collective-permute-start | bytes 147464 | tf_op jit(solution)/shard_map/ppermute | solution.py:328
  27.4 5.3 %shard_map.143 = (bf16[4,32,384]{2,1,0:T(8,128)(2,1)S(1)}, bf16[4,32,384]{2,1,0:T(8,128)(2,1)S(1)}, bf16[4,32,384]{2,1,0:T(8,128)(2,1)S(1)}, bf16[4,32,384]{2,1,0:T(8,128)(2,1)S(1)}, f32[8,192]{1,0:T(8,128)S(1)}) custom-call(bf16[2,4,32,192]{3,2,1,0:T(8,128)(2,1)S(1)} %copy-done.2, bf16[2,4,32,192]{3,2,1,0:T(8,128)(2,1)S(1)} %collective-permute-done.earlier_any, ...), custom_call_target="tpu_custom_call" | custom-call | flops 1019215872 | bytes 8388608 | tf_op jit(solution)/shard_map/pallas_call | solution.py:314
  33.1 4.3 %collective-permute-start.14 = (bf16[2,4,32,384]{3,2,1,0:T(8,128)(2,1)S(1)}, bf16[2,4,32,384]{3,2,1,0:T(8,128)(2,1)S(1)}, u32[]{:S(2)}, u32[]{:S(2)}) collective-permute-start(bf16[2,4,32,384]{3,2,1,0:T(8,128)(2,1)S(1)} %maximum_select_fusion.1.refs_4_), channel_id=1, source_target_pairs={{0,3},{1,2},{2,1},{3,0},{4,7},{5,6},{6,5},{7,4},{8,11},{9,10},{10,... | collective-permute-start | bytes 589832 | tf_op jit(solution)/shard_map/ppermute | solution.py:366
  38.4 2.7 %collective-permute-start.9 = (bf16[2,5,32,384]{3,2,1,0:T(8,128)(2,1)S(1)}, bf16[2,5,32,384]{3,2,1,0:T(8,128)(2,1)S(1)}, u32[]{:S(2)}, u32[]{:S(2)}) collective-permute-start(bf16[2,5,32,384]{3,2,1,0:T(8,128)(2,1)S(1)} %pad_maximum_fusion.1.refs_0_), channel_id=1, source_target_pairs={{0,1},{1,0},{2,3},{3,2},{4,5},{5,4},{6,7},{7,6},{8,9},{9,8},{10,11... | collective-permute-start | bytes 737288 | tf_op jit(solution)/shard_map/ppermute | solution.py:366
  44.4 13.3 %collective-permute-done.13.refs_6_ = bf16[2,4,32,384]{3,2,1,0:T(8,128)(2,1)S(1)} collective-permute-done((bf16[2,4,32,384]{3,2,1,0:T(8,128)(2,1)S(1)}, bf16[2,4,32,384]{3,2,1,0:T(8,128)(2,1)S(1)}, u32[]{:S(2)}, u32[]{:S(2)}) %collective-permute-start.13) | collective-permute-done | bytes 196640 | tf_op jit(solution)/shard_map/ppermute | solution.py:366
  57.6 1.9 %collective-permute-start.6 = (bf16[4,32,384]{2,1,0:T(8,128)(2,1)S(1)}, bf16[4,32,384]{2,1,0:T(8,128)(2,1)S(1)}, u32[]{:S(2)}, u32[]{:S(2)}) collective-permute-start(bf16[4,32,384]{2,1,0:T(8,128)(2,1)S(1)} %get-tuple-element.23.refs_9_.act2_ref), channel_id=1, source_target_pairs={{0,16},{1,17},{2,18},{3,19},{4,20},{5,21},{6,22},{7,23},{8,24},{9,... | collective-permute-start | bytes 294920 | tf_op jit(solution)/shard_map/ppermute | solution.py:328
  61.2 3.9 %shard_map.144 = (bf16[896,128]{1,0:T(8,128)(2,1)S(1)}, bf16[2,32,384]{2,1,0:T(8,128)(2,1)S(1)}, bf16[2,32,384]{2,1,0:T(8,128)(2,1)S(1)}) custom-call(bf16[2,5,32,384]{3,2,1,0:T(8,128)(2,1)S(1)} %pad_maximum_fusion.1.refs_0_, bf16[2,5,32,384]{3,2,1,0:T(8,128)(2,1)S(1)} %collective-permute-done.9.refs_1_, ...), custom_call_target="tpu_custom_call" | custom-call | flops 509607936 | bytes 8388608 | tf_op jit(solution)/shard_map/pallas_call | solution.py:314
  65.1 2.7 %collective-permute-start.15 = (bf16[2,32,384]{2,1,0:T(8,128)(2,1)S(1)}, bf16[2,32,384]{2,1,0:T(8,128)(2,1)S(1)}, u32[]{:S(2)}, u32[]{:S(2)}) collective-permute-start(bf16[2,32,384]{2,1,0:T(8,128)(2,1)S(1)} %get-tuple-element.27), channel_id=1, source_target_pairs={{0,1},{1,2},{2,3},{3,4},{4,5},{5,6},{6,7},{7,8},{8,9},{9,10},{10,1... | collective-permute-start | bytes 147464 | tf_op jit(solution)/shard_map/ppermute | solution.py:328
  69.2 5.2 %collective-permute-start.32 = (bf16[224,128]{1,0:T(8,128)(2,1)S(1)}, bf16[224,128]{1,0:T(8,128)(2,1)S(1)}, u32[]{:S(2)}, u32[]{:S(2)}) collective-permute-start(bf16[224,128]{1,0:T(8,128)(2,1)S(1)} %get-tuple-element.47), channel_id=1, source_target_pairs={{0,4},{1,5},{2,6},{3,7},{4,8},{5,9},{6,10},{7,11},{8,12},{9,13},{1... | collective-permute-start | bytes 172040 | tf_op jit(solution)/shard_map/ppermute | solution.py:370
  74.5 4.7 %shard_map.146 = bf16[1152,128]{1,0:T(8,128)(2,1)S(1)} custom-call(bf16[2,5,32,384]{3,2,1,0:T(8,128)(2,1)S(1)} %pad_maximum_fusion.1.refs_0_, bf16[2,5,32,384]{3,2,1,0:T(8,128)(2,1)S(1)} %collective-permute-done.9.refs_1_, bf16[2,5,32,384]{3,2,1,0:T(8,128)(2,1)S(1)} %collective-permute-done.10.refs_2_, ...), custom_call_target="tpu_custom_call" | custom-call | flops 509607936 | bytes 8388608 | tf_op jit(solution)/shard_map/pallas_call | solution.py:314
  80.1 2.3 %collective-permute-start.33 = (bf16[224,128]{1,0:T(8,128)(2,1)S(1)}, bf16[224,128]{1,0:T(8,128)(2,1)S(1)}, u32[]{:S(2)}, u32[]{:S(2)}) collective-permute-start(bf16[224,128]{1,0:T(8,128)(2,1)S(1)} %get-tuple-element.49), channel_id=1, source_target_pairs={{0,8},{1,9},{2,10},{3,11},{4,12},{5,13},{6,14},{7,15},{8,0},{9,1},... | collective-permute-start | bytes 172040 | tf_op jit(solution)/shard_map/ppermute | solution.py:370
  83.4 2.9 %collective-permute-start.21 = (bf16[288,128]{1,0:T(8,128)(2,1)S(1)}, bf16[288,128]{1,0:T(8,128)(2,1)S(1)}, u32[]{:S(2)}, u32[]{:S(2)}) collective-permute-start(bf16[288,128]{1,0:T(8,128)(2,1)S(1)} %get-tuple-element.45), channel_id=1, source_target_pairs={{0,12},{1,13},{2,14},{3,15},{4,0},{5,1},{6,2},{7,3},{8,4},{9,5},{1... | collective-permute-start | bytes 221192 | tf_op jit(solution)/shard_map/ppermute | solution.py:370
  89.0 6.4 %collective-permute-start.17 = (bf16[2,32,384]{2,1,0:T(8,128)(2,1)S(1)}, bf16[2,32,384]{2,1,0:T(8,128)(2,1)S(1)}, u32[]{:S(2)}, u32[]{:S(2)}) collective-permute-start(bf16[2,32,384]{2,1,0:T(8,128)(2,1)S(1)} %pad_maximum_fusion.8), channel_id=1, source_target_pairs={{0,16},{1,17},{2,18},{3,19},{4,20},{5,21},{6,22},{7,23},{8,24},{9,... | collective-permute-start | bytes 147464 | tf_op jit(solution)/shard_map/ppermute | solution.py:328
  96.8 2.7 %collective-permute-start.36 = (bf16[224,128]{1,0:T(8,128)(2,1)S(1)}, bf16[224,128]{1,0:T(8,128)(2,1)S(1)}, u32[]{:S(2)}, u32[]{:S(2)}) collective-permute-start(bf16[224,128]{1,0:T(8,128)(2,1)S(1)} %fusion.5), channel_id=1, source_target_pairs={{0,8},{1,9},{2,10},{3,11},{4,12},{5,13},{6,14},{7,15},{8,0},{9,1},... | collective-permute-start | bytes 172040 | tf_op jit(solution)/shard_map/ppermute | solution.py:370
  99.5 2.0 %collective-permute-start.35 = (bf16[224,128]{1,0:T(8,128)(2,1)S(1)}, bf16[224,128]{1,0:T(8,128)(2,1)S(1)}, u32[]{:S(2)}, u32[]{:S(2)}) collective-permute-start(bf16[224,128]{1,0:T(8,128)(2,1)S(1)} %fusion.5), channel_id=1, source_target_pairs={{0,4},{1,5},{2,6},{3,7},{4,8},{5,9},{6,10},{7,11},{8,12},{9,13},{1... | collective-permute-start | bytes 172040 | tf_op jit(solution)/shard_map/ppermute | solution.py:370
  101.6 6.4 %shard_map.145 = (bf16[2,4,32,192]{3,2,1,0:T(8,128)(2,1)}, bf16[2,4,32,192]{3,2,1,0:T(8,128)(2,1)}, f32[8,192]{1,0:T(8,128)S(1)}) custom-call(bf16[4,32,384]{2,1,0:T(8,128)(2,1)S(1)} %get-tuple-element.23.refs_9_.act2_ref, bf16[4,32,384]{2,1,0:T(8,128)(2,1)S(1)} %collective-permute-done.6.earlier_ref, ...), custom_call_target="tpu_custom_call" | custom-call | flops 1019215872 | bytes 8388608 | tf_op jit(solution)/shard_map/pallas_call | solution.py:314
  113.4 4.7 %collective-permute-done.23 = bf16[304,128]{1,0:T(8,128)(2,1)S(1)} collective-permute-done((bf16[304,128]{1,0:T(8,128)(2,1)S(1)}, bf16[304,128]{1,0:T(8,128)(2,1)S(1)}, u32[]{:S(2)}, u32[]{:S(2)}) %collective-permute-start.23) | collective-permute-done | bytes 77856 | tf_op jit(solution)/shard_map/ppermute | solution.py:370
  122.9 3.5 %collective-permute-done.39.refs_2_ = bf16[896,128]{1,0:T(8,128)(2,1)S(1)} collective-permute-done((bf16[896,128]{1,0:T(8,128)(2,1)S(1)}, bf16[896,128]{1,0:T(8,128)(2,1)S(1)}, u32[]{:S(2)}, u32[]{:S(2)}) %collective-permute-start.39) | collective-permute-done | bytes 229408 | tf_op jit(solution)/shard_map/ppermute | solution.py:366
  127.0 5.9 %collective-permute-done.27.refs_3_ = bf16[1168,128]{1,0:T(8,128)(2,1)S(1)} collective-permute-done((bf16[1168,128]{1,0:T(8,128)(2,1)S(1)}, bf16[1168,128]{1,0:T(8,128)(2,1)S(1)}, u32[]{:S(2)}, u32[]{:S(2)}) %collective-permute-start.27) | collective-permute-done | bytes 299040 | tf_op jit(solution)/shard_map/ppermute | solution.py:366
  132.8 4.9 %collective-permute-done.26.refs_2_ = bf16[1168,128]{1,0:T(8,128)(2,1)S(1)} collective-permute-done((bf16[1168,128]{1,0:T(8,128)(2,1)S(1)}, bf16[1168,128]{1,0:T(8,128)(2,1)S(1)}, u32[]{:S(2)}, u32[]{:S(2)}) %collective-permute-start.26) | collective-permute-done | bytes 299040 | tf_op jit(solution)/shard_map/ppermute | solution.py:366
  143.2 1.9 %shard_map.148 = (bf16[27,192,192]{2,1,0:T(8,128)(2,1)}, bf16[27,192,192]{2,1,0:T(8,128)(2,1)}) custom-call(bf16[1168,128]{1,0:T(8,128)(2,1)S(1)} %concatenate.61.refs_0_, bf16[1168,128]{1,0:T(8,128)(2,1)S(1)} %collective-permute-done.25.refs_1_, ...), custom_call_target="tpu_custom_call", output_to_operand_aliasing={{0}: (8, {}), {1}: (9, {})} | custom-call | bytes 8388608 | tf_op jit(solution)/shard_map/pallas_call | solution.py:314
  (156 shorter events, 44.4 us)
Async XLA Ops:
  0.6 21.1 %collective-permute-start = (bf16[2,4,32,192]{3,2,1,0:T(8,128)(2,1)}, bf16[2,4,32,192]{3,2,1,0:T(8,128)(2,1)S(1)}, u32[]{:S(2)}, u32[]{:S(2)}) collective-permute-start(bf16[2,4,32,192]{3,2,1,0:T(8,128)(2,1)} %feat_any.3), channel_id=1, source_target_pairs={{0,16},{1,17},{2,18},{3,19},{4,20},{5,21},{6,22},{7,23},{8,24},{9,... | collective-permute-start | bytes 294920 | tf_op jit(solution)/shard_map/ppermute | solution.py:328
  3.0 18.8 %collective-permute-start.1 = (bf16[2,4,32,192]{3,2,1,0:T(8,128)(2,1)}, bf16[2,4,32,192]{3,2,1,0:T(8,128)(2,1)S(1)}, u32[]{:S(2)}, u32[]{:S(2)}) collective-permute-start(bf16[2,4,32,192]{3,2,1,0:T(8,128)(2,1)} %cot_any.3), channel_id=1, source_target_pairs={{16,0},{17,1},{18,2},{19,3},{20,4},{21,5},{22,6},{23,7},{24,8},{25... | collective-permute-start | bytes 294920 | tf_op jit(solution)/shard_map/ppermute | solution.py:328
  37.6 23.6 %collective-permute-start.11 = (bf16[2,5,32,384]{3,2,1,0:T(8,128)(2,1)S(1)}, bf16[2,5,32,384]{3,2,1,0:T(8,128)(2,1)S(1)}, u32[]{:S(2)}, u32[]{:S(2)}) collective-permute-start(bf16[2,5,32,384]{3,2,1,0:T(8,128)(2,1)S(1)} %pad_maximum_fusion.1.refs_0_), channel_id=1, source_target_pairs={{0,3},{1,2},{2,1},{3,0},{4,7},{5,6},{6,5},{7,4},{8,11},{9,10},{10,... | collective-permute-start | bytes 737288 | tf_op jit(solution)/shard_map/ppermute | solution.py:366
  38.4 22.8 %collective-permute-start.10 = (bf16[2,5,32,384]{3,2,1,0:T(8,128)(2,1)S(1)}, bf16[2,5,32,384]{3,2,1,0:T(8,128)(2,1)S(1)}, u32[]{:S(2)}, u32[]{:S(2)}) collective-permute-start(bf16[2,5,32,384]{3,2,1,0:T(8,128)(2,1)S(1)} %pad_maximum_fusion.1.refs_0_), channel_id=1, source_target_pairs={{0,2},{1,3},{2,0},{3,1},{4,6},{5,7},{6,4},{7,5},{8,10},{9,11},{10,... | collective-permute-start | bytes 737288 | tf_op jit(solution)/shard_map/ppermute | solution.py:366
  38.4 22.8 %collective-permute-start.9 = (bf16[2,5,32,384]{3,2,1,0:T(8,128)(2,1)S(1)}, bf16[2,5,32,384]{3,2,1,0:T(8,128)(2,1)S(1)}, u32[]{:S(2)}, u32[]{:S(2)}) collective-permute-start(bf16[2,5,32,384]{3,2,1,0:T(8,128)(2,1)S(1)} %pad_maximum_fusion.1.refs_0_), channel_id=1, source_target_pairs={{0,1},{1,0},{2,3},{3,2},{4,5},{5,4},{6,7},{7,6},{8,9},{9,8},{10,11... | collective-permute-start | bytes 737288 | tf_op jit(solution)/shard_map/ppermute | solution.py:366
  41.6 16.1 %collective-permute-start.13 = (bf16[2,4,32,384]{3,2,1,0:T(8,128)(2,1)S(1)}, bf16[2,4,32,384]{3,2,1,0:T(8,128)(2,1)S(1)}, u32[]{:S(2)}, u32[]{:S(2)}) collective-permute-start(bf16[2,4,32,384]{3,2,1,0:T(8,128)(2,1)S(1)} %maximum_select_fusion.1.refs_4_), channel_id=1, source_target_pairs={{0,2},{1,3},{2,0},{3,1},{4,6},{5,7},{6,4},{7,5},{8,10},{9,11},{10,... | collective-permute-start | bytes 589832 | tf_op jit(solution)/shard_map/ppermute | solution.py:366
  43.3 16.2 %collective-permute-start.12 = (bf16[2,4,32,384]{3,2,1,0:T(8,128)(2,1)S(1)}, bf16[2,4,32,384]{3,2,1,0:T(8,128)(2,1)S(1)}, u32[]{:S(2)}, u32[]{:S(2)}) collective-permute-start(bf16[2,4,32,384]{3,2,1,0:T(8,128)(2,1)S(1)} %maximum_select_fusion.1.refs_4_), channel_id=1, source_target_pairs={{0,1},{1,0},{2,3},{3,2},{4,5},{5,4},{6,7},{7,6},{8,9},{9,8},{10,11... | collective-permute-start | bytes 589832 | tf_op jit(solution)/shard_map/ppermute | solution.py:366
  57.6 39.2 %collective-permute-start.6 = (bf16[4,32,384]{2,1,0:T(8,128)(2,1)S(1)}, bf16[4,32,384]{2,1,0:T(8,128)(2,1)S(1)}, u32[]{:S(2)}, u32[]{:S(2)}) collective-permute-start(bf16[4,32,384]{2,1,0:T(8,128)(2,1)S(1)} %get-tuple-element.23.refs_9_.act2_ref), channel_id=1, source_target_pairs={{0,16},{1,17},{2,18},{3,19},{4,20},{5,21},{6,22},{7,23},{8,24},{9,... | collective-permute-start | bytes 294920 | tf_op jit(solution)/shard_map/ppermute | solution.py:328
  59.6 39.9 %collective-permute-start.7 = (bf16[4,32,384]{2,1,0:T(8,128)(2,1)S(1)}, bf16[4,32,384]{2,1,0:T(8,128)(2,1)S(1)}, u32[]{:S(2)}, u32[]{:S(2)}) collective-permute-start(bf16[4,32,384]{2,1,0:T(8,128)(2,1)S(1)} %get-tuple-element.24.refs_10_.gmid_ref), channel_id=1, source_target_pairs={{16,0},{17,1},{18,2},{19,3},{20,4},{21,5},{22,6},{23,7},{24,8},{25... | collective-permute-start | bytes 294920 | tf_op jit(solution)/shard_map/ppermute | solution.py:328
  65.1 14.0 %collective-permute-start.15 = (bf16[2,32,384]{2,1,0:T(8,128)(2,1)S(1)}, bf16[2,32,384]{2,1,0:T(8,128)(2,1)S(1)}, u32[]{:S(2)}, u32[]{:S(2)}) collective-permute-start(bf16[2,32,384]{2,1,0:T(8,128)(2,1)S(1)} %get-tuple-element.27), channel_id=1, source_target_pairs={{0,1},{1,2},{2,3},{3,4},{4,5},{5,6},{6,7},{7,8},{8,9},{9,10},{10,1... | collective-permute-start | bytes 147464 | tf_op jit(solution)/shard_map/ppermute | solution.py:328
  67.9 12.2 %collective-permute-start.16 = (bf16[2,32,384]{2,1,0:T(8,128)(2,1)S(1)}, bf16[2,32,384]{2,1,0:T(8,128)(2,1)S(1)}, u32[]{:S(2)}, u32[]{:S(2)}) collective-permute-start(bf16[2,32,384]{2,1,0:T(8,128)(2,1)S(1)} %get-tuple-element.28), channel_id=1, source_target_pairs={{1,0},{2,1},{3,2},{4,3},{5,4},{6,5},{7,6},{8,7},{9,8},{10,9},{11,1... | collective-permute-start | bytes 147464 | tf_op jit(solution)/shard_map/ppermute | solution.py:328
  69.2 13.2 %collective-permute-start.32 = (bf16[224,128]{1,0:T(8,128)(2,1)S(1)}, bf16[224,128]{1,0:T(8,128)(2,1)S(1)}, u32[]{:S(2)}, u32[]{:S(2)}) collective-permute-start(bf16[224,128]{1,0:T(8,128)(2,1)S(1)} %get-tuple-element.47), channel_id=1, source_target_pairs={{0,4},{1,5},{2,6},{3,7},{4,8},{5,9},{6,10},{7,11},{8,12},{9,13},{1... | collective-permute-start | bytes 172040 | tf_op jit(solution)/shard_map/ppermute | solution.py:370
  83.4 11.9 %collective-permute-start.21 = (bf16[288,128]{1,0:T(8,128)(2,1)S(1)}, bf16[288,128]{1,0:T(8,128)(2,1)S(1)}, u32[]{:S(2)}, u32[]{:S(2)}) collective-permute-start(bf16[288,128]{1,0:T(8,128)(2,1)S(1)} %get-tuple-element.45), channel_id=1, source_target_pairs={{0,12},{1,13},{2,14},{3,15},{4,0},{5,1},{6,2},{7,3},{8,4},{9,5},{1... | collective-permute-start | bytes 221192 | tf_op jit(solution)/shard_map/ppermute | solution.py:370
  89.0 12.6 %collective-permute-start.17 = (bf16[2,32,384]{2,1,0:T(8,128)(2,1)S(1)}, bf16[2,32,384]{2,1,0:T(8,128)(2,1)S(1)}, u32[]{:S(2)}, u32[]{:S(2)}) collective-permute-start(bf16[2,32,384]{2,1,0:T(8,128)(2,1)S(1)} %pad_maximum_fusion.8), channel_id=1, source_target_pairs={{0,16},{1,17},{2,18},{3,19},{4,20},{5,21},{6,22},{7,23},{8,24},{9,... | collective-permute-start | bytes 147464 | tf_op jit(solution)/shard_map/ppermute | solution.py:328
  96.7 13.3 %collective-permute-start.37 = (bf16[224,128]{1,0:T(8,128)(2,1)S(1)}, bf16[224,128]{1,0:T(8,128)(2,1)S(1)}, u32[]{:S(2)}, u32[]{:S(2)}) collective-permute-start(bf16[224,128]{1,0:T(8,128)(2,1)S(1)} %fusion.5), channel_id=1, source_target_pairs={{0,12},{1,13},{2,14},{3,15},{4,0},{5,1},{6,2},{7,3},{8,4},{9,5},{1... | collective-permute-start | bytes 172040 | tf_op jit(solution)/shard_map/ppermute | solution.py:370
  96.8 13.8 %collective-permute-start.36 = (bf16[224,128]{1,0:T(8,128)(2,1)S(1)}, bf16[224,128]{1,0:T(8,128)(2,1)S(1)}, u32[]{:S(2)}, u32[]{:S(2)}) collective-permute-start(bf16[224,128]{1,0:T(8,128)(2,1)S(1)} %fusion.5), channel_id=1, source_target_pairs={{0,8},{1,9},{2,10},{3,11},{4,12},{5,13},{6,14},{7,15},{8,0},{9,1},... | collective-permute-start | bytes 172040 | tf_op jit(solution)/shard_map/ppermute | solution.py:370
  99.5 11.1 %collective-permute-start.35 = (bf16[224,128]{1,0:T(8,128)(2,1)S(1)}, bf16[224,128]{1,0:T(8,128)(2,1)S(1)}, u32[]{:S(2)}, u32[]{:S(2)}) collective-permute-start(bf16[224,128]{1,0:T(8,128)(2,1)S(1)} %fusion.5), channel_id=1, source_target_pairs={{0,4},{1,5},{2,6},{3,7},{4,8},{5,9},{6,10},{7,11},{8,12},{9,13},{1... | collective-permute-start | bytes 172040 | tf_op jit(solution)/shard_map/ppermute | solution.py:370
  111.6 11.3 %collective-permute-start.40 = (bf16[896,128]{1,0:T(8,128)(2,1)S(1)}, bf16[896,128]{1,0:T(8,128)(2,1)S(1)}, u32[]{:S(2)}, u32[]{:S(2)}) collective-permute-start(bf16[896,128]{1,0:T(8,128)(2,1)S(1)} %bitcast_select_fusion.1.refs_0_), channel_id=1, source_target_pairs={{0,3},{1,2},{2,1},{3,0},{4,7},{5,6},{6,5},{7,4},{8,11},{9,10},{10,... | collective-permute-start | bytes 688136 | tf_op jit(solution)/shard_map/ppermute | solution.py:366
  112.7 13.7 %collective-permute-start.39 = (bf16[896,128]{1,0:T(8,128)(2,1)S(1)}, bf16[896,128]{1,0:T(8,128)(2,1)S(1)}, u32[]{:S(2)}, u32[]{:S(2)}) collective-permute-start(bf16[896,128]{1,0:T(8,128)(2,1)S(1)} %bitcast_select_fusion.1.refs_0_), channel_id=1, source_target_pairs={{0,2},{1,3},{2,0},{3,1},{4,6},{5,7},{6,4},{7,5},{8,10},{9,11},{10,... | collective-permute-start | bytes 688136 | tf_op jit(solution)/shard_map/ppermute | solution.py:366
  119.4 13.5 %collective-permute-start.27 = (bf16[1168,128]{1,0:T(8,128)(2,1)S(1)}, bf16[1168,128]{1,0:T(8,128)(2,1)S(1)}, u32[]{:S(2)}, u32[]{:S(2)}) collective-permute-start(bf16[1168,128]{1,0:T(8,128)(2,1)S(1)} %concatenate.61.refs_0_), channel_id=1, source_target_pairs={{0,3},{1,2},{2,1},{3,0},{4,7},{5,6},{6,5},{7,4},{8,11},{9,10},{10,... | collective-permute-start | bytes 897032 | tf_op jit(solution)/shard_map/ppermute | solution.py:366
  121.2 16.6 %collective-permute-start.26 = (bf16[1168,128]{1,0:T(8,128)(2,1)S(1)}, bf16[1168,128]{1,0:T(8,128)(2,1)S(1)}, u32[]{:S(2)}, u32[]{:S(2)}) collective-permute-start(bf16[1168,128]{1,0:T(8,128)(2,1)S(1)} %concatenate.61.refs_0_), channel_id=1, source_target_pairs={{0,2},{1,3},{2,0},{3,1},{4,6},{5,7},{6,4},{7,5},{8,10},{9,11},{10,... | collective-permute-start | bytes 897032 | tf_op jit(solution)/shard_map/ppermute | solution.py:366
  122.9 15.6 %collective-permute-start.25 = (bf16[1168,128]{1,0:T(8,128)(2,1)S(1)}, bf16[1168,128]{1,0:T(8,128)(2,1)S(1)}, u32[]{:S(2)}, u32[]{:S(2)}) collective-permute-start(bf16[1168,128]{1,0:T(8,128)(2,1)S(1)} %concatenate.61.refs_0_), channel_id=1, source_target_pairs={{0,1},{1,0},{2,3},{3,2},{4,5},{5,4},{6,7},{7,6},{8,9},{9,8},{10,11... | collective-permute-start | bytes 897032 | tf_op jit(solution)/shard_map/ppermute | solution.py:366
  126.5 12.0 %collective-permute-start.44 = (bf16[896,128]{1,0:T(8,128)(2,1)S(1)}, bf16[896,128]{1,0:T(8,128)(2,1)S(1)}, u32[]{:S(2)}, u32[]{:S(2)}) collective-permute-start(bf16[896,128]{1,0:T(8,128)(2,1)S(1)} %collective-permute-done.40.refs_3_), channel_id=1, source_target_pairs={{0,16},{16,0},{1,17},{17,1},{2,18},{18,2},{3,19},{19,3},{4,20},{20... | collective-permute-start | bytes 688136 | tf_op jit(solution)/shard_map/ppermute | solution.py:489
  126.6 12.4 %collective-permute-start.43 = (bf16[896,128]{1,0:T(8,128)(2,1)S(1)}, bf16[896,128]{1,0:T(8,128)(2,1)S(1)}, u32[]{:S(2)}, u32[]{:S(2)}) collective-permute-start(bf16[896,128]{1,0:T(8,128)(2,1)S(1)} %collective-permute-done.39.refs_2_), channel_id=1, source_target_pairs={{0,16},{16,0},{1,17},{17,1},{2,18},{18,2},{3,19},{19,3},{4,20},{20... | collective-permute-start | bytes 688136 | tf_op jit(solution)/shard_map/ppermute | solution.py:489
  (32 other events, 334.4 us)

commit v4 on v3

--- a/solution.py
+++ b/solution.py
@@ -60,25 +60,65 @@
     return total.reshape(frames * rows * cols, chans)
 
 
-def fill_rows(window, at, edges, row):
+def is_odd():
+    return lax.axis_index("tm") % 2 == 1
+
+
+def by_core(odd_fn, even_fn):
+    pl.when(is_odd())(odd_fn)
+    pl.when(jnp.logical_not(is_odd()))(even_fn)
+
+
+def fill_packed(window, at, rows, packed):
     chans = window.shape[3]
     for f in range(2):
-        window[at + f, row] = edges[:, f * chans : (f + 1) * chans]
-
-
-def fill_edges(ahead, behind, above, below, passed_ahead, passed_behind):
+        window[at + f, rows] = packed[..., f * chans : (f + 1) * chans]
+
+
+def fill_far(ahead, behind, far, rows):
+    def put(window, at, value):
+        if value.shape[-1] == window.shape[3]:
+            window[pl.ds(at, 2), rows] = value
+        else:
+            fill_packed(window, at, rows, value)
+
+    if far.shape[0] == 2:
+        put(ahead, 0, far[0])
+        put(behind, 2, far[1])
+        return
+    zero = jnp.zeros(far.shape[1:], bf16)
+
+    def odd():
+        put(ahead, 0, far[0])
+        put(behind, 2, zero)
+
+    def even():
+        put(ahead, 0, zero)
+        put(behind, 2, far[0])
+
+    by_core(odd, even)
+
+
+def fill_edges(ahead, behind, above, below):
     last = ahead.shape[1] - 1
-    for row, own, i in ((0, above, 0), (last, below, 1)):
-        fill_rows(ahead, 2, own[0], row)
-        fill_rows(behind, 0, own[1], row)
-        fill_rows(ahead, 0, passed_ahead[i], row)
-        fill_rows(behind, 2, passed_behind[i], row)
-
-
-def fill_packed(window, at, packed):
-    rows, chans = packed.shape[0], window.shape[3]
-    for f in range(2):
-        window[at + f, 1 : rows + 1] = packed[..., f * chans : (f + 1) * chans]
+    places = ((ahead, 0), (ahead, 2), (behind, 0), (behind, 2))
+    for row, edges in ((0, above), (last, below)):
+        rows = pl.ds(row, 1)
+        if edges.shape[0] == 4:
+            for i, (window, at) in enumerate(places):
+                fill_packed(window, at, rows, edges[i : i + 1])
+            continue
+        zero = jnp.zeros((1,) + edges.shape[1:], bf16)
+
+        def odd():
+            for i, (window, at) in enumerate(places):
+                fill_packed(window, at, rows, edges[i : i + 1] if i < 3 else zero)
+
+        def even():
+            for i, (window, at) in enumerate(places):
+                fill_packed(window, at, rows, edges[i - 1 : i] if i > 0 else zero)
+
+        by_core(odd, even)
 
 
 def started(copies, sems):
@@ -92,39 +132,96 @@
     return jnp.concatenate([values[0], values[1]], axis=-1)
 
 
+def put_messages(groups, up_ref, down_ref):
+    for i, value in enumerate(groups):
+        up_ref[i] = value[value.shape[0] - 1]
+        down_ref[i] = value[0]
+
+
+def join_first_kernel(*refs):
+    refs, (y_ref, up_ref, down_ref) = refs[:-3], refs[-3:]
+    feat, cot, *far = [pack_frames(ref) for ref in refs]
+    if len(far) == 1:
+
+        def odd():
+            y_ref[0], y_ref[1] = far[0], feat
+            put_messages((far[0], feat, cot), up_ref, down_ref)
+
+        def even():
+            y_ref[0], y_ref[1] = cot, far[0]
+            put_messages((feat, cot, far[0]), up_ref, down_ref)
+
+    else:
+        put_messages((far[0], feat, cot, far[1]), up_ref, down_ref)
+
+        def odd():
+            y_ref[0], y_ref[1], y_ref[2] = far[2], far[0], feat
+
+        def even():
+            y_ref[0], y_ref[1], y_ref[2] = cot, far[1], far[2]
+
+    by_core(odd, even)
+
+
+def gate_kernel(keep_ref, give_ref, far_ref, _, up_ref, down_ref):
+    keep, give, far = keep_ref[...], give_ref[...], far_ref[...]
+
+    def odd():
+        put_messages((far[0], give, keep, far[-1])[: up_ref.shape[0]], up_ref, down_ref)
+
+    def even():
+        put_messages((far[0], keep, give, far[-1])[4 - up_ref.shape[0] :], up_ref, down_ref)
+
+    by_core(odd, even)
+
+
+def join_edge_kernel(keep_ref, other_ref, above_ref, below_ref, out_ref):
+    rows = keep_ref.shape[0]
+    top = lax.axis_index("height") % 4 == 0
+    edge = jnp.where(top, above_ref[...], below_ref[...])
+
+    def odd():
+        out_ref[0, :rows], out_ref[1, :rows] = other_ref[...], keep_ref[...]
+        out_ref[0, rows], out_ref[1, rows] = edge[0], edge[1]
+
+    def even():
+        out_ref[0, :rows], out_ref[1, :rows] = keep_ref[...], other_ref[...]
+        out_ref[0, rows], out_ref[1, rows] = edge[1], edge[2]
+
+    by_core(odd, even)
+
+
 def first_kernel(
-    feat_any, earlier_any, cot_any, later_any, above_ref, below_ref, pa_ref, pb_ref, w1_any, w2_any, b1_any, g1_any, g2_any,
-    act2_ref, gmid_ref, give_ref, keep_ref, sums_ref, ahead, behind, w1, w2, b1, g1, g2, sems,
+    _, __, feat_any, cot_any, far_ref, above_ref, below_ref, w1_any, w2_any, b1_any, g1_any, g2_any,
+    give_ref, keep_ref, sums_ref, ahead, behind, w1, w2, b1, g1, g2, sems,
 ):
     frames, rows, cols, chans = feat_any.shape
     own = pl.ds(1, rows)
     copies = started(
         (
             (feat_any, ahead.at[pl.ds(2, 2), own]),
-            (earlier_any, ahead.at[pl.ds(0, 2), own]),
             (g1_any, g1),
             (w1_any, w1),
             (b1_any, b1),
             (g2_any, g2),
             (cot_any, behind.at[pl.ds(0, 2), own]),
-            (later_any, behind.at[pl.ds(2, 2), own]),
             (w2_any, w2),
         ),
         sems,
     )
-    fill_edges(ahead, behind, above_ref, below_ref, pa_ref, pb_ref)
-    for copy in copies[:3]:
+    fill_far(ahead, behind, far_ref, own)
+    fill_edges(ahead, behind, above_ref, below_ref)
+    for copy in copies[:2]:
         copy.wait()
     for f in range(frames + 2):
         vals = ahead[f].astype(f32).reshape(-1, chans)
         ahead[f] = norm_silu(vals, g1[...]).astype(bf16).reshape(rows + 2, cols, chans)
-    for copy in copies[3:6]:
+    for copy in copies[2:5]:
         copy.wait()
     mid = (conv(ahead, w1, frames, rows, False) + b1[...]).astype(bf16).astype(f32)
     act2 = norm_silu(mid, g2[...]).astype(bf16).reshape(frames, rows, cols, chans)
     act2 = pack_frames(act2)
-    act2_ref[...] = act2
-    for copy in copies[6:]:
+    for copy in copies[5:]:
         copy.wait()
     grad = conv(behind, w2, frames, rows, True)
     gmid, d_gain = norm_silu_back(grad, mid, g2[...])
@@ -140,34 +237,40 @@
         axis=0,
     )
     gmid = pack_frames(gmid.reshape(frames, rows, cols, chans))
-    gmid_ref[...] = gmid
-    odd = lax.axis_index("tm") % 2 == 1
-
-    @pl.when(odd)
-    def _():
+
+    def odd():
         give_ref[...] = act2
         keep_ref[...] = gmid
 
-    @pl.when(jnp.logical_not(odd))
-    def _():
+    def even():
         give_ref[...] = gmid
         keep_ref[...] = act2
 
+    by_core(odd, even)
+
 
 def last_kernel(
-    act2_ref, earlier_ref, gmid_ref, later_ref, above_ref, below_ref, pa_ref, pb_ref,
+    keep_ref, give_ref, far_ref, above_ref, below_ref,
     feat_any, cot_any, w1_any, w2_any, b2_any, g1_any,
     out_ref, gin_ref, sums_ref, ahead, behind, feat, cot, w1, w2, b2, g1, sems,
 ):
     frames, rows, cols, chans = out_ref.shape
+    own = pl.ds(1, rows)
     copies = started(
         ((w2_any, w2), (b2_any, b2), (feat_any, feat), (w1_any, w1), (cot_any, cot), (g1_any, g1)), sems
     )
-    fill_packed(ahead, 0, earlier_ref)
-    fill_packed(ahead, 2, act2_ref)
-    fill_packed(behind, 0, gmid_ref)
-    fill_packed(behind, 2, later_ref)
-    fill_edges(ahead, behind, above_ref, below_ref, pa_ref, pb_ref)
+
+    def odd():
+        fill_packed(ahead, 2, own, give_ref[...])
+        fill_packed(behind, 0, own, keep_ref[...])
+
+    def even():
+        fill_packed(ahead, 2, own, keep_ref[...])
+        fill_packed(behind, 0, own, give_ref[...])
+
+    by_core(odd, even)
+    fill_far(ahead, behind, far_ref, own)
+    fill_edges(ahead, behind, above_ref, below_ref)
     for copy in copies[:3]:
         copy.wait()
     values = feat[...].astype(f32).reshape(-1, chans)
@@ -186,17 +289,10 @@
     return chans + chans // 2
 
 
-def wgrad_kernel(blocks, taps, passes, *refs):
+def wgrad_kernel(blocks, taps, *refs):
     xs, ys = refs[:4], refs[4:8]
-    gain_ref, refs = refs[8], refs[9:]
-    if passes:
-        (one_ref, two_ref, out_ref, up_ref, down_ref), refs = refs[:5], refs[5:]
-        for i, ref in enumerate((one_ref, two_ref)):
-            up_ref[i] = ref[ref.shape[0] - 1]
-            down_ref[i] = ref[0]
-    else:
-        out_ref, refs = refs[0], refs[1:]
-    plane, xk = refs
+    gain_ref = refs[8]
+    out_ref, plane, xk = refs[-3:]
     _, rows, cols, _ = ys[0].shape
     chans = gain_ref.shape[1]
     tall = 4 * rows
@@ -308,17 +404,18 @@
 
 vmem = pl.BlockSpec(memory_space=pltpu.VMEM)
 anywhere = pl.BlockSpec(memory_space=pl.ANY)
-
-
-def call(kernel, outs, args, flops, scratch=(), free=(), out_spec=vmem, **kw):
+in_hbm = pl.BlockSpec(memory_space=pltpu.HBM)
+
+
+def call(kernel, outs, args, us, mib, scratch=(), free=(), hbm=(), out_spec=vmem, **kw):
     return pl.pallas_call(
         kernel,
         out_shape=outs,
-        in_specs=[anywhere if i in free else vmem for i in range(len(args))],
+        in_specs=[in_hbm if i in hbm else anywhere if i in free else vmem for i in range(len(args))],
         out_specs=[out_spec] * len(outs),
         scratch_shapes=list(scratch),
-        compiler_params=pltpu.CompilerParams(vmem_limit_bytes=50 * 2**20),
-        cost_estimate=pl.CostEstimate(flops=flops, bytes_accessed=8 * 2**20, transcendentals=0),
+        compiler_params=pltpu.CompilerParams(vmem_limit_bytes=mib * 2**20),
+        cost_estimate=pl.CostEstimate(flops=0, bytes_accessed=int(us * 3.6e6), transcendentals=0),
         **kw,
     )(*args)
 
@@ -326,14 +423,6 @@
 def moved(value, axis, by):
     size = lax.axis_size(axis)
     return lax.ppermute(value, axis, [(i, i + by) for i in range(size) if 0 <= i + by < size])
-
-
-def edge_parts(up, down):
-    above = moved(up, "height", 1)
-    below = moved(down, "height", -1)
-    passed_ahead = moved(jnp.stack([above[0], below[0]]), "tm", 1)
-    passed_behind = moved(jnp.stack([above[1], below[1]]), "tm", -1)
-    return above, below, passed_ahead, passed_behind
 
 
 def total_of(pieces):
@@ -355,12 +444,10 @@
     line = lambda v: v.reshape(1, chans)
     local = jax.ShapeDtypeStruct(features.shape, bf16)
     sums = jax.ShapeDtypeStruct((8, chans), f32)
-    flops = 4 * frames * rows * cols * 27 * chans * chans
     window = pltpu.VMEM((frames + 2, rows + 2, cols, chans), bf16)
     weight = pltpu.VMEM(weight_one.shape, bf16)
     vector = pltpu.VMEM((1, chans), f32)
     packed_shape = jax.ShapeDtypeStruct((rows, cols, 2 * chans), bf16)
-    edge_shape = jax.ShapeDtypeStruct((2, cols, 2 * chans), bf16)
 
     def plane_move(value, d):
         return lax.ppermute(value, "height", [(i, i ^ d) for i in range(height)])
@@ -369,66 +456,71 @@
         pairs = [(z * 4 + j, (z + d) % planes * 4 + j) for z in range(planes) for j in range(4)]
         return lax.ppermute(value, "height", pairs)
 
-    up = jnp.stack([pack_frames(v[:, -1]) for v in (features, cotangent)])
-    down = jnp.stack([pack_frames(v[:, 0]) for v in (features, cotangent)])
-    above, below, passed_ahead, passed_behind = edge_parts(up, down)
-    earlier, later = moved(features, "tm", 1), moved(cotangent, "tm", -1)
-
-    top = p == 0
-    odd_y = [pack_frames(earlier), pack_frames(features)]
-    even_y = [pack_frames(cotangent), pack_frames(later)]
-    near = jnp.where(top, above, below)
-    odd_edge = [jnp.where(top, passed_ahead[0], passed_ahead[1]), near[0]]
-    even_edge = [near[1], jnp.where(top, passed_behind[0], passed_behind[1])]
-    if tm > 2:
-        extra = lax.ppermute(jnp.where(odd, even_y[1], odd_y[0]), "tm", swap)
-        odd_y, even_y = [extra, *odd_y], [*even_y, extra]
-        extra = lax.ppermute(jnp.where(odd, even_edge[1], odd_edge[0]), "tm", swap)
-        odd_edge, even_edge = [extra, *odd_edge], [*even_edge, extra]
-    blocks = len(odd_y)
-    y_own = jnp.where(odd, jnp.stack(odd_y), jnp.stack(even_y))
+    pair = tm == 2
+    blocks = 2 if pair else 3
+    messages = (jax.ShapeDtypeStruct((3 if pair else 4, cols, 2 * chans), bf16),) * 2
+    y_shape = jax.ShapeDtypeStruct((blocks, rows, cols, 2 * chans), bf16)
+    x_shape = jax.ShapeDtypeStruct((blocks, rows + 1, cols, 2 * chans), bf16)
+    if pair:
+        far = (lax.ppermute(jnp.where(odd, cotangent, features), "tm", swap),)
+        extra = ()
+    else:
+        far = (moved(features, "tm", 1), moved(cotangent, "tm", -1))
+        extra = (lax.ppermute(jnp.where(odd, far[1], far[0]), "tm", swap),)
+    y_own, up, down = call(join_first_kernel, (y_shape, *messages), (features, cotangent, *far, *extra), 1, 8)
+    above, below = moved(up, "height", 1), moved(down, "height", -1)
     ys = [y_own] + [plane_move(y_own, d) for d in (1, 2, 3)]
-    edge = jnp.where(odd, jnp.stack(odd_edge), jnp.stack(even_edge))[:, None]
-
-    act2, gmid, give, keep, sums_one = call(
+
+    give, keep, sums_one = call(
         first_kernel,
-        (packed_shape,) * 4 + (sums,),
+        (packed_shape, packed_shape, sums),
         (
-            features, earlier, cotangent, later, above, below, passed_ahead, passed_behind,
+            ys[1], ys[2], features, cotangent, jnp.stack(far), above, below,
             weight_one, weight_two, line(bias_one), line(gain_one), line(gain_two),
         ),
-        flops,
-        [window, window, weight, weight, vector, vector, vector, pltpu.SemaphoreType.DMA((9,))],
-        free=(0, 1, 2, 3, 8, 9, 10, 11, 12),
+        5,
+        62,
+        [window, window, weight, weight, vector, vector, vector, pltpu.SemaphoreType.DMA((7,))],
+        free=(0, 1),
+        hbm=(2, 3, 7, 8, 9, 10, 11),
     )
     other = lax.ppermute(give, "tm", swap)
-    x_own = jnp.where(odd, jnp.stack([other, keep]), jnp.stack([keep, other]))
-    if blocks > 2:
-        x_own = jnp.concatenate([x_own, jnp.zeros((blocks - 2, *x_own.shape[1:]), bf16)])
-    x_own = jnp.concatenate([x_own, edge], axis=1)
+    if pair:
+        (x_own,) = call(join_edge_kernel, (x_shape,), (keep, other, above, below), 1, 6)
+        far = lax.ppermute(keep, "tm", swap)[None]
+    else:
+        edge = jnp.where(p == 0, above, below)
+        extra = lax.ppermute(jnp.where(odd, edge[3], edge[0]), "tm", swap)
+        edge = jnp.where(odd, jnp.stack([extra, edge[0], edge[1]]), jnp.stack([edge[2], edge[3], extra]))
+        x_own = jnp.where(odd, jnp.stack([other, keep, keep]), jnp.stack([keep, other, other]))
+        x_own = jnp.concatenate([x_own, edge[:, None]], axis=1)
+        act2, gmid = jnp.where(odd, give, keep), jnp.where(odd, keep, give)
+        far = jnp.stack([moved(act2, "tm", 1), moved(gmid, "tm", -1)])
     xs = [x_own] + [plane_move(x_own, d) for d in (1, 2, 3)]
-
-    earlier2, later2 = moved(act2, "tm", 1), moved(gmid, "tm", -1)
+    before = ()
 
     step = pack_rows(chans)
     unit = 16 * planes
     cells = (2 * frames, 4 * rows, cols, chans)
     parts = []
-    for n, taps in enumerate(chunks):
+    for taps in chunks:
         packed = -(-taps[1] * step // unit) * unit
-        passes = n == 0
-        flat, *ends = call(
-            functools.partial(wgrad_kernel, blocks, taps, passes),
-            (jax.ShapeDtypeStruct((packed, 128), bf16),) + (edge_shape,) * (2 * passes),
-            (*xs, *ys, line(gain_one)) + (act2, gmid) * passes,
-            flops // 2,
-            [
+        (flat,) = call(
+            functools.partial(wgrad_kernel, blocks, taps),
+            (jax.ShapeDtypeStruct((packed, 128), bf16),),
+            (*xs, *ys, line(gain_one), *before),
+            4,
+            24,
+            free=tuple(range(9, 9 + len(before))),
+            scratch=[
                 pltpu.VMEM((2 * frames + 2, 4 * rows + 2, cols, chans), bf16),
                 pltpu.VMEM((3, *cells), bf16),
             ],
         )
-        if passes:
-            edges2 = edge_parts(*ends)
+        if not before:
+            up, down = call(gate_kernel, messages, (keep, give, far, flat), 1, 6, free=(3,))
+            above, below = moved(up, "height", 1), moved(down, "height", -1)
+        before = (flat,)
         flat = flat.reshape(planes, packed // planes, 128)
         arrived = [column_move(piece_at(flat, (q + d) % planes), d) for d in range(1, planes)]
         part = total_of([piece_at(flat, q), *arrived])
@@ -443,15 +535,16 @@
         last_kernel,
         (local, local, sums),
         (
-            act2, earlier2, gmid, later2, *edges2, features, cotangent,
+            keep, give, far, above, below, features, cotangent,
             weight_one, weight_two, line(bias_two), line(gain_one),
         ),
-        flops,
+        6,
+        62,
         [
             window, window, local_scratch, local_scratch, weight, weight, vector, vector,
             pltpu.SemaphoreType.DMA((6,)),
         ],
-        free=(8, 9, 10, 11, 12, 13),
+        hbm=(5, 6, 7, 8, 9, 10),
     )
 
     small = jnp.concatenate([sums_one[:3], sums_two[:1]]).reshape(-1, 128)
@@ -494,7 +587,8 @@
             functools.partial(unpack_kernel, taps, held),
             (gradient, gradient),
             (*got, *others, *grads),
-            0,
+            2,
+            12,
             [pltpu.VMEM((8 * taps[1], chans, chans), bf16), pltpu.SemaphoreType.DMA((8 * taps[1],))],
             free=(8, 9),
             out_spec=anywhere,

time: 146 us -> 132 us (0.904)
  starting transfers between devices: 63 us -> 48.7 us
  Pallas kernels: 23.9 us -> 27.7 us
  waiting for transfers between devices: 44 us -> 41.4 us
    ppermute x12 -> x4, starting transfers between devices: 27.5 us -> 6.72 us  [moved(): lax.ppermute(value, axis, [(i, i + by) for i in range(size) if 0 <= i + b...]
    pallas_call x6 -> x9, Pallas kernels: 23.9 us -> 27.7 us  [call(): pl.pallas_call(kernel, out_shape=outs, in_specs=[in_hbm if i in hbm else...]
    ppermute x12, starting transfers between devices: 14 us -> 17.5 us  [plane_move(): return lax.ppermute(value, 'height', [(i, i ^ d) for i in range(height)])]
    ppermute x12, waiting for transfers between devices: 30.2 us -> 26.7 us  [plane_move(): return lax.ppermute(value, 'height', [(i, i ^ d) for i in range(height)])]
    squeeze x6 -> x0, local copies, waits for them, and re-layouts: 3.34 us -> none  [pack_frames(): return jnp.concatenate([values[0], values[1]], axis=-1)]
    ppermute x8, starting transfers between devices: 1.01 us -> 2.88 us  [body(): others = [lax.ppermute(g, 'tm', swap) for g in got]]
    ppermute x12, waiting for transfers between devices: 7.11 us -> 5.52 us  [column_move(): return lax.ppermute(value, 'height', pairs)]
    ppermute x1, waiting for transfers between devices: 0.01 us -> 1.48 us  [body(): other = lax.ppermute(give, 'tm', swap)]
  transfers between devices with their start and end apart: 45 -> 39, of which waited for: 14 -> 11; matrix products, arithmetic and copies ran while one was open for 5% -> 3% of each run, Pallas kernels for 12% -> 13%
where the time goes in v4:
time: 132 us
  starting transfers between devices  48.7 us (37%)
  waiting for transfers between devices  41.4 us (31%)
  Pallas kernels  27.7 us (21%)
  local copies, waits for them, and re-layouts  11 us (8%)
  other arithmetic  1.59 us (1%)
    pallas_call x9, Pallas kernels, call(): pl.pallas_call(kernel, out_shape=outs, in_specs=[in_hbm if i in hbm else...  27.7 us
    ppermute x12, waiting for transfers between devices, plane_move(): return lax.ppermute(value, 'height', [(i, i ^ d) for i in range(height)])  26.7 us
    ppermute x12, starting transfers between devices, column_move(): return lax.ppermute(value, 'height', pairs)  20.9 us
    ppermute x12, starting transfers between devices, plane_move(): return lax.ppermute(value, 'height', [(i, i ^ d) for i in range(height)])  17.5 us
    unnamed x36, local copies, waits for them, and re-layouts  7.08 us
    ppermute x4, starting transfers between devices, moved(): lax.ppermute(value, axis, [(i, i + by) for i in range(size) if 0 <= i + b...  6.72 us
    ppermute x12, waiting for transfers between devices, column_move(): return lax.ppermute(value, 'height', pairs)  5.52 us
    ppermute x4, waiting for transfers between devices, moved(): lax.ppermute(value, axis, [(i, i + by) for i in range(size) if 0 <= i + b...  4.95 us
  transfers between devices with their start and end apart: 39, of which 11 were waited for; matrix products, arithmetic and copies ran while one was open for 3% of the time, Pallas kernels for 13%

profile of v4, /device:TPU:0, one launch (start us, length us, event | category | flops | bytes accessed | tf_op | source)
XLA Modules:
  0.0 131.7 jit_solution(15956722589722977975)
XLA Ops:
  5.0 2.9 %collective-permute-start.2 = (bf16[2,4,32,384]{3,2,1,0:T(8,128)(2,1)S(1)}, bf16[2,4,32,384]{3,2,1,0:T(8,128)(2,1)S(1)}, u32[]{:S(2)}, u32[]{:S(2)}) collective-permute-start(bf16[2,4,32,384]{3,2,1,0:T(8,128)(2,1)S(1)} %get-tuple-element.23.refs_4_), channel_id=1, source_target_pairs={{0,2},{1,3},{2,0},{3,1},{4,6},{5,7},{6,4},{7,5},{8,10},{9,11},{10,... | collective-permute-start | bytes 589832 | tf_op jit(solution)/shard_map/ppermute | solution.py:453
  9.5 2.4 %collective-permute-start.3 = (bf16[3,32,384]{2,1,0:T(8,128)(2,1)S(1)}, bf16[3,32,384]{2,1,0:T(8,128)(2,1)S(1)}, u32[]{:S(2)}, u32[]{:S(2)}) collective-permute-start(bf16[3,32,384]{2,1,0:T(8,128)(2,1)S(1)} %get-tuple-element.24), channel_id=1, source_target_pairs={{0,1},{1,2},{2,3},{3,4},{4,5},{5,6},{6,7},{7,8},{8,9},{9,10},{10,1... | collective-permute-start | bytes 221192 | tf_op jit(solution)/shard_map/ppermute | solution.py:425
  13.2 2.0 %collective-permute-done.3.above_ref = bf16[3,32,384]{2,1,0:T(8,128)(2,1)S(1)} collective-permute-done((bf16[3,32,384]{2,1,0:T(8,128)(2,1)S(1)}, bf16[3,32,384]{2,1,0:T(8,128)(2,1)S(1)}, u32[]{:S(2)}, u32[]{:S(2)}) %collective-permute-start.3) | collective-permute-done | bytes 73760 | tf_op jit(solution)/shard_map/ppermute | solution.py:425
  15.3 2.9 %collective-permute-done.4.below_ref = bf16[3,32,384]{2,1,0:T(8,128)(2,1)S(1)} collective-permute-done((bf16[3,32,384]{2,1,0:T(8,128)(2,1)S(1)}, bf16[3,32,384]{2,1,0:T(8,128)(2,1)S(1)}, u32[]{:S(2)}, u32[]{:S(2)}) %collective-permute-start.4) | collective-permute-done | bytes 73760 | tf_op jit(solution)/shard_map/ppermute | solution.py:425
  18.9 7.8 %shard_map.144 = (bf16[4,32,384]{2,1,0:T(8,128)(2,1)}, bf16[4,32,384]{2,1,0:T(8,128)(2,1)}, f32[8,192]{1,0:T(8,128)}) custom-call(bf16[2,4,32,384]{3,2,1,0:T(8,128)(2,1)} %copy-done.4, bf16[2,4,32,384]{3,2,1,0:T(8,128)(2,1)} %copy-done.2, bf16[2,4,32,192]{3,2,1,0:T(8,128)(2,1)} %feat_any.3, bf16[2,4,32,192]{3,2,1,0:T(8,128)(2,1)} %cot_any.3, ...), custom_call_target="tpu_custom_call" | custom-call | bytes 18000000 | tf_op jit(solution)/shard_map/pallas_call | solution.py:411
  31.0 5.3 %collective-permute-start.9 = (bf16[2,5,32,384]{3,2,1,0:T(8,128)(2,1)S(1)}, bf16[2,5,32,384]{3,2,1,0:T(8,128)(2,1)S(1)}, u32[]{:S(2)}, u32[]{:S(2)}) collective-permute-start(bf16[2,5,32,384]{3,2,1,0:T(8,128)(2,1)S(1)} %shard_map.145.refs_0_), channel_id=1, source_target_pairs={{0,3},{1,2},{2,1},{3,0},{4,7},{5,6},{6,5},{7,4},{8,11},{9,10},{10,... | collective-permute-start | bytes 737288 | tf_op jit(solution)/shard_map/ppermute | solution.py:453
  37.3 2.9 %collective-permute-start.10 = (bf16[2,4,32,384]{3,2,1,0:T(8,128)(2,1)S(1)}, bf16[2,4,32,384]{3,2,1,0:T(8,128)(2,1)S(1)}, u32[]{:S(2)}, u32[]{:S(2)}) collective-permute-start(bf16[2,4,32,384]{3,2,1,0:T(8,128)(2,1)S(1)} %get-tuple-element.23.refs_4_), channel_id=1, source_target_pairs={{0,3},{1,2},{2,1},{3,0},{4,7},{5,6},{6,5},{7,4},{8,11},{9,10},{10,... | collective-permute-start | bytes 589832 | tf_op jit(solution)/shard_map/ppermute | solution.py:453
  41.1 11.0 %collective-permute-done.10.refs_7_ = bf16[2,4,32,384]{3,2,1,0:T(8,128)(2,1)S(1)} collective-permute-done((bf16[2,4,32,384]{3,2,1,0:T(8,128)(2,1)S(1)}, bf16[2,4,32,384]{3,2,1,0:T(8,128)(2,1)S(1)}, u32[]{:S(2)}, u32[]{:S(2)}) %collective-permute-start.10) | collective-permute-done | bytes 196640 | tf_op jit(solution)/shard_map/ppermute | solution.py:453
  54.0 3.9 %shard_map.146._.refs_9_ = bf16[896,128]{1,0:T(8,128)(2,1)S(1)} custom-call(bf16[2,5,32,384]{3,2,1,0:T(8,128)(2,1)S(1)} %shard_map.145.refs_0_, bf16[2,5,32,384]{3,2,1,0:T(8,128)(2,1)S(1)} %collective-permute-done.7.refs_1_, bf16[2,5,32,384]{3,2,1,0:T(8,128)(2,1)S(1)} %collective-permute-done.8.refs_2_, ...), custom_call_target="tpu_custom_call" | custom-call | bytes 14400000 | tf_op jit(solution)/shard_map/pallas_call | solution.py:411
  61.0 6.3 %collective-permute-start.26 = (bf16[224,128]{1,0:T(8,128)(2,1)S(1)}, bf16[224,128]{1,0:T(8,128)(2,1)S(1)}, u32[]{:S(2)}, u32[]{:S(2)}) collective-permute-start(bf16[224,128]{1,0:T(8,128)(2,1)S(1)} %get-tuple-element.47), channel_id=1, source_target_pairs={{0,4},{1,5},{2,6},{3,7},{4,8},{5,9},{6,10},{7,11},{8,12},{9,13},{1... | collective-permute-start | bytes 172040 | tf_op jit(solution)/shard_map/ppermute | solution.py:457
  68.1 2.2 %collective-permute-start.27 = (bf16[224,128]{1,0:T(8,128)(2,1)S(1)}, bf16[224,128]{1,0:T(8,128)(2,1)S(1)}, u32[]{:S(2)}, u32[]{:S(2)}) collective-permute-start(bf16[224,128]{1,0:T(8,128)(2,1)S(1)} %get-tuple-element.49), channel_id=1, source_target_pairs={{0,8},{1,9},{2,10},{3,11},{4,12},{5,13},{6,14},{7,15},{8,0},{9,1},... | collective-permute-start | bytes 172040 | tf_op jit(solution)/shard_map/ppermute | solution.py:457
  70.3 4.7 %shard_map.149 = bf16[1152,128]{1,0:T(8,128)(2,1)S(1)} custom-call(bf16[2,5,32,384]{3,2,1,0:T(8,128)(2,1)S(1)} %shard_map.145.refs_0_, bf16[2,5,32,384]{3,2,1,0:T(8,128)(2,1)S(1)} %collective-permute-done.7.refs_1_, bf16[2,5,32,384]{3,2,1,0:T(8,128)(2,1)S(1)} %collective-permute-done.8.refs_2_, bf16[2,5,32,384]{3,2,1,0:T(8,128)(2,1)S(1)} %collective-permute-done.9.refs_3_, ...), custom_call_target="tpu_custom_call" | custom-call | bytes 14400000 | tf_op jit(solution)/shard_map/pallas_call | solution.py:411
  75.4 3.5 %collective-permute-start.15 = (bf16[288,128]{1,0:T(8,128)(2,1)S(1)}, bf16[288,128]{1,0:T(8,128)(2,1)S(1)}, u32[]{:S(2)}, u32[]{:S(2)}) collective-permute-start(bf16[288,128]{1,0:T(8,128)(2,1)S(1)} %get-tuple-element.45), channel_id=1, source_target_pairs={{0,12},{1,13},{2,14},{3,15},{4,0},{5,1},{6,2},{7,3},{8,4},{9,5},{1... | collective-permute-start | bytes 221192 | tf_op jit(solution)/shard_map/ppermute | solution.py:457
  79.9 2.2 %collective-permute-start.30 = (bf16[224,128]{1,0:T(8,128)(2,1)S(1)}, bf16[224,128]{1,0:T(8,128)(2,1)S(1)}, u32[]{:S(2)}, u32[]{:S(2)}) collective-permute-start(bf16[224,128]{1,0:T(8,128)(2,1)S(1)} %fusion.5), channel_id=1, source_target_pairs={{0,8},{1,9},{2,10},{3,11},{4,12},{5,13},{6,14},{7,15},{8,0},{9,1},... | collective-permute-start | bytes 172040 | tf_op jit(solution)/shard_map/ppermute | solution.py:457
  82.1 7.5 %shard_map.148 = (bf16[2,4,32,192]{3,2,1,0:T(8,128)(2,1)}, bf16[2,4,32,192]{3,2,1,0:T(8,128)(2,1)}, f32[8,192]{1,0:T(8,128)}) custom-call(bf16[4,32,384]{2,1,0:T(8,128)(2,1)} %get-tuple-element.26.keep_ref, bf16[4,32,384]{2,1,0:T(8,128)(2,1)} %get-tuple-element.27.give_ref, bf16[1,4,32,384]{3,2,1,0:T(8,128)(2,1)} %bitcast.51, ...), custom_call_target="tpu_custom_call" | custom-call | bytes 21600000 | tf_op jit(solution)/shard_map/pallas_call | solution.py:411
  90.4 2.0 %collective-permute-start.29 = (bf16[224,128]{1,0:T(8,128)(2,1)S(1)}, bf16[224,128]{1,0:T(8,128)(2,1)S(1)}, u32[]{:S(2)}, u32[]{:S(2)}) collective-permute-start(bf16[224,128]{1,0:T(8,128)(2,1)S(1)} %fusion.5), channel_id=1, source_target_pairs={{0,4},{1,5},{2,6},{3,7},{4,8},{5,9},{6,10},{7,11},{8,12},{9,13},{1... | collective-permute-start | bytes 172040 | tf_op jit(solution)/shard_map/ppermute | solution.py:457
  92.4 1.9 %collective-permute-start.18 = (bf16[304,128]{1,0:T(8,128)(2,1)S(1)}, bf16[304,128]{1,0:T(8,128)(2,1)S(1)}, u32[]{:S(2)}, u32[]{:S(2)}) collective-permute-start(bf16[304,128]{1,0:T(8,128)(2,1)S(1)} %pad_maximum_fusion.2), channel_id=1, source_target_pairs={{0,12},{1,13},{2,14},{3,15},{4,0},{5,1},{6,2},{7,3},{8,4},{9,5},{1... | collective-permute-start | bytes 233480 | tf_op jit(solution)/shard_map/ppermute | solution.py:457
  99.4 4.1 %collective-permute-done.17 = bf16[304,128]{1,0:T(8,128)(2,1)S(1)} collective-permute-done((bf16[304,128]{1,0:T(8,128)(2,1)S(1)}, bf16[304,128]{1,0:T(8,128)(2,1)S(1)}, u32[]{:S(2)}, u32[]{:S(2)}) %collective-permute-start.17) | collective-permute-done | bytes 77856 | tf_op jit(solution)/shard_map/ppermute | solution.py:457
  105.7 2.6 %collective-permute-start.20 = (bf16[1168,128]{1,0:T(8,128)(2,1)S(1)}, bf16[1168,128]{1,0:T(8,128)(2,1)S(1)}, u32[]{:S(2)}, u32[]{:S(2)}) collective-permute-start(bf16[1168,128]{1,0:T(8,128)(2,1)S(1)} %concatenate.11.refs_0_), channel_id=1, source_target_pairs={{0,2},{1,3},{2,0},{3,1},{4,6},{5,7},{6,4},{7,5},{8,10},{9,11},{10,... | collective-permute-start | bytes 897032 | tf_op jit(solution)/shard_map/ppermute | solution.py:453
  108.3 4.8 %collective-permute-done.33.refs_2_ = bf16[896,128]{1,0:T(8,128)(2,1)S(1)} collective-permute-done((bf16[896,128]{1,0:T(8,128)(2,1)S(1)}, bf16[896,128]{1,0:T(8,128)(2,1)S(1)}, u32[]{:S(2)}, u32[]{:S(2)}) %collective-permute-start.33) | collective-permute-done | bytes 229408 | tf_op jit(solution)/shard_map/ppermute | solution.py:453
  113.6 5.9 %collective-permute-done.21.refs_3_ = bf16[1168,128]{1,0:T(8,128)(2,1)S(1)} collective-permute-done((bf16[1168,128]{1,0:T(8,128)(2,1)S(1)}, bf16[1168,128]{1,0:T(8,128)(2,1)S(1)}, u32[]{:S(2)}, u32[]{:S(2)}) %collective-permute-start.21) | collective-permute-done | bytes 299040 | tf_op jit(solution)/shard_map/ppermute | solution.py:453
  119.5 5.0 %collective-permute-done.20.refs_2_ = bf16[1168,128]{1,0:T(8,128)(2,1)S(1)} collective-permute-done((bf16[1168,128]{1,0:T(8,128)(2,1)S(1)}, bf16[1168,128]{1,0:T(8,128)(2,1)S(1)}, u32[]{:S(2)}, u32[]{:S(2)}) %collective-permute-start.20) | collective-permute-done | bytes 299040 | tf_op jit(solution)/shard_map/ppermute | solution.py:453
  125.5 1.7 %collective-permute-done.36.refs_5_ = bf16[896,128]{1,0:T(8,128)(2,1)S(1)} collective-permute-done((bf16[896,128]{1,0:T(8,128)(2,1)S(1)}, bf16[896,128]{1,0:T(8,128)(2,1)S(1)}, u32[]{:S(2)}, u32[]{:S(2)}) %collective-permute-start.36) | collective-permute-done | bytes 229408 | tf_op jit(solution)/shard_map/ppermute | solution.py:582
  129.6 1.9 %shard_map.151 = (bf16[27,192,192]{2,1,0:T(8,128)(2,1)}, bf16[27,192,192]{2,1,0:T(8,128)(2,1)}) custom-call(bf16[1168,128]{1,0:T(8,128)(2,1)S(1)} %concatenate.11.refs_0_, bf16[1168,128]{1,0:T(8,128)(2,1)S(1)} %collective-permute-done.19.refs_1_, ...), custom_call_target="tpu_custom_call", output_to_operand_aliasing={{0}: (8, {}), {1}: (9, {})} | custom-call | bytes 7200000 | tf_op jit(solution)/shard_map/pallas_call | solution.py:411
  (133 shorter events, 32.9 us)
Async XLA Ops:
  5.0 13.1 %collective-permute-start.2 = (bf16[2,4,32,384]{3,2,1,0:T(8,128)(2,1)S(1)}, bf16[2,4,32,384]{3,2,1,0:T(8,128)(2,1)S(1)}, u32[]{:S(2)}, u32[]{:S(2)}) collective-permute-start(bf16[2,4,32,384]{3,2,1,0:T(8,128)(2,1)S(1)} %get-tuple-element.23.refs_4_), channel_id=1, source_target_pairs={{0,2},{1,3},{2,0},{3,1},{4,6},{5,7},{6,4},{7,5},{8,10},{9,11},{10,... | collective-permute-start | bytes 589832 | tf_op jit(solution)/shard_map/ppermute | solution.py:453
  8.0 10.2 %collective-permute-start.1 = (bf16[2,4,32,384]{3,2,1,0:T(8,128)(2,1)S(1)}, bf16[2,4,32,384]{3,2,1,0:T(8,128)(2,1)S(1)}, u32[]{:S(2)}, u32[]{:S(2)}) collective-permute-start(bf16[2,4,32,384]{3,2,1,0:T(8,128)(2,1)S(1)} %get-tuple-element.23.refs_4_), channel_id=1, source_target_pairs={{0,1},{1,0},{2,3},{3,2},{4,5},{5,4},{6,7},{7,6},{8,9},{9,8},{10,11... | collective-permute-start | bytes 589832 | tf_op jit(solution)/shard_map/ppermute | solution.py:453
  31.0 21.1 %collective-permute-start.9 = (bf16[2,5,32,384]{3,2,1,0:T(8,128)(2,1)S(1)}, bf16[2,5,32,384]{3,2,1,0:T(8,128)(2,1)S(1)}, u32[]{:S(2)}, u32[]{:S(2)}) collective-permute-start(bf16[2,5,32,384]{3,2,1,0:T(8,128)(2,1)S(1)} %shard_map.145.refs_0_), channel_id=1, source_target_pairs={{0,3},{1,2},{2,1},{3,0},{4,7},{5,6},{6,5},{7,4},{8,11},{9,10},{10,... | collective-permute-start | bytes 737288 | tf_op jit(solution)/shard_map/ppermute | solution.py:453
  36.3 15.8 %collective-permute-start.8 = (bf16[2,5,32,384]{3,2,1,0:T(8,128)(2,1)S(1)}, bf16[2,5,32,384]{3,2,1,0:T(8,128)(2,1)S(1)}, u32[]{:S(2)}, u32[]{:S(2)}) collective-permute-start(bf16[2,5,32,384]{3,2,1,0:T(8,128)(2,1)S(1)} %shard_map.145.refs_0_), channel_id=1, source_target_pairs={{0,2},{1,3},{2,0},{3,1},{4,6},{5,7},{6,4},{7,5},{8,10},{9,11},{10,... | collective-permute-start | bytes 737288 | tf_op jit(solution)/shard_map/ppermute | solution.py:453
  36.3 15.8 %collective-permute-start.7 = (bf16[2,5,32,384]{3,2,1,0:T(8,128)(2,1)S(1)}, bf16[2,5,32,384]{3,2,1,0:T(8,128)(2,1)S(1)}, u32[]{:S(2)}, u32[]{:S(2)}) collective-permute-start(bf16[2,5,32,384]{3,2,1,0:T(8,128)(2,1)S(1)} %shard_map.145.refs_0_), channel_id=1, source_target_pairs={{0,1},{1,0},{2,3},{3,2},{4,5},{5,4},{6,7},{7,6},{8,9},{9,8},{10,11... | collective-permute-start | bytes 737288 | tf_op jit(solution)/shard_map/ppermute | solution.py:453
  37.3 14.7 %collective-permute-start.10 = (bf16[2,4,32,384]{3,2,1,0:T(8,128)(2,1)S(1)}, bf16[2,4,32,384]{3,2,1,0:T(8,128)(2,1)S(1)}, u32[]{:S(2)}, u32[]{:S(2)}) collective-permute-start(bf16[2,4,32,384]{3,2,1,0:T(8,128)(2,1)S(1)} %get-tuple-element.23.refs_4_), channel_id=1, source_target_pairs={{0,3},{1,2},{2,1},{3,0},{4,7},{5,6},{6,5},{7,4},{8,11},{9,10},{10,... | collective-permute-start | bytes 589832 | tf_op jit(solution)/shard_map/ppermute | solution.py:453
  40.3 17.6 %collective-permute-start.5 = (bf16[4,32,384]{2,1,0:T(8,128)(2,1)}, bf16[4,32,384]{2,1,0:T(8,128)(2,1)S(1)}, u32[]{:S(2)}, u32[]{:S(2)}) collective-permute-start(bf16[4,32,384]{2,1,0:T(8,128)(2,1)} %get-tuple-element.26.keep_ref), channel_id=1, source_target_pairs={{0,16},{16,0},{1,17},{17,1},{2,18},{18,2},{3,19},{19,3},{4,20},{20... | collective-permute-start | bytes 294920 | tf_op jit(solution)/shard_map/ppermute | solution.py:490
  58.0 21.0 %collective-permute-start.11 = (bf16[3,32,384]{2,1,0:T(8,128)(2,1)S(1)}, bf16[3,32,384]{2,1,0:T(8,128)(2,1)S(1)}, u32[]{:S(2)}, u32[]{:S(2)}) collective-permute-start(bf16[3,32,384]{2,1,0:T(8,128)(2,1)S(1)} %get-tuple-element.28), channel_id=1, source_target_pairs={{0,1},{1,2},{2,3},{3,4},{4,5},{5,6},{6,7},{7,8},{8,9},{9,10},{10,1... | collective-permute-start | bytes 221192 | tf_op jit(solution)/shard_map/ppermute | solution.py:425
  59.7 20.2 %collective-permute-start.12 = (bf16[3,32,384]{2,1,0:T(8,128)(2,1)S(1)}, bf16[3,32,384]{2,1,0:T(8,128)(2,1)S(1)}, u32[]{:S(2)}, u32[]{:S(2)}) collective-permute-start(bf16[3,32,384]{2,1,0:T(8,128)(2,1)S(1)} %get-tuple-element.29), channel_id=1, source_target_pairs={{1,0},{2,1},{3,2},{4,3},{5,4},{6,5},{7,6},{8,7},{9,8},{10,9},{11,1... | collective-permute-start | bytes 221192 | tf_op jit(solution)/shard_map/ppermute | solution.py:425
  61.0 14.0 %collective-permute-start.26 = (bf16[224,128]{1,0:T(8,128)(2,1)S(1)}, bf16[224,128]{1,0:T(8,128)(2,1)S(1)}, u32[]{:S(2)}, u32[]{:S(2)}) collective-permute-start(bf16[224,128]{1,0:T(8,128)(2,1)S(1)} %get-tuple-element.47), channel_id=1, source_target_pairs={{0,4},{1,5},{2,6},{3,7},{4,8},{5,9},{6,10},{7,11},{8,12},{9,13},{1... | collective-permute-start | bytes 172040 | tf_op jit(solution)/shard_map/ppermute | solution.py:457
  68.1 10.8 %collective-permute-start.27 = (bf16[224,128]{1,0:T(8,128)(2,1)S(1)}, bf16[224,128]{1,0:T(8,128)(2,1)S(1)}, u32[]{:S(2)}, u32[]{:S(2)}) collective-permute-start(bf16[224,128]{1,0:T(8,128)(2,1)S(1)} %get-tuple-element.49), channel_id=1, source_target_pairs={{0,8},{1,9},{2,10},{3,11},{4,12},{5,13},{6,14},{7,15},{8,0},{9,1},... | collective-permute-start | bytes 172040 | tf_op jit(solution)/shard_map/ppermute | solution.py:457
  75.1 15.3 %collective-permute-start.13 = (bf16[288,128]{1,0:T(8,128)(2,1)S(1)}, bf16[288,128]{1,0:T(8,128)(2,1)S(1)}, u32[]{:S(2)}, u32[]{:S(2)}) collective-permute-start(bf16[288,128]{1,0:T(8,128)(2,1)S(1)} %get-tuple-element.44), channel_id=1, source_target_pairs={{0,4},{1,5},{2,6},{3,7},{4,8},{5,9},{6,10},{7,11},{8,12},{9,13},{1... | collective-permute-start | bytes 221192 | tf_op jit(solution)/shard_map/ppermute | solution.py:457
  75.4 16.9 %collective-permute-start.15 = (bf16[288,128]{1,0:T(8,128)(2,1)S(1)}, bf16[288,128]{1,0:T(8,128)(2,1)S(1)}, u32[]{:S(2)}, u32[]{:S(2)}) collective-permute-start(bf16[288,128]{1,0:T(8,128)(2,1)S(1)} %get-tuple-element.45), channel_id=1, source_target_pairs={{0,12},{1,13},{2,14},{3,15},{4,0},{5,1},{6,2},{7,3},{8,4},{9,5},{1... | collective-permute-start | bytes 221192 | tf_op jit(solution)/shard_map/ppermute | solution.py:457
  78.9 13.4 %collective-permute-start.14 = (bf16[288,128]{1,0:T(8,128)(2,1)S(1)}, bf16[288,128]{1,0:T(8,128)(2,1)S(1)}, u32[]{:S(2)}, u32[]{:S(2)}) collective-permute-start(bf16[288,128]{1,0:T(8,128)(2,1)S(1)} %get-tuple-element.46), channel_id=1, source_target_pairs={{0,8},{1,9},{2,10},{3,11},{4,12},{5,13},{6,14},{7,15},{8,0},{9,1},... | collective-permute-start | bytes 221192 | tf_op jit(solution)/shard_map/ppermute | solution.py:457
  79.0 15.4 %collective-permute-start.31 = (bf16[224,128]{1,0:T(8,128)(2,1)S(1)}, bf16[224,128]{1,0:T(8,128)(2,1)S(1)}, u32[]{:S(2)}, u32[]{:S(2)}) collective-permute-start(bf16[224,128]{1,0:T(8,128)(2,1)S(1)} %fusion.5), channel_id=1, source_target_pairs={{0,12},{1,13},{2,14},{3,15},{4,0},{5,1},{6,2},{7,3},{8,4},{9,5},{1... | collective-permute-start | bytes 172040 | tf_op jit(solution)/shard_map/ppermute | solution.py:457
  79.9 15.2 %collective-permute-start.30 = (bf16[224,128]{1,0:T(8,128)(2,1)S(1)}, bf16[224,128]{1,0:T(8,128)(2,1)S(1)}, u32[]{:S(2)}, u32[]{:S(2)}) collective-permute-start(bf16[224,128]{1,0:T(8,128)(2,1)S(1)} %fusion.5), channel_id=1, source_target_pairs={{0,8},{1,9},{2,10},{3,11},{4,12},{5,13},{6,14},{7,15},{8,0},{9,1},... | collective-permute-start | bytes 172040 | tf_op jit(solution)/shard_map/ppermute | solution.py:457
  98.7 9.6 %collective-permute-start.34 = (bf16[896,128]{1,0:T(8,128)(2,1)S(1)}, bf16[896,128]{1,0:T(8,128)(2,1)S(1)}, u32[]{:S(2)}, u32[]{:S(2)}) collective-permute-start(bf16[896,128]{1,0:T(8,128)(2,1)S(1)} %bitcast_select_fusion.1.refs_0_), channel_id=1, source_target_pairs={{0,3},{1,2},{2,1},{3,0},{4,7},{5,6},{6,5},{7,4},{8,11},{9,10},{10,... | collective-permute-start | bytes 688136 | tf_op jit(solution)/shard_map/ppermute | solution.py:453
  99.4 13.7 %collective-permute-start.33 = (bf16[896,128]{1,0:T(8,128)(2,1)S(1)}, bf16[896,128]{1,0:T(8,128)(2,1)S(1)}, u32[]{:S(2)}, u32[]{:S(2)}) collective-permute-start(bf16[896,128]{1,0:T(8,128)(2,1)S(1)} %bitcast_select_fusion.1.refs_0_), channel_id=1, source_target_pairs={{0,2},{1,3},{2,0},{3,1},{4,6},{5,7},{6,4},{7,5},{8,10},{9,11},{10,... | collective-permute-start | bytes 688136 | tf_op jit(solution)/shard_map/ppermute | solution.py:453
  103.5 9.6 %collective-permute-start.32 = (bf16[896,128]{1,0:T(8,128)(2,1)S(1)}, bf16[896,128]{1,0:T(8,128)(2,1)S(1)}, u32[]{:S(2)}, u32[]{:S(2)}) collective-permute-start(bf16[896,128]{1,0:T(8,128)(2,1)S(1)} %bitcast_select_fusion.1.refs_0_), channel_id=1, source_target_pairs={{0,1},{1,0},{2,3},{3,2},{4,5},{5,4},{6,7},{7,6},{8,9},{9,8},{10,11... | collective-permute-start | bytes 688136 | tf_op jit(solution)/shard_map/ppermute | solution.py:453
  104.7 14.7 %collective-permute-start.21 = (bf16[1168,128]{1,0:T(8,128)(2,1)S(1)}, bf16[1168,128]{1,0:T(8,128)(2,1)S(1)}, u32[]{:S(2)}, u32[]{:S(2)}) collective-permute-start(bf16[1168,128]{1,0:T(8,128)(2,1)S(1)} %concatenate.11.refs_0_), channel_id=1, source_target_pairs={{0,3},{1,2},{2,1},{3,0},{4,7},{5,6},{6,5},{7,4},{8,11},{9,10},{10,... | collective-permute-start | bytes 897032 | tf_op jit(solution)/shard_map/ppermute | solution.py:453
  105.7 18.8 %collective-permute-start.20 = (bf16[1168,128]{1,0:T(8,128)(2,1)S(1)}, bf16[1168,128]{1,0:T(8,128)(2,1)S(1)}, u32[]{:S(2)}, u32[]{:S(2)}) collective-permute-start(bf16[1168,128]{1,0:T(8,128)(2,1)S(1)} %concatenate.11.refs_0_), channel_id=1, source_target_pairs={{0,2},{1,3},{2,0},{3,1},{4,6},{5,7},{6,4},{7,5},{8,10},{9,11},{10,... | collective-permute-start | bytes 897032 | tf_op jit(solution)/shard_map/ppermute | solution.py:453
  108.3 16.2 %collective-permute-start.19 = (bf16[1168,128]{1,0:T(8,128)(2,1)S(1)}, bf16[1168,128]{1,0:T(8,128)(2,1)S(1)}, u32[]{:S(2)}, u32[]{:S(2)}) collective-permute-start(bf16[1168,128]{1,0:T(8,128)(2,1)S(1)} %concatenate.11.refs_0_), channel_id=1, source_target_pairs={{0,1},{1,0},{2,3},{3,2},{4,5},{5,4},{6,7},{7,6},{8,9},{9,8},{10,11... | collective-permute-start | bytes 897032 | tf_op jit(solution)/shard_map/ppermute | solution.py:453
  113.1 11.9 %collective-permute-start.38 = (bf16[896,128]{1,0:T(8,128)(2,1)S(1)}, bf16[896,128]{1,0:T(8,128)(2,1)S(1)}, u32[]{:S(2)}, u32[]{:S(2)}) collective-permute-start(bf16[896,128]{1,0:T(8,128)(2,1)S(1)} %collective-permute-done.34.refs_3_), channel_id=1, source_target_pairs={{0,16},{16,0},{1,17},{17,1},{2,18},{18,2},{3,19},{19,3},{4,20},{20... | collective-permute-start | bytes 688136 | tf_op jit(solution)/shard_map/ppermute | solution.py:582
  113.1 11.9 %collective-permute-start.37 = (bf16[896,128]{1,0:T(8,128)(2,1)S(1)}, bf16[896,128]{1,0:T(8,128)(2,1)S(1)}, u32[]{:S(2)}, u32[]{:S(2)}) collective-permute-start(bf16[896,128]{1,0:T(8,128)(2,1)S(1)} %collective-permute-done.33.refs_2_), channel_id=1, source_target_pairs={{0,16},{16,0},{1,17},{17,1},{2,18},{18,2},{3,19},{19,3},{4,20},{20... | collective-permute-start | bytes 688136 | tf_op jit(solution)/shard_map/ppermute | solution.py:582
  (33 other events, 228.6 us)

commit v5 on v4

--- a/solution.py
+++ b/solution.py
@@ -140,25 +140,26 @@
 
 def join_first_kernel(*refs):
     refs, (y_ref, up_ref, down_ref) = refs[:-3], refs[-3:]
-    feat, cot, *far = [pack_frames(ref) for ref in refs]
+    keep, give, *far = [pack_frames(ref) for ref in refs]
     if len(far) == 1:
 
         def odd():
-            y_ref[0], y_ref[1] = far[0], feat
-            put_messages((far[0], feat, cot), up_ref, down_ref)
+            y_ref[0], y_ref[1] = far[0], keep
+            put_messages((far[0], keep, give), up_ref, down_ref)
 
         def even():
-            y_ref[0], y_ref[1] = cot, far[0]
-            put_messages((feat, cot, far[0]), up_ref, down_ref)
+            y_ref[0], y_ref[1] = keep, far[0]
+            put_messages((give, keep, far[0]), up_ref, down_ref)
 
     else:
-        put_messages((far[0], feat, cot, far[1]), up_ref, down_ref)
 
         def odd():
-            y_ref[0], y_ref[1], y_ref[2] = far[2], far[0], feat
+            y_ref[0], y_ref[1], y_ref[2] = far[2], far[0], keep
+            put_messages((far[0], keep, give, far[1]), up_ref, down_ref)
 
         def even():
-            y_ref[0], y_ref[1], y_ref[2] = cot, far[1], far[2]
+            y_ref[0], y_ref[1], y_ref[2] = keep, far[1], far[2]
+            put_messages((far[0], give, keep, far[1]), up_ref, down_ref)
 
     by_core(odd, even)
 
@@ -191,40 +192,39 @@
     by_core(odd, even)
 
 
+def fetch_kernel(w1_any, w2_any, b1_any, g1_any, b2_any, g2_any, w1_ref, w2_ref, vec_ref, sems):
+    vectors = [(ref, vec_ref.at[pl.ds(i, 1)]) for i, ref in enumerate((b1_any, g1_any, b2_any, g2_any))]
+    for copy in started([(w1_any, w1_ref), (w2_any, w2_ref), *vectors], sems):
+        copy.wait()
+
+
 def first_kernel(
-    _, __, feat_any, cot_any, far_ref, above_ref, below_ref, w1_any, w2_any, b1_any, g1_any, g2_any,
-    give_ref, keep_ref, sums_ref, ahead, behind, w1, w2, b1, g1, g2, sems,
+    _, __, ___, keep_in, give_in, far_ref, above_ref, below_ref, w1, w2, vec_ref,
+    give_ref, keep_ref, sums_ref, ahead, behind,
 ):
-    frames, rows, cols, chans = feat_any.shape
+    frames, rows, cols, chans = keep_in.shape
     own = pl.ds(1, rows)
-    copies = started(
-        (
-            (feat_any, ahead.at[pl.ds(2, 2), own]),
-            (g1_any, g1),
-            (w1_any, w1),
-            (b1_any, b1),
-            (g2_any, g2),
-            (cot_any, behind.at[pl.ds(0, 2), own]),
-            (w2_any, w2),
-        ),
-        sems,
-    )
+    b1, g1, g2 = vec_ref[0:1], vec_ref[1:2], vec_ref[3:4]
+
+    def odd_in():
+        ahead[pl.ds(2, 2), own] = keep_in[...]
+        behind[pl.ds(0, 2), own] = give_in[...]
+
+    def even_in():
+        ahead[pl.ds(2, 2), own] = give_in[...]
+        behind[pl.ds(0, 2), own] = keep_in[...]
+
+    by_core(odd_in, even_in)
     fill_far(ahead, behind, far_ref, own)
     fill_edges(ahead, behind, above_ref, below_ref)
-    for copy in copies[:2]:
-        copy.wait()
     for f in range(frames + 2):
         vals = ahead[f].astype(f32).reshape(-1, chans)
-        ahead[f] = norm_silu(vals, g1[...]).astype(bf16).reshape(rows + 2, cols, chans)
-    for copy in copies[2:5]:
-        copy.wait()
-    mid = (conv(ahead, w1, frames, rows, False) + b1[...]).astype(bf16).astype(f32)
-    act2 = norm_silu(mid, g2[...]).astype(bf16).reshape(frames, rows, cols, chans)
+        ahead[f] = norm_silu(vals, g1).astype(bf16).reshape(rows + 2, cols, chans)
+    mid = (conv(ahead, w1, frames, rows, False) + b1).astype(bf16).astype(f32)
+    act2 = norm_silu(mid, g2).astype(bf16).reshape(frames, rows, cols, chans)
     act2 = pack_frames(act2)
-    for copy in copies[5:]:
-        copy.wait()
     grad = conv(behind, w2, frames, rows, True)
-    gmid, d_gain = norm_silu_back(grad, mid, g2[...])
+    gmid, d_gain = norm_silu_back(grad, mid, g2)
     gmid = gmid.astype(bf16)
     cot = behind[:2, 1 : rows + 1].astype(f32).reshape(-1, chans)
     sums_ref[...] = jnp.concatenate(
@@ -250,15 +250,12 @@
 
 
 def last_kernel(
-    keep_ref, give_ref, far_ref, above_ref, below_ref,
-    feat_any, cot_any, w1_any, w2_any, b2_any, g1_any,
-    out_ref, gin_ref, sums_ref, ahead, behind, feat, cot, w1, w2, b2, g1, sems,
+    keep_ref, give_ref, far_ref, above_ref, below_ref, keep_in, give_in, w1, w2, vec_ref,
+    out_ref, gin_ref, sums_ref, ahead, behind,
 ):
     frames, rows, cols, chans = out_ref.shape
     own = pl.ds(1, rows)
-    copies = started(
-        ((w2_any, w2), (b2_any, b2), (feat_any, feat), (w1_any, w1), (cot_any, cot), (g1_any, g1)), sems
-    )
+    g1, b2 = vec_ref[1:2], vec_ref[2:3]
 
     def odd():
         fill_packed(ahead, 2, own, give_ref[...])
@@ -271,16 +268,12 @@
     by_core(odd, even)
     fill_far(ahead, behind, far_ref, own)
     fill_edges(ahead, behind, above_ref, below_ref)
-    for copy in copies[:3]:
-        copy.wait()
-    values = feat[...].astype(f32).reshape(-1, chans)
-    out = values + conv(ahead, w2, frames, rows, False) + b2[...]
+    feat = jnp.where(is_odd(), keep_in[...], give_in[...]).astype(f32).reshape(-1, chans)
+    out = feat + conv(ahead, w2, frames, rows, False) + b2
     out_ref[...] = out.astype(bf16).reshape(out_ref.shape)
-    for copy in copies[3:]:
-        copy.wait()
     grad = conv(behind, w1, frames, rows, True)
-    d_vals, d_gain = norm_silu_back(grad, values, g1[...])
-    gin = d_vals + cot[...].astype(f32).reshape(-1, chans)
+    d_vals, d_gain = norm_silu_back(grad, feat, g1)
+    gin = d_vals + jnp.where(is_odd(), give_in[...], keep_in[...]).astype(f32).reshape(-1, chans)
     gin_ref[...] = gin.astype(bf16).reshape(gin_ref.shape)
     sums_ref[...] = jnp.concatenate([d_gain, jnp.zeros((7, chans), f32)], axis=0)
 
@@ -289,12 +282,17 @@
     return chans + chans // 2
 
 
-def wgrad_kernel(blocks, taps, *refs):
+def chunk_rows(count, chans, planes):
+    unit = 16 * planes
+    return -(-count * pack_rows(chans) // unit) * unit
+
+
+def wgrad_kernel(blocks, planes, *refs):
     xs, ys = refs[:4], refs[4:8]
-    gain_ref = refs[8]
+    gain = refs[8][1:2]
     out_ref, plane, xk = refs[-3:]
     _, rows, cols, _ = ys[0].shape
-    chans = gain_ref.shape[1]
+    chans = gain.shape[1]
     tall = 4 * rows
     cells = 4 * tall * cols
     odd = lax.axis_index("tm") % 2 == 1
@@ -313,7 +311,7 @@
                 @pl.when(odd)
                 def _():
                     flat = part.astype(f32).reshape(-1, chans)
-                    plane[place] = norm_silu(flat, gain_ref[...]).astype(bf16).reshape(part.shape)
+                    plane[place] = norm_silu(flat, gain).astype(bf16).reshape(part.shape)
 
                 @pl.when(jnp.logical_not(odd))
                 def _():
@@ -341,35 +339,44 @@
 
     step = pack_rows(chans)
     dims = (((0,), (0,)), ((), ()))
-    first, count = taps
     half = chans // 2
-
-    def store(base, grad):
-        grad = grad.astype(bf16)
-        out_ref[base : base + chans] = grad[:, :128]
-        out_ref[base + chans : base + step] = jnp.concatenate(
-            [grad[:half, 128:], grad[half:, 128:]], axis=1
-        )
-
-    for j in range(count):
-        tap = jnp.minimum(p * taps_each + first + j, taps_all - 1)
-        t, h, k = tap // 9, tap // 3 % 3, tap % 3
-
-        @pl.when(odd)
-        def _():
-            piece = plane[pl.ds(t, 4), pl.ds(h, tall)].reshape(cells, chans)
-            x = xk[k].reshape(cells, chans)
-            store(j * step, lax.dot_general(piece, x, dims, preferred_element_type=f32))
-
-        @pl.when(jnp.logical_not(odd))
-        def _():
-            piece = plane[pl.ds(2 - t, 4), pl.ds(2 - h, tall)].reshape(cells, chans)
-            x = xk[2 - k].reshape(cells, chans)
-            store(j * step, lax.dot_general(x, piece, dims, preferred_element_type=f32))
-
-    used = count * step
-    if used < out_ref.shape[0]:
-        out_ref[used:] = jnp.zeros((out_ref.shape[0] - used, 128), bf16)
+    offset = 0
+    for first, count in chunks:
+        share = chunk_rows(count, chans, planes) // planes
+
+        def put(row, values, offset=offset, share=share):
+            at = 0
+            while at < values.shape[0]:
+                q, r = divmod(row + at, share)
+                n = min(share - r, values.shape[0] - at)
+                out_ref[q, offset + r : offset + r + n] = values[at : at + n]
+                at += n
+
+        def store(row, grad, put=put):
+            grad = grad.astype(bf16)
+            put(row, grad[:, :128])
+            put(row + chans, jnp.concatenate([grad[:half, 128:], grad[half:, 128:]], axis=1))
+
+        for j in range(count):
+            tap = jnp.minimum(p * taps_each + first + j, taps_all - 1)
+            t, h, k = tap // 9, tap // 3 % 3, tap % 3
+
+            @pl.when(odd)
+            def _():
+                piece = plane[pl.ds(t, 4), pl.ds(h, tall)].reshape(cells, chans)
+                x = xk[k].reshape(cells, chans)
+                store(j * step, lax.dot_general(piece, x, dims, preferred_element_type=f32))
+
+            @pl.when(jnp.logical_not(odd))
+            def _():
+                piece = plane[pl.ds(2 - t, 4), pl.ds(2 - h, tall)].reshape(cells, chans)
+                x = xk[2 - k].reshape(cells, chans)
+                store(j * step, lax.dot_general(x, piece, dims, preferred_element_type=f32))
+
+        spare = share * planes - count * step
+        if spare:
+            put(count * step, jnp.zeros((spare, 128), bf16))
+        offset += share
 
 
 def unpack_kernel(taps, held, *refs):
@@ -415,7 +422,7 @@
         out_specs=[out_spec] * len(outs),
         scratch_shapes=list(scratch),
         compiler_params=pltpu.CompilerParams(vmem_limit_bytes=mib * 2**20),
-        cost_estimate=pl.CostEstimate(flops=0, bytes_accessed=int(us * 3.6e6), transcendentals=0),
+        cost_estimate=pl.CostEstimate(flops=int(us * 1.1e9), bytes_accessed=1024, transcendentals=0),
         **kw,
     )(*args)
 
@@ -445,8 +452,6 @@
     local = jax.ShapeDtypeStruct(features.shape, bf16)
     sums = jax.ShapeDtypeStruct((8, chans), f32)
     window = pltpu.VMEM((frames + 2, rows + 2, cols, chans), bf16)
-    weight = pltpu.VMEM(weight_one.shape, bf16)
-    vector = pltpu.VMEM((1, chans), f32)
     packed_shape = jax.ShapeDtypeStruct((rows, cols, 2 * chans), bf16)
 
     def plane_move(value, d):
@@ -461,28 +466,35 @@
     messages = (jax.ShapeDtypeStruct((3 if pair else 4, cols, 2 * chans), bf16),) * 2
     y_shape = jax.ShapeDtypeStruct((blocks, rows, cols, 2 * chans), bf16)
     x_shape = jax.ShapeDtypeStruct((blocks, rows + 1, cols, 2 * chans), bf16)
+    raw_give, raw_keep = jnp.where(odd, cotangent, features), jnp.where(odd, features, cotangent)
     if pair:
-        far = (lax.ppermute(jnp.where(odd, cotangent, features), "tm", swap),)
+        far = (lax.ppermute(raw_give, "tm", swap),)
         extra = ()
     else:
         far = (moved(features, "tm", 1), moved(cotangent, "tm", -1))
         extra = (lax.ppermute(jnp.where(odd, far[1], far[0]), "tm", swap),)
-    y_own, up, down = call(join_first_kernel, (y_shape, *messages), (features, cotangent, *far, *extra), 1, 8)
+    held = jax.ShapeDtypeStruct(weight_one.shape, bf16)
+    w1, w2, vec = call(
+        fetch_kernel,
+        (held, held, jax.ShapeDtypeStruct((8, chans), f32)),
+        (weight_one, weight_two, line(bias_one), line(gain_one), line(bias_two), line(gain_two)),
+        3,
+        8,
+        [pltpu.SemaphoreType.DMA((6,))],
+        hbm=range(6),
+    )
+    y_own, up, down = call(join_first_kernel, (y_shape, *messages), (raw_keep, raw_give, *far, *extra), 1, 8)
     above, below = moved(up, "height", 1), moved(down, "height", -1)
     ys = [y_own] + [plane_move(y_own, d) for d in (1, 2, 3)]
 
     give, keep, sums_one = call(
         first_kernel,
         (packed_shape, packed_shape, sums),
-        (
-            ys[1], ys[2], features, cotangent, jnp.stack(far), above, below,
-            weight_one, weight_two, line(bias_one), line(gain_one), line(gain_two),
-        ),
+        (*ys[1:], raw_keep, raw_give, jnp.stack(far), above, below, w1, w2, vec),
         5,
-        62,
-        [window, window, weight, weight, vector, vector, vector, pltpu.SemaphoreType.DMA((7,))],
-        free=(0, 1),
-        hbm=(2, 3, 7, 8, 9, 10, 11),
+        20,
+        [window, window],
+        free=(0, 1, 2),
     )
     other = lax.ppermute(give, "tm", swap)
     if pair:
@@ -497,54 +509,37 @@
         act2, gmid = jnp.where(odd, give, keep), jnp.where(odd, keep, give)
         far = jnp.stack([moved(act2, "tm", 1), moved(gmid, "tm", -1)])
     xs = [x_own] + [plane_move(x_own, d) for d in (1, 2, 3)]
-    before = ()
-
-    step = pack_rows(chans)
-    unit = 16 * planes
-    cells = (2 * frames, 4 * rows, cols, chans)
-    parts = []
-    for taps in chunks:
-        packed = -(-taps[1] * step // unit) * unit
-        (flat,) = call(
-            functools.partial(wgrad_kernel, blocks, taps),
-            (jax.ShapeDtypeStruct((packed, 128), bf16),),
-            (*xs, *ys, line(gain_one), *before),
-            4,
-            24,
-            free=tuple(range(9, 9 + len(before))),
-            scratch=[
-                pltpu.VMEM((2 * frames + 2, 4 * rows + 2, cols, chans), bf16),
-                pltpu.VMEM((3, *cells), bf16),
-            ],
-        )
-        if not before:
-            up, down = call(gate_kernel, messages, (keep, give, far, flat), 1, 6, free=(3,))
-            above, below = moved(up, "height", 1), moved(down, "height", -1)
-        before = (flat,)
-        flat = flat.reshape(planes, packed // planes, 128)
-        arrived = [column_move(piece_at(flat, (q + d) % planes), d) for d in range(1, planes)]
-        part = total_of([piece_at(flat, q), *arrived])
-        hop = 2
-        while hop < tm:
-            part = part + lax.ppermute(part, "tm", [(i, i ^ hop) for i in range(tm)])
-            hop *= 2
-        parts.append(part.astype(bf16))
-
-    local_scratch = pltpu.VMEM(features.shape, bf16)
+    up, down = call(gate_kernel, messages, (keep, give, far, xs[1]), 1, 6, free=(3,))
+    above, below = moved(up, "height", 1), moved(down, "height", -1)
+
+    shares = [chunk_rows(count, chans, planes) // planes for _, count in chunks]
+    (flat,) = call(
+        functools.partial(wgrad_kernel, blocks, planes),
+        (jax.ShapeDtypeStruct((planes, sum(shares), 128), bf16),),
+        (*xs, *ys, vec),
+        7,
+        24,
+        [
+            pltpu.VMEM((2 * frames + 2, 4 * rows + 2, cols, chans), bf16),
+            pltpu.VMEM((3, 2 * frames, 4 * rows, cols, chans), bf16),
+        ],
+    )
+    arrived = [column_move(piece_at(flat, (q + d) % planes), d) for d in range(1, planes)]
+    part = total_of([piece_at(flat, q), *arrived])
+    hop = 2
+    while hop < tm:
+        part = part + lax.ppermute(part, "tm", [(i, i ^ hop) for i in range(tm)])
+        hop *= 2
+    part = part.astype(bf16)
+    parts = jnp.split(part, [sum(shares[:n]) for n in range(1, len(shares))])
+
     block_out, grad_input, sums_two = call(
         last_kernel,
         (local, local, sums),
-        (
-            keep, give, far, above, below, features, cotangent,
-            weight_one, weight_two, line(bias_two), line(gain_one),
-        ),
+        (keep, give, far, above, below, raw_keep, raw_give, w1, w2, vec),
         6,
-        62,
-        [
-            window, window, local_scratch, local_scratch, weight, weight, vector, vector,
-            pltpu.SemaphoreType.DMA((6,)),
-        ],
-        hbm=(5, 6, 7, 8, 9, 10),
+        20,
+        [window, window],
     )
 
     small = jnp.concatenate([sums_one[:3], sums_two[:1]]).reshape(-1, 128)

time: 132 us -> 105 us (0.80)
  starting transfers between devices: 48.7 us -> 37.4 us
  Pallas kernels: 27.7 us -> 16.8 us
  local copies, waits for them, and re-layouts: 11 us -> 4.39 us
  waiting for transfers between devices: 41.4 us -> 42.8 us
    pallas_call x9, Pallas kernels: 27.7 us -> 16.8 us  [call(): pl.pallas_call(kernel, out_shape=outs, in_specs=[in_hbm if i in hbm else...]
    ppermute x12 -> x9, waiting for transfers between devices: 5.52 us -> 14.2 us  [column_move(): return lax.ppermute(value, 'height', pairs)]
    ppermute x12 -> x9, starting transfers between devices: 20.9 us -> 12.3 us  [column_move(): return lax.ppermute(value, 'height', pairs)]
    ppermute x12, waiting for transfers between devices: 26.7 us -> 20.2 us  [plane_move(): return lax.ppermute(value, 'height', [(i, i ^ d) for i in range(height)])]
    unnamed x36, local copies, waits for them, and re-layouts: 7.08 us -> 1.82 us
    ppermute x12, starting transfers between devices: 17.5 us -> 13 us  [plane_move(): return lax.ppermute(value, 'height', [(i, i ^ d) for i in range(height)])]
    ppermute x4, starting transfers between devices: 6.72 us -> 10 us  [moved(): lax.ppermute(value, axis, [(i, i + by) for i in range(size) if 0 <= i + b...]
    ppermute x8, waiting for transfers between devices: 1.76 us -> 0.14 us  [body(): others = [lax.ppermute(g, 'tm', swap) for g in got]]
  transfers between devices with their start and end apart: 39 -> 36, of which waited for: 11 -> 18; matrix products, arithmetic and copies ran while one was open for 3% -> 2% of each run, Pallas kernels for 13% -> 11%
where the time goes in v5:
time: 105 us
  waiting for transfers between devices  42.8 us (41%)
  starting transfers between devices  37.4 us (36%)
  Pallas kernels  16.8 us (16%)
  local copies, waits for them, and re-layouts  4.39 us (4%)
  other arithmetic  1.79 us (2%)
  between operations  1.44 us (1%)
    ppermute x12, waiting for transfers between devices, plane_move(): return lax.ppermute(value, 'height', [(i, i ^ d) for i in range(height)])  20.2 us
    pallas_call x9, Pallas kernels, call(): pl.pallas_call(kernel, out_shape=outs, in_specs=[in_hbm if i in hbm else...  16.8 us
    ppermute x9, waiting for transfers between devices, column_move(): return lax.ppermute(value, 'height', pairs)  14.2 us
    ppermute x12, starting transfers between devices, plane_move(): return lax.ppermute(value, 'height', [(i, i ^ d) for i in range(height)])  13 us
    ppermute x9, starting transfers between devices, column_move(): return lax.ppermute(value, 'height', pairs)  12.3 us
    ppermute x4, starting transfers between devices, moved(): lax.ppermute(value, axis, [(i, i + by) for i in range(size) if 0 <= i + b...  10 us
    ppermute x4, waiting for transfers between devices, moved(): lax.ppermute(value, axis, [(i, i + by) for i in range(size) if 0 <= i + b...  4.8 us
  transfers between devices with their start and end apart: 36, of which 18 were waited for; matrix products, arithmetic and copies ran while one was open for 2% of the time, Pallas kernels for 11%

profile of v5, /device:TPU:0, one launch (start us, length us, event | category | flops | bytes accessed | tf_op | source)
XLA Modules:
  0.0 104.7 jit_solution(13987924606799249355)
XLA Ops:
  3.5 3.9 %collective-permute-start.3 = (bf16[2,4,32,384]{3,2,1,0:T(8,128)(2,1)S(1)}, bf16[2,4,32,384]{3,2,1,0:T(8,128)(2,1)S(1)}, u32[]{:S(2)}, u32[]{:S(2)}) collective-permute-start(bf16[2,4,32,384]{3,2,1,0:T(8,128)(2,1)S(1)} %get-tuple-element.26.refs_4_), channel_id=1, source_target_pairs={{0,3},{1,2},{2,1},{3,0},{4,7},{5,6},{6,5},{7,4},{8,11},{9,10},{10,... | collective-permute-start | bytes 589832 | tf_op jit(solution)/shard_map/ppermute | solution.py:458
  8.0 3.8 %collective-permute-start.4 = (bf16[3,32,384]{2,1,0:T(8,128)(2,1)S(1)}, bf16[3,32,384]{2,1,0:T(8,128)(2,1)S(1)}, u32[]{:S(2)}, u32[]{:S(2)}) collective-permute-start(bf16[3,32,384]{2,1,0:T(8,128)(2,1)S(1)} %get-tuple-element.27), channel_id=1, source_target_pairs={{0,1},{1,2},{2,3},{3,4},{4,5},{5,6},{6,7},{7,8},{8,9},{9,10},{10,1... | collective-permute-start | bytes 221192 | tf_op jit(solution)/shard_map/ppermute | solution.py:432
  13.2 1.7 %copy-done.1 = bf16[3,3,3,192,192]{4,3,2,1,0:T(8,128)(2,1)S(1)} copy-done((bf16[3,3,3,192,192]{4,3,2,1,0:T(8,128)(2,1)S(1)}, bf16[3,3,3,192,192]{4,3,2,1,0:T(8,128)(2,1)}, u32[]{:S(2)}) %copy-start.1) | copy-done | bytes 1990680
  15.5 3.8 %collective-permute-done.4.above_ref = bf16[3,32,384]{2,1,0:T(8,128)(2,1)S(1)} collective-permute-done((bf16[3,32,384]{2,1,0:T(8,128)(2,1)S(1)}, bf16[3,32,384]{2,1,0:T(8,128)(2,1)S(1)}, u32[]{:S(2)}, u32[]{:S(2)}) %collective-permute-start.4) | collective-permute-done | bytes 73760 | tf_op jit(solution)/shard_map/ppermute | solution.py:432
  20.3 2.7 %shard_map.145 = (bf16[4,32,384]{2,1,0:T(8,128)(2,1)S(1)}, bf16[4,32,384]{2,1,0:T(8,128)(2,1)S(1)}, f32[8,192]{1,0:T(8,128)S(1)}) custom-call(bf16[2,4,32,384]{3,2,1,0:T(8,128)(2,1)S(1)} %collective-permute-done.1._.refs_5_, bf16[2,4,32,384]{3,2,1,0:T(8,128)(2,1)S(1)} %collective-permute-done.2.__.refs_6_, ...), custom_call_target="tpu_custom_call" | custom-call | flops 5500000256 | bytes 1024 | tf_op jit(solution)/shard_map/pallas_call | solution.py:418
  24.5 1.6 %collective-permute-start.8 = (bf16[2,5,32,384]{3,2,1,0:T(8,128)(2,1)S(1)}, bf16[2,5,32,384]{3,2,1,0:T(8,128)(2,1)S(1)}, u32[]{:S(2)}, u32[]{:S(2)}) collective-permute-start(bf16[2,5,32,384]{3,2,1,0:T(8,128)(2,1)S(1)} %shard_map.146.refs_0_), channel_id=1, source_target_pairs={{0,1},{1,0},{2,3},{3,2},{4,5},{5,4},{6,7},{7,6},{8,9},{9,8},{10,11... | collective-permute-start | bytes 737288 | tf_op jit(solution)/shard_map/ppermute | solution.py:458
  29.9 3.5 %collective-permute-done.8._.refs_1_ = bf16[2,5,32,384]{3,2,1,0:T(8,128)(2,1)S(1)} collective-permute-done((bf16[2,5,32,384]{3,2,1,0:T(8,128)(2,1)S(1)}, bf16[2,5,32,384]{3,2,1,0:T(8,128)(2,1)S(1)}, u32[]{:S(2)}, u32[]{:S(2)}) %collective-permute-start.8) | collective-permute-done | bytes 245792 | tf_op jit(solution)/shard_map/ppermute | solution.py:458
  33.4 3.4 %collective-permute-start.9 = (bf16[3,32,384]{2,1,0:T(8,128)(2,1)S(1)}, bf16[3,32,384]{2,1,0:T(8,128)(2,1)S(1)}, u32[]{:S(2)}, u32[]{:S(2)}) collective-permute-start(bf16[3,32,384]{2,1,0:T(8,128)(2,1)S(1)} %get-tuple-element.34), channel_id=1, source_target_pairs={{0,1},{1,2},{2,3},{3,4},{4,5},{5,6},{6,7},{7,8},{8,9},{9,10},{10,1... | collective-permute-start | bytes 221192 | tf_op jit(solution)/shard_map/ppermute | solution.py:432
  36.9 1.6 %collective-permute-start.10 = (bf16[3,32,384]{2,1,0:T(8,128)(2,1)S(1)}, bf16[3,32,384]{2,1,0:T(8,128)(2,1)S(1)}, u32[]{:S(2)}, u32[]{:S(2)}) collective-permute-start(bf16[3,32,384]{2,1,0:T(8,128)(2,1)S(1)} %get-tuple-element.35), channel_id=1, source_target_pairs={{1,0},{2,1},{3,2},{4,3},{5,4},{6,5},{7,6},{8,7},{9,8},{10,9},{11,1... | collective-permute-start | bytes 221192 | tf_op jit(solution)/shard_map/ppermute | solution.py:432
  38.4 1.5 %collective-permute-done.11.refs_2_ = bf16[2,5,32,384]{3,2,1,0:T(8,128)(2,1)S(1)} collective-permute-done((bf16[2,5,32,384]{3,2,1,0:T(8,128)(2,1)S(1)}, bf16[2,5,32,384]{3,2,1,0:T(8,128)(2,1)S(1)}, u32[]{:S(2)}, u32[]{:S(2)}) %collective-permute-start.11) | collective-permute-done | bytes 245792 | tf_op jit(solution)/shard_map/ppermute | solution.py:458
  40.0 6.5 %shard_map.149 = bf16[4,512,128]{2,1,0:T(8,128)(2,1)S(1)} custom-call(bf16[2,5,32,384]{3,2,1,0:T(8,128)(2,1)S(1)} %shard_map.146.refs_0_, bf16[2,5,32,384]{3,2,1,0:T(8,128)(2,1)S(1)} %collective-permute-done.8._.refs_1_, bf16[2,5,32,384]{3,2,1,0:T(8,128)(2,1)S(1)} %collective-permute-done.11.refs_2_, ...), custom_call_target="tpu_custom_call" | custom-call | flops 7699999744 | bytes 1024 | tf_op jit(solution)/shard_map/pallas_call | solution.py:418
  46.5 3.1 %collective-permute-start.13 = (bf16[512,128]{1,0:T(8,128)(2,1)S(1)}, bf16[512,128]{1,0:T(8,128)(2,1)S(1)}, u32[]{:S(2)}, u32[]{:S(2)}) collective-permute-start(bf16[512,128]{1,0:T(8,128)(2,1)S(1)} %get-tuple-element.50), channel_id=1, source_target_pairs={{0,4},{1,5},{2,6},{3,7},{4,8},{5,9},{6,10},{7,11},{8,12},{9,13},{1... | collective-permute-start | bytes 393224 | tf_op jit(solution)/shard_map/ppermute | solution.py:462
  49.6 2.1 %collective-permute-start.15 = (bf16[512,128]{1,0:T(8,128)(2,1)S(1)}, bf16[512,128]{1,0:T(8,128)(2,1)S(1)}, u32[]{:S(2)}, u32[]{:S(2)}) collective-permute-start(bf16[512,128]{1,0:T(8,128)(2,1)S(1)} %get-tuple-element.51), channel_id=1, source_target_pairs={{0,12},{1,13},{2,14},{3,15},{4,0},{5,1},{6,2},{7,3},{8,4},{9,5},{1... | collective-permute-start | bytes 393224 | tf_op jit(solution)/shard_map/ppermute | solution.py:462
  52.6 3.3 %shard_map.148 = (bf16[2,4,32,192]{3,2,1,0:T(8,128)(2,1)}, bf16[2,4,32,192]{3,2,1,0:T(8,128)(2,1)}, f32[8,192]{1,0:T(8,128)S(1)}) custom-call(bf16[4,32,384]{2,1,0:T(8,128)(2,1)S(1)} %get-tuple-element.32.keep_ref, bf16[4,32,384]{2,1,0:T(8,128)(2,1)S(1)} %get-tuple-element.33.give_ref, bf16[1,4,32,384]{3,2,1,0:T(8,128)(2,1)S(1)} %bitcast.38, ...), custom_call_target="tpu_custom_call" | custom-call | flops 6600000000 | bytes 1024 | tf_op jit(solution)/shard_map/pallas_call | solution.py:418
  56.1 2.3 %collective-permute-done.15 = bf16[512,128]{1,0:T(8,128)(2,1)S(1)} collective-permute-done((bf16[512,128]{1,0:T(8,128)(2,1)S(1)}, bf16[512,128]{1,0:T(8,128)(2,1)S(1)}, u32[]{:S(2)}, u32[]{:S(2)}) %collective-permute-start.15) | collective-permute-done | bytes 131104 | tf_op jit(solution)/shard_map/ppermute | solution.py:462
  58.3 5.9 %collective-permute-done.14 = bf16[512,128]{1,0:T(8,128)(2,1)S(1)} collective-permute-done((bf16[512,128]{1,0:T(8,128)(2,1)S(1)}, bf16[512,128]{1,0:T(8,128)(2,1)S(1)}, u32[]{:S(2)}, u32[]{:S(2)}) %collective-permute-start.14) | collective-permute-done | bytes 131104 | tf_op jit(solution)/shard_map/ppermute | solution.py:462
  64.5 2.4 %collective-permute-start.26 = (bf16[224,128]{1,0:T(8,128)(2,1)S(1)}, bf16[224,128]{1,0:T(8,128)(2,1)S(1)}, u32[]{:S(2)}, u32[]{:S(2)}) collective-permute-start(bf16[224,128]{1,0:T(8,128)(2,1)S(1)} %get-tuple-element.56), channel_id=1, source_target_pairs={{0,4},{1,5},{2,6},{3,7},{4,8},{5,9},{6,10},{7,11},{8,12},{9,13},{1... | collective-permute-start | bytes 172040 | tf_op jit(solution)/shard_map/ppermute | solution.py:462
  74.8 4.0 %collective-permute-done.17 = bf16[304,128]{1,0:T(8,128)(2,1)S(1)} collective-permute-done((bf16[304,128]{1,0:T(8,128)(2,1)S(1)}, bf16[304,128]{1,0:T(8,128)(2,1)S(1)}, u32[]{:S(2)}, u32[]{:S(2)}) %collective-permute-start.17) | collective-permute-done | bytes 77856 | tf_op jit(solution)/shard_map/ppermute | solution.py:462
  80.1 2.3 %collective-permute-start.21 = (bf16[1168,128]{1,0:T(8,128)(2,1)S(1)}, bf16[1168,128]{1,0:T(8,128)(2,1)S(1)}, u32[]{:S(2)}, u32[]{:S(2)}) collective-permute-start(bf16[1168,128]{1,0:T(8,128)(2,1)S(1)} %concatenate.11.refs_0_), channel_id=1, source_target_pairs={{0,3},{1,2},{2,1},{3,0},{4,7},{5,6},{6,5},{7,4},{8,11},{9,10},{10,... | collective-permute-start | bytes 897032 | tf_op jit(solution)/shard_map/ppermute | solution.py:458
  83.6 4.1 %collective-permute-done.30.refs_2_ = bf16[896,128]{1,0:T(8,128)(2,1)S(1)} collective-permute-done((bf16[896,128]{1,0:T(8,128)(2,1)S(1)}, bf16[896,128]{1,0:T(8,128)(2,1)S(1)}, u32[]{:S(2)}, u32[]{:S(2)}) %collective-permute-start.30) | collective-permute-done | bytes 229408 | tf_op jit(solution)/shard_map/ppermute | solution.py:458
  88.2 5.9 %collective-permute-done.21.refs_3_ = bf16[1168,128]{1,0:T(8,128)(2,1)S(1)} collective-permute-done((bf16[1168,128]{1,0:T(8,128)(2,1)S(1)}, bf16[1168,128]{1,0:T(8,128)(2,1)S(1)}, u32[]{:S(2)}, u32[]{:S(2)}) %collective-permute-start.21) | collective-permute-done | bytes 299040 | tf_op jit(solution)/shard_map/ppermute | solution.py:458
  94.1 5.0 %collective-permute-done.20.refs_2_ = bf16[1168,128]{1,0:T(8,128)(2,1)S(1)} collective-permute-done((bf16[1168,128]{1,0:T(8,128)(2,1)S(1)}, bf16[1168,128]{1,0:T(8,128)(2,1)S(1)}, u32[]{:S(2)}, u32[]{:S(2)}) %collective-permute-start.20) | collective-permute-done | bytes 299040 | tf_op jit(solution)/shard_map/ppermute | solution.py:458
  100.1 1.7 %shard_map.150 = (bf16[27,192,192]{2,1,0:T(8,128)(2,1)}, bf16[27,192,192]{2,1,0:T(8,128)(2,1)}) custom-call(bf16[896,128]{1,0:T(8,128)(2,1)S(1)} %bitcast_select_fusion.1.refs_0_, bf16[896,128]{1,0:T(8,128)(2,1)S(1)} %collective-permute-done.29.refs_1_, bf16[896,128]{1,0:T(8,128)(2,1)S(1)} %collective-permute-done.30.refs_2_, ...), custom_call_target="tpu_custom_call" | custom-call | flops 2200000000 | bytes 1024 | tf_op jit(solution)/shard_map/pallas_call | solution.py:418
  102.6 1.9 %shard_map.151 = (bf16[27,192,192]{2,1,0:T(8,128)(2,1)}, bf16[27,192,192]{2,1,0:T(8,128)(2,1)}) custom-call(bf16[1168,128]{1,0:T(8,128)(2,1)S(1)} %concatenate.11.refs_0_, bf16[1168,128]{1,0:T(8,128)(2,1)S(1)} %collective-permute-done.19.refs_1_, ...), custom_call_target="tpu_custom_call", output_to_operand_aliasing={{0}: (8, {}), {1}: (9, {})} | custom-call | flops 2200000000 | bytes 1024 | tf_op jit(solution)/shard_map/pallas_call | solution.py:418
  (127 shorter events, 25.3 us)
Async XLA Ops:
  3.5 16.8 %collective-permute-start.3 = (bf16[2,4,32,384]{3,2,1,0:T(8,128)(2,1)S(1)}, bf16[2,4,32,384]{3,2,1,0:T(8,128)(2,1)S(1)}, u32[]{:S(2)}, u32[]{:S(2)}) collective-permute-start(bf16[2,4,32,384]{3,2,1,0:T(8,128)(2,1)S(1)} %get-tuple-element.26.refs_4_), channel_id=1, source_target_pairs={{0,3},{1,2},{2,1},{3,0},{4,7},{5,6},{6,5},{7,4},{8,11},{9,10},{10,... | collective-permute-start | bytes 589832 | tf_op jit(solution)/shard_map/ppermute | solution.py:458
  7.4 12.9 %collective-permute-start.2 = (bf16[2,4,32,384]{3,2,1,0:T(8,128)(2,1)S(1)}, bf16[2,4,32,384]{3,2,1,0:T(8,128)(2,1)S(1)}, u32[]{:S(2)}, u32[]{:S(2)}) collective-permute-start(bf16[2,4,32,384]{3,2,1,0:T(8,128)(2,1)S(1)} %get-tuple-element.26.refs_4_), channel_id=1, source_target_pairs={{0,2},{1,3},{2,0},{3,1},{4,6},{5,7},{6,4},{7,5},{8,10},{9,11},{10,... | collective-permute-start | bytes 589832 | tf_op jit(solution)/shard_map/ppermute | solution.py:458
  7.9 12.4 %collective-permute-start.1 = (bf16[2,4,32,384]{3,2,1,0:T(8,128)(2,1)S(1)}, bf16[2,4,32,384]{3,2,1,0:T(8,128)(2,1)S(1)}, u32[]{:S(2)}, u32[]{:S(2)}) collective-permute-start(bf16[2,4,32,384]{3,2,1,0:T(8,128)(2,1)S(1)} %get-tuple-element.26.refs_4_), channel_id=1, source_target_pairs={{0,1},{1,0},{2,3},{3,2},{4,5},{5,4},{6,7},{7,6},{8,9},{9,8},{10,11... | collective-permute-start | bytes 589832 | tf_op jit(solution)/shard_map/ppermute | solution.py:458
  8.0 11.3 %collective-permute-start.4 = (bf16[3,32,384]{2,1,0:T(8,128)(2,1)S(1)}, bf16[3,32,384]{2,1,0:T(8,128)(2,1)S(1)}, u32[]{:S(2)}, u32[]{:S(2)}) collective-permute-start(bf16[3,32,384]{2,1,0:T(8,128)(2,1)S(1)} %get-tuple-element.27), channel_id=1, source_target_pairs={{0,1},{1,2},{2,3},{3,4},{4,5},{5,6},{6,7},{7,8},{8,9},{9,10},{10,1... | collective-permute-start | bytes 221192 | tf_op jit(solution)/shard_map/ppermute | solution.py:432
  11.8 8.4 %collective-permute-start.5 = (bf16[3,32,384]{2,1,0:T(8,128)(2,1)S(1)}, bf16[3,32,384]{2,1,0:T(8,128)(2,1)S(1)}, u32[]{:S(2)}, u32[]{:S(2)}) collective-permute-start(bf16[3,32,384]{2,1,0:T(8,128)(2,1)S(1)} %get-tuple-element.28), channel_id=1, source_target_pairs={{1,0},{2,1},{3,2},{4,3},{5,4},{6,5},{7,6},{8,7},{9,8},{10,9},{11,1... | collective-permute-start | bytes 221192 | tf_op jit(solution)/shard_map/ppermute | solution.py:432
  24.5 8.9 %collective-permute-start.8 = (bf16[2,5,32,384]{3,2,1,0:T(8,128)(2,1)S(1)}, bf16[2,5,32,384]{3,2,1,0:T(8,128)(2,1)S(1)}, u32[]{:S(2)}, u32[]{:S(2)}) collective-permute-start(bf16[2,5,32,384]{3,2,1,0:T(8,128)(2,1)S(1)} %shard_map.146.refs_0_), channel_id=1, source_target_pairs={{0,1},{1,0},{2,3},{3,2},{4,5},{5,4},{6,7},{7,6},{8,9},{9,8},{10,11... | collective-permute-start | bytes 737288 | tf_op jit(solution)/shard_map/ppermute | solution.py:458
  26.1 12.3 %collective-permute-start.12 = (bf16[2,5,32,384]{3,2,1,0:T(8,128)(2,1)S(1)}, bf16[2,5,32,384]{3,2,1,0:T(8,128)(2,1)S(1)}, u32[]{:S(2)}, u32[]{:S(2)}) collective-permute-start(bf16[2,5,32,384]{3,2,1,0:T(8,128)(2,1)S(1)} %shard_map.146.refs_0_), channel_id=1, source_target_pairs={{0,3},{1,2},{2,1},{3,0},{4,7},{5,6},{6,5},{7,4},{8,11},{9,10},{10,... | collective-permute-start | bytes 737288 | tf_op jit(solution)/shard_map/ppermute | solution.py:458
  26.8 13.1 %collective-permute-start.11 = (bf16[2,5,32,384]{3,2,1,0:T(8,128)(2,1)S(1)}, bf16[2,5,32,384]{3,2,1,0:T(8,128)(2,1)S(1)}, u32[]{:S(2)}, u32[]{:S(2)}) collective-permute-start(bf16[2,5,32,384]{3,2,1,0:T(8,128)(2,1)S(1)} %shard_map.146.refs_0_), channel_id=1, source_target_pairs={{0,2},{1,3},{2,0},{3,1},{4,6},{5,7},{6,4},{7,5},{8,10},{9,11},{10,... | collective-permute-start | bytes 737288 | tf_op jit(solution)/shard_map/ppermute | solution.py:458
  33.4 19.2 %collective-permute-start.9 = (bf16[3,32,384]{2,1,0:T(8,128)(2,1)S(1)}, bf16[3,32,384]{2,1,0:T(8,128)(2,1)S(1)}, u32[]{:S(2)}, u32[]{:S(2)}) collective-permute-start(bf16[3,32,384]{2,1,0:T(8,128)(2,1)S(1)} %get-tuple-element.34), channel_id=1, source_target_pairs={{0,1},{1,2},{2,3},{3,4},{4,5},{5,6},{6,7},{7,8},{8,9},{9,10},{10,1... | collective-permute-start | bytes 221192 | tf_op jit(solution)/shard_map/ppermute | solution.py:432
  36.9 15.7 %collective-permute-start.10 = (bf16[3,32,384]{2,1,0:T(8,128)(2,1)S(1)}, bf16[3,32,384]{2,1,0:T(8,128)(2,1)S(1)}, u32[]{:S(2)}, u32[]{:S(2)}) collective-permute-start(bf16[3,32,384]{2,1,0:T(8,128)(2,1)S(1)} %get-tuple-element.35), channel_id=1, source_target_pairs={{1,0},{2,1},{3,2},{4,3},{5,4},{6,5},{7,6},{8,7},{9,8},{10,9},{11,1... | collective-permute-start | bytes 221192 | tf_op jit(solution)/shard_map/ppermute | solution.py:432
  46.5 9.6 %collective-permute-start.13 = (bf16[512,128]{1,0:T(8,128)(2,1)S(1)}, bf16[512,128]{1,0:T(8,128)(2,1)S(1)}, u32[]{:S(2)}, u32[]{:S(2)}) collective-permute-start(bf16[512,128]{1,0:T(8,128)(2,1)S(1)} %get-tuple-element.50), channel_id=1, source_target_pairs={{0,4},{1,5},{2,6},{3,7},{4,8},{5,9},{6,10},{7,11},{8,12},{9,13},{1... | collective-permute-start | bytes 393224 | tf_op jit(solution)/shard_map/ppermute | solution.py:462
  49.6 8.8 %collective-permute-start.15 = (bf16[512,128]{1,0:T(8,128)(2,1)S(1)}, bf16[512,128]{1,0:T(8,128)(2,1)S(1)}, u32[]{:S(2)}, u32[]{:S(2)}) collective-permute-start(bf16[512,128]{1,0:T(8,128)(2,1)S(1)} %get-tuple-element.51), channel_id=1, source_target_pairs={{0,12},{1,13},{2,14},{3,15},{4,0},{5,1},{6,2},{7,3},{8,4},{9,5},{1... | collective-permute-start | bytes 393224 | tf_op jit(solution)/shard_map/ppermute | solution.py:462
  51.7 12.6 %collective-permute-start.14 = (bf16[512,128]{1,0:T(8,128)(2,1)S(1)}, bf16[512,128]{1,0:T(8,128)(2,1)S(1)}, u32[]{:S(2)}, u32[]{:S(2)}) collective-permute-start(bf16[512,128]{1,0:T(8,128)(2,1)S(1)} %get-tuple-element.52), channel_id=1, source_target_pairs={{0,8},{1,9},{2,10},{3,11},{4,12},{5,13},{6,14},{7,15},{8,0},{9,1},... | collective-permute-start | bytes 393224 | tf_op jit(solution)/shard_map/ppermute | solution.py:462
  68.9 9.9 %collective-permute-start.17 = (bf16[304,128]{1,0:T(8,128)(2,1)S(1)}, bf16[304,128]{1,0:T(8,128)(2,1)S(1)}, u32[]{:S(2)}, u32[]{:S(2)}) collective-permute-start(bf16[304,128]{1,0:T(8,128)(2,1)S(1)} %pad_maximum_fusion.2), channel_id=1, source_target_pairs={{0,8},{1,9},{2,10},{3,11},{4,12},{5,13},{6,14},{7,15},{8,0},{9,1},... | collective-permute-start | bytes 233480 | tf_op jit(solution)/shard_map/ppermute | solution.py:462
  71.3 7.5 %collective-permute-start.16 = (bf16[304,128]{1,0:T(8,128)(2,1)S(1)}, bf16[304,128]{1,0:T(8,128)(2,1)S(1)}, u32[]{:S(2)}, u32[]{:S(2)}) collective-permute-start(bf16[304,128]{1,0:T(8,128)(2,1)S(1)} %pad_maximum_fusion.2), channel_id=1, source_target_pairs={{0,4},{1,5},{2,6},{3,7},{4,8},{5,9},{6,10},{7,11},{8,12},{9,13},{1... | collective-permute-start | bytes 233480 | tf_op jit(solution)/shard_map/ppermute | solution.py:462
  73.1 9.2 %collective-permute-start.32 = (bf16[896,128]{1,0:T(8,128)(2,1)S(1)}, bf16[896,128]{1,0:T(8,128)(2,1)S(1)}, u32[]{:S(2)}, u32[]{:S(2)}) collective-permute-start(bf16[896,128]{1,0:T(8,128)(2,1)S(1)} %bitcast_select_fusion.1.refs_0_), channel_id=1, source_target_pairs={{0,16},{16,0},{1,17},{17,1},{2,18},{18,2},{3,19},{19,3},{4,20},{20... | collective-permute-start | bytes 688136 | tf_op jit(solution)/shard_map/ppermute | solution.py:577
  73.2 10.4 %collective-permute-start.31 = (bf16[896,128]{1,0:T(8,128)(2,1)S(1)}, bf16[896,128]{1,0:T(8,128)(2,1)S(1)}, u32[]{:S(2)}, u32[]{:S(2)}) collective-permute-start(bf16[896,128]{1,0:T(8,128)(2,1)S(1)} %bitcast_select_fusion.1.refs_0_), channel_id=1, source_target_pairs={{0,3},{1,2},{2,1},{3,0},{4,7},{5,6},{6,5},{7,4},{8,11},{9,10},{10,... | collective-permute-start | bytes 688136 | tf_op jit(solution)/shard_map/ppermute | solution.py:458
  73.8 13.8 %collective-permute-start.30 = (bf16[896,128]{1,0:T(8,128)(2,1)S(1)}, bf16[896,128]{1,0:T(8,128)(2,1)S(1)}, u32[]{:S(2)}, u32[]{:S(2)}) collective-permute-start(bf16[896,128]{1,0:T(8,128)(2,1)S(1)} %bitcast_select_fusion.1.refs_0_), channel_id=1, source_target_pairs={{0,2},{1,3},{2,0},{3,1},{4,6},{5,7},{6,4},{7,5},{8,10},{9,11},{10,... | collective-permute-start | bytes 688136 | tf_op jit(solution)/shard_map/ppermute | solution.py:458
  78.8 8.8 %collective-permute-start.29 = (bf16[896,128]{1,0:T(8,128)(2,1)S(1)}, bf16[896,128]{1,0:T(8,128)(2,1)S(1)}, u32[]{:S(2)}, u32[]{:S(2)}) collective-permute-start(bf16[896,128]{1,0:T(8,128)(2,1)S(1)} %bitcast_select_fusion.1.refs_0_), channel_id=1, source_target_pairs={{0,1},{1,0},{2,3},{3,2},{4,5},{5,4},{6,7},{7,6},{8,9},{9,8},{10,11... | collective-permute-start | bytes 688136 | tf_op jit(solution)/shard_map/ppermute | solution.py:458
  80.1 14.0 %collective-permute-start.21 = (bf16[1168,128]{1,0:T(8,128)(2,1)S(1)}, bf16[1168,128]{1,0:T(8,128)(2,1)S(1)}, u32[]{:S(2)}, u32[]{:S(2)}) collective-permute-start(bf16[1168,128]{1,0:T(8,128)(2,1)S(1)} %concatenate.11.refs_0_), channel_id=1, source_target_pairs={{0,3},{1,2},{2,1},{3,0},{4,7},{5,6},{6,5},{7,4},{8,11},{9,10},{10,... | collective-permute-start | bytes 897032 | tf_op jit(solution)/shard_map/ppermute | solution.py:458
  82.3 16.7 %collective-permute-start.20 = (bf16[1168,128]{1,0:T(8,128)(2,1)S(1)}, bf16[1168,128]{1,0:T(8,128)(2,1)S(1)}, u32[]{:S(2)}, u32[]{:S(2)}) collective-permute-start(bf16[1168,128]{1,0:T(8,128)(2,1)S(1)} %concatenate.11.refs_0_), channel_id=1, source_target_pairs={{0,2},{1,3},{2,0},{3,1},{4,6},{5,7},{6,4},{7,5},{8,10},{9,11},{10,... | collective-permute-start | bytes 897032 | tf_op jit(solution)/shard_map/ppermute | solution.py:458
  83.6 15.7 %collective-permute-start.19 = (bf16[1168,128]{1,0:T(8,128)(2,1)S(1)}, bf16[1168,128]{1,0:T(8,128)(2,1)S(1)}, u32[]{:S(2)}, u32[]{:S(2)}) collective-permute-start(bf16[1168,128]{1,0:T(8,128)(2,1)S(1)} %concatenate.11.refs_0_), channel_id=1, source_target_pairs={{0,1},{1,0},{2,3},{3,2},{4,5},{5,4},{6,7},{7,6},{8,9},{9,8},{10,11... | collective-permute-start | bytes 897032 | tf_op jit(solution)/shard_map/ppermute | solution.py:458
  87.7 11.9 %collective-permute-start.35 = (bf16[896,128]{1,0:T(8,128)(2,1)S(1)}, bf16[896,128]{1,0:T(8,128)(2,1)S(1)}, u32[]{:S(2)}, u32[]{:S(2)}) collective-permute-start(bf16[896,128]{1,0:T(8,128)(2,1)S(1)} %collective-permute-done.31.refs_3_), channel_id=1, source_target_pairs={{0,16},{16,0},{1,17},{17,1},{2,18},{18,2},{3,19},{19,3},{4,20},{20... | collective-permute-start | bytes 688136 | tf_op jit(solution)/shard_map/ppermute | solution.py:577
  87.7 12.2 %collective-permute-start.34 = (bf16[896,128]{1,0:T(8,128)(2,1)S(1)}, bf16[896,128]{1,0:T(8,128)(2,1)S(1)}, u32[]{:S(2)}, u32[]{:S(2)}) collective-permute-start(bf16[896,128]{1,0:T(8,128)(2,1)S(1)} %collective-permute-done.30.refs_2_), channel_id=1, source_target_pairs={{0,16},{16,0},{1,17},{17,1},{2,18},{18,2},{3,19},{19,3},{4,20},{20... | collective-permute-start | bytes 688136 | tf_op jit(solution)/shard_map/ppermute | solution.py:577
  (30 other events, 237.7 us)

commit v6 on v5

--- a/solution.py
+++ b/solution.py
@@ -290,7 +290,7 @@
 def wgrad_kernel(blocks, planes, *refs):
     xs, ys = refs[:4], refs[4:8]
     gain = refs[8][1:2]
-    out_ref, plane, xk = refs[-3:]
+    outs, (plane, xt) = refs[9:-2], refs[-2:]
     _, rows, cols, _ = ys[0].shape
     chans = gain.shape[1]
     tall = 4 * rows
@@ -298,7 +298,7 @@
     odd = lax.axis_index("tm") % 2 == 1
     p = lax.axis_index("height") % 4
     single = blocks == 2
-    start = jnp.where(odd, 2, 0) if single else 0
+    base = jnp.where(odd, 2, 0) if single else 0
     if single:
         plane[pl.ds(jnp.where(odd, 0, 4), 2)] = jnp.zeros((2,) + plane.shape[1:], bf16)
 
@@ -306,7 +306,7 @@
         for b in range(blocks):
             for f in range(2):
                 part = values[b, :, :, f * chans : (f + 1) * chans]
-                place = (start + 2 * b + f, pl.ds(row, count))
+                place = (base + 2 * b + f, pl.ds(row, count))
 
                 @pl.when(odd)
                 def _():
@@ -320,14 +320,19 @@
     for d in range(4):
         at = p ^ d
         put_y(ys[d][...], 1 + rows * at, rows)
+        block = rows * cols
+        column = lax.broadcasted_iota(jnp.int32, (chans, block), 1) % cols
         for b in range(2):
             for f in range(2):
                 part = xs[d][b, :rows, :, f * chans : (f + 1) * chans]
-                wide = part.astype(f32)
-                place = (2 * b + f, pl.ds(rows * at, rows))
-                xk[(0,) + place] = shift_cols(wide, 1).astype(bf16)
-                xk[(1,) + place] = part
-                xk[(2,) + place] = shift_cols(wide, -1).astype(bf16)
+                part = part.astype(f32).reshape(block, chans).T
+                start = pl.multiple_of((2 * b + f) * tall * cols + at * block, block)
+                place = (slice(None), pl.ds(start, block))
+                after = jnp.where(column == cols - 1, 0.0, pltpu.roll(part, block - 1, 1))
+                before = jnp.where(column == 0, 0.0, pltpu.roll(part, 1, 1))
+                xt[(0,) + place] = after.astype(bf16)
+                xt[(1,) + place] = part.astype(bf16)
+                xt[(2,) + place] = before.astype(bf16)
 
         @pl.when(at == 0)
         def _():
@@ -338,18 +343,16 @@
             put_y(xs[d][:, rows:], tall + 1, 1)
 
     step = pack_rows(chans)
-    dims = (((0,), (0,)), ((), ()))
     half = chans // 2
-    offset = 0
-    for first, count in chunks:
+    for (first, count), out_ref in zip(chunks, outs):
         share = chunk_rows(count, chans, planes) // planes
 
-        def put(row, values, offset=offset, share=share):
+        def put(row, values, out_ref=out_ref, share=share):
             at = 0
             while at < values.shape[0]:
                 q, r = divmod(row + at, share)
                 n = min(share - r, values.shape[0] - at)
-                out_ref[q, offset + r : offset + r + n] = values[at : at + n]
+                out_ref[q, r : r + n] = values[at : at + n]
                 at += n
 
         def store(row, grad, put=put):
@@ -359,24 +362,39 @@
 
         for j in range(count):
             tap = jnp.minimum(p * taps_each + first + j, taps_all - 1)
+            tap = jnp.where(odd, tap, taps_all - 1 - tap)
             t, h, k = tap // 9, tap // 3 % 3, tap % 3
+            piece = plane[pl.ds(t, 4), pl.ds(h, tall)].reshape(cells, chans)
+            grad = jnp.dot(xt[k], piece, preferred_element_type=f32)
 
             @pl.when(odd)
             def _():
-                piece = plane[pl.ds(t, 4), pl.ds(h, tall)].reshape(cells, chans)
-                x = xk[k].reshape(cells, chans)
-                store(j * step, lax.dot_general(piece, x, dims, preferred_element_type=f32))
+                store(j * step, grad.T)
 
             @pl.when(jnp.logical_not(odd))
             def _():
-                piece = plane[pl.ds(2 - t, 4), pl.ds(2 - h, tall)].reshape(cells, chans)
-                x = xk[2 - k].reshape(cells, chans)
-                store(j * step, lax.dot_general(x, piece, dims, preferred_element_type=f32))
+                store(j * step, grad)
 
         spare = share * planes - count * step
         if spare:
             put(count * step, jnp.zeros((spare, 128), bf16))
-        offset += share
+
+
+def halves(total):
+    high = total.astype(bf16)
+    return jnp.concatenate([high, (total - high.astype(f32)).astype(bf16)])
+
+
+def assemble_kernel(planes, size, *refs):
+    pieces, out_ref = refs[:planes], refs[-1]
+    q = lax.axis_index("height") // 4
+    for d, piece in enumerate(pieces):
+        start = pl.multiple_of((q - d + planes) % planes * size, 16)
+        out_ref[pl.ds(start, size)] = piece[:size]
+    if pieces[0].shape[0] > size:
+        total = functools.reduce(lambda a, b: a + b, [piece[size:].astype(f32) for piece in pieces])
+        half = total.shape[0] // 2
+        out_ref[planes * size :] = halves(total[:half] + total[half:])
 
 
 def unpack_kernel(taps, held, *refs):
@@ -512,26 +530,29 @@
     up, down = call(gate_kernel, messages, (keep, give, far, xs[1]), 1, 6, free=(3,))
     above, below = moved(up, "height", 1), moved(down, "height", -1)
 
-    shares = [chunk_rows(count, chans, planes) // planes for _, count in chunks]
-    (flat,) = call(
+    flats = call(
         functools.partial(wgrad_kernel, blocks, planes),
-        (jax.ShapeDtypeStruct((planes, sum(shares), 128), bf16),),
+        [
+            jax.ShapeDtypeStruct((planes, chunk_rows(count, chans, planes) // planes, 128), bf16)
+            for _, count in chunks
+        ],
         (*xs, *ys, vec),
-        7,
+        6,
         24,
         [
             pltpu.VMEM((2 * frames + 2, 4 * rows + 2, cols, chans), bf16),
-            pltpu.VMEM((3, 2 * frames, 4 * rows, cols, chans), bf16),
+            pltpu.VMEM((3, chans, 8 * frames * rows * cols), bf16),
         ],
     )
-    arrived = [column_move(piece_at(flat, (q + d) % planes), d) for d in range(1, planes)]
-    part = total_of([piece_at(flat, q), *arrived])
-    hop = 2
-    while hop < tm:
-        part = part + lax.ppermute(part, "tm", [(i, i ^ hop) for i in range(tm)])
-        hop *= 2
-    part = part.astype(bf16)
-    parts = jnp.split(part, [sum(shares[:n]) for n in range(1, len(shares))])
+    parts = []
+    for flat in flats:
+        arrived = [column_move(piece_at(flat, (q + d) % planes), d) for d in range(1, planes)]
+        part = total_of([piece_at(flat, q), *arrived])
+        hop = 2
+        while hop < tm:
+            part = part + lax.ppermute(part, "tm", [(i, i ^ hop) for i in range(tm)])
+            hop *= 2
+        parts.append(part.astype(bf16))
 
     block_out, grad_input, sums_two = call(
         last_kernel,
@@ -543,17 +564,9 @@
     )
 
     small = jnp.concatenate([sums_one[:3], sums_two[:1]]).reshape(-1, 128)
-    count = small.shape[0]
-
-    def with_small(value, small):
-        high = small.astype(bf16)
-        low = (small - high.astype(f32)).astype(bf16)
-        pad = jnp.zeros((-2 * count % 16, 128), bf16)
-        return jnp.concatenate([value, high, low, pad])
-
-    def without_small(pieces, rows):
-        total = total_of([v[rows : rows + count].astype(f32) + v[rows + count : rows + 2 * count].astype(f32) for v in pieces])
-        return [v[:rows] for v in pieces], total
+    used = small.shape[0]
+    count = -(-used // 8) * 8
+    small = jnp.pad(small, ((0, count - used), (0, 0)))
 
     hop = 2
     while hop < tm:
@@ -561,22 +574,29 @@
         hop *= 2
 
     gradient = jax.ShapeDtypeStruct((taps_all, chans, chans), bf16)
-    grads = ()
+    grads, gate = (), ()
     for n, (part, taps) in enumerate(zip(parts, chunks)):
         last = n == len(parts) - 1
         size = part.shape[0]
-        send = with_small(part, small) if last else part
+        send = jnp.concatenate([part, halves(small)]) if last else part
         got = [send] + [column_move(send, d) for d in range(1, planes)]
-        if last:
-            got, small = without_small(got, size)
-        stack = jnp.stack(got)
-        quarter = jnp.take(stack, (q - jnp.arange(planes)) % planes, axis=0).reshape(-1, 128)
-        size = quarter.shape[0]
-        send = with_small(quarter, small) if last else quarter
-        got = [send] + [plane_move(send, d) for d in (1, 2, 3)]
+        (send,) = call(
+            functools.partial(assemble_kernel, planes, size),
+            (jax.ShapeDtypeStruct((planes * size + send.shape[0] - size, 128), bf16),),
+            (*got, *gate),
+            1,
+            6,
+            free=(planes,) if gate else (),
+        )
+        one, two = plane_move(send, 1), plane_move(send, 2)
+        gate = (one,)
+        cut = send.shape[0] // 32 * 16
+        three = jnp.concatenate([plane_move(two[:cut], 1), plane_move(one[cut:], 2)])
+        got = [send, one, two, three]
         others = [lax.ppermute(g, "tm", swap) for g in got]
         if last:
-            _, small = without_small(got + others, size)
+            small = total_of([v[planes * size :] for v in got + others])
+            small = (small[:count] + small[count:])[:used]
         held = len(grads) > 0
         grads = call(
             functools.partial(unpack_kernel, taps, held),
@@ -585,7 +605,7 @@
             2,
             12,
             [pltpu.VMEM((8 * taps[1], chans, chans), bf16), pltpu.SemaphoreType.DMA((8 * taps[1],))],
-            free=(8, 9),
+            free=(8, 9) if held else (),
             out_spec=anywhere,
             input_output_aliases={8: 0, 9: 1} if held else {},
         )

time: 105 us -> 106 us (level)
  starting transfers between devices: 37.4 us -> 44.1 us
  waiting for transfers between devices: 42.8 us -> 38.3 us
  local copies, waits for them, and re-layouts: 4.39 us -> 2.66 us
  Pallas kernels: 16.8 us -> 18.4 us
    ppermute x12 -> x14, waiting for transfers between devices: 20.2 us -> 16.1 us  [plane_move(): return lax.ppermute(value, 'height', [(i, i ^ d) for i in range(height)])]
    ppermute x9 -> x12, starting transfers between devices: 12.3 us -> 15.9 us  [column_move(): return lax.ppermute(value, 'height', pairs)]
    ppermute x12 -> x14, starting transfers between devices: 13 us -> 16.4 us  [plane_move(): return lax.ppermute(value, 'height', [(i, i ^ d) for i in range(height)])]
    pallas_call x9 -> x11, Pallas kernels: 16.8 us -> 18.4 us  [call(): pl.pallas_call(kernel, out_shape=outs, in_specs=[in_hbm if i in hbm else...]
    gather x2 -> x0, local copies, waits for them, and re-layouts: 1.2 us -> none  [body(): jnp.take(stack, (q - jnp.arange(planes)) % planes, axis=0).reshape(-1, 128)]
    ppermute x9 -> x12, waiting for transfers between devices: 14.2 us -> 13.7 us  [column_move(): return lax.ppermute(value, 'height', pairs)]
  transfers between devices with their start and end apart: 36 -> 41, of which waited for: 18 -> 18; matrix products, arithmetic and copies ran while one was open for 2% -> 0% of each run, Pallas kernels for 11% -> 13%
where the time goes in v6:
time: 106 us
  starting transfers between devices  44.1 us (42%)
  waiting for transfers between devices  38.3 us (36%)
  Pallas kernels  18.4 us (17%)
  local copies, waits for them, and re-layouts  2.66 us (3%)
  between operations  1.31 us (1%)
  other arithmetic  1.26 us (1%)
    pallas_call x11, Pallas kernels, call(): pl.pallas_call(kernel, out_shape=outs, in_specs=[in_hbm if i in hbm else...  18.4 us
    ppermute x14, starting transfers between devices, plane_move(): return lax.ppermute(value, 'height', [(i, i ^ d) for i in range(height)])  16.4 us
    ppermute x14, waiting for transfers between devices, plane_move(): return lax.ppermute(value, 'height', [(i, i ^ d) for i in range(height)])  16.1 us
    ppermute x12, starting transfers between devices, column_move(): return lax.ppermute(value, 'height', pairs)  15.9 us
    ppermute x12, waiting for transfers between devices, column_move(): return lax.ppermute(value, 'height', pairs)  13.7 us
    ppermute x4, starting transfers between devices, moved(): lax.ppermute(value, axis, [(i, i + by) for i in range(size) if 0 <= i + b...  10 us
    ppermute x4, waiting for transfers between devices, moved(): lax.ppermute(value, axis, [(i, i + by) for i in range(size) if 0 <= i + b...  4.81 us
  transfers between devices with their start and end apart: 41, of which 18 were waited for; matrix products, arithmetic and copies ran while one was open for 0% of the time, Pallas kernels for 13%

profile of v6, /device:TPU:0, one launch (start us, length us, event | category | flops | bytes accessed | tf_op | source)
XLA Modules:
  0.0 106.0 jit_solution(4534538693096916621)
XLA Ops:
  3.5 3.9 %collective-permute-start.3 = (bf16[2,4,32,384]{3,2,1,0:T(8,128)(2,1)S(1)}, bf16[2,4,32,384]{3,2,1,0:T(8,128)(2,1)S(1)}, u32[]{:S(2)}, u32[]{:S(2)}) collective-permute-start(bf16[2,4,32,384]{3,2,1,0:T(8,128)(2,1)S(1)} %get-tuple-element.28.refs_4_), channel_id=1, source_target_pairs={{0,3},{1,2},{2,1},{3,0},{4,7},{5,6},{6,5},{7,4},{8,11},{9,10},{10,... | collective-permute-start | bytes 589832 | tf_op jit(solution)/shard_map/ppermute | solution.py:476
  8.0 3.8 %collective-permute-start.4 = (bf16[3,32,384]{2,1,0:T(8,128)(2,1)S(1)}, bf16[3,32,384]{2,1,0:T(8,128)(2,1)S(1)}, u32[]{:S(2)}, u32[]{:S(2)}) collective-permute-start(bf16[3,32,384]{2,1,0:T(8,128)(2,1)S(1)} %get-tuple-element.29), channel_id=1, source_target_pairs={{0,1},{1,2},{2,3},{3,4},{4,5},{5,6},{6,7},{7,8},{8,9},{9,10},{10,1... | collective-permute-start | bytes 221192 | tf_op jit(solution)/shard_map/ppermute | solution.py:450
  13.2 1.7 %copy-done.1 = bf16[3,3,3,192,192]{4,3,2,1,0:T(8,128)(2,1)S(1)} copy-done((bf16[3,3,3,192,192]{4,3,2,1,0:T(8,128)(2,1)S(1)}, bf16[3,3,3,192,192]{4,3,2,1,0:T(8,128)(2,1)}, u32[]{:S(2)}) %copy-start.1) | copy-done | bytes 1990680
  15.4 3.9 %collective-permute-done.4.above_ref = bf16[3,32,384]{2,1,0:T(8,128)(2,1)S(1)} collective-permute-done((bf16[3,32,384]{2,1,0:T(8,128)(2,1)S(1)}, bf16[3,32,384]{2,1,0:T(8,128)(2,1)S(1)}, u32[]{:S(2)}, u32[]{:S(2)}) %collective-permute-start.4) | collective-permute-done | bytes 73760 | tf_op jit(solution)/shard_map/ppermute | solution.py:450
  20.3 2.8 %shard_map.145 = (bf16[4,32,384]{2,1,0:T(8,128)(2,1)S(1)}, bf16[4,32,384]{2,1,0:T(8,128)(2,1)S(1)}, f32[8,192]{1,0:T(8,128)S(1)}) custom-call(bf16[2,4,32,384]{3,2,1,0:T(8,128)(2,1)S(1)} %collective-permute-done.1._.refs_5_, bf16[2,4,32,384]{3,2,1,0:T(8,128)(2,1)S(1)} %collective-permute-done.2.__.refs_6_, ...), custom_call_target="tpu_custom_call" | custom-call | flops 5500000256 | bytes 1024 | tf_op jit(solution)/shard_map/pallas_call | solution.py:436
  29.4 4.0 %collective-permute-done.8._.refs_1_ = bf16[2,5,32,384]{3,2,1,0:T(8,128)(2,1)S(1)} collective-permute-done((bf16[2,5,32,384]{3,2,1,0:T(8,128)(2,1)S(1)}, bf16[2,5,32,384]{3,2,1,0:T(8,128)(2,1)S(1)}, u32[]{:S(2)}, u32[]{:S(2)}) %collective-permute-start.8) | collective-permute-done | bytes 245792 | tf_op jit(solution)/shard_map/ppermute | solution.py:476
  33.5 3.4 %collective-permute-start.9 = (bf16[3,32,384]{2,1,0:T(8,128)(2,1)S(1)}, bf16[3,32,384]{2,1,0:T(8,128)(2,1)S(1)}, u32[]{:S(2)}, u32[]{:S(2)}) collective-permute-start(bf16[3,32,384]{2,1,0:T(8,128)(2,1)S(1)} %get-tuple-element.36), channel_id=1, source_target_pairs={{0,1},{1,2},{2,3},{3,4},{4,5},{5,6},{6,7},{7,8},{8,9},{9,10},{10,1... | collective-permute-start | bytes 221192 | tf_op jit(solution)/shard_map/ppermute | solution.py:450
  39.9 7.8 %shard_map.149 = (bf16[4,224,128]{2,1,0:T(8,128)(2,1)S(1)}, bf16[4,288,128]{2,1,0:T(8,128)(2,1)S(1)}) custom-call(bf16[2,5,32,384]{3,2,1,0:T(8,128)(2,1)S(1)} %shard_map.146.refs_0_, bf16[2,5,32,384]{3,2,1,0:T(8,128)(2,1)S(1)} %collective-permute-done.8._.refs_1_, bf16[2,5,32,384]{3,2,1,0:T(8,128)(2,1)S(1)} %collective-permute-done.11.refs_2_, ...), custom_call_target="tpu_custom_call" | custom-call | flops 6600000000 | bytes 1024 | tf_op jit(solution)/shard_map/pallas_call | solution.py:436
  47.7 3.1 %collective-permute-start.19 = (bf16[224,128]{1,0:T(8,128)(2,1)S(1)}, bf16[224,128]{1,0:T(8,128)(2,1)S(1)}, u32[]{:S(2)}, u32[]{:S(2)}) collective-permute-start(bf16[224,128]{1,0:T(8,128)(2,1)S(1)} %get-tuple-element.57), channel_id=1, source_target_pairs={{0,4},{1,5},{2,6},{3,7},{4,8},{5,9},{6,10},{7,11},{8,12},{9,13},{1... | collective-permute-start | bytes 172040 | tf_op jit(solution)/shard_map/ppermute | solution.py:480
  50.9 2.1 %collective-permute-start.21 = (bf16[224,128]{1,0:T(8,128)(2,1)S(1)}, bf16[224,128]{1,0:T(8,128)(2,1)S(1)}, u32[]{:S(2)}, u32[]{:S(2)}) collective-permute-start(bf16[224,128]{1,0:T(8,128)(2,1)S(1)} %get-tuple-element.58), channel_id=1, source_target_pairs={{0,12},{1,13},{2,14},{3,15},{4,0},{5,1},{6,2},{7,3},{8,4},{9,5},{1... | collective-permute-start | bytes 172040 | tf_op jit(solution)/shard_map/ppermute | solution.py:480
  56.8 2.2 %collective-permute-start.15 = (bf16[288,128]{1,0:T(8,128)(2,1)S(1)}, bf16[288,128]{1,0:T(8,128)(2,1)S(1)}, u32[]{:S(2)}, u32[]{:S(2)}) collective-permute-start(bf16[288,128]{1,0:T(8,128)(2,1)S(1)} %get-tuple-element.53), channel_id=1, source_target_pairs={{0,12},{1,13},{2,14},{3,15},{4,0},{5,1},{6,2},{7,3},{8,4},{9,5},{1... | collective-permute-start | bytes 221192 | tf_op jit(solution)/shard_map/ppermute | solution.py:480
  59.8 2.6 %collective-permute-start.24 = (bf16[224,128]{1,0:T(8,128)(2,1)S(1)}, bf16[224,128]{1,0:T(8,128)(2,1)S(1)}, u32[]{:S(2)}, u32[]{:S(2)}) collective-permute-start(bf16[224,128]{1,0:T(8,128)(2,1)S(1)} %fusion.5.refs_0_), channel_id=1, source_target_pairs={{0,12},{1,13},{2,14},{3,15},{4,0},{5,1},{6,2},{7,3},{8,4},{9,5},{1... | collective-permute-start | bytes 172040 | tf_op jit(solution)/shard_map/ppermute | solution.py:480
  62.4 2.0 %collective-permute-start.23 = (bf16[224,128]{1,0:T(8,128)(2,1)S(1)}, bf16[224,128]{1,0:T(8,128)(2,1)S(1)}, u32[]{:S(2)}, u32[]{:S(2)}) collective-permute-start(bf16[224,128]{1,0:T(8,128)(2,1)S(1)} %fusion.5.refs_0_), channel_id=1, source_target_pairs={{0,8},{1,9},{2,10},{3,11},{4,12},{5,13},{6,14},{7,15},{8,0},{9,1},... | collective-permute-start | bytes 172040 | tf_op jit(solution)/shard_map/ppermute | solution.py:480
  64.4 3.5 %shard_map.148 = (bf16[2,4,32,192]{3,2,1,0:T(8,128)(2,1)}, bf16[2,4,32,192]{3,2,1,0:T(8,128)(2,1)}, f32[8,192]{1,0:T(8,128)S(1)}) custom-call(bf16[4,32,384]{2,1,0:T(8,128)(2,1)S(1)} %get-tuple-element.34.keep_ref, bf16[4,32,384]{2,1,0:T(8,128)(2,1)S(1)} %get-tuple-element.35.give_ref, bf16[1,4,32,384]{3,2,1,0:T(8,128)(2,1)S(1)} %bitcast.29, ...), custom_call_target="tpu_custom_call" | custom-call | flops 6600000000 | bytes 1024 | tf_op jit(solution)/shard_map/pallas_call | solution.py:436
  68.3 1.8 %collective-permute-done.23.refs_2_ = bf16[224,128]{1,0:T(8,128)(2,1)S(1)} collective-permute-done((bf16[224,128]{1,0:T(8,128)(2,1)S(1)}, bf16[224,128]{1,0:T(8,128)(2,1)S(1)}, u32[]{:S(2)}, u32[]{:S(2)}) %collective-permute-start.23) | collective-permute-done | bytes 57376 | tf_op jit(solution)/shard_map/ppermute | solution.py:480
  70.1 3.9 %collective-permute-done.22.refs_1_ = bf16[224,128]{1,0:T(8,128)(2,1)S(1)} collective-permute-done((bf16[224,128]{1,0:T(8,128)(2,1)S(1)}, bf16[224,128]{1,0:T(8,128)(2,1)S(1)}, u32[]{:S(2)}, u32[]{:S(2)}) %collective-permute-start.22) | collective-permute-done | bytes 57376 | tf_op jit(solution)/shard_map/ppermute | solution.py:480
  74.4 1.8 %collective-permute-start.16 = (bf16[304,128]{1,0:T(8,128)(2,1)S(1)}, bf16[304,128]{1,0:T(8,128)(2,1)S(1)}, u32[]{:S(2)}, u32[]{:S(2)}) collective-permute-start(bf16[304,128]{1,0:T(8,128)(2,1)S(1)} %pad_maximum_fusion.refs_0_), channel_id=1, source_target_pairs={{0,4},{1,5},{2,6},{3,7},{4,8},{5,9},{6,10},{7,11},{8,12},{9,13},{1... | collective-permute-start | bytes 233480 | tf_op jit(solution)/shard_map/ppermute | solution.py:480
  77.1 3.5 %collective-permute-done.18.refs_3_ = bf16[304,128]{1,0:T(8,128)(2,1)S(1)} collective-permute-done((bf16[304,128]{1,0:T(8,128)(2,1)S(1)}, bf16[304,128]{1,0:T(8,128)(2,1)S(1)}, u32[]{:S(2)}, u32[]{:S(2)}) %collective-permute-start.18) | collective-permute-done | bytes 77856 | tf_op jit(solution)/shard_map/ppermute | solution.py:480
  83.1 1.7 %collective-permute-start.26 = (bf16[1168,128]{1,0:T(8,128)(2,1)S(1)}, bf16[1168,128]{1,0:T(8,128)(2,1)S(1)}, u32[]{:S(2)}, u32[]{:S(2)}) collective-permute-start(bf16[1168,128]{1,0:T(8,128)(2,1)S(1)} %shard_map.151.refs_0_), channel_id=1, source_target_pairs={{0,1},{1,0},{2,3},{3,2},{4,5},{5,4},{6,7},{7,6},{8,9},{9,8},{10,11... | collective-permute-start | bytes 897032 | tf_op jit(solution)/shard_map/ppermute | solution.py:476
  86.5 3.7 %collective-permute-done.27.refs_2_ = bf16[1168,128]{1,0:T(8,128)(2,1)S(1)} collective-permute-done((bf16[1168,128]{1,0:T(8,128)(2,1)S(1)}, bf16[1168,128]{1,0:T(8,128)(2,1)S(1)}, u32[]{:S(2)}, u32[]{:S(2)}) %collective-permute-start.27) | collective-permute-done | bytes 299040 | tf_op jit(solution)/shard_map/ppermute | solution.py:476
  90.2 2.0 %collective-permute-done.35 = bf16[448,128]{1,0:T(8,128)(2,1)S(1)} collective-permute-done((bf16[448,128]{1,0:T(8,128)(2,1)S(1)}, bf16[448,128]{1,0:T(8,128)(2,1)S(1)}, u32[]{:S(2)}, u32[]{:S(2)}) %collective-permute-start.35) | collective-permute-done | bytes 114720 | tf_op jit(solution)/shard_map/ppermute | solution.py:476
  95.4 1.9 %collective-permute-done.28 = bf16[576,128]{1,0:T(8,128)(2,1)S(1)} collective-permute-done((bf16[576,128]{1,0:T(8,128)(2,1)S(1)}, bf16[576,128]{1,0:T(8,128)(2,1)S(1)}, u32[]{:S(2)}, u32[]{:S(2)}) %collective-permute-start.28) | collective-permute-done | bytes 147488 | tf_op jit(solution)/shard_map/ppermute | solution.py:476
  97.4 3.1 %collective-permute-done.29 = bf16[592,128]{1,0:T(8,128)(2,1)S(1)} collective-permute-done((bf16[592,128]{1,0:T(8,128)(2,1)S(1)}, bf16[592,128]{1,0:T(8,128)(2,1)S(1)}, u32[]{:S(2)}, u32[]{:S(2)}) %collective-permute-start.29) | collective-permute-done | bytes 151584 | tf_op jit(solution)/shard_map/ppermute | solution.py:476
  103.9 1.9 %shard_map.153 = (bf16[27,192,192]{2,1,0:T(8,128)(2,1)}, bf16[27,192,192]{2,1,0:T(8,128)(2,1)}) custom-call(bf16[1168,128]{1,0:T(8,128)(2,1)S(1)} %shard_map.151.refs_0_, bf16[1168,128]{1,0:T(8,128)(2,1)S(1)} %collective-permute-done.26.refs_1_, bf16[1168,128]{1,0:T(8,128)(2,1)S(1)} %collective-permute-done.27.refs_2_, ...), custom_call_target="tpu_custom_call", output_to_operand_aliasing={{0}: (8, {}), {1}: (9, {})} | custom-call | flops 2200000000 | bytes 1024 | tf_op jit(solution)/shard_map/pallas_call | solution.py:436
  (125 shorter events, 32.7 us)
Async XLA Ops:
  3.5 16.8 %collective-permute-start.3 = (bf16[2,4,32,384]{3,2,1,0:T(8,128)(2,1)S(1)}, bf16[2,4,32,384]{3,2,1,0:T(8,128)(2,1)S(1)}, u32[]{:S(2)}, u32[]{:S(2)}) collective-permute-start(bf16[2,4,32,384]{3,2,1,0:T(8,128)(2,1)S(1)} %get-tuple-element.28.refs_4_), channel_id=1, source_target_pairs={{0,3},{1,2},{2,1},{3,0},{4,7},{5,6},{6,5},{7,4},{8,11},{9,10},{10,... | collective-permute-start | bytes 589832 | tf_op jit(solution)/shard_map/ppermute | solution.py:476
  7.4 12.9 %collective-permute-start.2 = (bf16[2,4,32,384]{3,2,1,0:T(8,128)(2,1)S(1)}, bf16[2,4,32,384]{3,2,1,0:T(8,128)(2,1)S(1)}, u32[]{:S(2)}, u32[]{:S(2)}) collective-permute-start(bf16[2,4,32,384]{3,2,1,0:T(8,128)(2,1)S(1)} %get-tuple-element.28.refs_4_), channel_id=1, source_target_pairs={{0,2},{1,3},{2,0},{3,1},{4,6},{5,7},{6,4},{7,5},{8,10},{9,11},{10,... | collective-permute-start | bytes 589832 | tf_op jit(solution)/shard_map/ppermute | solution.py:476
  7.9 12.4 %collective-permute-start.1 = (bf16[2,4,32,384]{3,2,1,0:T(8,128)(2,1)S(1)}, bf16[2,4,32,384]{3,2,1,0:T(8,128)(2,1)S(1)}, u32[]{:S(2)}, u32[]{:S(2)}) collective-permute-start(bf16[2,4,32,384]{3,2,1,0:T(8,128)(2,1)S(1)} %get-tuple-element.28.refs_4_), channel_id=1, source_target_pairs={{0,1},{1,0},{2,3},{3,2},{4,5},{5,4},{6,7},{7,6},{8,9},{9,8},{10,11... | collective-permute-start | bytes 589832 | tf_op jit(solution)/shard_map/ppermute | solution.py:476
  8.0 11.3 %collective-permute-start.4 = (bf16[3,32,384]{2,1,0:T(8,128)(2,1)S(1)}, bf16[3,32,384]{2,1,0:T(8,128)(2,1)S(1)}, u32[]{:S(2)}, u32[]{:S(2)}) collective-permute-start(bf16[3,32,384]{2,1,0:T(8,128)(2,1)S(1)} %get-tuple-element.29), channel_id=1, source_target_pairs={{0,1},{1,2},{2,3},{3,4},{4,5},{5,6},{6,7},{7,8},{8,9},{9,10},{10,1... | collective-permute-start | bytes 221192 | tf_op jit(solution)/shard_map/ppermute | solution.py:450
  11.8 8.4 %collective-permute-start.5 = (bf16[3,32,384]{2,1,0:T(8,128)(2,1)S(1)}, bf16[3,32,384]{2,1,0:T(8,128)(2,1)S(1)}, u32[]{:S(2)}, u32[]{:S(2)}) collective-permute-start(bf16[3,32,384]{2,1,0:T(8,128)(2,1)S(1)} %get-tuple-element.30), channel_id=1, source_target_pairs={{1,0},{2,1},{3,2},{4,3},{5,4},{6,5},{7,6},{8,7},{9,8},{10,9},{11,1... | collective-permute-start | bytes 221192 | tf_op jit(solution)/shard_map/ppermute | solution.py:450
  24.6 8.9 %collective-permute-start.8 = (bf16[2,5,32,384]{3,2,1,0:T(8,128)(2,1)S(1)}, bf16[2,5,32,384]{3,2,1,0:T(8,128)(2,1)S(1)}, u32[]{:S(2)}, u32[]{:S(2)}) collective-permute-start(bf16[2,5,32,384]{3,2,1,0:T(8,128)(2,1)S(1)} %shard_map.146.refs_0_), channel_id=1, source_target_pairs={{0,1},{1,0},{2,3},{3,2},{4,5},{5,4},{6,7},{7,6},{8,9},{9,8},{10,11... | collective-permute-start | bytes 737288 | tf_op jit(solution)/shard_map/ppermute | solution.py:476
  26.1 12.3 %collective-permute-start.12 = (bf16[2,5,32,384]{3,2,1,0:T(8,128)(2,1)S(1)}, bf16[2,5,32,384]{3,2,1,0:T(8,128)(2,1)S(1)}, u32[]{:S(2)}, u32[]{:S(2)}) collective-permute-start(bf16[2,5,32,384]{3,2,1,0:T(8,128)(2,1)S(1)} %shard_map.146.refs_0_), channel_id=1, source_target_pairs={{0,3},{1,2},{2,1},{3,0},{4,7},{5,6},{6,5},{7,4},{8,11},{9,10},{10,... | collective-permute-start | bytes 737288 | tf_op jit(solution)/shard_map/ppermute | solution.py:476
  26.8 13.1 %collective-permute-start.11 = (bf16[2,5,32,384]{3,2,1,0:T(8,128)(2,1)S(1)}, bf16[2,5,32,384]{3,2,1,0:T(8,128)(2,1)S(1)}, u32[]{:S(2)}, u32[]{:S(2)}) collective-permute-start(bf16[2,5,32,384]{3,2,1,0:T(8,128)(2,1)S(1)} %shard_map.146.refs_0_), channel_id=1, source_target_pairs={{0,2},{1,3},{2,0},{3,1},{4,6},{5,7},{6,4},{7,5},{8,10},{9,11},{10,... | collective-permute-start | bytes 737288 | tf_op jit(solution)/shard_map/ppermute | solution.py:476
  33.5 26.3 %collective-permute-start.9 = (bf16[3,32,384]{2,1,0:T(8,128)(2,1)S(1)}, bf16[3,32,384]{2,1,0:T(8,128)(2,1)S(1)}, u32[]{:S(2)}, u32[]{:S(2)}) collective-permute-start(bf16[3,32,384]{2,1,0:T(8,128)(2,1)S(1)} %get-tuple-element.36), channel_id=1, source_target_pairs={{0,1},{1,2},{2,3},{3,4},{4,5},{5,6},{6,7},{7,8},{8,9},{9,10},{10,1... | collective-permute-start | bytes 221192 | tf_op jit(solution)/shard_map/ppermute | solution.py:450
  36.9 25.5 %collective-permute-start.10 = (bf16[3,32,384]{2,1,0:T(8,128)(2,1)S(1)}, bf16[3,32,384]{2,1,0:T(8,128)(2,1)S(1)}, u32[]{:S(2)}, u32[]{:S(2)}) collective-permute-start(bf16[3,32,384]{2,1,0:T(8,128)(2,1)S(1)} %get-tuple-element.37), channel_id=1, source_target_pairs={{1,0},{2,1},{3,2},{4,3},{5,4},{6,5},{7,6},{8,7},{9,8},{10,9},{11,1... | collective-permute-start | bytes 221192 | tf_op jit(solution)/shard_map/ppermute | solution.py:450
  55.2 12.8 %collective-permute-start.13 = (bf16[288,128]{1,0:T(8,128)(2,1)S(1)}, bf16[288,128]{1,0:T(8,128)(2,1)S(1)}, u32[]{:S(2)}, u32[]{:S(2)}) collective-permute-start(bf16[288,128]{1,0:T(8,128)(2,1)S(1)} %get-tuple-element.52), channel_id=1, source_target_pairs={{0,4},{1,5},{2,6},{3,7},{4,8},{5,9},{6,10},{7,11},{8,12},{9,13},{1... | collective-permute-start | bytes 221192 | tf_op jit(solution)/shard_map/ppermute | solution.py:480
  56.8 11.4 %collective-permute-start.15 = (bf16[288,128]{1,0:T(8,128)(2,1)S(1)}, bf16[288,128]{1,0:T(8,128)(2,1)S(1)}, u32[]{:S(2)}, u32[]{:S(2)}) collective-permute-start(bf16[288,128]{1,0:T(8,128)(2,1)S(1)} %get-tuple-element.53), channel_id=1, source_target_pairs={{0,12},{1,13},{2,14},{3,15},{4,0},{5,1},{6,2},{7,3},{8,4},{9,5},{1... | collective-permute-start | bytes 221192 | tf_op jit(solution)/shard_map/ppermute | solution.py:480
  59.6 8.6 %collective-permute-start.14 = (bf16[288,128]{1,0:T(8,128)(2,1)S(1)}, bf16[288,128]{1,0:T(8,128)(2,1)S(1)}, u32[]{:S(2)}, u32[]{:S(2)}) collective-permute-start(bf16[288,128]{1,0:T(8,128)(2,1)S(1)} %get-tuple-element.54), channel_id=1, source_target_pairs={{0,8},{1,9},{2,10},{3,11},{4,12},{5,13},{6,14},{7,15},{8,0},{9,1},... | collective-permute-start | bytes 221192 | tf_op jit(solution)/shard_map/ppermute | solution.py:480
  59.8 8.5 %collective-permute-start.24 = (bf16[224,128]{1,0:T(8,128)(2,1)S(1)}, bf16[224,128]{1,0:T(8,128)(2,1)S(1)}, u32[]{:S(2)}, u32[]{:S(2)}) collective-permute-start(bf16[224,128]{1,0:T(8,128)(2,1)S(1)} %fusion.5.refs_0_), channel_id=1, source_target_pairs={{0,12},{1,13},{2,14},{3,15},{4,0},{5,1},{6,2},{7,3},{8,4},{9,5},{1... | collective-permute-start | bytes 172040 | tf_op jit(solution)/shard_map/ppermute | solution.py:480
  62.4 7.7 %collective-permute-start.23 = (bf16[224,128]{1,0:T(8,128)(2,1)S(1)}, bf16[224,128]{1,0:T(8,128)(2,1)S(1)}, u32[]{:S(2)}, u32[]{:S(2)}) collective-permute-start(bf16[224,128]{1,0:T(8,128)(2,1)S(1)} %fusion.5.refs_0_), channel_id=1, source_target_pairs={{0,8},{1,9},{2,10},{3,11},{4,12},{5,13},{6,14},{7,15},{8,0},{9,1},... | collective-permute-start | bytes 172040 | tf_op jit(solution)/shard_map/ppermute | solution.py:480
  74.0 8.2 %collective-permute-start.25 = (bf16[896,128]{1,0:T(8,128)(2,1)S(1)}, bf16[896,128]{1,0:T(8,128)(2,1)S(1)}, u32[]{:S(2)}, u32[]{:S(2)}) collective-permute-start(bf16[896,128]{1,0:T(8,128)(2,1)S(1)} %shard_map.150.refs_0_), channel_id=1, source_target_pairs={{0,1},{1,0},{2,3},{3,2},{4,5},{5,4},{6,7},{7,6},{8,9},{9,8},{10,11... | collective-permute-start | bytes 688136 | tf_op jit(solution)/shard_map/ppermute | solution.py:476
  74.4 7.8 %collective-permute-start.17 = (bf16[304,128]{1,0:T(8,128)(2,1)S(1)}, bf16[304,128]{1,0:T(8,128)(2,1)S(1)}, u32[]{:S(2)}, u32[]{:S(2)}) collective-permute-start(bf16[304,128]{1,0:T(8,128)(2,1)S(1)} %pad_maximum_fusion.refs_0_), channel_id=1, source_target_pairs={{0,8},{1,9},{2,10},{3,11},{4,12},{5,13},{6,14},{7,15},{8,0},{9,1},... | collective-permute-start | bytes 233480 | tf_op jit(solution)/shard_map/ppermute | solution.py:480
  74.4 7.8 %collective-permute-start.16 = (bf16[304,128]{1,0:T(8,128)(2,1)S(1)}, bf16[304,128]{1,0:T(8,128)(2,1)S(1)}, u32[]{:S(2)}, u32[]{:S(2)}) collective-permute-start(bf16[304,128]{1,0:T(8,128)(2,1)S(1)} %pad_maximum_fusion.refs_0_), channel_id=1, source_target_pairs={{0,4},{1,5},{2,6},{3,7},{4,8},{5,9},{6,10},{7,11},{8,12},{9,13},{1... | collective-permute-start | bytes 233480 | tf_op jit(solution)/shard_map/ppermute | solution.py:480
  76.2 8.6 %collective-permute-start.34 = (bf16[896,128]{1,0:T(8,128)(2,1)S(1)}, bf16[896,128]{1,0:T(8,128)(2,1)S(1)}, u32[]{:S(2)}, u32[]{:S(2)}) collective-permute-start(bf16[896,128]{1,0:T(8,128)(2,1)S(1)} %shard_map.150.refs_0_), channel_id=1, source_target_pairs={{0,2},{1,3},{2,0},{3,1},{4,6},{5,7},{6,4},{7,5},{8,10},{9,11},{10,... | collective-permute-start | bytes 688136 | tf_op jit(solution)/shard_map/ppermute | solution.py:476
  82.2 8.0 %collective-permute-start.27 = (bf16[1168,128]{1,0:T(8,128)(2,1)S(1)}, bf16[1168,128]{1,0:T(8,128)(2,1)S(1)}, u32[]{:S(2)}, u32[]{:S(2)}) collective-permute-start(bf16[1168,128]{1,0:T(8,128)(2,1)S(1)} %shard_map.151.refs_0_), channel_id=1, source_target_pairs={{0,2},{1,3},{2,0},{3,1},{4,6},{5,7},{6,4},{7,5},{8,10},{9,11},{10,... | collective-permute-start | bytes 897032 | tf_op jit(solution)/shard_map/ppermute | solution.py:476
  83.1 10.8 %collective-permute-start.26 = (bf16[1168,128]{1,0:T(8,128)(2,1)S(1)}, bf16[1168,128]{1,0:T(8,128)(2,1)S(1)}, u32[]{:S(2)}, u32[]{:S(2)}) collective-permute-start(bf16[1168,128]{1,0:T(8,128)(2,1)S(1)} %shard_map.151.refs_0_), channel_id=1, source_target_pairs={{0,1},{1,0},{2,3},{3,2},{4,5},{5,4},{6,7},{7,6},{8,9},{9,8},{10,11... | collective-permute-start | bytes 897032 | tf_op jit(solution)/shard_map/ppermute | solution.py:476
  85.2 15.3 %collective-permute-start.37 = (bf16[896,128]{1,0:T(8,128)(2,1)S(1)}, bf16[896,128]{1,0:T(8,128)(2,1)S(1)}, u32[]{:S(2)}, u32[]{:S(2)}) collective-permute-start(bf16[896,128]{1,0:T(8,128)(2,1)S(1)} %shard_map.150.refs_0_), channel_id=1, source_target_pairs={{0,16},{16,0},{1,17},{17,1},{2,18},{18,2},{3,19},{19,3},{4,20},{20... | collective-permute-start | bytes 688136 | tf_op jit(solution)/shard_map/ppermute | solution.py:596
  85.2 8.8 %collective-permute-start.36 = (bf16[448,128]{1,0:T(8,128)(2,1)S(1)}, bf16[448,128]{1,0:T(8,128)(2,1)S(1)}, u32[]{:S(2)}, u32[]{:S(2)}) collective-permute-start(bf16[448,128]{1,0:T(8,128)(2,1)S(1)} %slice.88), channel_id=1, source_target_pairs={{0,2},{1,3},{2,0},{3,1},{4,6},{5,7},{6,4},{7,5},{8,10},{9,11},{10,... | collective-permute-start | bytes 344072 | tf_op jit(solution)/shard_map/ppermute | solution.py:476
  90.2 10.8 %collective-permute-start.39 = (bf16[896,128]{1,0:T(8,128)(2,1)S(1)}, bf16[896,128]{1,0:T(8,128)(2,1)S(1)}, u32[]{:S(2)}, u32[]{:S(2)}) collective-permute-start(bf16[896,128]{1,0:T(8,128)(2,1)S(1)} %collective-permute-done.34.refs_2_), channel_id=1, source_target_pairs={{0,16},{16,0},{1,17},{17,1},{2,18},{18,2},{3,19},{19,3},{4,20},{20... | collective-permute-start | bytes 688136 | tf_op jit(solution)/shard_map/ppermute | solution.py:596
  (33 other events, 266.1 us)

commit v7 on v5

--- a/solution.py
+++ b/solution.py
@@ -377,6 +377,23 @@
         if spare:
             put(count * step, jnp.zeros((spare, 128), bf16))
         offset += share
+
+
+def halves(total):
+    high = total.astype(bf16)
+    return jnp.concatenate([high, (total - high.astype(f32)).astype(bf16)])
+
+
+def assemble_kernel(planes, size, *refs):
+    pieces, out_ref = refs[:planes], refs[-1]
+    q = lax.axis_index("height") // 4
+    for d, piece in enumerate(pieces):
+        start = pl.multiple_of((q - d + planes) % planes * size, 16)
+        out_ref[pl.ds(start, size)] = piece[:size]
+    if pieces[0].shape[0] > size:
+        total = functools.reduce(lambda a, b: a + b, [piece[size:].astype(f32) for piece in pieces])
+        half = total.shape[0] // 2
+        out_ref[planes * size :] = halves(total[:half] + total[half:])
 
 
 def unpack_kernel(taps, held, *refs):
@@ -543,17 +560,9 @@
     )
 
     small = jnp.concatenate([sums_one[:3], sums_two[:1]]).reshape(-1, 128)
-    count = small.shape[0]
-
-    def with_small(value, small):
-        high = small.astype(bf16)
-        low = (small - high.astype(f32)).astype(bf16)
-        pad = jnp.zeros((-2 * count % 16, 128), bf16)
-        return jnp.concatenate([value, high, low, pad])
-
-    def without_small(pieces, rows):
-        total = total_of([v[rows : rows + count].astype(f32) + v[rows + count : rows + 2 * count].astype(f32) for v in pieces])
-        return [v[:rows] for v in pieces], total
+    used = small.shape[0]
+    count = -(-used // 8) * 8
+    small = jnp.pad(small, ((0, count - used), (0, 0)))
 
     hop = 2
     while hop < tm:
@@ -561,22 +570,30 @@
         hop *= 2
 
     gradient = jax.ShapeDtypeStruct((taps_all, chans, chans), bf16)
-    grads = ()
+    grads, gate = (), ()
     for n, (part, taps) in enumerate(zip(parts, chunks)):
         last = n == len(parts) - 1
         size = part.shape[0]
-        send = with_small(part, small) if last else part
+        send = jnp.concatenate([part, halves(small)]) if last else part
         got = [send] + [column_move(send, d) for d in range(1, planes)]
-        if last:
-            got, small = without_small(got, size)
-        stack = jnp.stack(got)
-        quarter = jnp.take(stack, (q - jnp.arange(planes)) % planes, axis=0).reshape(-1, 128)
-        size = quarter.shape[0]
-        send = with_small(quarter, small) if last else quarter
-        got = [send] + [plane_move(send, d) for d in (1, 2, 3)]
+        (send,) = call(
+            functools.partial(assemble_kernel, planes, size),
+            (jax.ShapeDtypeStruct((planes * size + send.shape[0] - size, 128), bf16),),
+            got,
+            1,
+            6,
+        )
+        one, two = plane_move(send, 1), plane_move(send, 2)
+        cut = send.shape[0] // 32 * 16
+        if False:
+            three = jnp.concatenate([plane_move(two[:cut], 1), plane_move(one[cut:], 2)])
+        else:
+            three = plane_move(send, 3)
+        got = [send, one, two, three]
         others = [lax.ppermute(g, "tm", swap) for g in got]
         if last:
-            _, small = without_small(got + others, size)
+            small = total_of([v[planes * size :] for v in got + others])
+            small = (small[:count] + small[count:])[:used]
         held = len(grads) > 0
         grads = call(
             functools.partial(unpack_kernel, taps, held),
@@ -585,7 +602,7 @@
             2,
             12,
             [pltpu.VMEM((8 * taps[1], chans, chans), bf16), pltpu.SemaphoreType.DMA((8 * taps[1],))],
-            free=(8, 9),
+            free=(8, 9) if held else (),
             out_spec=anywhere,
             input_output_aliases={8: 0, 9: 1} if held else {},
         )

time: 105 us -> 103 us (0.981)
  starting transfers between devices: 37.4 us -> 40.3 us
  waiting for transfers between devices: 42.8 us -> 40.6 us
  local copies, waits for them, and re-layouts: 4.39 us -> 2.58 us
    ppermute x9, starting transfers between devices: 12.3 us -> 15 us  [column_move(): return lax.ppermute(value, 'height', pairs)]
    ppermute x9, waiting for transfers between devices: 14.2 us -> 12.1 us  [column_move(): return lax.ppermute(value, 'height', pairs)]
    ppermute x4, waiting for transfers between devices: 4.8 us -> 3.6 us  [moved(): lax.ppermute(value, axis, [(i, i + by) for i in range(size) if 0 <= i + b...]
    gather x2 -> x0, local copies, waits for them, and re-layouts: 1.2 us -> none  [body(): jnp.take(stack, (q - jnp.arange(planes)) % planes, axis=0).reshape(-1, 128)]
    pallas_call x9 -> x11, Pallas kernels: 16.8 us -> 16.9 us  [call(): pl.pallas_call(kernel, out_shape=outs, in_specs=[in_hbm if i in hbm else...]
  transfers between devices with their start and end apart: 36 -> 36, of which waited for: 18 -> 16; matrix products, arithmetic and copies ran while one was open for 2% -> 0% of each run, Pallas kernels for 11% -> 12%
where the time goes in v7:
time: 103 us
  waiting for transfers between devices  40.6 us (39%)
  starting transfers between devices  40.3 us (39%)
  Pallas kernels  16.9 us (16%)
  local copies, waits for them, and re-layouts  2.58 us (3%)
  between operations  1.29 us (1%)
  other arithmetic  1.26 us (1%)
    ppermute x12, waiting for transfers between devices, plane_move(): return lax.ppermute(value, 'height', [(i, i ^ d) for i in range(height)])  21.1 us
    pallas_call x11, Pallas kernels, call(): pl.pallas_call(kernel, out_shape=outs, in_specs=[in_hbm if i in hbm else...  16.9 us
    ppermute x9, starting transfers between devices, column_move(): return lax.ppermute(value, 'height', pairs)  15 us
    ppermute x12, starting transfers between devices, plane_move(): return lax.ppermute(value, 'height', [(i, i ^ d) for i in range(height)])  12.5 us
    ppermute x9, waiting for transfers between devices, column_move(): return lax.ppermute(value, 'height', pairs)  12.1 us
    ppermute x4, starting transfers between devices, moved(): lax.ppermute(value, axis, [(i, i + by) for i in range(size) if 0 <= i + b...  10.7 us
    ppermute x4, waiting for transfers between devices, moved(): lax.ppermute(value, axis, [(i, i + by) for i in range(size) if 0 <= i + b...  3.6 us
  transfers between devices with their start and end apart: 36, of which 16 were waited for; matrix products, arithmetic and copies ran while one was open for 0% of the time, Pallas kernels for 12%

profile of v7, /device:TPU:0, one launch (start us, length us, event | category | flops | bytes accessed | tf_op | source)
XLA Modules:
  0.0 102.9 jit_solution(18232776897240616674)
XLA Ops:
  3.5 2.9 %collective-permute-start.1 = (bf16[2,4,32,384]{3,2,1,0:T(8,128)(2,1)S(1)}, bf16[2,4,32,384]{3,2,1,0:T(8,128)(2,1)S(1)}, u32[]{:S(2)}, u32[]{:S(2)}) collective-permute-start(bf16[2,4,32,384]{3,2,1,0:T(8,128)(2,1)S(1)} %get-tuple-element.26.refs_4_), channel_id=1, source_target_pairs={{0,1},{1,0},{2,3},{3,2},{4,5},{5,4},{6,7},{7,6},{8,9},{9,8},{10,11... | collective-permute-start | bytes 589832 | tf_op jit(solution)/shard_map/ppermute | solution.py:475
  8.0 3.8 %collective-permute-start.4 = (bf16[3,32,384]{2,1,0:T(8,128)(2,1)S(1)}, bf16[3,32,384]{2,1,0:T(8,128)(2,1)S(1)}, u32[]{:S(2)}, u32[]{:S(2)}) collective-permute-start(bf16[3,32,384]{2,1,0:T(8,128)(2,1)S(1)} %get-tuple-element.27), channel_id=1, source_target_pairs={{0,1},{1,2},{2,3},{3,4},{4,5},{5,6},{6,7},{7,8},{8,9},{9,10},{10,1... | collective-permute-start | bytes 221192 | tf_op jit(solution)/shard_map/ppermute | solution.py:449
  13.2 1.7 %copy-done.1 = bf16[3,3,3,192,192]{4,3,2,1,0:T(8,128)(2,1)S(1)} copy-done((bf16[3,3,3,192,192]{4,3,2,1,0:T(8,128)(2,1)S(1)}, bf16[3,3,3,192,192]{4,3,2,1,0:T(8,128)(2,1)}, u32[]{:S(2)}) %copy-start.1) | copy-done | bytes 1990680
  15.5 2.1 %collective-permute-done.4.above_ref = bf16[3,32,384]{2,1,0:T(8,128)(2,1)S(1)} collective-permute-done((bf16[3,32,384]{2,1,0:T(8,128)(2,1)S(1)}, bf16[3,32,384]{2,1,0:T(8,128)(2,1)S(1)}, u32[]{:S(2)}, u32[]{:S(2)}) %collective-permute-start.4) | collective-permute-done | bytes 73760 | tf_op jit(solution)/shard_map/ppermute | solution.py:449
  19.1 2.7 %shard_map.145 = (bf16[4,32,384]{2,1,0:T(8,128)(2,1)S(1)}, bf16[4,32,384]{2,1,0:T(8,128)(2,1)S(1)}, f32[8,192]{1,0:T(8,128)S(1)}) custom-call(bf16[2,4,32,384]{3,2,1,0:T(8,128)(2,1)S(1)} %collective-permute-done.1._.refs_5_, bf16[2,4,32,384]{3,2,1,0:T(8,128)(2,1)S(1)} %collective-permute-done.2.__.refs_6_, ...), custom_call_target="tpu_custom_call" | custom-call | flops 5500000256 | bytes 1024 | tf_op jit(solution)/shard_map/pallas_call | solution.py:435
  23.3 2.7 %collective-permute-start.8 = (bf16[2,5,32,384]{3,2,1,0:T(8,128)(2,1)S(1)}, bf16[2,5,32,384]{3,2,1,0:T(8,128)(2,1)S(1)}, u32[]{:S(2)}, u32[]{:S(2)}) collective-permute-start(bf16[2,5,32,384]{3,2,1,0:T(8,128)(2,1)S(1)} %shard_map.146.refs_0_), channel_id=1, source_target_pairs={{0,1},{1,0},{2,3},{3,2},{4,5},{5,4},{6,7},{7,6},{8,9},{9,8},{10,11... | collective-permute-start | bytes 737288 | tf_op jit(solution)/shard_map/ppermute | solution.py:475
  28.9 3.9 %collective-permute-done.8._.refs_1_ = bf16[2,5,32,384]{3,2,1,0:T(8,128)(2,1)S(1)} collective-permute-done((bf16[2,5,32,384]{3,2,1,0:T(8,128)(2,1)S(1)}, bf16[2,5,32,384]{3,2,1,0:T(8,128)(2,1)S(1)}, u32[]{:S(2)}, u32[]{:S(2)}) %collective-permute-start.8) | collective-permute-done | bytes 245792 | tf_op jit(solution)/shard_map/ppermute | solution.py:475
  32.8 4.0 %collective-permute-start.9 = (bf16[3,32,384]{2,1,0:T(8,128)(2,1)S(1)}, bf16[3,32,384]{2,1,0:T(8,128)(2,1)S(1)}, u32[]{:S(2)}, u32[]{:S(2)}) collective-permute-start(bf16[3,32,384]{2,1,0:T(8,128)(2,1)S(1)} %get-tuple-element.34), channel_id=1, source_target_pairs={{0,1},{1,2},{2,3},{3,4},{4,5},{5,6},{6,7},{7,8},{8,9},{9,10},{10,1... | collective-permute-start | bytes 221192 | tf_op jit(solution)/shard_map/ppermute | solution.py:449
  36.8 1.6 %collective-permute-start.10 = (bf16[3,32,384]{2,1,0:T(8,128)(2,1)S(1)}, bf16[3,32,384]{2,1,0:T(8,128)(2,1)S(1)}, u32[]{:S(2)}, u32[]{:S(2)}) collective-permute-start(bf16[3,32,384]{2,1,0:T(8,128)(2,1)S(1)} %get-tuple-element.35), channel_id=1, source_target_pairs={{1,0},{2,1},{3,2},{4,3},{5,4},{6,5},{7,6},{8,7},{9,8},{10,9},{11,1... | collective-permute-start | bytes 221192 | tf_op jit(solution)/shard_map/ppermute | solution.py:449
  39.4 6.5 %shard_map.149 = bf16[4,512,128]{2,1,0:T(8,128)(2,1)S(1)} custom-call(bf16[2,5,32,384]{3,2,1,0:T(8,128)(2,1)S(1)} %shard_map.146.refs_0_, bf16[2,5,32,384]{3,2,1,0:T(8,128)(2,1)S(1)} %collective-permute-done.8._.refs_1_, bf16[2,5,32,384]{3,2,1,0:T(8,128)(2,1)S(1)} %collective-permute-done.11.refs_2_, ...), custom_call_target="tpu_custom_call" | custom-call | flops 7699999744 | bytes 1024 | tf_op jit(solution)/shard_map/pallas_call | solution.py:435
  45.9 5.1 %collective-permute-start.15 = (bf16[512,128]{1,0:T(8,128)(2,1)S(1)}, bf16[512,128]{1,0:T(8,128)(2,1)S(1)}, u32[]{:S(2)}, u32[]{:S(2)}) collective-permute-start(bf16[512,128]{1,0:T(8,128)(2,1)S(1)} %get-tuple-element.49), channel_id=1, source_target_pairs={{0,12},{1,13},{2,14},{3,15},{4,0},{5,1},{6,2},{7,3},{8,4},{9,5},{1... | collective-permute-start | bytes 393224 | tf_op jit(solution)/shard_map/ppermute | solution.py:479
  52.0 3.3 %shard_map.148 = (bf16[2,4,32,192]{3,2,1,0:T(8,128)(2,1)}, bf16[2,4,32,192]{3,2,1,0:T(8,128)(2,1)}, f32[8,192]{1,0:T(8,128)S(1)}) custom-call(bf16[4,32,384]{2,1,0:T(8,128)(2,1)S(1)} %get-tuple-element.32.keep_ref, bf16[4,32,384]{2,1,0:T(8,128)(2,1)S(1)} %get-tuple-element.33.give_ref, bf16[1,4,32,384]{3,2,1,0:T(8,128)(2,1)S(1)} %bitcast.20, ...), custom_call_target="tpu_custom_call" | custom-call | flops 6600000000 | bytes 1024 | tf_op jit(solution)/shard_map/pallas_call | solution.py:435
  55.4 8.4 %collective-permute-done.14 = bf16[512,128]{1,0:T(8,128)(2,1)S(1)} collective-permute-done((bf16[512,128]{1,0:T(8,128)(2,1)S(1)}, bf16[512,128]{1,0:T(8,128)(2,1)S(1)}, u32[]{:S(2)}, u32[]{:S(2)}) %collective-permute-start.14) | collective-permute-done | bytes 131104 | tf_op jit(solution)/shard_map/ppermute | solution.py:479
  64.5 2.0 %collective-permute-start.27 = (bf16[224,128]{1,0:T(8,128)(2,1)S(1)}, bf16[224,128]{1,0:T(8,128)(2,1)S(1)}, u32[]{:S(2)}, u32[]{:S(2)}) collective-permute-start(bf16[224,128]{1,0:T(8,128)(2,1)S(1)} %split.9.refs_0_), channel_id=1, source_target_pairs={{0,8},{1,9},{2,10},{3,11},{4,12},{5,13},{6,14},{7,15},{8,0},{9,1},... | collective-permute-start | bytes 172040 | tf_op jit(solution)/shard_map/ppermute | solution.py:479
  66.5 2.8 %collective-permute-start.28 = (bf16[224,128]{1,0:T(8,128)(2,1)S(1)}, bf16[224,128]{1,0:T(8,128)(2,1)S(1)}, u32[]{:S(2)}, u32[]{:S(2)}) collective-permute-start(bf16[224,128]{1,0:T(8,128)(2,1)S(1)} %split.9.refs_0_), channel_id=1, source_target_pairs={{0,12},{1,13},{2,14},{3,15},{4,0},{5,1},{6,2},{7,3},{8,4},{9,5},{1... | collective-permute-start | bytes 172040 | tf_op jit(solution)/shard_map/ppermute | solution.py:479
  70.3 2.9 %collective-permute-start.18 = (bf16[304,128]{1,0:T(8,128)(2,1)S(1)}, bf16[304,128]{1,0:T(8,128)(2,1)S(1)}, u32[]{:S(2)}, u32[]{:S(2)}) collective-permute-start(bf16[304,128]{1,0:T(8,128)(2,1)S(1)} %pad_maximum_fusion.refs_0_), channel_id=1, source_target_pairs={{0,12},{1,13},{2,14},{3,15},{4,0},{5,1},{6,2},{7,3},{8,4},{9,5},{1... | collective-permute-start | bytes 233480 | tf_op jit(solution)/shard_map/ppermute | solution.py:479
  74.4 2.1 %collective-permute-done.16.refs_1_ = bf16[304,128]{1,0:T(8,128)(2,1)S(1)} collective-permute-done((bf16[304,128]{1,0:T(8,128)(2,1)S(1)}, bf16[304,128]{1,0:T(8,128)(2,1)S(1)}, u32[]{:S(2)}, u32[]{:S(2)}) %collective-permute-start.16) | collective-permute-done | bytes 77856 | tf_op jit(solution)/shard_map/ppermute | solution.py:479
  78.2 3.6 %collective-permute-done.29.refs_1_ = bf16[896,128]{1,0:T(8,128)(2,1)S(1)} collective-permute-done((bf16[896,128]{1,0:T(8,128)(2,1)S(1)}, bf16[896,128]{1,0:T(8,128)(2,1)S(1)}, u32[]{:S(2)}, u32[]{:S(2)}) %collective-permute-start.29) | collective-permute-done | bytes 229408 | tf_op jit(solution)/shard_map/ppermute | solution.py:475
  81.8 2.0 %collective-permute-done.30.refs_2_ = bf16[896,128]{1,0:T(8,128)(2,1)S(1)} collective-permute-done((bf16[896,128]{1,0:T(8,128)(2,1)S(1)}, bf16[896,128]{1,0:T(8,128)(2,1)S(1)}, u32[]{:S(2)}, u32[]{:S(2)}) %collective-permute-start.30) | collective-permute-done | bytes 229408 | tf_op jit(solution)/shard_map/ppermute | solution.py:475
  83.9 2.2 %collective-permute-start.21 = (bf16[1168,128]{1,0:T(8,128)(2,1)S(1)}, bf16[1168,128]{1,0:T(8,128)(2,1)S(1)}, u32[]{:S(2)}, u32[]{:S(2)}) collective-permute-start(bf16[1168,128]{1,0:T(8,128)(2,1)S(1)} %shard_map.150.refs_0_), channel_id=1, source_target_pairs={{0,3},{1,2},{2,1},{3,0},{4,7},{5,6},{6,5},{7,4},{8,11},{9,10},{10,... | collective-permute-start | bytes 897032 | tf_op jit(solution)/shard_map/ppermute | solution.py:475
  86.6 6.5 %collective-permute-done.19.refs_1_ = bf16[1168,128]{1,0:T(8,128)(2,1)S(1)} collective-permute-done((bf16[1168,128]{1,0:T(8,128)(2,1)S(1)}, bf16[1168,128]{1,0:T(8,128)(2,1)S(1)}, u32[]{:S(2)}, u32[]{:S(2)}) %collective-permute-start.19) | collective-permute-done | bytes 299040 | tf_op jit(solution)/shard_map/ppermute | solution.py:475
  93.1 4.1 %collective-permute-done.20.refs_2_ = bf16[1168,128]{1,0:T(8,128)(2,1)S(1)} collective-permute-done((bf16[1168,128]{1,0:T(8,128)(2,1)S(1)}, bf16[1168,128]{1,0:T(8,128)(2,1)S(1)}, u32[]{:S(2)}, u32[]{:S(2)}) %collective-permute-start.20) | collective-permute-done | bytes 299040 | tf_op jit(solution)/shard_map/ppermute | solution.py:475
  98.3 1.7 %shard_map.152 = (bf16[27,192,192]{2,1,0:T(8,128)(2,1)}, bf16[27,192,192]{2,1,0:T(8,128)(2,1)}) custom-call(bf16[896,128]{1,0:T(8,128)(2,1)S(1)} %shard_map.151.refs_0_, bf16[896,128]{1,0:T(8,128)(2,1)S(1)} %collective-permute-done.29.refs_1_, bf16[896,128]{1,0:T(8,128)(2,1)S(1)} %collective-permute-done.30.refs_2_, ...), custom_call_target="tpu_custom_call" | custom-call | flops 2200000000 | bytes 1024 | tf_op jit(solution)/shard_map/pallas_call | solution.py:435
  100.8 1.9 %shard_map.153 = (bf16[27,192,192]{2,1,0:T(8,128)(2,1)}, bf16[27,192,192]{2,1,0:T(8,128)(2,1)}) custom-call(bf16[1168,128]{1,0:T(8,128)(2,1)S(1)} %shard_map.150.refs_0_, bf16[1168,128]{1,0:T(8,128)(2,1)S(1)} %collective-permute-done.19.refs_1_, bf16[1168,128]{1,0:T(8,128)(2,1)S(1)} %collective-permute-done.20.refs_2_, ...), custom_call_target="tpu_custom_call", output_to_operand_aliasing={{0}: (8, {}), {1}: (9, {})} | custom-call | flops 2200000000 | bytes 1024 | tf_op jit(solution)/shard_map/pallas_call | solution.py:435
  (111 shorter events, 21.0 us)
Async XLA Ops:
  3.5 15.6 %collective-permute-start.1 = (bf16[2,4,32,384]{3,2,1,0:T(8,128)(2,1)S(1)}, bf16[2,4,32,384]{3,2,1,0:T(8,128)(2,1)S(1)}, u32[]{:S(2)}, u32[]{:S(2)}) collective-permute-start(bf16[2,4,32,384]{3,2,1,0:T(8,128)(2,1)S(1)} %get-tuple-element.26.refs_4_), channel_id=1, source_target_pairs={{0,1},{1,0},{2,3},{3,2},{4,5},{5,4},{6,7},{7,6},{8,9},{9,8},{10,11... | collective-permute-start | bytes 589832 | tf_op jit(solution)/shard_map/ppermute | solution.py:475
  6.4 12.6 %collective-permute-start.2 = (bf16[2,4,32,384]{3,2,1,0:T(8,128)(2,1)S(1)}, bf16[2,4,32,384]{3,2,1,0:T(8,128)(2,1)S(1)}, u32[]{:S(2)}, u32[]{:S(2)}) collective-permute-start(bf16[2,4,32,384]{3,2,1,0:T(8,128)(2,1)S(1)} %get-tuple-element.26.refs_4_), channel_id=1, source_target_pairs={{0,2},{1,3},{2,0},{3,1},{4,6},{5,7},{6,4},{7,5},{8,10},{9,11},{10,... | collective-permute-start | bytes 589832 | tf_op jit(solution)/shard_map/ppermute | solution.py:475
  7.9 11.1 %collective-permute-start.3 = (bf16[2,4,32,384]{3,2,1,0:T(8,128)(2,1)S(1)}, bf16[2,4,32,384]{3,2,1,0:T(8,128)(2,1)S(1)}, u32[]{:S(2)}, u32[]{:S(2)}) collective-permute-start(bf16[2,4,32,384]{3,2,1,0:T(8,128)(2,1)S(1)} %get-tuple-element.26.refs_4_), channel_id=1, source_target_pairs={{0,3},{1,2},{2,1},{3,0},{4,7},{5,6},{6,5},{7,4},{8,11},{9,10},{10,... | collective-permute-start | bytes 589832 | tf_op jit(solution)/shard_map/ppermute | solution.py:475
  8.0 9.6 %collective-permute-start.4 = (bf16[3,32,384]{2,1,0:T(8,128)(2,1)S(1)}, bf16[3,32,384]{2,1,0:T(8,128)(2,1)S(1)}, u32[]{:S(2)}, u32[]{:S(2)}) collective-permute-start(bf16[3,32,384]{2,1,0:T(8,128)(2,1)S(1)} %get-tuple-element.27), channel_id=1, source_target_pairs={{0,1},{1,2},{2,3},{3,4},{4,5},{5,6},{6,7},{7,8},{8,9},{9,10},{10,1... | collective-permute-start | bytes 221192 | tf_op jit(solution)/shard_map/ppermute | solution.py:449
  23.3 9.5 %collective-permute-start.8 = (bf16[2,5,32,384]{3,2,1,0:T(8,128)(2,1)S(1)}, bf16[2,5,32,384]{3,2,1,0:T(8,128)(2,1)S(1)}, u32[]{:S(2)}, u32[]{:S(2)}) collective-permute-start(bf16[2,5,32,384]{3,2,1,0:T(8,128)(2,1)S(1)} %shard_map.146.refs_0_), channel_id=1, source_target_pairs={{0,1},{1,0},{2,3},{3,2},{4,5},{5,4},{6,7},{7,6},{8,9},{9,8},{10,11... | collective-permute-start | bytes 737288 | tf_op jit(solution)/shard_map/ppermute | solution.py:475
  26.0 13.3 %collective-permute-start.11 = (bf16[2,5,32,384]{3,2,1,0:T(8,128)(2,1)S(1)}, bf16[2,5,32,384]{3,2,1,0:T(8,128)(2,1)S(1)}, u32[]{:S(2)}, u32[]{:S(2)}) collective-permute-start(bf16[2,5,32,384]{3,2,1,0:T(8,128)(2,1)S(1)} %shard_map.146.refs_0_), channel_id=1, source_target_pairs={{0,2},{1,3},{2,0},{3,1},{4,6},{5,7},{6,4},{7,5},{8,10},{9,11},{10,... | collective-permute-start | bytes 737288 | tf_op jit(solution)/shard_map/ppermute | solution.py:475
  27.2 12.1 %collective-permute-start.12 = (bf16[2,5,32,384]{3,2,1,0:T(8,128)(2,1)S(1)}, bf16[2,5,32,384]{3,2,1,0:T(8,128)(2,1)S(1)}, u32[]{:S(2)}, u32[]{:S(2)}) collective-permute-start(bf16[2,5,32,384]{3,2,1,0:T(8,128)(2,1)S(1)} %shard_map.146.refs_0_), channel_id=1, source_target_pairs={{0,3},{1,2},{2,1},{3,0},{4,7},{5,6},{6,5},{7,4},{8,11},{9,10},{10,... | collective-permute-start | bytes 737288 | tf_op jit(solution)/shard_map/ppermute | solution.py:475
  32.8 19.2 %collective-permute-start.9 = (bf16[3,32,384]{2,1,0:T(8,128)(2,1)S(1)}, bf16[3,32,384]{2,1,0:T(8,128)(2,1)S(1)}, u32[]{:S(2)}, u32[]{:S(2)}) collective-permute-start(bf16[3,32,384]{2,1,0:T(8,128)(2,1)S(1)} %get-tuple-element.34), channel_id=1, source_target_pairs={{0,1},{1,2},{2,3},{3,4},{4,5},{5,6},{6,7},{7,8},{8,9},{9,10},{10,1... | collective-permute-start | bytes 221192 | tf_op jit(solution)/shard_map/ppermute | solution.py:449
  36.8 15.2 %collective-permute-start.10 = (bf16[3,32,384]{2,1,0:T(8,128)(2,1)S(1)}, bf16[3,32,384]{2,1,0:T(8,128)(2,1)S(1)}, u32[]{:S(2)}, u32[]{:S(2)}) collective-permute-start(bf16[3,32,384]{2,1,0:T(8,128)(2,1)S(1)} %get-tuple-element.35), channel_id=1, source_target_pairs={{1,0},{2,1},{3,2},{4,3},{5,4},{6,5},{7,6},{8,7},{9,8},{10,9},{11,1... | collective-permute-start | bytes 221192 | tf_op jit(solution)/shard_map/ppermute | solution.py:449
  45.9 9.6 %collective-permute-start.15 = (bf16[512,128]{1,0:T(8,128)(2,1)S(1)}, bf16[512,128]{1,0:T(8,128)(2,1)S(1)}, u32[]{:S(2)}, u32[]{:S(2)}) collective-permute-start(bf16[512,128]{1,0:T(8,128)(2,1)S(1)} %get-tuple-element.49), channel_id=1, source_target_pairs={{0,12},{1,13},{2,14},{3,15},{4,0},{5,1},{6,2},{7,3},{8,4},{9,5},{1... | collective-permute-start | bytes 393224 | tf_op jit(solution)/shard_map/ppermute | solution.py:479
  51.0 12.9 %collective-permute-start.14 = (bf16[512,128]{1,0:T(8,128)(2,1)S(1)}, bf16[512,128]{1,0:T(8,128)(2,1)S(1)}, u32[]{:S(2)}, u32[]{:S(2)}) collective-permute-start(bf16[512,128]{1,0:T(8,128)(2,1)S(1)} %get-tuple-element.50), channel_id=1, source_target_pairs={{0,8},{1,9},{2,10},{3,11},{4,12},{5,13},{6,14},{7,15},{8,0},{9,1},... | collective-permute-start | bytes 393224 | tf_op jit(solution)/shard_map/ppermute | solution.py:479
  51.0 12.9 %collective-permute-start.13 = (bf16[512,128]{1,0:T(8,128)(2,1)S(1)}, bf16[512,128]{1,0:T(8,128)(2,1)S(1)}, u32[]{:S(2)}, u32[]{:S(2)}) collective-permute-start(bf16[512,128]{1,0:T(8,128)(2,1)S(1)} %get-tuple-element.48), channel_id=1, source_target_pairs={{0,4},{1,5},{2,6},{3,7},{4,8},{5,9},{6,10},{7,11},{8,12},{9,13},{1... | collective-permute-start | bytes 393224 | tf_op jit(solution)/shard_map/ppermute | solution.py:479
  64.5 8.7 %collective-permute-start.27 = (bf16[224,128]{1,0:T(8,128)(2,1)S(1)}, bf16[224,128]{1,0:T(8,128)(2,1)S(1)}, u32[]{:S(2)}, u32[]{:S(2)}) collective-permute-start(bf16[224,128]{1,0:T(8,128)(2,1)S(1)} %split.9.refs_0_), channel_id=1, source_target_pairs={{0,8},{1,9},{2,10},{3,11},{4,12},{5,13},{6,14},{7,15},{8,0},{9,1},... | collective-permute-start | bytes 172040 | tf_op jit(solution)/shard_map/ppermute | solution.py:479
  69.3 8.8 %collective-permute-start.17 = (bf16[304,128]{1,0:T(8,128)(2,1)S(1)}, bf16[304,128]{1,0:T(8,128)(2,1)S(1)}, u32[]{:S(2)}, u32[]{:S(2)}) collective-permute-start(bf16[304,128]{1,0:T(8,128)(2,1)S(1)} %pad_maximum_fusion.refs_0_), channel_id=1, source_target_pairs={{0,8},{1,9},{2,10},{3,11},{4,12},{5,13},{6,14},{7,15},{8,0},{9,1},... | collective-permute-start | bytes 233480 | tf_op jit(solution)/shard_map/ppermute | solution.py:479
  70.3 7.9 %collective-permute-start.18 = (bf16[304,128]{1,0:T(8,128)(2,1)S(1)}, bf16[304,128]{1,0:T(8,128)(2,1)S(1)}, u32[]{:S(2)}, u32[]{:S(2)}) collective-permute-start(bf16[304,128]{1,0:T(8,128)(2,1)S(1)} %pad_maximum_fusion.refs_0_), channel_id=1, source_target_pairs={{0,12},{1,13},{2,14},{3,15},{4,0},{5,1},{6,2},{7,3},{8,4},{9,5},{1... | collective-permute-start | bytes 233480 | tf_op jit(solution)/shard_map/ppermute | solution.py:479
  73.2 8.6 %collective-permute-start.29 = (bf16[896,128]{1,0:T(8,128)(2,1)S(1)}, bf16[896,128]{1,0:T(8,128)(2,1)S(1)}, u32[]{:S(2)}, u32[]{:S(2)}) collective-permute-start(bf16[896,128]{1,0:T(8,128)(2,1)S(1)} %shard_map.151.refs_0_), channel_id=1, source_target_pairs={{0,1},{1,0},{2,3},{3,2},{4,5},{5,4},{6,7},{7,6},{8,9},{9,8},{10,11... | collective-permute-start | bytes 688136 | tf_op jit(solution)/shard_map/ppermute | solution.py:475
  73.3 10.6 %collective-permute-start.30 = (bf16[896,128]{1,0:T(8,128)(2,1)S(1)}, bf16[896,128]{1,0:T(8,128)(2,1)S(1)}, u32[]{:S(2)}, u32[]{:S(2)}) collective-permute-start(bf16[896,128]{1,0:T(8,128)(2,1)S(1)} %shard_map.151.refs_0_), channel_id=1, source_target_pairs={{0,2},{1,3},{2,0},{3,1},{4,6},{5,7},{6,4},{7,5},{8,10},{9,11},{10,... | collective-permute-start | bytes 688136 | tf_op jit(solution)/shard_map/ppermute | solution.py:475
  76.4 9.7 %collective-permute-start.31 = (bf16[896,128]{1,0:T(8,128)(2,1)S(1)}, bf16[896,128]{1,0:T(8,128)(2,1)S(1)}, u32[]{:S(2)}, u32[]{:S(2)}) collective-permute-start(bf16[896,128]{1,0:T(8,128)(2,1)S(1)} %shard_map.151.refs_0_), channel_id=1, source_target_pairs={{0,3},{1,2},{2,1},{3,0},{4,7},{5,6},{6,5},{7,4},{8,11},{9,10},{10,... | collective-permute-start | bytes 688136 | tf_op jit(solution)/shard_map/ppermute | solution.py:475
  78.1 8.0 %collective-permute-start.32 = (bf16[896,128]{1,0:T(8,128)(2,1)S(1)}, bf16[896,128]{1,0:T(8,128)(2,1)S(1)}, u32[]{:S(2)}, u32[]{:S(2)}) collective-permute-start(bf16[896,128]{1,0:T(8,128)(2,1)S(1)} %shard_map.151.refs_0_), channel_id=1, source_target_pairs={{0,16},{16,0},{1,17},{17,1},{2,18},{18,2},{3,19},{19,3},{4,20},{20... | collective-permute-start | bytes 688136 | tf_op jit(solution)/shard_map/ppermute | solution.py:593
  78.2 15.0 %collective-permute-start.19 = (bf16[1168,128]{1,0:T(8,128)(2,1)S(1)}, bf16[1168,128]{1,0:T(8,128)(2,1)S(1)}, u32[]{:S(2)}, u32[]{:S(2)}) collective-permute-start(bf16[1168,128]{1,0:T(8,128)(2,1)S(1)} %shard_map.150.refs_0_), channel_id=1, source_target_pairs={{0,1},{1,0},{2,3},{3,2},{4,5},{5,4},{6,7},{7,6},{8,9},{9,8},{10,11... | collective-permute-start | bytes 897032 | tf_op jit(solution)/shard_map/ppermute | solution.py:475
  81.8 15.5 %collective-permute-start.20 = (bf16[1168,128]{1,0:T(8,128)(2,1)S(1)}, bf16[1168,128]{1,0:T(8,128)(2,1)S(1)}, u32[]{:S(2)}, u32[]{:S(2)}) collective-permute-start(bf16[1168,128]{1,0:T(8,128)(2,1)S(1)} %shard_map.150.refs_0_), channel_id=1, source_target_pairs={{0,2},{1,3},{2,0},{3,1},{4,6},{5,7},{6,4},{7,5},{8,10},{9,11},{10,... | collective-permute-start | bytes 897032 | tf_op jit(solution)/shard_map/ppermute | solution.py:475
  83.9 13.4 %collective-permute-start.21 = (bf16[1168,128]{1,0:T(8,128)(2,1)S(1)}, bf16[1168,128]{1,0:T(8,128)(2,1)S(1)}, u32[]{:S(2)}, u32[]{:S(2)}) collective-permute-start(bf16[1168,128]{1,0:T(8,128)(2,1)S(1)} %shard_map.150.refs_0_), channel_id=1, source_target_pairs={{0,3},{1,2},{2,1},{3,0},{4,7},{5,6},{6,5},{7,4},{8,11},{9,10},{10,... | collective-permute-start | bytes 897032 | tf_op jit(solution)/shard_map/ppermute | solution.py:475
  86.1 11.7 %collective-permute-start.33 = (bf16[896,128]{1,0:T(8,128)(2,1)S(1)}, bf16[896,128]{1,0:T(8,128)(2,1)S(1)}, u32[]{:S(2)}, u32[]{:S(2)}) collective-permute-start(bf16[896,128]{1,0:T(8,128)(2,1)S(1)} %collective-permute-done.29.refs_1_), channel_id=1, source_target_pairs={{0,16},{16,0},{1,17},{17,1},{2,18},{18,2},{3,19},{19,3},{4,20},{20... | collective-permute-start | bytes 688136 | tf_op jit(solution)/shard_map/ppermute | solution.py:593
  86.1 11.8 %collective-permute-start.34 = (bf16[896,128]{1,0:T(8,128)(2,1)S(1)}, bf16[896,128]{1,0:T(8,128)(2,1)S(1)}, u32[]{:S(2)}, u32[]{:S(2)}) collective-permute-start(bf16[896,128]{1,0:T(8,128)(2,1)S(1)} %collective-permute-done.30.refs_2_), channel_id=1, source_target_pairs={{0,16},{16,0},{1,17},{17,1},{2,18},{18,2},{3,19},{19,3},{4,20},{20... | collective-permute-start | bytes 688136 | tf_op jit(solution)/shard_map/ppermute | solution.py:593
  (30 other events, 238.5 us)

commit v8 on v7

--- a/solution.py
+++ b/solution.py
@@ -287,39 +287,51 @@
     return -(-count * pack_rows(chans) // unit) * unit
 
 
+def put_y(plane, blocks, values, row, count, gain):
+    chans = plane.shape[3]
+    base = jnp.where(is_odd(), 2, 0) if blocks == 2 else 0
+    for b in range(blocks):
+        for f in range(2):
+            part = values[b, :, :, f * chans : (f + 1) * chans]
+            place = (base + 2 * b + f, pl.ds(row, count))
+
+            def odd():
+                flat = part.astype(f32).reshape(-1, chans)
+                plane[place] = norm_silu(flat, gain).astype(bf16).reshape(part.shape)
+
+            def even():
+                plane[place] = part
+
+            by_core(odd, even)
+
+
+def plane_kernel(blocks, *refs):
+    ys, gain, plane = refs[:4], refs[4][1:2], refs[-1]
+    rows = ys[0].shape[1]
+    p = lax.axis_index("height") % 4
+    if blocks == 2:
+        plane[pl.ds(jnp.where(is_odd(), 0, 4), 2)] = jnp.zeros((2,) + plane.shape[1:], bf16)
+    for d in range(4):
+        put_y(plane, blocks, ys[d][...], 1 + rows * (p ^ d), rows, gain)
+
+
 def wgrad_kernel(blocks, planes, *refs):
-    xs, ys = refs[:4], refs[4:8]
-    gain = refs[8][1:2]
+    xs, plane_in, gain = refs[:4], refs[4], refs[5][1:2]
     out_ref, plane, xk = refs[-3:]
-    _, rows, cols, _ = ys[0].shape
-    chans = gain.shape[1]
+    _, rows, cols, _ = xs[0].shape
+    rows -= 1
+    chans = plane.shape[3]
     tall = 4 * rows
     cells = 4 * tall * cols
-    odd = lax.axis_index("tm") % 2 == 1
+    odd = is_odd()
     p = lax.axis_index("height") % 4
-    single = blocks == 2
-    start = jnp.where(odd, 2, 0) if single else 0
-    if single:
-        plane[pl.ds(jnp.where(odd, 0, 4), 2)] = jnp.zeros((2,) + plane.shape[1:], bf16)
-
-    def put_y(values, row, count):
-        for b in range(blocks):
-            for f in range(2):
-                part = values[b, :, :, f * chans : (f + 1) * chans]
-                place = (start + 2 * b + f, pl.ds(row, count))
-
-                @pl.when(odd)
-                def _():
-                    flat = part.astype(f32).reshape(-1, chans)
-                    plane[place] = norm_silu(flat, gain).astype(bf16).reshape(part.shape)
-
-                @pl.when(jnp.logical_not(odd))
-                def _():
-                    plane[place] = part
-
+    plane[:, 1 : tall + 1] = plane_in[:, 1 : tall + 1]
+    if blocks == 2:
+        empty = jnp.zeros((2, 1, cols, chans), bf16)
+        for row in (0, tall + 1):
+            plane[pl.ds(jnp.where(odd, 0, 4), 2), row : row + 1] = empty
     for d in range(4):
         at = p ^ d
-        put_y(ys[d][...], 1 + rows * at, rows)
         for b in range(2):
             for f in range(2):
                 part = xs[d][b, :rows, :, f * chans : (f + 1) * chans]
@@ -331,11 +343,11 @@
 
         @pl.when(at == 0)
         def _():
-            put_y(xs[d][:, rows:], 0, 1)
+            put_y(plane, blocks, xs[d][:, rows:], 0, 1, gain)
 
         @pl.when(at == 3)
         def _():
-            put_y(xs[d][:, rows:], tall + 1, 1)
+            put_y(plane, blocks, xs[d][:, rows:], tall + 1, 1, gain)
 
     step = pack_rows(chans)
     dims = (((0,), (0,)), ((), ()))
@@ -399,6 +411,7 @@
 def unpack_kernel(taps, held, *refs):
     pieces = refs[:8]
     outs, stage, sems = refs[8 + 2 * held : 10 + 2 * held], refs[-2], refs[-1]
+    more = refs[10 + 2 * held : -2]
     first, count = taps
     chans = stage.shape[1]
     half = chans // 2
@@ -422,6 +435,12 @@
                 copy = pltpu.make_async_copy(stage.at[slot], outs[which].at[tap], sems.at[slot])
                 pl.when(good)(copy.start)
                 made.append((good, copy))
+    if more:
+        sums = functools.reduce(lambda a, b: a + b, [src[src.shape[0] - 16 :].astype(f32) for src in pieces])
+        sums = sums[:8] + sums[8:]
+        for i in range(4):
+            row = jnp.concatenate([sums[2 * i : 2 * i + 1], sums[2 * i + 1 : 2 * i + 2, : chans - 128]], axis=1)
+            more[0][i : i + 1] = row.astype(bf16)
     for good, copy in made:
         pl.when(good)(copy.wait)
 
@@ -431,12 +450,12 @@
 in_hbm = pl.BlockSpec(memory_space=pltpu.HBM)
 
 
-def call(kernel, outs, args, us, mib, scratch=(), free=(), hbm=(), out_spec=vmem, **kw):
+def call(kernel, outs, args, us, mib, scratch=(), free=(), hbm=(), out_specs=None, **kw):
     return pl.pallas_call(
         kernel,
         out_shape=outs,
         in_specs=[in_hbm if i in hbm else anywhere if i in free else vmem for i in range(len(args))],
-        out_specs=[out_spec] * len(outs),
+        out_specs=out_specs or [vmem] * len(outs),
         scratch_shapes=list(scratch),
         compiler_params=pltpu.CompilerParams(vmem_limit_bytes=mib * 2**20),
         cost_estimate=pl.CostEstimate(flops=int(us * 1.1e9), bytes_accessed=1024, transcendentals=0),
@@ -529,12 +548,20 @@
     up, down = call(gate_kernel, messages, (keep, give, far, xs[1]), 1, 6, free=(3,))
     above, below = moved(up, "height", 1), moved(down, "height", -1)
 
+    (plane,) = call(
+        functools.partial(plane_kernel, blocks),
+        (jax.ShapeDtypeStruct((2 * frames + 2, 4 * rows + 2, cols, chans), bf16),),
+        (*ys, vec, x_own),
+        3,
+        8,
+        free=(5,),
+    )
     shares = [chunk_rows(count, chans, planes) // planes for _, count in chunks]
     (flat,) = call(
         functools.partial(wgrad_kernel, blocks, planes),
         (jax.ShapeDtypeStruct((planes, sum(shares), 128), bf16),),
-        (*xs, *ys, vec),
-        7,
+        (*xs, plane, vec),
+        6,
         24,
         [
             pltpu.VMEM((2 * frames + 2, 4 * rows + 2, cols, chans), bf16),
@@ -559,10 +586,8 @@
         [window, window],
     )
 
-    small = jnp.concatenate([sums_one[:3], sums_two[:1]]).reshape(-1, 128)
-    used = small.shape[0]
-    count = -(-used // 8) * 8
-    small = jnp.pad(small, ((0, count - used), (0, 0)))
+    small = jnp.concatenate([sums_one[:3], sums_two[:1]])
+    small = jnp.pad(small, ((0, 0), (0, -chans % 128))).reshape(-1, 128)
 
     hop = 2
     while hop < tm:
@@ -591,24 +616,20 @@
             three = plane_move(send, 3)
         got = [send, one, two, three]
         others = [lax.ppermute(g, "tm", swap) for g in got]
-        if last:
-            small = total_of([v[planes * size :] for v in got + others])
-            small = (small[:count] + small[count:])[:used]
         held = len(grads) > 0
         grads = call(
             functools.partial(unpack_kernel, taps, held),
-            (gradient, gradient),
+            (gradient, gradient) + (jax.ShapeDtypeStruct((4, chans), bf16),) * last,
             (*got, *others, *grads),
             2,
             12,
             [pltpu.VMEM((8 * taps[1], chans, chans), bf16), pltpu.SemaphoreType.DMA((8 * taps[1],))],
             free=(8, 9) if held else (),
-            out_spec=anywhere,
+            out_specs=[anywhere, anywhere] + [vmem] * last,
             input_output_aliases={8: 0, 9: 1} if held else {},
         )
-    grad_one, grad_two = grads
+    grad_one, grad_two, small = grads
     shape = weight_one.shape
-    small = small.reshape(4, chans).astype(bf16)
     return (
         block_out,
         grad_input,

time: 103 us -> 109 us (1.058)
  waiting for transfers between devices: 40.6 us -> 43.9 us
  starting transfers between devices: 40.3 us -> 42.3 us
    ppermute x12, waiting for transfers between devices: 21.1 us -> 24.7 us  [plane_move(): return lax.ppermute(value, 'height', [(i, i ^ d) for i in range(height)])]
    ppermute x12, starting transfers between devices: 12.5 us -> 15 us  [plane_move(): return lax.ppermute(value, 'height', [(i, i ^ d) for i in range(height)])]
    ppermute x1, waiting for transfers between devices: 1.3 us -> 0.01 us  [body(): far = lax.ppermute(keep, 'tm', swap)[None]]
    ppermute x4, waiting for transfers between devices: 3.6 us -> 4.81 us  [moved(): lax.ppermute(value, axis, [(i, i + by) for i in range(size) if 0 <= i + b...]
    unnamed x36 -> x32, local copies, waits for them, and re-layouts: 1.82 us -> 2.7 us
    pallas_call x11 -> x12, Pallas kernels: 16.9 us -> 16.9 us  [call(): pl.pallas_call(kernel, out_shape=outs, in_specs=[in_hbm if i in hbm else...]
  transfers between devices with their start and end apart: 36 -> 36, of which waited for: 16 -> 14; matrix products, arithmetic and copies ran while one was open for 0% -> 0% of each run, Pallas kernels for 12% -> 11%
where the time goes in v8:
time: 109 us
  waiting for transfers between devices  43.9 us (40%)
  starting transfers between devices  42.3 us (39%)
  Pallas kernels  16.9 us (16%)
  local copies, waits for them, and re-layouts  3.29 us (3%)
  other arithmetic  1.24 us (1%)
  between operations  1.2 us (1%)
    ppermute x12, waiting for transfers between devices, plane_move(): return lax.ppermute(value, 'height', [(i, i ^ d) for i in range(height)])  24.7 us
    pallas_call x12, Pallas kernels, call(): pl.pallas_call(kernel, out_shape=outs, in_specs=[in_hbm if i in hbm else...  16.9 us
    ppermute x12, starting transfers between devices, plane_move(): return lax.ppermute(value, 'height', [(i, i ^ d) for i in range(height)])  15 us
    ppermute x9, starting transfers between devices, column_move(): return lax.ppermute(value, 'height', pairs)  14.1 us
    ppermute x9, waiting for transfers between devices, column_move(): return lax.ppermute(value, 'height', pairs)  12.5 us
    ppermute x4, starting transfers between devices, moved(): lax.ppermute(value, axis, [(i, i + by) for i in range(size) if 0 <= i + b...  10.6 us
    ppermute x4, waiting for transfers between devices, moved(): lax.ppermute(value, axis, [(i, i + by) for i in range(size) if 0 <= i + b...  4.81 us
    unnamed x32, local copies, waits for them, and re-layouts  2.7 us
  transfers between devices with their start and end apart: 36, of which 14 were waited for; matrix products, arithmetic and copies ran while one was open for 0% of the time, Pallas kernels for 11%

profile of v8, /device:TPU:0, one launch (start us, length us, event | category | flops | bytes accessed | tf_op | source)
XLA Modules:
  0.0 108.8 jit_solution(13428438816705815406)
XLA Ops:
  3.5 3.9 %collective-permute-start.3 = (bf16[2,4,32,384]{3,2,1,0:T(8,128)(2,1)S(1)}, bf16[2,4,32,384]{3,2,1,0:T(8,128)(2,1)S(1)}, u32[]{:S(2)}, u32[]{:S(2)}) collective-permute-start(bf16[2,4,32,384]{3,2,1,0:T(8,128)(2,1)S(1)} %get-tuple-element.27.refs_0_), channel_id=1, source_target_pairs={{0,3},{1,2},{2,1},{3,0},{4,7},{5,6},{6,5},{7,4},{8,11},{9,10},{10,... | collective-permute-start | bytes 589832 | tf_op jit(solution)/shard_map/ppermute | solution.py:494
  8.0 3.8 %collective-permute-start.4 = (bf16[3,32,384]{2,1,0:T(8,128)(2,1)S(1)}, bf16[3,32,384]{2,1,0:T(8,128)(2,1)S(1)}, u32[]{:S(2)}, u32[]{:S(2)}) collective-permute-start(bf16[3,32,384]{2,1,0:T(8,128)(2,1)S(1)} %get-tuple-element.28), channel_id=1, source_target_pairs={{0,1},{1,2},{2,3},{3,4},{4,5},{5,6},{6,7},{7,8},{8,9},{9,10},{10,1... | collective-permute-start | bytes 221192 | tf_op jit(solution)/shard_map/ppermute | solution.py:468
  13.2 1.7 %copy-done.1 = bf16[3,3,3,192,192]{4,3,2,1,0:T(8,128)(2,1)S(1)} copy-done((bf16[3,3,3,192,192]{4,3,2,1,0:T(8,128)(2,1)S(1)}, bf16[3,3,3,192,192]{4,3,2,1,0:T(8,128)(2,1)}, u32[]{:S(2)}) %copy-start.1) | copy-done | bytes 1990680
  15.4 3.9 %collective-permute-done.4.above_ref = bf16[3,32,384]{2,1,0:T(8,128)(2,1)S(1)} collective-permute-done((bf16[3,32,384]{2,1,0:T(8,128)(2,1)S(1)}, bf16[3,32,384]{2,1,0:T(8,128)(2,1)S(1)}, u32[]{:S(2)}, u32[]{:S(2)}) %collective-permute-start.4) | collective-permute-done | bytes 73760 | tf_op jit(solution)/shard_map/ppermute | solution.py:468
  20.3 2.7 %shard_map.145 = (bf16[4,32,384]{2,1,0:T(8,128)(2,1)S(1)}, bf16[4,32,384]{2,1,0:T(8,128)(2,1)S(1)}, f32[8,192]{1,0:T(8,128)S(1)}) custom-call(bf16[2,4,32,384]{3,2,1,0:T(8,128)(2,1)S(1)} %collective-permute-done.1._.refs_1_, bf16[2,4,32,384]{3,2,1,0:T(8,128)(2,1)S(1)} %collective-permute-done.2.__.refs_2_, ...), custom_call_target="tpu_custom_call" | custom-call | flops 5500000256 | bytes 1024 | tf_op jit(solution)/shard_map/pallas_call | solution.py:454
  25.4 2.2 %collective-permute-start.12 = (bf16[2,5,32,384]{3,2,1,0:T(8,128)(2,1)S(1)}, bf16[2,5,32,384]{3,2,1,0:T(8,128)(2,1)S(1)}, u32[]{:S(2)}, u32[]{:S(2)}) collective-permute-start(bf16[2,5,32,384]{3,2,1,0:T(8,128)(2,1)S(1)} %shard_map.146.refs_5_.refs_0_), channel_id=1, source_target_pairs={{0,3},{1,2},{2,1},{3,0},{4,7},{5,6},{6,5},{7,4},{8,11},{9,10},{10,... | collective-permute-start | bytes 737288 | tf_op jit(solution)/shard_map/ppermute | solution.py:494
  30.0 8.9 %collective-permute-done.8._.refs_1_ = bf16[2,5,32,384]{3,2,1,0:T(8,128)(2,1)S(1)} collective-permute-done((bf16[2,5,32,384]{3,2,1,0:T(8,128)(2,1)S(1)}, bf16[2,5,32,384]{3,2,1,0:T(8,128)(2,1)S(1)}, u32[]{:S(2)}, u32[]{:S(2)}) %collective-permute-start.8) | collective-permute-done | bytes 245792 | tf_op jit(solution)/shard_map/ppermute | solution.py:494
  38.9 3.9 %collective-permute-start.9 = (bf16[3,32,384]{2,1,0:T(8,128)(2,1)S(1)}, bf16[3,32,384]{2,1,0:T(8,128)(2,1)S(1)}, u32[]{:S(2)}, u32[]{:S(2)}) collective-permute-start(bf16[3,32,384]{2,1,0:T(8,128)(2,1)S(1)} %get-tuple-element.35), channel_id=1, source_target_pairs={{0,1},{1,2},{2,3},{3,4},{4,5},{5,6},{6,7},{7,8},{8,9},{9,10},{10,1... | collective-permute-start | bytes 221192 | tf_op jit(solution)/shard_map/ppermute | solution.py:468
  44.5 5.5 %shard_map.150 = bf16[4,512,128]{2,1,0:T(8,128)(2,1)S(1)} custom-call(bf16[2,5,32,384]{3,2,1,0:T(8,128)(2,1)S(1)} %shard_map.146.refs_5_.refs_0_, bf16[2,5,32,384]{3,2,1,0:T(8,128)(2,1)S(1)} %collective-permute-done.8._.refs_1_, bf16[2,5,32,384]{3,2,1,0:T(8,128)(2,1)S(1)} %collective-permute-done.11.refs_2_, ...), custom_call_target="tpu_custom_call" | custom-call | flops 6600000000 | bytes 1024 | tf_op jit(solution)/shard_map/pallas_call | solution.py:454
  50.0 4.0 %collective-permute-start.13 = (bf16[512,128]{1,0:T(8,128)(2,1)S(1)}, bf16[512,128]{1,0:T(8,128)(2,1)S(1)}, u32[]{:S(2)}, u32[]{:S(2)}) collective-permute-start(bf16[512,128]{1,0:T(8,128)(2,1)S(1)} %get-tuple-element.52), channel_id=1, source_target_pairs={{0,4},{1,5},{2,6},{3,7},{4,8},{5,9},{6,10},{7,11},{8,12},{9,13},{1... | collective-permute-start | bytes 393224 | tf_op jit(solution)/shard_map/ppermute | solution.py:498
  54.0 2.1 %collective-permute-start.15 = (bf16[512,128]{1,0:T(8,128)(2,1)S(1)}, bf16[512,128]{1,0:T(8,128)(2,1)S(1)}, u32[]{:S(2)}, u32[]{:S(2)}) collective-permute-start(bf16[512,128]{1,0:T(8,128)(2,1)S(1)} %get-tuple-element.53), channel_id=1, source_target_pairs={{0,12},{1,13},{2,14},{3,15},{4,0},{5,1},{6,2},{7,3},{8,4},{9,5},{1... | collective-permute-start | bytes 393224 | tf_op jit(solution)/shard_map/ppermute | solution.py:498
  57.1 3.3 %shard_map.148 = (bf16[2,4,32,192]{3,2,1,0:T(8,128)(2,1)}, bf16[2,4,32,192]{3,2,1,0:T(8,128)(2,1)}, f32[8,192]{1,0:T(8,128)S(1)}) custom-call(bf16[4,32,384]{2,1,0:T(8,128)(2,1)S(1)} %get-tuple-element.33.keep_ref, bf16[4,32,384]{2,1,0:T(8,128)(2,1)S(1)} %get-tuple-element.34.give_ref, bf16[1,4,32,384]{3,2,1,0:T(8,128)(2,1)S(1)} %bitcast.19, ...), custom_call_target="tpu_custom_call" | custom-call | flops 6600000000 | bytes 1024 | tf_op jit(solution)/shard_map/pallas_call | solution.py:454
  61.6 6.2 %collective-permute-done.14 = bf16[512,128]{1,0:T(8,128)(2,1)S(1)} collective-permute-done((bf16[512,128]{1,0:T(8,128)(2,1)S(1)}, bf16[512,128]{1,0:T(8,128)(2,1)S(1)}, u32[]{:S(2)}, u32[]{:S(2)}) %collective-permute-start.14) | collective-permute-done | bytes 131104 | tf_op jit(solution)/shard_map/ppermute | solution.py:498
  67.9 1.7 %collective-permute-start.28 = (bf16[224,128]{1,0:T(8,128)(2,1)S(1)}, bf16[224,128]{1,0:T(8,128)(2,1)S(1)}, u32[]{:S(2)}, u32[]{:S(2)}) collective-permute-start(bf16[224,128]{1,0:T(8,128)(2,1)S(1)} %split.9.refs_0_), channel_id=1, source_target_pairs={{0,12},{1,13},{2,14},{3,15},{4,0},{5,1},{6,2},{7,3},{8,4},{9,5},{1... | collective-permute-start | bytes 172040 | tf_op jit(solution)/shard_map/ppermute | solution.py:498
  70.2 3.2 %collective-permute-start.18 = (bf16[304,128]{1,0:T(8,128)(2,1)S(1)}, bf16[304,128]{1,0:T(8,128)(2,1)S(1)}, u32[]{:S(2)}, u32[]{:S(2)}) collective-permute-start(bf16[304,128]{1,0:T(8,128)(2,1)S(1)} %pad_maximum_fusion.refs_0_), channel_id=1, source_target_pairs={{0,12},{1,13},{2,14},{3,15},{4,0},{5,1},{6,2},{7,3},{8,4},{9,5},{1... | collective-permute-start | bytes 233480 | tf_op jit(solution)/shard_map/ppermute | solution.py:498
  74.9 2.0 %collective-permute-done.27.refs_2_ = bf16[224,128]{1,0:T(8,128)(2,1)S(1)} collective-permute-done((bf16[224,128]{1,0:T(8,128)(2,1)S(1)}, bf16[224,128]{1,0:T(8,128)(2,1)S(1)}, u32[]{:S(2)}, u32[]{:S(2)}) %collective-permute-start.27) | collective-permute-done | bytes 57376 | tf_op jit(solution)/shard_map/ppermute | solution.py:498
  79.5 3.1 %collective-permute-done.17.refs_2_ = bf16[304,128]{1,0:T(8,128)(2,1)S(1)} collective-permute-done((bf16[304,128]{1,0:T(8,128)(2,1)S(1)}, bf16[304,128]{1,0:T(8,128)(2,1)S(1)}, u32[]{:S(2)}, u32[]{:S(2)}) %collective-permute-start.17) | collective-permute-done | bytes 77856 | tf_op jit(solution)/shard_map/ppermute | solution.py:498
  82.7 2.0 %collective-permute-start.21 = (bf16[1168,128]{1,0:T(8,128)(2,1)S(1)}, bf16[1168,128]{1,0:T(8,128)(2,1)S(1)}, u32[]{:S(2)}, u32[]{:S(2)}) collective-permute-start(bf16[1168,128]{1,0:T(8,128)(2,1)S(1)} %shard_map.151.refs_0_), channel_id=1, source_target_pairs={{0,3},{1,2},{2,1},{3,0},{4,7},{5,6},{6,5},{7,4},{8,11},{9,10},{10,... | collective-permute-start | bytes 897032 | tf_op jit(solution)/shard_map/ppermute | solution.py:494
  84.7 1.6 %collective-permute-start.20 = (bf16[1168,128]{1,0:T(8,128)(2,1)S(1)}, bf16[1168,128]{1,0:T(8,128)(2,1)S(1)}, u32[]{:S(2)}, u32[]{:S(2)}) collective-permute-start(bf16[1168,128]{1,0:T(8,128)(2,1)S(1)} %shard_map.151.refs_0_), channel_id=1, source_target_pairs={{0,2},{1,3},{2,0},{3,1},{4,6},{5,7},{6,4},{7,5},{8,10},{9,11},{10,... | collective-permute-start | bytes 897032 | tf_op jit(solution)/shard_map/ppermute | solution.py:494
  87.4 4.1 %collective-permute-done.30.refs_2_ = bf16[896,128]{1,0:T(8,128)(2,1)S(1)} collective-permute-done((bf16[896,128]{1,0:T(8,128)(2,1)S(1)}, bf16[896,128]{1,0:T(8,128)(2,1)S(1)}, u32[]{:S(2)}, u32[]{:S(2)}) %collective-permute-start.30) | collective-permute-done | bytes 229408 | tf_op jit(solution)/shard_map/ppermute | solution.py:494
  92.0 5.9 %collective-permute-done.21.refs_3_ = bf16[1168,128]{1,0:T(8,128)(2,1)S(1)} collective-permute-done((bf16[1168,128]{1,0:T(8,128)(2,1)S(1)}, bf16[1168,128]{1,0:T(8,128)(2,1)S(1)}, u32[]{:S(2)}, u32[]{:S(2)}) %collective-permute-start.21) | collective-permute-done | bytes 299040 | tf_op jit(solution)/shard_map/ppermute | solution.py:494
  97.9 5.6 %collective-permute-done.20.refs_2_ = bf16[1168,128]{1,0:T(8,128)(2,1)S(1)} collective-permute-done((bf16[1168,128]{1,0:T(8,128)(2,1)S(1)}, bf16[1168,128]{1,0:T(8,128)(2,1)S(1)}, u32[]{:S(2)}, u32[]{:S(2)}) %collective-permute-start.20) | collective-permute-done | bytes 299040 | tf_op jit(solution)/shard_map/ppermute | solution.py:494
  104.5 1.7 %shard_map.153 = (bf16[27,192,192]{2,1,0:T(8,128)(2,1)}, bf16[27,192,192]{2,1,0:T(8,128)(2,1)}) custom-call(bf16[896,128]{1,0:T(8,128)(2,1)S(1)} %shard_map.152.refs_0_, bf16[896,128]{1,0:T(8,128)(2,1)S(1)} %collective-permute-done.29.refs_1_, bf16[896,128]{1,0:T(8,128)(2,1)S(1)} %collective-permute-done.30.refs_2_, ...), custom_call_target="tpu_custom_call" | custom-call | flops 2200000000 | bytes 1024 | tf_op jit(solution)/shard_map/pallas_call | solution.py:454
  106.3 1.9 %shard_map.154 = (bf16[27,192,192]{2,1,0:T(8,128)(2,1)}, bf16[27,192,192]{2,1,0:T(8,128)(2,1)}, bf16[4,192]{1,0:T(4,128)(2,1)S(1)}) custom-call(bf16[1168,128]{1,0:T(8,128)(2,1)S(1)} %shard_map.151.refs_0_, bf16[1168,128]{1,0:T(8,128)(2,1)S(1)} %collective-permute-done.19.refs_1_, ...), custom_call_target="tpu_custom_call", output_to_operand_aliasing={{0}: (8, {}), {1}: (9, {})} | custom-call | flops 2200000000 | bytes 1024 | tf_op jit(solution)/shard_map/pallas_call | solution.py:454
  (104 shorter events, 22.8 us)
Async XLA Ops:
  3.5 16.8 %collective-permute-start.3 = (bf16[2,4,32,384]{3,2,1,0:T(8,128)(2,1)S(1)}, bf16[2,4,32,384]{3,2,1,0:T(8,128)(2,1)S(1)}, u32[]{:S(2)}, u32[]{:S(2)}) collective-permute-start(bf16[2,4,32,384]{3,2,1,0:T(8,128)(2,1)S(1)} %get-tuple-element.27.refs_0_), channel_id=1, source_target_pairs={{0,3},{1,2},{2,1},{3,0},{4,7},{5,6},{6,5},{7,4},{8,11},{9,10},{10,... | collective-permute-start | bytes 589832 | tf_op jit(solution)/shard_map/ppermute | solution.py:494
  7.4 12.9 %collective-permute-start.2 = (bf16[2,4,32,384]{3,2,1,0:T(8,128)(2,1)S(1)}, bf16[2,4,32,384]{3,2,1,0:T(8,128)(2,1)S(1)}, u32[]{:S(2)}, u32[]{:S(2)}) collective-permute-start(bf16[2,4,32,384]{3,2,1,0:T(8,128)(2,1)S(1)} %get-tuple-element.27.refs_0_), channel_id=1, source_target_pairs={{0,2},{1,3},{2,0},{3,1},{4,6},{5,7},{6,4},{7,5},{8,10},{9,11},{10,... | collective-permute-start | bytes 589832 | tf_op jit(solution)/shard_map/ppermute | solution.py:494
  7.9 12.4 %collective-permute-start.1 = (bf16[2,4,32,384]{3,2,1,0:T(8,128)(2,1)S(1)}, bf16[2,4,32,384]{3,2,1,0:T(8,128)(2,1)S(1)}, u32[]{:S(2)}, u32[]{:S(2)}) collective-permute-start(bf16[2,4,32,384]{3,2,1,0:T(8,128)(2,1)S(1)} %get-tuple-element.27.refs_0_), channel_id=1, source_target_pairs={{0,1},{1,0},{2,3},{3,2},{4,5},{5,4},{6,7},{7,6},{8,9},{9,8},{10,11... | collective-permute-start | bytes 589832 | tf_op jit(solution)/shard_map/ppermute | solution.py:494
  8.0 11.3 %collective-permute-start.4 = (bf16[3,32,384]{2,1,0:T(8,128)(2,1)S(1)}, bf16[3,32,384]{2,1,0:T(8,128)(2,1)S(1)}, u32[]{:S(2)}, u32[]{:S(2)}) collective-permute-start(bf16[3,32,384]{2,1,0:T(8,128)(2,1)S(1)} %get-tuple-element.28), channel_id=1, source_target_pairs={{0,1},{1,2},{2,3},{3,4},{4,5},{5,6},{6,7},{7,8},{8,9},{9,10},{10,1... | collective-permute-start | bytes 221192 | tf_op jit(solution)/shard_map/ppermute | solution.py:468
  11.8 8.4 %collective-permute-start.5 = (bf16[3,32,384]{2,1,0:T(8,128)(2,1)S(1)}, bf16[3,32,384]{2,1,0:T(8,128)(2,1)S(1)}, u32[]{:S(2)}, u32[]{:S(2)}) collective-permute-start(bf16[3,32,384]{2,1,0:T(8,128)(2,1)S(1)} %get-tuple-element.29), channel_id=1, source_target_pairs={{1,0},{2,1},{3,2},{4,3},{5,4},{6,5},{7,6},{8,7},{9,8},{10,9},{11,1... | collective-permute-start | bytes 221192 | tf_op jit(solution)/shard_map/ppermute | solution.py:468
  25.4 19.1 %collective-permute-start.12 = (bf16[2,5,32,384]{3,2,1,0:T(8,128)(2,1)S(1)}, bf16[2,5,32,384]{3,2,1,0:T(8,128)(2,1)S(1)}, u32[]{:S(2)}, u32[]{:S(2)}) collective-permute-start(bf16[2,5,32,384]{3,2,1,0:T(8,128)(2,1)S(1)} %shard_map.146.refs_5_.refs_0_), channel_id=1, source_target_pairs={{0,3},{1,2},{2,1},{3,0},{4,7},{5,6},{6,5},{7,4},{8,11},{9,10},{10,... | collective-permute-start | bytes 737288 | tf_op jit(solution)/shard_map/ppermute | solution.py:494
  27.6 16.9 %collective-permute-start.11 = (bf16[2,5,32,384]{3,2,1,0:T(8,128)(2,1)S(1)}, bf16[2,5,32,384]{3,2,1,0:T(8,128)(2,1)S(1)}, u32[]{:S(2)}, u32[]{:S(2)}) collective-permute-start(bf16[2,5,32,384]{3,2,1,0:T(8,128)(2,1)S(1)} %shard_map.146.refs_5_.refs_0_), channel_id=1, source_target_pairs={{0,2},{1,3},{2,0},{3,1},{4,6},{5,7},{6,4},{7,5},{8,10},{9,11},{10,... | collective-permute-start | bytes 737288 | tf_op jit(solution)/shard_map/ppermute | solution.py:494
  28.4 10.5 %collective-permute-start.8 = (bf16[2,5,32,384]{3,2,1,0:T(8,128)(2,1)S(1)}, bf16[2,5,32,384]{3,2,1,0:T(8,128)(2,1)S(1)}, u32[]{:S(2)}, u32[]{:S(2)}) collective-permute-start(bf16[2,5,32,384]{3,2,1,0:T(8,128)(2,1)S(1)} %shard_map.146.refs_5_.refs_0_), channel_id=1, source_target_pairs={{0,1},{1,0},{2,3},{3,2},{4,5},{5,4},{6,7},{7,6},{8,9},{9,8},{10,11... | collective-permute-start | bytes 737288 | tf_op jit(solution)/shard_map/ppermute | solution.py:494
  38.9 18.2 %collective-permute-start.9 = (bf16[3,32,384]{2,1,0:T(8,128)(2,1)S(1)}, bf16[3,32,384]{2,1,0:T(8,128)(2,1)S(1)}, u32[]{:S(2)}, u32[]{:S(2)}) collective-permute-start(bf16[3,32,384]{2,1,0:T(8,128)(2,1)S(1)} %get-tuple-element.35), channel_id=1, source_target_pairs={{0,1},{1,2},{2,3},{3,4},{4,5},{5,6},{6,7},{7,8},{8,9},{9,10},{10,1... | collective-permute-start | bytes 221192 | tf_op jit(solution)/shard_map/ppermute | solution.py:468
  42.9 14.2 %collective-permute-start.10 = (bf16[3,32,384]{2,1,0:T(8,128)(2,1)S(1)}, bf16[3,32,384]{2,1,0:T(8,128)(2,1)S(1)}, u32[]{:S(2)}, u32[]{:S(2)}) collective-permute-start(bf16[3,32,384]{2,1,0:T(8,128)(2,1)S(1)} %get-tuple-element.36), channel_id=1, source_target_pairs={{1,0},{2,1},{3,2},{4,3},{5,4},{6,5},{7,6},{8,7},{9,8},{10,9},{11,1... | collective-permute-start | bytes 221192 | tf_op jit(solution)/shard_map/ppermute | solution.py:468
  50.0 10.4 %collective-permute-start.13 = (bf16[512,128]{1,0:T(8,128)(2,1)S(1)}, bf16[512,128]{1,0:T(8,128)(2,1)S(1)}, u32[]{:S(2)}, u32[]{:S(2)}) collective-permute-start(bf16[512,128]{1,0:T(8,128)(2,1)S(1)} %get-tuple-element.52), channel_id=1, source_target_pairs={{0,4},{1,5},{2,6},{3,7},{4,8},{5,9},{6,10},{7,11},{8,12},{9,13},{1... | collective-permute-start | bytes 393224 | tf_op jit(solution)/shard_map/ppermute | solution.py:498
  56.1 11.6 %collective-permute-start.14 = (bf16[512,128]{1,0:T(8,128)(2,1)S(1)}, bf16[512,128]{1,0:T(8,128)(2,1)S(1)}, u32[]{:S(2)}, u32[]{:S(2)}) collective-permute-start(bf16[512,128]{1,0:T(8,128)(2,1)S(1)} %get-tuple-element.54), channel_id=1, source_target_pairs={{0,8},{1,9},{2,10},{3,11},{4,12},{5,13},{6,14},{7,15},{8,0},{9,1},... | collective-permute-start | bytes 393224 | tf_op jit(solution)/shard_map/ppermute | solution.py:498
  70.2 7.9 %collective-permute-start.18 = (bf16[304,128]{1,0:T(8,128)(2,1)S(1)}, bf16[304,128]{1,0:T(8,128)(2,1)S(1)}, u32[]{:S(2)}, u32[]{:S(2)}) collective-permute-start(bf16[304,128]{1,0:T(8,128)(2,1)S(1)} %pad_maximum_fusion.refs_0_), channel_id=1, source_target_pairs={{0,12},{1,13},{2,14},{3,15},{4,0},{5,1},{6,2},{7,3},{8,4},{9,5},{1... | collective-permute-start | bytes 233480 | tf_op jit(solution)/shard_map/ppermute | solution.py:498
  73.4 9.3 %collective-permute-start.17 = (bf16[304,128]{1,0:T(8,128)(2,1)S(1)}, bf16[304,128]{1,0:T(8,128)(2,1)S(1)}, u32[]{:S(2)}, u32[]{:S(2)}) collective-permute-start(bf16[304,128]{1,0:T(8,128)(2,1)S(1)} %pad_maximum_fusion.refs_0_), channel_id=1, source_target_pairs={{0,8},{1,9},{2,10},{3,11},{4,12},{5,13},{6,14},{7,15},{8,0},{9,1},... | collective-permute-start | bytes 233480 | tf_op jit(solution)/shard_map/ppermute | solution.py:498
  74.5 8.1 %collective-permute-start.16 = (bf16[304,128]{1,0:T(8,128)(2,1)S(1)}, bf16[304,128]{1,0:T(8,128)(2,1)S(1)}, u32[]{:S(2)}, u32[]{:S(2)}) collective-permute-start(bf16[304,128]{1,0:T(8,128)(2,1)S(1)} %pad_maximum_fusion.refs_0_), channel_id=1, source_target_pairs={{0,4},{1,5},{2,6},{3,7},{4,8},{5,9},{6,10},{7,11},{8,12},{9,13},{1... | collective-permute-start | bytes 233480 | tf_op jit(solution)/shard_map/ppermute | solution.py:498
  77.0 7.7 %collective-permute-start.32 = (bf16[896,128]{1,0:T(8,128)(2,1)S(1)}, bf16[896,128]{1,0:T(8,128)(2,1)S(1)}, u32[]{:S(2)}, u32[]{:S(2)}) collective-permute-start(bf16[896,128]{1,0:T(8,128)(2,1)S(1)} %shard_map.152.refs_0_), channel_id=1, source_target_pairs={{0,16},{16,0},{1,17},{17,1},{2,18},{18,2},{3,19},{19,3},{4,20},{20... | collective-permute-start | bytes 688136 | tf_op jit(solution)/shard_map/ppermute | solution.py:618
  77.1 9.4 %collective-permute-start.31 = (bf16[896,128]{1,0:T(8,128)(2,1)S(1)}, bf16[896,128]{1,0:T(8,128)(2,1)S(1)}, u32[]{:S(2)}, u32[]{:S(2)}) collective-permute-start(bf16[896,128]{1,0:T(8,128)(2,1)S(1)} %shard_map.152.refs_0_), channel_id=1, source_target_pairs={{0,3},{1,2},{2,1},{3,0},{4,7},{5,6},{6,5},{7,4},{8,11},{9,10},{10,... | collective-permute-start | bytes 688136 | tf_op jit(solution)/shard_map/ppermute | solution.py:494
  78.1 13.4 %collective-permute-start.30 = (bf16[896,128]{1,0:T(8,128)(2,1)S(1)}, bf16[896,128]{1,0:T(8,128)(2,1)S(1)}, u32[]{:S(2)}, u32[]{:S(2)}) collective-permute-start(bf16[896,128]{1,0:T(8,128)(2,1)S(1)} %shard_map.152.refs_0_), channel_id=1, source_target_pairs={{0,2},{1,3},{2,0},{3,1},{4,6},{5,7},{6,4},{7,5},{8,10},{9,11},{10,... | collective-permute-start | bytes 688136 | tf_op jit(solution)/shard_map/ppermute | solution.py:494
  82.6 8.8 %collective-permute-start.29 = (bf16[896,128]{1,0:T(8,128)(2,1)S(1)}, bf16[896,128]{1,0:T(8,128)(2,1)S(1)}, u32[]{:S(2)}, u32[]{:S(2)}) collective-permute-start(bf16[896,128]{1,0:T(8,128)(2,1)S(1)} %shard_map.152.refs_0_), channel_id=1, source_target_pairs={{0,1},{1,0},{2,3},{3,2},{4,5},{5,4},{6,7},{7,6},{8,9},{9,8},{10,11... | collective-permute-start | bytes 688136 | tf_op jit(solution)/shard_map/ppermute | solution.py:494
  82.7 15.2 %collective-permute-start.21 = (bf16[1168,128]{1,0:T(8,128)(2,1)S(1)}, bf16[1168,128]{1,0:T(8,128)(2,1)S(1)}, u32[]{:S(2)}, u32[]{:S(2)}) collective-permute-start(bf16[1168,128]{1,0:T(8,128)(2,1)S(1)} %shard_map.151.refs_0_), channel_id=1, source_target_pairs={{0,3},{1,2},{2,1},{3,0},{4,7},{5,6},{6,5},{7,4},{8,11},{9,10},{10,... | collective-permute-start | bytes 897032 | tf_op jit(solution)/shard_map/ppermute | solution.py:494
  84.7 18.8 %collective-permute-start.20 = (bf16[1168,128]{1,0:T(8,128)(2,1)S(1)}, bf16[1168,128]{1,0:T(8,128)(2,1)S(1)}, u32[]{:S(2)}, u32[]{:S(2)}) collective-permute-start(bf16[1168,128]{1,0:T(8,128)(2,1)S(1)} %shard_map.151.refs_0_), channel_id=1, source_target_pairs={{0,2},{1,3},{2,0},{3,1},{4,6},{5,7},{6,4},{7,5},{8,10},{9,11},{10,... | collective-permute-start | bytes 897032 | tf_op jit(solution)/shard_map/ppermute | solution.py:494
  86.5 17.0 %collective-permute-start.19 = (bf16[1168,128]{1,0:T(8,128)(2,1)S(1)}, bf16[1168,128]{1,0:T(8,128)(2,1)S(1)}, u32[]{:S(2)}, u32[]{:S(2)}) collective-permute-start(bf16[1168,128]{1,0:T(8,128)(2,1)S(1)} %shard_map.151.refs_0_), channel_id=1, source_target_pairs={{0,1},{1,0},{2,3},{3,2},{4,5},{5,4},{6,7},{7,6},{8,9},{9,8},{10,11... | collective-permute-start | bytes 897032 | tf_op jit(solution)/shard_map/ppermute | solution.py:494
  91.5 12.5 %collective-permute-start.35 = (bf16[896,128]{1,0:T(8,128)(2,1)S(1)}, bf16[896,128]{1,0:T(8,128)(2,1)S(1)}, u32[]{:S(2)}, u32[]{:S(2)}) collective-permute-start(bf16[896,128]{1,0:T(8,128)(2,1)S(1)} %collective-permute-done.31.refs_3_), channel_id=1, source_target_pairs={{0,16},{16,0},{1,17},{17,1},{2,18},{18,2},{3,19},{19,3},{4,20},{20... | collective-permute-start | bytes 688136 | tf_op jit(solution)/shard_map/ppermute | solution.py:618
  91.5 12.6 %collective-permute-start.34 = (bf16[896,128]{1,0:T(8,128)(2,1)S(1)}, bf16[896,128]{1,0:T(8,128)(2,1)S(1)}, u32[]{:S(2)}, u32[]{:S(2)}) collective-permute-start(bf16[896,128]{1,0:T(8,128)(2,1)S(1)} %collective-permute-done.30.refs_2_), channel_id=1, source_target_pairs={{0,16},{16,0},{1,17},{17,1},{2,18},{18,2},{3,19},{19,3},{4,20},{20... | collective-permute-start | bytes 688136 | tf_op jit(solution)/shard_map/ppermute | solution.py:618
  (28 other events, 183.9 us)

commit v9 on v8

--- a/solution.py
+++ b/solution.py
@@ -552,7 +552,7 @@
         functools.partial(plane_kernel, blocks),
         (jax.ShapeDtypeStruct((2 * frames + 2, 4 * rows + 2, cols, chans), bf16),),
         (*ys, vec, x_own),
-        3,
+        0.1,
         8,
         free=(5,),
     )

time: 109 us -> 104 us (0.954)
  starting transfers between devices: 42.3 us -> 39.3 us
  waiting for transfers between devices: 43.9 us -> 42.8 us
    ppermute x12, starting transfers between devices: 15 us -> 13.5 us  [plane_move(): return lax.ppermute(value, 'height', [(i, i ^ d) for i in range(height)])]
    ppermute x12, waiting for transfers between devices: 24.7 us -> 23.5 us  [plane_move(): return lax.ppermute(value, 'height', [(i, i ^ d) for i in range(height)])]
    unnamed x32 -> x20, local copies, waits for them, and re-layouts: 2.7 us -> 1.79 us
  transfers between devices with their start and end apart: 36 -> 36, of which waited for: 14 -> 16; matrix products, arithmetic and copies ran while one was open for 0% -> 0% of each run, Pallas kernels for 11% -> 12%
where the time goes in v9:
time: 104 us
  waiting for transfers between devices  42.8 us (41%)
  starting transfers between devices  39.3 us (38%)
  Pallas kernels  16.9 us (16%)
  local copies, waits for them, and re-layouts  2.39 us (2%)
  other arithmetic  1.24 us (1%)
    ppermute x12, waiting for transfers between devices, plane_move(): return lax.ppermute(value, 'height', [(i, i ^ d) for i in range(height)])  23.5 us
    pallas_call x12, Pallas kernels, call(): pl.pallas_call(kernel, out_shape=outs, in_specs=[in_hbm if i in hbm else...  16.9 us
    ppermute x12, starting transfers between devices, plane_move(): return lax.ppermute(value, 'height', [(i, i ^ d) for i in range(height)])  13.5 us
    ppermute x9, starting transfers between devices, column_move(): return lax.ppermute(value, 'height', pairs)  13.5 us
    ppermute x9, waiting for transfers between devices, column_move(): return lax.ppermute(value, 'height', pairs)  11.8 us
    ppermute x4, starting transfers between devices, moved(): lax.ppermute(value, axis, [(i, i + by) for i in range(size) if 0 <= i + b...  10 us
    ppermute x4, waiting for transfers between devices, moved(): lax.ppermute(value, axis, [(i, i + by) for i in range(size) if 0 <= i + b...  4.81 us
  transfers between devices with their start and end apart: 36, of which 16 were waited for; matrix products, arithmetic and copies ran while one was open for 0% of the time, Pallas kernels for 12%

profile of v9, /device:TPU:0, one launch (start us, length us, event | category | flops | bytes accessed | tf_op | source)
XLA Modules:
  0.0 103.7 jit_solution(3221962299858660381)
XLA Ops:
  3.5 3.9 %collective-permute-start.3 = (bf16[2,4,32,384]{3,2,1,0:T(8,128)(2,1)S(1)}, bf16[2,4,32,384]{3,2,1,0:T(8,128)(2,1)S(1)}, u32[]{:S(2)}, u32[]{:S(2)}) collective-permute-start(bf16[2,4,32,384]{3,2,1,0:T(8,128)(2,1)S(1)} %get-tuple-element.27.refs_0_), channel_id=1, source_target_pairs={{0,3},{1,2},{2,1},{3,0},{4,7},{5,6},{6,5},{7,4},{8,11},{9,10},{10,... | collective-permute-start | bytes 589832 | tf_op jit(solution)/shard_map/ppermute | solution.py:494
  8.0 3.8 %collective-permute-start.4 = (bf16[3,32,384]{2,1,0:T(8,128)(2,1)S(1)}, bf16[3,32,384]{2,1,0:T(8,128)(2,1)S(1)}, u32[]{:S(2)}, u32[]{:S(2)}) collective-permute-start(bf16[3,32,384]{2,1,0:T(8,128)(2,1)S(1)} %get-tuple-element.28), channel_id=1, source_target_pairs={{0,1},{1,2},{2,3},{3,4},{4,5},{5,6},{6,7},{7,8},{8,9},{9,10},{10,1... | collective-permute-start | bytes 221192 | tf_op jit(solution)/shard_map/ppermute | solution.py:468
  13.2 1.7 %copy-done.1 = bf16[3,3,3,192,192]{4,3,2,1,0:T(8,128)(2,1)S(1)} copy-done((bf16[3,3,3,192,192]{4,3,2,1,0:T(8,128)(2,1)S(1)}, bf16[3,3,3,192,192]{4,3,2,1,0:T(8,128)(2,1)}, u32[]{:S(2)}) %copy-start.1) | copy-done | bytes 1990680
  15.4 3.9 %collective-permute-done.4.above_ref = bf16[3,32,384]{2,1,0:T(8,128)(2,1)S(1)} collective-permute-done((bf16[3,32,384]{2,1,0:T(8,128)(2,1)S(1)}, bf16[3,32,384]{2,1,0:T(8,128)(2,1)S(1)}, u32[]{:S(2)}, u32[]{:S(2)}) %collective-permute-start.4) | collective-permute-done | bytes 73760 | tf_op jit(solution)/shard_map/ppermute | solution.py:468
  20.3 2.7 %shard_map.145 = (bf16[4,32,384]{2,1,0:T(8,128)(2,1)S(1)}, bf16[4,32,384]{2,1,0:T(8,128)(2,1)S(1)}, f32[8,192]{1,0:T(8,128)S(1)}) custom-call(bf16[2,4,32,384]{3,2,1,0:T(8,128)(2,1)S(1)} %collective-permute-done.1._.refs_1_, bf16[2,4,32,384]{3,2,1,0:T(8,128)(2,1)S(1)} %collective-permute-done.2.__.refs_2_, ...), custom_call_target="tpu_custom_call" | custom-call | flops 5500000256 | bytes 1024 | tf_op jit(solution)/shard_map/pallas_call | solution.py:454
  24.4 1.6 %collective-permute-start.8 = (bf16[2,5,32,384]{3,2,1,0:T(8,128)(2,1)S(1)}, bf16[2,5,32,384]{3,2,1,0:T(8,128)(2,1)S(1)}, u32[]{:S(2)}, u32[]{:S(2)}) collective-permute-start(bf16[2,5,32,384]{3,2,1,0:T(8,128)(2,1)S(1)} %shard_map.146.refs_5_.refs_0_), channel_id=1, source_target_pairs={{0,1},{1,0},{2,3},{3,2},{4,5},{5,4},{6,7},{7,6},{8,9},{9,8},{10,11... | collective-permute-start | bytes 737288 | tf_op jit(solution)/shard_map/ppermute | solution.py:494
  29.3 4.0 %collective-permute-done.8._.refs_1_ = bf16[2,5,32,384]{3,2,1,0:T(8,128)(2,1)S(1)} collective-permute-done((bf16[2,5,32,384]{3,2,1,0:T(8,128)(2,1)S(1)}, bf16[2,5,32,384]{3,2,1,0:T(8,128)(2,1)S(1)}, u32[]{:S(2)}, u32[]{:S(2)}) %collective-permute-start.8) | collective-permute-done | bytes 245792 | tf_op jit(solution)/shard_map/ppermute | solution.py:494
  33.3 3.4 %collective-permute-start.9 = (bf16[3,32,384]{2,1,0:T(8,128)(2,1)S(1)}, bf16[3,32,384]{2,1,0:T(8,128)(2,1)S(1)}, u32[]{:S(2)}, u32[]{:S(2)}) collective-permute-start(bf16[3,32,384]{2,1,0:T(8,128)(2,1)S(1)} %get-tuple-element.35), channel_id=1, source_target_pairs={{0,1},{1,2},{2,3},{3,4},{4,5},{5,6},{6,7},{7,8},{8,9},{9,10},{10,1... | collective-permute-start | bytes 221192 | tf_op jit(solution)/shard_map/ppermute | solution.py:468
  39.8 5.5 %shard_map.150 = bf16[4,512,128]{2,1,0:T(8,128)(2,1)S(1)} custom-call(bf16[2,5,32,384]{3,2,1,0:T(8,128)(2,1)S(1)} %shard_map.146.refs_5_.refs_0_, bf16[2,5,32,384]{3,2,1,0:T(8,128)(2,1)S(1)} %collective-permute-done.8._.refs_1_, bf16[2,5,32,384]{3,2,1,0:T(8,128)(2,1)S(1)} %collective-permute-done.11.refs_2_, ...), custom_call_target="tpu_custom_call" | custom-call | flops 6600000000 | bytes 1024 | tf_op jit(solution)/shard_map/pallas_call | solution.py:454
  45.3 3.1 %collective-permute-start.13 = (bf16[512,128]{1,0:T(8,128)(2,1)S(1)}, bf16[512,128]{1,0:T(8,128)(2,1)S(1)}, u32[]{:S(2)}, u32[]{:S(2)}) collective-permute-start(bf16[512,128]{1,0:T(8,128)(2,1)S(1)} %get-tuple-element.52), channel_id=1, source_target_pairs={{0,4},{1,5},{2,6},{3,7},{4,8},{5,9},{6,10},{7,11},{8,12},{9,13},{1... | collective-permute-start | bytes 393224 | tf_op jit(solution)/shard_map/ppermute | solution.py:498
  48.4 2.1 %collective-permute-start.15 = (bf16[512,128]{1,0:T(8,128)(2,1)S(1)}, bf16[512,128]{1,0:T(8,128)(2,1)S(1)}, u32[]{:S(2)}, u32[]{:S(2)}) collective-permute-start(bf16[512,128]{1,0:T(8,128)(2,1)S(1)} %get-tuple-element.53), channel_id=1, source_target_pairs={{0,12},{1,13},{2,14},{3,15},{4,0},{5,1},{6,2},{7,3},{8,4},{9,5},{1... | collective-permute-start | bytes 393224 | tf_op jit(solution)/shard_map/ppermute | solution.py:498
  51.5 3.3 %shard_map.148 = (bf16[2,4,32,192]{3,2,1,0:T(8,128)(2,1)}, bf16[2,4,32,192]{3,2,1,0:T(8,128)(2,1)}, f32[8,192]{1,0:T(8,128)S(1)}) custom-call(bf16[4,32,384]{2,1,0:T(8,128)(2,1)S(1)} %get-tuple-element.33.keep_ref, bf16[4,32,384]{2,1,0:T(8,128)(2,1)S(1)} %get-tuple-element.34.give_ref, bf16[1,4,32,384]{3,2,1,0:T(8,128)(2,1)S(1)} %bitcast.19, ...), custom_call_target="tpu_custom_call" | custom-call | flops 6600000000 | bytes 1024 | tf_op jit(solution)/shard_map/pallas_call | solution.py:454
  55.4 5.9 %collective-permute-done.14 = bf16[512,128]{1,0:T(8,128)(2,1)S(1)} collective-permute-done((bf16[512,128]{1,0:T(8,128)(2,1)S(1)}, bf16[512,128]{1,0:T(8,128)(2,1)S(1)}, u32[]{:S(2)}, u32[]{:S(2)}) %collective-permute-start.14) | collective-permute-done | bytes 131104 | tf_op jit(solution)/shard_map/ppermute | solution.py:498
  61.5 2.3 %collective-permute-start.28 = (bf16[224,128]{1,0:T(8,128)(2,1)S(1)}, bf16[224,128]{1,0:T(8,128)(2,1)S(1)}, u32[]{:S(2)}, u32[]{:S(2)}) collective-permute-start(bf16[224,128]{1,0:T(8,128)(2,1)S(1)} %split.9.refs_0_), channel_id=1, source_target_pairs={{0,12},{1,13},{2,14},{3,15},{4,0},{5,1},{6,2},{7,3},{8,4},{9,5},{1... | collective-permute-start | bytes 172040 | tf_op jit(solution)/shard_map/ppermute | solution.py:498
  64.4 3.2 %collective-permute-start.18 = (bf16[304,128]{1,0:T(8,128)(2,1)S(1)}, bf16[304,128]{1,0:T(8,128)(2,1)S(1)}, u32[]{:S(2)}, u32[]{:S(2)}) collective-permute-start(bf16[304,128]{1,0:T(8,128)(2,1)S(1)} %pad_maximum_fusion.refs_0_), channel_id=1, source_target_pairs={{0,12},{1,13},{2,14},{3,15},{4,0},{5,1},{6,2},{7,3},{8,4},{9,5},{1... | collective-permute-start | bytes 233480 | tf_op jit(solution)/shard_map/ppermute | solution.py:498
  68.8 2.7 %collective-permute-done.27.refs_2_ = bf16[224,128]{1,0:T(8,128)(2,1)S(1)} collective-permute-done((bf16[224,128]{1,0:T(8,128)(2,1)S(1)}, bf16[224,128]{1,0:T(8,128)(2,1)S(1)}, u32[]{:S(2)}, u32[]{:S(2)}) %collective-permute-start.27) | collective-permute-done | bytes 57376 | tf_op jit(solution)/shard_map/ppermute | solution.py:498
  71.6 1.8 %collective-permute-start.31 = (bf16[896,128]{1,0:T(8,128)(2,1)S(1)}, bf16[896,128]{1,0:T(8,128)(2,1)S(1)}, u32[]{:S(2)}, u32[]{:S(2)}) collective-permute-start(bf16[896,128]{1,0:T(8,128)(2,1)S(1)} %shard_map.152.refs_0_), channel_id=1, source_target_pairs={{0,3},{1,2},{2,1},{3,0},{4,7},{5,6},{6,5},{7,4},{8,11},{9,10},{10,... | collective-permute-start | bytes 688136 | tf_op jit(solution)/shard_map/ppermute | solution.py:494
  73.4 2.5 %collective-permute-done.17.refs_2_ = bf16[304,128]{1,0:T(8,128)(2,1)S(1)} collective-permute-done((bf16[304,128]{1,0:T(8,128)(2,1)S(1)}, bf16[304,128]{1,0:T(8,128)(2,1)S(1)}, u32[]{:S(2)}, u32[]{:S(2)}) %collective-permute-start.17) | collective-permute-done | bytes 77856 | tf_op jit(solution)/shard_map/ppermute | solution.py:498
  77.2 2.4 %collective-permute-start.20 = (bf16[1168,128]{1,0:T(8,128)(2,1)S(1)}, bf16[1168,128]{1,0:T(8,128)(2,1)S(1)}, u32[]{:S(2)}, u32[]{:S(2)}) collective-permute-start(bf16[1168,128]{1,0:T(8,128)(2,1)S(1)} %shard_map.151.refs_0_), channel_id=1, source_target_pairs={{0,2},{1,3},{2,0},{3,1},{4,6},{5,7},{6,4},{7,5},{8,10},{9,11},{10,... | collective-permute-start | bytes 897032 | tf_op jit(solution)/shard_map/ppermute | solution.py:494
  81.2 4.8 %collective-permute-done.30.refs_2_ = bf16[896,128]{1,0:T(8,128)(2,1)S(1)} collective-permute-done((bf16[896,128]{1,0:T(8,128)(2,1)S(1)}, bf16[896,128]{1,0:T(8,128)(2,1)S(1)}, u32[]{:S(2)}, u32[]{:S(2)}) %collective-permute-start.30) | collective-permute-done | bytes 229408 | tf_op jit(solution)/shard_map/ppermute | solution.py:494
  86.5 5.9 %collective-permute-done.21.refs_3_ = bf16[1168,128]{1,0:T(8,128)(2,1)S(1)} collective-permute-done((bf16[1168,128]{1,0:T(8,128)(2,1)S(1)}, bf16[1168,128]{1,0:T(8,128)(2,1)S(1)}, u32[]{:S(2)}, u32[]{:S(2)}) %collective-permute-start.21) | collective-permute-done | bytes 299040 | tf_op jit(solution)/shard_map/ppermute | solution.py:494
  92.4 5.9 %collective-permute-done.20.refs_2_ = bf16[1168,128]{1,0:T(8,128)(2,1)S(1)} collective-permute-done((bf16[1168,128]{1,0:T(8,128)(2,1)S(1)}, bf16[1168,128]{1,0:T(8,128)(2,1)S(1)}, u32[]{:S(2)}, u32[]{:S(2)}) %collective-permute-start.20) | collective-permute-done | bytes 299040 | tf_op jit(solution)/shard_map/ppermute | solution.py:494
  99.3 1.7 %shard_map.153 = (bf16[27,192,192]{2,1,0:T(8,128)(2,1)}, bf16[27,192,192]{2,1,0:T(8,128)(2,1)}) custom-call(bf16[896,128]{1,0:T(8,128)(2,1)S(1)} %shard_map.152.refs_0_, bf16[896,128]{1,0:T(8,128)(2,1)S(1)} %collective-permute-done.29.refs_1_, bf16[896,128]{1,0:T(8,128)(2,1)S(1)} %collective-permute-done.30.refs_2_, ...), custom_call_target="tpu_custom_call" | custom-call | flops 2200000000 | bytes 1024 | tf_op jit(solution)/shard_map/pallas_call | solution.py:454
  101.2 1.9 %shard_map.154 = (bf16[27,192,192]{2,1,0:T(8,128)(2,1)}, bf16[27,192,192]{2,1,0:T(8,128)(2,1)}, bf16[4,192]{1,0:T(4,128)(2,1)S(1)}) custom-call(bf16[1168,128]{1,0:T(8,128)(2,1)S(1)} %shard_map.151.refs_0_, bf16[1168,128]{1,0:T(8,128)(2,1)S(1)} %collective-permute-done.19.refs_1_, ...), custom_call_target="tpu_custom_call", output_to_operand_aliasing={{0}: (8, {}), {1}: (9, {})} | custom-call | flops 2200000000 | bytes 1024 | tf_op jit(solution)/shard_map/pallas_call | solution.py:454
  (92 shorter events, 22.7 us)
Async XLA Ops:
  3.5 16.8 %collective-permute-start.3 = (bf16[2,4,32,384]{3,2,1,0:T(8,128)(2,1)S(1)}, bf16[2,4,32,384]{3,2,1,0:T(8,128)(2,1)S(1)}, u32[]{:S(2)}, u32[]{:S(2)}) collective-permute-start(bf16[2,4,32,384]{3,2,1,0:T(8,128)(2,1)S(1)} %get-tuple-element.27.refs_0_), channel_id=1, source_target_pairs={{0,3},{1,2},{2,1},{3,0},{4,7},{5,6},{6,5},{7,4},{8,11},{9,10},{10,... | collective-permute-start | bytes 589832 | tf_op jit(solution)/shard_map/ppermute | solution.py:494
  7.4 12.9 %collective-permute-start.2 = (bf16[2,4,32,384]{3,2,1,0:T(8,128)(2,1)S(1)}, bf16[2,4,32,384]{3,2,1,0:T(8,128)(2,1)S(1)}, u32[]{:S(2)}, u32[]{:S(2)}) collective-permute-start(bf16[2,4,32,384]{3,2,1,0:T(8,128)(2,1)S(1)} %get-tuple-element.27.refs_0_), channel_id=1, source_target_pairs={{0,2},{1,3},{2,0},{3,1},{4,6},{5,7},{6,4},{7,5},{8,10},{9,11},{10,... | collective-permute-start | bytes 589832 | tf_op jit(solution)/shard_map/ppermute | solution.py:494
  7.9 12.4 %collective-permute-start.1 = (bf16[2,4,32,384]{3,2,1,0:T(8,128)(2,1)S(1)}, bf16[2,4,32,384]{3,2,1,0:T(8,128)(2,1)S(1)}, u32[]{:S(2)}, u32[]{:S(2)}) collective-permute-start(bf16[2,4,32,384]{3,2,1,0:T(8,128)(2,1)S(1)} %get-tuple-element.27.refs_0_), channel_id=1, source_target_pairs={{0,1},{1,0},{2,3},{3,2},{4,5},{5,4},{6,7},{7,6},{8,9},{9,8},{10,11... | collective-permute-start | bytes 589832 | tf_op jit(solution)/shard_map/ppermute | solution.py:494
  8.0 11.3 %collective-permute-start.4 = (bf16[3,32,384]{2,1,0:T(8,128)(2,1)S(1)}, bf16[3,32,384]{2,1,0:T(8,128)(2,1)S(1)}, u32[]{:S(2)}, u32[]{:S(2)}) collective-permute-start(bf16[3,32,384]{2,1,0:T(8,128)(2,1)S(1)} %get-tuple-element.28), channel_id=1, source_target_pairs={{0,1},{1,2},{2,3},{3,4},{4,5},{5,6},{6,7},{7,8},{8,9},{9,10},{10,1... | collective-permute-start | bytes 221192 | tf_op jit(solution)/shard_map/ppermute | solution.py:468
  11.8 8.4 %collective-permute-start.5 = (bf16[3,32,384]{2,1,0:T(8,128)(2,1)S(1)}, bf16[3,32,384]{2,1,0:T(8,128)(2,1)S(1)}, u32[]{:S(2)}, u32[]{:S(2)}) collective-permute-start(bf16[3,32,384]{2,1,0:T(8,128)(2,1)S(1)} %get-tuple-element.29), channel_id=1, source_target_pairs={{1,0},{2,1},{3,2},{4,3},{5,4},{6,5},{7,6},{8,7},{9,8},{10,9},{11,1... | collective-permute-start | bytes 221192 | tf_op jit(solution)/shard_map/ppermute | solution.py:468
  24.4 8.9 %collective-permute-start.8 = (bf16[2,5,32,384]{3,2,1,0:T(8,128)(2,1)S(1)}, bf16[2,5,32,384]{3,2,1,0:T(8,128)(2,1)S(1)}, u32[]{:S(2)}, u32[]{:S(2)}) collective-permute-start(bf16[2,5,32,384]{3,2,1,0:T(8,128)(2,1)S(1)} %shard_map.146.refs_5_.refs_0_), channel_id=1, source_target_pairs={{0,1},{1,0},{2,3},{3,2},{4,5},{5,4},{6,7},{7,6},{8,9},{9,8},{10,11... | collective-permute-start | bytes 737288 | tf_op jit(solution)/shard_map/ppermute | solution.py:494
  26.0 12.3 %collective-permute-start.12 = (bf16[2,5,32,384]{3,2,1,0:T(8,128)(2,1)S(1)}, bf16[2,5,32,384]{3,2,1,0:T(8,128)(2,1)S(1)}, u32[]{:S(2)}, u32[]{:S(2)}) collective-permute-start(bf16[2,5,32,384]{3,2,1,0:T(8,128)(2,1)S(1)} %shard_map.146.refs_5_.refs_0_), channel_id=1, source_target_pairs={{0,3},{1,2},{2,1},{3,0},{4,7},{5,6},{6,5},{7,4},{8,11},{9,10},{10,... | collective-permute-start | bytes 737288 | tf_op jit(solution)/shard_map/ppermute | solution.py:494
  26.7 13.1 %collective-permute-start.11 = (bf16[2,5,32,384]{3,2,1,0:T(8,128)(2,1)S(1)}, bf16[2,5,32,384]{3,2,1,0:T(8,128)(2,1)S(1)}, u32[]{:S(2)}, u32[]{:S(2)}) collective-permute-start(bf16[2,5,32,384]{3,2,1,0:T(8,128)(2,1)S(1)} %shard_map.146.refs_5_.refs_0_), channel_id=1, source_target_pairs={{0,2},{1,3},{2,0},{3,1},{4,6},{5,7},{6,4},{7,5},{8,10},{9,11},{10,... | collective-permute-start | bytes 737288 | tf_op jit(solution)/shard_map/ppermute | solution.py:494
  33.3 18.2 %collective-permute-start.9 = (bf16[3,32,384]{2,1,0:T(8,128)(2,1)S(1)}, bf16[3,32,384]{2,1,0:T(8,128)(2,1)S(1)}, u32[]{:S(2)}, u32[]{:S(2)}) collective-permute-start(bf16[3,32,384]{2,1,0:T(8,128)(2,1)S(1)} %get-tuple-element.35), channel_id=1, source_target_pairs={{0,1},{1,2},{2,3},{3,4},{4,5},{5,6},{6,7},{7,8},{8,9},{9,10},{10,1... | collective-permute-start | bytes 221192 | tf_op jit(solution)/shard_map/ppermute | solution.py:468
  36.8 14.7 %collective-permute-start.10 = (bf16[3,32,384]{2,1,0:T(8,128)(2,1)S(1)}, bf16[3,32,384]{2,1,0:T(8,128)(2,1)S(1)}, u32[]{:S(2)}, u32[]{:S(2)}) collective-permute-start(bf16[3,32,384]{2,1,0:T(8,128)(2,1)S(1)} %get-tuple-element.36), channel_id=1, source_target_pairs={{1,0},{2,1},{3,2},{4,3},{5,4},{6,5},{7,6},{8,7},{9,8},{10,9},{11,1... | collective-permute-start | bytes 221192 | tf_op jit(solution)/shard_map/ppermute | solution.py:468
  45.3 9.5 %collective-permute-start.13 = (bf16[512,128]{1,0:T(8,128)(2,1)S(1)}, bf16[512,128]{1,0:T(8,128)(2,1)S(1)}, u32[]{:S(2)}, u32[]{:S(2)}) collective-permute-start(bf16[512,128]{1,0:T(8,128)(2,1)S(1)} %get-tuple-element.52), channel_id=1, source_target_pairs={{0,4},{1,5},{2,6},{3,7},{4,8},{5,9},{6,10},{7,11},{8,12},{9,13},{1... | collective-permute-start | bytes 393224 | tf_op jit(solution)/shard_map/ppermute | solution.py:498
  50.5 10.8 %collective-permute-start.14 = (bf16[512,128]{1,0:T(8,128)(2,1)S(1)}, bf16[512,128]{1,0:T(8,128)(2,1)S(1)}, u32[]{:S(2)}, u32[]{:S(2)}) collective-permute-start(bf16[512,128]{1,0:T(8,128)(2,1)S(1)} %get-tuple-element.54), channel_id=1, source_target_pairs={{0,8},{1,9},{2,10},{3,11},{4,12},{5,13},{6,14},{7,15},{8,0},{9,1},... | collective-permute-start | bytes 393224 | tf_op jit(solution)/shard_map/ppermute | solution.py:498
  63.8 7.7 %collective-permute-start.27 = (bf16[224,128]{1,0:T(8,128)(2,1)S(1)}, bf16[224,128]{1,0:T(8,128)(2,1)S(1)}, u32[]{:S(2)}, u32[]{:S(2)}) collective-permute-start(bf16[224,128]{1,0:T(8,128)(2,1)S(1)} %split.9.refs_0_), channel_id=1, source_target_pairs={{0,8},{1,9},{2,10},{3,11},{4,12},{5,13},{6,14},{7,15},{8,0},{9,1},... | collective-permute-start | bytes 172040 | tf_op jit(solution)/shard_map/ppermute | solution.py:498
  63.8 7.7 %collective-permute-start.26 = (bf16[224,128]{1,0:T(8,128)(2,1)S(1)}, bf16[224,128]{1,0:T(8,128)(2,1)S(1)}, u32[]{:S(2)}, u32[]{:S(2)}) collective-permute-start(bf16[224,128]{1,0:T(8,128)(2,1)S(1)} %split.9.refs_0_), channel_id=1, source_target_pairs={{0,4},{1,5},{2,6},{3,7},{4,8},{5,9},{6,10},{7,11},{8,12},{9,13},{1... | collective-permute-start | bytes 172040 | tf_op jit(solution)/shard_map/ppermute | solution.py:498
  64.4 9.0 %collective-permute-start.18 = (bf16[304,128]{1,0:T(8,128)(2,1)S(1)}, bf16[304,128]{1,0:T(8,128)(2,1)S(1)}, u32[]{:S(2)}, u32[]{:S(2)}) collective-permute-start(bf16[304,128]{1,0:T(8,128)(2,1)S(1)} %pad_maximum_fusion.refs_0_), channel_id=1, source_target_pairs={{0,12},{1,13},{2,14},{3,15},{4,0},{5,1},{6,2},{7,3},{8,4},{9,5},{1... | collective-permute-start | bytes 233480 | tf_op jit(solution)/shard_map/ppermute | solution.py:498
  67.6 8.3 %collective-permute-start.17 = (bf16[304,128]{1,0:T(8,128)(2,1)S(1)}, bf16[304,128]{1,0:T(8,128)(2,1)S(1)}, u32[]{:S(2)}, u32[]{:S(2)}) collective-permute-start(bf16[304,128]{1,0:T(8,128)(2,1)S(1)} %pad_maximum_fusion.refs_0_), channel_id=1, source_target_pairs={{0,8},{1,9},{2,10},{3,11},{4,12},{5,13},{6,14},{7,15},{8,0},{9,1},... | collective-permute-start | bytes 233480 | tf_op jit(solution)/shard_map/ppermute | solution.py:498
  71.6 9.4 %collective-permute-start.31 = (bf16[896,128]{1,0:T(8,128)(2,1)S(1)}, bf16[896,128]{1,0:T(8,128)(2,1)S(1)}, u32[]{:S(2)}, u32[]{:S(2)}) collective-permute-start(bf16[896,128]{1,0:T(8,128)(2,1)S(1)} %shard_map.152.refs_0_), channel_id=1, source_target_pairs={{0,3},{1,2},{2,1},{3,0},{4,7},{5,6},{6,5},{7,4},{8,11},{9,10},{10,... | collective-permute-start | bytes 688136 | tf_op jit(solution)/shard_map/ppermute | solution.py:494
  73.4 12.6 %collective-permute-start.30 = (bf16[896,128]{1,0:T(8,128)(2,1)S(1)}, bf16[896,128]{1,0:T(8,128)(2,1)S(1)}, u32[]{:S(2)}, u32[]{:S(2)}) collective-permute-start(bf16[896,128]{1,0:T(8,128)(2,1)S(1)} %shard_map.152.refs_0_), channel_id=1, source_target_pairs={{0,2},{1,3},{2,0},{3,1},{4,6},{5,7},{6,4},{7,5},{8,10},{9,11},{10,... | collective-permute-start | bytes 688136 | tf_op jit(solution)/shard_map/ppermute | solution.py:494
  76.0 10.1 %collective-permute-start.29 = (bf16[896,128]{1,0:T(8,128)(2,1)S(1)}, bf16[896,128]{1,0:T(8,128)(2,1)S(1)}, u32[]{:S(2)}, u32[]{:S(2)}) collective-permute-start(bf16[896,128]{1,0:T(8,128)(2,1)S(1)} %shard_map.152.refs_0_), channel_id=1, source_target_pairs={{0,1},{1,0},{2,3},{3,2},{4,5},{5,4},{6,7},{7,6},{8,9},{9,8},{10,11... | collective-permute-start | bytes 688136 | tf_op jit(solution)/shard_map/ppermute | solution.py:494
  76.1 16.3 %collective-permute-start.21 = (bf16[1168,128]{1,0:T(8,128)(2,1)S(1)}, bf16[1168,128]{1,0:T(8,128)(2,1)S(1)}, u32[]{:S(2)}, u32[]{:S(2)}) collective-permute-start(bf16[1168,128]{1,0:T(8,128)(2,1)S(1)} %shard_map.151.refs_0_), channel_id=1, source_target_pairs={{0,3},{1,2},{2,1},{3,0},{4,7},{5,6},{6,5},{7,4},{8,11},{9,10},{10,... | collective-permute-start | bytes 897032 | tf_op jit(solution)/shard_map/ppermute | solution.py:494
  77.2 21.1 %collective-permute-start.20 = (bf16[1168,128]{1,0:T(8,128)(2,1)S(1)}, bf16[1168,128]{1,0:T(8,128)(2,1)S(1)}, u32[]{:S(2)}, u32[]{:S(2)}) collective-permute-start(bf16[1168,128]{1,0:T(8,128)(2,1)S(1)} %shard_map.151.refs_0_), channel_id=1, source_target_pairs={{0,2},{1,3},{2,0},{3,1},{4,6},{5,7},{6,4},{7,5},{8,10},{9,11},{10,... | collective-permute-start | bytes 897032 | tf_op jit(solution)/shard_map/ppermute | solution.py:494
  81.1 17.3 %collective-permute-start.19 = (bf16[1168,128]{1,0:T(8,128)(2,1)S(1)}, bf16[1168,128]{1,0:T(8,128)(2,1)S(1)}, u32[]{:S(2)}, u32[]{:S(2)}) collective-permute-start(bf16[1168,128]{1,0:T(8,128)(2,1)S(1)} %shard_map.151.refs_0_), channel_id=1, source_target_pairs={{0,1},{1,0},{2,3},{3,2},{4,5},{5,4},{6,7},{7,6},{8,9},{9,8},{10,11... | collective-permute-start | bytes 897032 | tf_op jit(solution)/shard_map/ppermute | solution.py:494
  86.0 12.8 %collective-permute-start.35 = (bf16[896,128]{1,0:T(8,128)(2,1)S(1)}, bf16[896,128]{1,0:T(8,128)(2,1)S(1)}, u32[]{:S(2)}, u32[]{:S(2)}) collective-permute-start(bf16[896,128]{1,0:T(8,128)(2,1)S(1)} %collective-permute-done.31.refs_3_), channel_id=1, source_target_pairs={{0,16},{16,0},{1,17},{17,1},{2,18},{18,2},{3,19},{19,3},{4,20},{20... | collective-permute-start | bytes 688136 | tf_op jit(solution)/shard_map/ppermute | solution.py:618
  86.0 12.9 %collective-permute-start.34 = (bf16[896,128]{1,0:T(8,128)(2,1)S(1)}, bf16[896,128]{1,0:T(8,128)(2,1)S(1)}, u32[]{:S(2)}, u32[]{:S(2)}) collective-permute-start(bf16[896,128]{1,0:T(8,128)(2,1)S(1)} %collective-permute-done.30.refs_2_), channel_id=1, source_target_pairs={{0,16},{16,0},{1,17},{17,1},{2,18},{18,2},{3,19},{19,3},{4,20},{20... | collective-permute-start | bytes 688136 | tf_op jit(solution)/shard_map/ppermute | solution.py:618
  (22 other events, 156.9 us)

commit v10 on v9

--- a/solution.py
+++ b/solution.py
@@ -199,7 +199,7 @@
 
 
 def first_kernel(
-    _, __, ___, keep_in, give_in, far_ref, above_ref, below_ref, w1, w2, vec_ref,
+    _, keep_in, give_in, far_ref, above_ref, below_ref, w1, w2, vec_ref,
     give_ref, keep_ref, sums_ref, ahead, behind,
 ):
     frames, rows, cols, chans = keep_in.shape
@@ -526,11 +526,11 @@
     give, keep, sums_one = call(
         first_kernel,
         (packed_shape, packed_shape, sums),
-        (*ys[1:], raw_keep, raw_give, jnp.stack(far), above, below, w1, w2, vec),
+        (ys[3], raw_keep, raw_give, jnp.stack(far), above, below, w1, w2, vec),
         5,
         20,
         [window, window],
-        free=(0, 1, 2),
+        free=(0,),
     )
     other = lax.ppermute(give, "tm", swap)
     if pair:

time: 104 us -> 109 us (1.048)
  starting transfers between devices: 39.3 us -> 43.7 us
    ppermute x4, waiting for transfers between devices: 4.81 us -> 0.01 us  [moved(): lax.ppermute(value, axis, [(i, i + by) for i in range(size) if 0 <= i + b...]
    ppermute x12, waiting for transfers between devices: 23.5 us -> 27.3 us  [plane_move(): return lax.ppermute(value, 'height', [(i, i ^ d) for i in range(height)])]
    ppermute x9, waiting for transfers between devices: 11.8 us -> 14.8 us  [column_move(): return lax.ppermute(value, 'height', pairs)]
    ppermute x12, starting transfers between devices: 13.5 us -> 15.4 us  [plane_move(): return lax.ppermute(value, 'height', [(i, i ^ d) for i in range(height)])]
    ppermute x4, starting transfers between devices: 10 us -> 11.6 us  [moved(): lax.ppermute(value, axis, [(i, i + by) for i in range(size) if 0 <= i + b...]
    ppermute x1, waiting for transfers between devices: 1.29 us -> 0.1 us  [body(): other = lax.ppermute(give, 'tm', swap)]
  transfers between devices with their start and end apart: 36 -> 36, of which waited for: 16 -> 14; matrix products, arithmetic and copies ran while one was open for 0% -> 0% of each run, Pallas kernels for 12% -> 11%
where the time goes in v10:
time: 109 us
  starting transfers between devices  43.7 us (40%)
  waiting for transfers between devices  43.4 us (40%)
  Pallas kernels  16.9 us (16%)
  local copies, waits for them, and re-layouts  2.39 us (2%)
  other arithmetic  1.24 us (1%)
    ppermute x12, waiting for transfers between devices, plane_move(): return lax.ppermute(value, 'height', [(i, i ^ d) for i in range(height)])  27.3 us
    pallas_call x12, Pallas kernels, call(): pl.pallas_call(kernel, out_shape=outs, in_specs=[in_hbm if i in hbm else...  16.9 us
    ppermute x12, starting transfers between devices, plane_move(): return lax.ppermute(value, 'height', [(i, i ^ d) for i in range(height)])  15.4 us
    ppermute x9, waiting for transfers between devices, column_move(): return lax.ppermute(value, 'height', pairs)  14.8 us
    ppermute x9, starting transfers between devices, column_move(): return lax.ppermute(value, 'height', pairs)  14.6 us
    ppermute x4, starting transfers between devices, moved(): lax.ppermute(value, axis, [(i, i + by) for i in range(size) if 0 <= i + b...  11.6 us
  transfers between devices with their start and end apart: 36, of which 14 were waited for; matrix products, arithmetic and copies ran while one was open for 0% of the time, Pallas kernels for 11%

profile of v10, /device:TPU:0, one launch (start us, length us, event | category | flops | bytes accessed | tf_op | source)
XLA Modules:
  0.0 108.7 jit_solution(10004745902820139719)
XLA Ops:
  3.5 4.8 %collective-permute-start.2 = (bf16[3,32,384]{2,1,0:T(8,128)(2,1)S(1)}, bf16[3,32,384]{2,1,0:T(8,128)(2,1)S(1)}, u32[]{:S(2)}, u32[]{:S(2)}) collective-permute-start(bf16[3,32,384]{2,1,0:T(8,128)(2,1)S(1)} %get-tuple-element.28), channel_id=1, source_target_pairs={{0,1},{1,2},{2,3},{3,4},{4,5},{5,6},{6,7},{7,8},{8,9},{9,10},{10,1... | collective-permute-start | bytes 221192 | tf_op jit(solution)/shard_map/ppermute | solution.py:468
  9.6 3.7 %collective-permute-start.1 = (bf16[2,4,32,384]{3,2,1,0:T(8,128)(2,1)S(1)}, bf16[2,4,32,384]{3,2,1,0:T(8,128)(2,1)S(1)}, u32[]{:S(2)}, u32[]{:S(2)}) collective-permute-start(bf16[2,4,32,384]{3,2,1,0:T(8,128)(2,1)S(1)} %get-tuple-element.27.refs_0_), channel_id=1, source_target_pairs={{0,3},{1,2},{2,1},{3,0},{4,7},{5,6},{6,5},{7,4},{8,11},{9,10},{10,... | collective-permute-start | bytes 589832 | tf_op jit(solution)/shard_map/ppermute | solution.py:494
  13.3 1.7 %copy-done.1 = bf16[3,3,3,192,192]{4,3,2,1,0:T(8,128)(2,1)S(1)} copy-done((bf16[3,3,3,192,192]{4,3,2,1,0:T(8,128)(2,1)S(1)}, bf16[3,3,3,192,192]{4,3,2,1,0:T(8,128)(2,1)}, u32[]{:S(2)}) %copy-start.1) | copy-done | bytes 1990680
  15.6 3.8 %collective-permute-done.1._.refs_3_ = bf16[2,4,32,384]{3,2,1,0:T(8,128)(2,1)S(1)} collective-permute-done((bf16[2,4,32,384]{3,2,1,0:T(8,128)(2,1)S(1)}, bf16[2,4,32,384]{3,2,1,0:T(8,128)(2,1)S(1)}, u32[]{:S(2)}, u32[]{:S(2)}) %collective-permute-start.1) | collective-permute-done | bytes 196640 | tf_op jit(solution)/shard_map/ppermute | solution.py:494
  19.4 2.7 %shard_map.145 = (bf16[4,32,384]{2,1,0:T(8,128)(2,1)S(1)}, bf16[4,32,384]{2,1,0:T(8,128)(2,1)S(1)}, f32[8,192]{1,0:T(8,128)S(1)}) custom-call(bf16[2,4,32,384]{3,2,1,0:T(8,128)(2,1)S(1)} %collective-permute-done.1._.refs_3_, bf16[2,4,32,192]{3,2,1,0:T(8,128)(2,1)S(1)} %get-tuple-element.56.refs_0_.keep_in, ...), custom_call_target="tpu_custom_call" | custom-call | flops 5500000256 | bytes 1024 | tf_op jit(solution)/shard_map/pallas_call | solution.py:454
  23.5 2.1 %collective-permute-start.6 = (bf16[2,5,32,384]{3,2,1,0:T(8,128)(2,1)S(1)}, bf16[2,5,32,384]{3,2,1,0:T(8,128)(2,1)S(1)}, u32[]{:S(2)}, u32[]{:S(2)}) collective-permute-start(bf16[2,5,32,384]{3,2,1,0:T(8,128)(2,1)S(1)} %shard_map.146.refs_5_.refs_0_), channel_id=1, source_target_pairs={{0,1},{1,0},{2,3},{3,2},{4,5},{5,4},{6,7},{7,6},{8,9},{9,8},{10,11... | collective-permute-start | bytes 737288 | tf_op jit(solution)/shard_map/ppermute | solution.py:494
  25.7 2.6 %collective-permute-start.10 = (bf16[2,5,32,384]{3,2,1,0:T(8,128)(2,1)S(1)}, bf16[2,5,32,384]{3,2,1,0:T(8,128)(2,1)S(1)}, u32[]{:S(2)}, u32[]{:S(2)}) collective-permute-start(bf16[2,5,32,384]{3,2,1,0:T(8,128)(2,1)S(1)} %shard_map.146.refs_5_.refs_0_), channel_id=1, source_target_pairs={{0,3},{1,2},{2,1},{3,0},{4,7},{5,6},{6,5},{7,4},{8,11},{9,10},{10,... | collective-permute-start | bytes 737288 | tf_op jit(solution)/shard_map/ppermute | solution.py:494
  29.5 7.1 %collective-permute-done.11.refs_1_ = bf16[2,4,32,384]{3,2,1,0:T(8,128)(2,1)S(1)} collective-permute-done((bf16[2,4,32,384]{3,2,1,0:T(8,128)(2,1)S(1)}, bf16[2,4,32,384]{3,2,1,0:T(8,128)(2,1)S(1)}, u32[]{:S(2)}, u32[]{:S(2)}) %collective-permute-start.11) | collective-permute-done | bytes 196640 | tf_op jit(solution)/shard_map/ppermute | solution.py:494
  37.7 4.0 %collective-permute-start.7 = (bf16[3,32,384]{2,1,0:T(8,128)(2,1)S(1)}, bf16[3,32,384]{2,1,0:T(8,128)(2,1)S(1)}, u32[]{:S(2)}, u32[]{:S(2)}) collective-permute-start(bf16[3,32,384]{2,1,0:T(8,128)(2,1)S(1)} %get-tuple-element.35), channel_id=1, source_target_pairs={{0,1},{1,2},{2,3},{3,4},{4,5},{5,6},{6,7},{7,8},{8,9},{9,10},{10,1... | collective-permute-start | bytes 221192 | tf_op jit(solution)/shard_map/ppermute | solution.py:468
  43.3 5.5 %shard_map.150 = bf16[4,512,128]{2,1,0:T(8,128)(2,1)S(1)} custom-call(bf16[2,5,32,384]{3,2,1,0:T(8,128)(2,1)S(1)} %shard_map.146.refs_5_.refs_0_, bf16[2,5,32,384]{3,2,1,0:T(8,128)(2,1)S(1)} %collective-permute-done.6._.refs_1_, bf16[2,5,32,384]{3,2,1,0:T(8,128)(2,1)S(1)} %collective-permute-done.9.refs_2_, ...), custom_call_target="tpu_custom_call" | custom-call | flops 6600000000 | bytes 1024 | tf_op jit(solution)/shard_map/pallas_call | solution.py:454
  48.8 4.5 %collective-permute-start.13 = (bf16[512,128]{1,0:T(8,128)(2,1)S(1)}, bf16[512,128]{1,0:T(8,128)(2,1)S(1)}, u32[]{:S(2)}, u32[]{:S(2)}) collective-permute-start(bf16[512,128]{1,0:T(8,128)(2,1)S(1)} %get-tuple-element.52), channel_id=1, source_target_pairs={{0,4},{1,5},{2,6},{3,7},{4,8},{5,9},{6,10},{7,11},{8,12},{9,13},{1... | collective-permute-start | bytes 393224 | tf_op jit(solution)/shard_map/ppermute | solution.py:498
  53.3 2.1 %collective-permute-start.15 = (bf16[512,128]{1,0:T(8,128)(2,1)S(1)}, bf16[512,128]{1,0:T(8,128)(2,1)S(1)}, u32[]{:S(2)}, u32[]{:S(2)}) collective-permute-start(bf16[512,128]{1,0:T(8,128)(2,1)S(1)} %get-tuple-element.53), channel_id=1, source_target_pairs={{0,12},{1,13},{2,14},{3,15},{4,0},{5,1},{6,2},{7,3},{8,4},{9,5},{1... | collective-permute-start | bytes 393224 | tf_op jit(solution)/shard_map/ppermute | solution.py:498
  56.4 3.3 %shard_map.148 = (bf16[2,4,32,192]{3,2,1,0:T(8,128)(2,1)}, bf16[2,4,32,192]{3,2,1,0:T(8,128)(2,1)}, f32[8,192]{1,0:T(8,128)S(1)}) custom-call(bf16[4,32,384]{2,1,0:T(8,128)(2,1)S(1)} %get-tuple-element.33.keep_ref, bf16[4,32,384]{2,1,0:T(8,128)(2,1)S(1)} %get-tuple-element.34.give_ref, bf16[1,4,32,384]{3,2,1,0:T(8,128)(2,1)S(1)} %bitcast.19, ...), custom_call_target="tpu_custom_call" | custom-call | flops 6600000000 | bytes 1024 | tf_op jit(solution)/shard_map/pallas_call | solution.py:454
  59.7 2.1 %collective-permute-done.15 = bf16[512,128]{1,0:T(8,128)(2,1)S(1)} collective-permute-done((bf16[512,128]{1,0:T(8,128)(2,1)S(1)}, bf16[512,128]{1,0:T(8,128)(2,1)S(1)}, u32[]{:S(2)}, u32[]{:S(2)}) %collective-permute-start.15) | collective-permute-done | bytes 131104 | tf_op jit(solution)/shard_map/ppermute | solution.py:498
  61.8 6.2 %collective-permute-done.14 = bf16[512,128]{1,0:T(8,128)(2,1)S(1)} collective-permute-done((bf16[512,128]{1,0:T(8,128)(2,1)S(1)}, bf16[512,128]{1,0:T(8,128)(2,1)S(1)}, u32[]{:S(2)}, u32[]{:S(2)}) %collective-permute-start.14) | collective-permute-done | bytes 131104 | tf_op jit(solution)/shard_map/ppermute | solution.py:498
  70.4 3.2 %collective-permute-start.18 = (bf16[304,128]{1,0:T(8,128)(2,1)S(1)}, bf16[304,128]{1,0:T(8,128)(2,1)S(1)}, u32[]{:S(2)}, u32[]{:S(2)}) collective-permute-start(bf16[304,128]{1,0:T(8,128)(2,1)S(1)} %pad_maximum_fusion.refs_0_), channel_id=1, source_target_pairs={{0,12},{1,13},{2,14},{3,15},{4,0},{5,1},{6,2},{7,3},{8,4},{9,5},{1... | collective-permute-start | bytes 233480 | tf_op jit(solution)/shard_map/ppermute | solution.py:498
  75.1 2.1 %collective-permute-done.27.refs_2_ = bf16[224,128]{1,0:T(8,128)(2,1)S(1)} collective-permute-done((bf16[224,128]{1,0:T(8,128)(2,1)S(1)}, bf16[224,128]{1,0:T(8,128)(2,1)S(1)}, u32[]{:S(2)}, u32[]{:S(2)}) %collective-permute-start.27) | collective-permute-done | bytes 57376 | tf_op jit(solution)/shard_map/ppermute | solution.py:498
  78.7 4.5 %collective-permute-done.17.refs_2_ = bf16[304,128]{1,0:T(8,128)(2,1)S(1)} collective-permute-done((bf16[304,128]{1,0:T(8,128)(2,1)S(1)}, bf16[304,128]{1,0:T(8,128)(2,1)S(1)}, u32[]{:S(2)}, u32[]{:S(2)}) %collective-permute-start.17) | collective-permute-done | bytes 77856 | tf_op jit(solution)/shard_map/ppermute | solution.py:498
  83.2 1.8 %collective-permute-start.21 = (bf16[1168,128]{1,0:T(8,128)(2,1)S(1)}, bf16[1168,128]{1,0:T(8,128)(2,1)S(1)}, u32[]{:S(2)}, u32[]{:S(2)}) collective-permute-start(bf16[1168,128]{1,0:T(8,128)(2,1)S(1)} %shard_map.151.refs_0_), channel_id=1, source_target_pairs={{0,3},{1,2},{2,1},{3,0},{4,7},{5,6},{6,5},{7,4},{8,11},{9,10},{10,... | collective-permute-start | bytes 897032 | tf_op jit(solution)/shard_map/ppermute | solution.py:494
  85.1 1.7 %collective-permute-start.20 = (bf16[1168,128]{1,0:T(8,128)(2,1)S(1)}, bf16[1168,128]{1,0:T(8,128)(2,1)S(1)}, u32[]{:S(2)}, u32[]{:S(2)}) collective-permute-start(bf16[1168,128]{1,0:T(8,128)(2,1)S(1)} %shard_map.151.refs_0_), channel_id=1, source_target_pairs={{0,2},{1,3},{2,0},{3,1},{4,6},{5,7},{6,4},{7,5},{8,10},{9,11},{10,... | collective-permute-start | bytes 897032 | tf_op jit(solution)/shard_map/ppermute | solution.py:494
  86.8 4.9 %collective-permute-done.30.refs_2_ = bf16[896,128]{1,0:T(8,128)(2,1)S(1)} collective-permute-done((bf16[896,128]{1,0:T(8,128)(2,1)S(1)}, bf16[896,128]{1,0:T(8,128)(2,1)S(1)}, u32[]{:S(2)}, u32[]{:S(2)}) %collective-permute-start.30) | collective-permute-done | bytes 229408 | tf_op jit(solution)/shard_map/ppermute | solution.py:494
  92.2 5.9 %collective-permute-done.21.refs_3_ = bf16[1168,128]{1,0:T(8,128)(2,1)S(1)} collective-permute-done((bf16[1168,128]{1,0:T(8,128)(2,1)S(1)}, bf16[1168,128]{1,0:T(8,128)(2,1)S(1)}, u32[]{:S(2)}, u32[]{:S(2)}) %collective-permute-start.21) | collective-permute-done | bytes 299040 | tf_op jit(solution)/shard_map/ppermute | solution.py:494
  98.1 5.2 %collective-permute-done.20.refs_2_ = bf16[1168,128]{1,0:T(8,128)(2,1)S(1)} collective-permute-done((bf16[1168,128]{1,0:T(8,128)(2,1)S(1)}, bf16[1168,128]{1,0:T(8,128)(2,1)S(1)}, u32[]{:S(2)}, u32[]{:S(2)}) %collective-permute-start.20) | collective-permute-done | bytes 299040 | tf_op jit(solution)/shard_map/ppermute | solution.py:494
  106.2 1.9 %shard_map.154 = (bf16[27,192,192]{2,1,0:T(8,128)(2,1)}, bf16[27,192,192]{2,1,0:T(8,128)(2,1)}, bf16[4,192]{1,0:T(4,128)(2,1)S(1)}) custom-call(bf16[1168,128]{1,0:T(8,128)(2,1)S(1)} %shard_map.151.refs_0_, bf16[1168,128]{1,0:T(8,128)(2,1)S(1)} %collective-permute-done.19.refs_1_, ...), custom_call_target="tpu_custom_call", output_to_operand_aliasing={{0}: (8, {}), {1}: (9, {})} | custom-call | flops 2200000000 | bytes 1024 | tf_op jit(solution)/shard_map/pallas_call | solution.py:454
  (92 shorter events, 20.3 us)
Async XLA Ops:
  3.5 12.0 %collective-permute-start.2 = (bf16[3,32,384]{2,1,0:T(8,128)(2,1)S(1)}, bf16[3,32,384]{2,1,0:T(8,128)(2,1)S(1)}, u32[]{:S(2)}, u32[]{:S(2)}) collective-permute-start(bf16[3,32,384]{2,1,0:T(8,128)(2,1)S(1)} %get-tuple-element.28), channel_id=1, source_target_pairs={{0,1},{1,2},{2,3},{3,4},{4,5},{5,6},{6,7},{7,8},{8,9},{9,10},{10,1... | collective-permute-start | bytes 221192 | tf_op jit(solution)/shard_map/ppermute | solution.py:468
  9.6 9.8 %collective-permute-start.1 = (bf16[2,4,32,384]{3,2,1,0:T(8,128)(2,1)S(1)}, bf16[2,4,32,384]{3,2,1,0:T(8,128)(2,1)S(1)}, u32[]{:S(2)}, u32[]{:S(2)}) collective-permute-start(bf16[2,4,32,384]{3,2,1,0:T(8,128)(2,1)S(1)} %get-tuple-element.27.refs_0_), channel_id=1, source_target_pairs={{0,3},{1,2},{2,1},{3,0},{4,7},{5,6},{6,5},{7,4},{8,11},{9,10},{10,... | collective-permute-start | bytes 589832 | tf_op jit(solution)/shard_map/ppermute | solution.py:494
  23.5 14.2 %collective-permute-start.6 = (bf16[2,5,32,384]{3,2,1,0:T(8,128)(2,1)S(1)}, bf16[2,5,32,384]{3,2,1,0:T(8,128)(2,1)S(1)}, u32[]{:S(2)}, u32[]{:S(2)}) collective-permute-start(bf16[2,5,32,384]{3,2,1,0:T(8,128)(2,1)S(1)} %shard_map.146.refs_5_.refs_0_), channel_id=1, source_target_pairs={{0,1},{1,0},{2,3},{3,2},{4,5},{5,4},{6,7},{7,6},{8,9},{9,8},{10,11... | collective-permute-start | bytes 737288 | tf_op jit(solution)/shard_map/ppermute | solution.py:494
  25.6 10.9 %collective-permute-start.11 = (bf16[2,4,32,384]{3,2,1,0:T(8,128)(2,1)S(1)}, bf16[2,4,32,384]{3,2,1,0:T(8,128)(2,1)S(1)}, u32[]{:S(2)}, u32[]{:S(2)}) collective-permute-start(bf16[2,4,32,384]{3,2,1,0:T(8,128)(2,1)S(1)} %get-tuple-element.27.refs_0_), channel_id=1, source_target_pairs={{0,1},{1,0},{2,3},{3,2},{4,5},{5,4},{6,7},{7,6},{8,9},{9,8},{10,11... | collective-permute-start | bytes 589832 | tf_op jit(solution)/shard_map/ppermute | solution.py:494
  25.7 17.5 %collective-permute-start.10 = (bf16[2,5,32,384]{3,2,1,0:T(8,128)(2,1)S(1)}, bf16[2,5,32,384]{3,2,1,0:T(8,128)(2,1)S(1)}, u32[]{:S(2)}, u32[]{:S(2)}) collective-permute-start(bf16[2,5,32,384]{3,2,1,0:T(8,128)(2,1)S(1)} %shard_map.146.refs_5_.refs_0_), channel_id=1, source_target_pairs={{0,3},{1,2},{2,1},{3,0},{4,7},{5,6},{6,5},{7,4},{8,11},{9,10},{10,... | collective-permute-start | bytes 737288 | tf_op jit(solution)/shard_map/ppermute | solution.py:494
  28.3 15.0 %collective-permute-start.9 = (bf16[2,5,32,384]{3,2,1,0:T(8,128)(2,1)S(1)}, bf16[2,5,32,384]{3,2,1,0:T(8,128)(2,1)S(1)}, u32[]{:S(2)}, u32[]{:S(2)}) collective-permute-start(bf16[2,5,32,384]{3,2,1,0:T(8,128)(2,1)S(1)} %shard_map.146.refs_5_.refs_0_), channel_id=1, source_target_pairs={{0,2},{1,3},{2,0},{3,1},{4,6},{5,7},{6,4},{7,5},{8,10},{9,11},{10,... | collective-permute-start | bytes 737288 | tf_op jit(solution)/shard_map/ppermute | solution.py:494
  29.5 8.2 %collective-permute-start.4 = (bf16[4,32,384]{2,1,0:T(8,128)(2,1)S(1)}, bf16[4,32,384]{2,1,0:T(8,128)(2,1)S(1)}, u32[]{:S(2)}, u32[]{:S(2)}) collective-permute-start(bf16[4,32,384]{2,1,0:T(8,128)(2,1)S(1)} %get-tuple-element.33.keep_ref), channel_id=1, source_target_pairs={{0,16},{16,0},{1,17},{17,1},{2,18},{18,2},{3,19},{19,3},{4,20},{20... | collective-permute-start | bytes 294920 | tf_op jit(solution)/shard_map/ppermute | solution.py:538
  37.7 18.6 %collective-permute-start.7 = (bf16[3,32,384]{2,1,0:T(8,128)(2,1)S(1)}, bf16[3,32,384]{2,1,0:T(8,128)(2,1)S(1)}, u32[]{:S(2)}, u32[]{:S(2)}) collective-permute-start(bf16[3,32,384]{2,1,0:T(8,128)(2,1)S(1)} %get-tuple-element.35), channel_id=1, source_target_pairs={{0,1},{1,2},{2,3},{3,4},{4,5},{5,6},{6,7},{7,8},{8,9},{9,10},{10,1... | collective-permute-start | bytes 221192 | tf_op jit(solution)/shard_map/ppermute | solution.py:468
  41.7 14.6 %collective-permute-start.8 = (bf16[3,32,384]{2,1,0:T(8,128)(2,1)S(1)}, bf16[3,32,384]{2,1,0:T(8,128)(2,1)S(1)}, u32[]{:S(2)}, u32[]{:S(2)}) collective-permute-start(bf16[3,32,384]{2,1,0:T(8,128)(2,1)S(1)} %get-tuple-element.36), channel_id=1, source_target_pairs={{1,0},{2,1},{3,2},{4,3},{5,4},{6,5},{7,6},{8,7},{9,8},{10,9},{11,1... | collective-permute-start | bytes 221192 | tf_op jit(solution)/shard_map/ppermute | solution.py:468
  48.8 10.9 %collective-permute-start.13 = (bf16[512,128]{1,0:T(8,128)(2,1)S(1)}, bf16[512,128]{1,0:T(8,128)(2,1)S(1)}, u32[]{:S(2)}, u32[]{:S(2)}) collective-permute-start(bf16[512,128]{1,0:T(8,128)(2,1)S(1)} %get-tuple-element.52), channel_id=1, source_target_pairs={{0,4},{1,5},{2,6},{3,7},{4,8},{5,9},{6,10},{7,11},{8,12},{9,13},{1... | collective-permute-start | bytes 393224 | tf_op jit(solution)/shard_map/ppermute | solution.py:498
  53.3 8.5 %collective-permute-start.15 = (bf16[512,128]{1,0:T(8,128)(2,1)S(1)}, bf16[512,128]{1,0:T(8,128)(2,1)S(1)}, u32[]{:S(2)}, u32[]{:S(2)}) collective-permute-start(bf16[512,128]{1,0:T(8,128)(2,1)S(1)} %get-tuple-element.53), channel_id=1, source_target_pairs={{0,12},{1,13},{2,14},{3,15},{4,0},{5,1},{6,2},{7,3},{8,4},{9,5},{1... | collective-permute-start | bytes 393224 | tf_op jit(solution)/shard_map/ppermute | solution.py:498
  55.4 12.6 %collective-permute-start.14 = (bf16[512,128]{1,0:T(8,128)(2,1)S(1)}, bf16[512,128]{1,0:T(8,128)(2,1)S(1)}, u32[]{:S(2)}, u32[]{:S(2)}) collective-permute-start(bf16[512,128]{1,0:T(8,128)(2,1)S(1)} %get-tuple-element.54), channel_id=1, source_target_pairs={{0,8},{1,9},{2,10},{3,11},{4,12},{5,13},{6,14},{7,15},{8,0},{9,1},... | collective-permute-start | bytes 393224 | tf_op jit(solution)/shard_map/ppermute | solution.py:498
  70.4 7.4 %collective-permute-start.18 = (bf16[304,128]{1,0:T(8,128)(2,1)S(1)}, bf16[304,128]{1,0:T(8,128)(2,1)S(1)}, u32[]{:S(2)}, u32[]{:S(2)}) collective-permute-start(bf16[304,128]{1,0:T(8,128)(2,1)S(1)} %pad_maximum_fusion.refs_0_), channel_id=1, source_target_pairs={{0,12},{1,13},{2,14},{3,15},{4,0},{5,1},{6,2},{7,3},{8,4},{9,5},{1... | collective-permute-start | bytes 233480 | tf_op jit(solution)/shard_map/ppermute | solution.py:498
  73.6 9.6 %collective-permute-start.17 = (bf16[304,128]{1,0:T(8,128)(2,1)S(1)}, bf16[304,128]{1,0:T(8,128)(2,1)S(1)}, u32[]{:S(2)}, u32[]{:S(2)}) collective-permute-start(bf16[304,128]{1,0:T(8,128)(2,1)S(1)} %pad_maximum_fusion.refs_0_), channel_id=1, source_target_pairs={{0,8},{1,9},{2,10},{3,11},{4,12},{5,13},{6,14},{7,15},{8,0},{9,1},... | collective-permute-start | bytes 233480 | tf_op jit(solution)/shard_map/ppermute | solution.py:498
  74.8 8.4 %collective-permute-start.16 = (bf16[304,128]{1,0:T(8,128)(2,1)S(1)}, bf16[304,128]{1,0:T(8,128)(2,1)S(1)}, u32[]{:S(2)}, u32[]{:S(2)}) collective-permute-start(bf16[304,128]{1,0:T(8,128)(2,1)S(1)} %pad_maximum_fusion.refs_0_), channel_id=1, source_target_pairs={{0,4},{1,5},{2,6},{3,7},{4,8},{5,9},{6,10},{7,11},{8,12},{9,13},{1... | collective-permute-start | bytes 233480 | tf_op jit(solution)/shard_map/ppermute | solution.py:498
  77.3 7.8 %collective-permute-start.32 = (bf16[896,128]{1,0:T(8,128)(2,1)S(1)}, bf16[896,128]{1,0:T(8,128)(2,1)S(1)}, u32[]{:S(2)}, u32[]{:S(2)}) collective-permute-start(bf16[896,128]{1,0:T(8,128)(2,1)S(1)} %shard_map.152.refs_0_), channel_id=1, source_target_pairs={{0,16},{16,0},{1,17},{17,1},{2,18},{18,2},{3,19},{19,3},{4,20},{20... | collective-permute-start | bytes 688136 | tf_op jit(solution)/shard_map/ppermute | solution.py:618
  77.4 9.4 %collective-permute-start.31 = (bf16[896,128]{1,0:T(8,128)(2,1)S(1)}, bf16[896,128]{1,0:T(8,128)(2,1)S(1)}, u32[]{:S(2)}, u32[]{:S(2)}) collective-permute-start(bf16[896,128]{1,0:T(8,128)(2,1)S(1)} %shard_map.152.refs_0_), channel_id=1, source_target_pairs={{0,3},{1,2},{2,1},{3,0},{4,7},{5,6},{6,5},{7,4},{8,11},{9,10},{10,... | collective-permute-start | bytes 688136 | tf_op jit(solution)/shard_map/ppermute | solution.py:494
  77.9 13.8 %collective-permute-start.30 = (bf16[896,128]{1,0:T(8,128)(2,1)S(1)}, bf16[896,128]{1,0:T(8,128)(2,1)S(1)}, u32[]{:S(2)}, u32[]{:S(2)}) collective-permute-start(bf16[896,128]{1,0:T(8,128)(2,1)S(1)} %shard_map.152.refs_0_), channel_id=1, source_target_pairs={{0,2},{1,3},{2,0},{3,1},{4,6},{5,7},{6,4},{7,5},{8,10},{9,11},{10,... | collective-permute-start | bytes 688136 | tf_op jit(solution)/shard_map/ppermute | solution.py:494
  83.2 8.5 %collective-permute-start.29 = (bf16[896,128]{1,0:T(8,128)(2,1)S(1)}, bf16[896,128]{1,0:T(8,128)(2,1)S(1)}, u32[]{:S(2)}, u32[]{:S(2)}) collective-permute-start(bf16[896,128]{1,0:T(8,128)(2,1)S(1)} %shard_map.152.refs_0_), channel_id=1, source_target_pairs={{0,1},{1,0},{2,3},{3,2},{4,5},{5,4},{6,7},{7,6},{8,9},{9,8},{10,11... | collective-permute-start | bytes 688136 | tf_op jit(solution)/shard_map/ppermute | solution.py:494
  83.2 14.9 %collective-permute-start.21 = (bf16[1168,128]{1,0:T(8,128)(2,1)S(1)}, bf16[1168,128]{1,0:T(8,128)(2,1)S(1)}, u32[]{:S(2)}, u32[]{:S(2)}) collective-permute-start(bf16[1168,128]{1,0:T(8,128)(2,1)S(1)} %shard_map.151.refs_0_), channel_id=1, source_target_pairs={{0,3},{1,2},{2,1},{3,0},{4,7},{5,6},{6,5},{7,4},{8,11},{9,10},{10,... | collective-permute-start | bytes 897032 | tf_op jit(solution)/shard_map/ppermute | solution.py:494
  85.1 18.2 %collective-permute-start.20 = (bf16[1168,128]{1,0:T(8,128)(2,1)S(1)}, bf16[1168,128]{1,0:T(8,128)(2,1)S(1)}, u32[]{:S(2)}, u32[]{:S(2)}) collective-permute-start(bf16[1168,128]{1,0:T(8,128)(2,1)S(1)} %shard_map.151.refs_0_), channel_id=1, source_target_pairs={{0,2},{1,3},{2,0},{3,1},{4,6},{5,7},{6,4},{7,5},{8,10},{9,11},{10,... | collective-permute-start | bytes 897032 | tf_op jit(solution)/shard_map/ppermute | solution.py:494
  86.8 16.6 %collective-permute-start.19 = (bf16[1168,128]{1,0:T(8,128)(2,1)S(1)}, bf16[1168,128]{1,0:T(8,128)(2,1)S(1)}, u32[]{:S(2)}, u32[]{:S(2)}) collective-permute-start(bf16[1168,128]{1,0:T(8,128)(2,1)S(1)} %shard_map.151.refs_0_), channel_id=1, source_target_pairs={{0,1},{1,0},{2,3},{3,2},{4,5},{5,4},{6,7},{7,6},{8,9},{9,8},{10,11... | collective-permute-start | bytes 897032 | tf_op jit(solution)/shard_map/ppermute | solution.py:494
  91.7 12.1 %collective-permute-start.35 = (bf16[896,128]{1,0:T(8,128)(2,1)S(1)}, bf16[896,128]{1,0:T(8,128)(2,1)S(1)}, u32[]{:S(2)}, u32[]{:S(2)}) collective-permute-start(bf16[896,128]{1,0:T(8,128)(2,1)S(1)} %collective-permute-done.31.refs_3_), channel_id=1, source_target_pairs={{0,16},{16,0},{1,17},{17,1},{2,18},{18,2},{3,19},{19,3},{4,20},{20... | collective-permute-start | bytes 688136 | tf_op jit(solution)/shard_map/ppermute | solution.py:618
  91.7 12.2 %collective-permute-start.34 = (bf16[896,128]{1,0:T(8,128)(2,1)S(1)}, bf16[896,128]{1,0:T(8,128)(2,1)S(1)}, u32[]{:S(2)}, u32[]{:S(2)}) collective-permute-start(bf16[896,128]{1,0:T(8,128)(2,1)S(1)} %collective-permute-done.30.refs_2_), channel_id=1, source_target_pairs={{0,16},{16,0},{1,17},{17,1},{2,18},{18,2},{3,19},{19,3},{4,20},{20... | collective-permute-start | bytes 688136 | tf_op jit(solution)/shard_map/ppermute | solution.py:618
  (22 other events, 162.1 us)

commit v11 on v9

--- a/solution.py
+++ b/solution.py
@@ -408,11 +408,8 @@
         out_ref[planes * size :] = halves(total[:half] + total[half:])
 
 
-def unpack_kernel(taps, held, *refs):
-    pieces = refs[:8]
-    outs, stage, sems = refs[8 + 2 * held : 10 + 2 * held], refs[-2], refs[-1]
-    more = refs[10 + 2 * held : -2]
-    first, count = taps
+def unpack_kernel(*refs):
+    pieces, outs, more, stage, sems = refs[:-8], refs[-8:-6], refs[-6:-2], refs[-2], refs[-1]
     chans = stage.shape[1]
     half = chans // 2
     step = pack_rows(chans)
@@ -420,9 +417,10 @@
     p = lax.axis_index("height") % 4
     made = []
     for n, src in enumerate(pieces):
+        first, count = chunks[n // 8]
         for j in range(count):
             tap = (p ^ (n % 4)) * taps_each + first + j
-            slot = n * count + j
+            slot = len(made) // 2
             high = src[j * step + chans : (j + 1) * step]
             stage[slot, :, :128] = src[j * step : j * step + chans]
             stage[slot, :half, 128:] = high[:, : chans - 128]
@@ -430,17 +428,17 @@
             real = tap < taps_all
             tap = jnp.minimum(tap, taps_all - 1)
             for which in range(2):
-                good = odd if (which == 0) == (n < 4) else jnp.logical_not(odd)
+                good = odd if (which == 0) == (n % 8 < 4) else jnp.logical_not(odd)
                 good = jnp.logical_and(good, real)
                 copy = pltpu.make_async_copy(stage.at[slot], outs[which].at[tap], sems.at[slot])
                 pl.when(good)(copy.start)
                 made.append((good, copy))
     if more:
-        sums = functools.reduce(lambda a, b: a + b, [src[src.shape[0] - 16 :].astype(f32) for src in pieces])
+        sums = functools.reduce(lambda a, b: a + b, [src[src.shape[0] - 16 :].astype(f32) for src in pieces[-8:]])
         sums = sums[:8] + sums[8:]
         for i in range(4):
             row = jnp.concatenate([sums[2 * i : 2 * i + 1], sums[2 * i + 1 : 2 * i + 2, : chans - 128]], axis=1)
-            more[0][i : i + 1] = row.astype(bf16)
+            more[i][...] = row.astype(bf16)
     for good, copy in made:
         pl.when(good)(copy.wait)
 
@@ -595,7 +593,7 @@
         hop *= 2
 
     gradient = jax.ShapeDtypeStruct((taps_all, chans, chans), bf16)
-    grads, gate = (), ()
+    final = []
     for n, (part, taps) in enumerate(zip(parts, chunks)):
         last = n == len(parts) - 1
         size = part.shape[0]
@@ -616,19 +614,19 @@
             three = plane_move(send, 3)
         got = [send, one, two, three]
         others = [lax.ppermute(g, "tm", swap) for g in got]
-        held = len(grads) > 0
-        grads = call(
-            functools.partial(unpack_kernel, taps, held),
-            (gradient, gradient) + (jax.ShapeDtypeStruct((4, chans), bf16),) * last,
-            (*got, *others, *grads),
-            2,
-            12,
-            [pltpu.VMEM((8 * taps[1], chans, chans), bf16), pltpu.SemaphoreType.DMA((8 * taps[1],))],
-            free=(8, 9) if held else (),
-            out_specs=[anywhere, anywhere] + [vmem] * last,
-            input_output_aliases={8: 0, 9: 1} if held else {},
-        )
-    grad_one, grad_two, small = grads
+        final += [*got, *others]
+    slots = 8 * taps_each
+    grads = call(
+        unpack_kernel,
+        (gradient, gradient) + (jax.ShapeDtypeStruct((1, chans), bf16),) * 4,
+        final,
+        3,
+        16,
+        [pltpu.VMEM((slots, chans, chans), bf16), pltpu.SemaphoreType.DMA((slots,))],
+        out_specs=[anywhere, anywhere] + [vmem] * 4,
+    )
+    grad_one, grad_two, *small = grads
+    small = [v.reshape(chans) for v in small]
     shape = weight_one.shape
     return (
         block_out,

time: 104 us -> 107 us (1.029)
  other arithmetic: 1.24 us -> 3.36 us
  waiting for transfers between devices: 42.8 us -> 44.6 us
    ppermute x9, waiting for transfers between devices: 11.8 us -> 14.6 us  [column_move(): return lax.ppermute(value, 'height', pairs)]
    ppermute x12, waiting for transfers between devices: 23.5 us -> 21 us  [plane_move(): return lax.ppermute(value, 'height', [(i, i ^ d) for i in range(height)])]
    pallas_call x0 -> x4, other arithmetic: none -> 2.12 us  [call(): pl.pallas_call(kernel, out_shape=outs, in_specs=[in_hbm if i in hbm else...]
    ppermute x8, waiting for transfers between devices: 0.14 us -> 1.67 us  [body(): others = [lax.ppermute(g, 'tm', swap) for g in got]]
    pallas_call x12 -> x11, Pallas kernels: 16.9 us -> 16.2 us  [call(): pl.pallas_call(kernel, out_shape=outs, in_specs=[in_hbm if i in hbm else...]
  transfers between devices with their start and end apart: 36 -> 36, of which waited for: 16 -> 18; matrix products, arithmetic and copies ran while one was open for 0% -> 0% of each run, Pallas kernels for 12% -> 10%
where the time goes in v11:
time: 107 us; the launch traced here: 106 us
  waiting for transfers between devices  44.6 us (42%)
  starting transfers between devices  39.4 us (37%)
  Pallas kernels  16.2 us (15%)
  other arithmetic  3.36 us (3%)
  local copies, waits for them, and re-layouts  1.85 us (2%)
    ppermute x12, waiting for transfers between devices, plane_move(): return lax.ppermute(value, 'height', [(i, i ^ d) for i in range(height)])  21 us
    pallas_call x11, Pallas kernels, call(): pl.pallas_call(kernel, out_shape=outs, in_specs=[in_hbm if i in hbm else...  16.2 us
    ppermute x9, waiting for transfers between devices, column_move(): return lax.ppermute(value, 'height', pairs)  14.6 us
    ppermute x12, starting transfers between devices, plane_move(): return lax.ppermute(value, 'height', [(i, i ^ d) for i in range(height)])  14.3 us
    ppermute x9, starting transfers between devices, column_move(): return lax.ppermute(value, 'height', pairs)  13.8 us
    ppermute x4, starting transfers between devices, moved(): lax.ppermute(value, axis, [(i, i + by) for i in range(size) if 0 <= i + b...  10 us
    ppermute x4, waiting for transfers between devices, moved(): lax.ppermute(value, axis, [(i, i + by) for i in range(size) if 0 <= i + b...  4.81 us
  transfers between devices with their start and end apart: 36, of which 18 were waited for; matrix products, arithmetic and copies ran while one was open for 0% of the time, Pallas kernels for 10%

profile of v11, /device:TPU:0, one launch (start us, length us, event | category | flops | bytes accessed | tf_op | source)
XLA Modules:
  0.0 106.4 jit_solution(11433103545727507786)
XLA Ops:
  3.5 3.9 %collective-permute-start.3 = (bf16[2,4,32,384]{3,2,1,0:T(8,128)(2,1)S(1)}, bf16[2,4,32,384]{3,2,1,0:T(8,128)(2,1)S(1)}, u32[]{:S(2)}, u32[]{:S(2)}) collective-permute-start(bf16[2,4,32,384]{3,2,1,0:T(8,128)(2,1)S(1)} %get-tuple-element.28.refs_0_), channel_id=1, source_target_pairs={{0,3},{1,2},{2,1},{3,0},{4,7},{5,6},{6,5},{7,4},{8,11},{9,10},{10,... | collective-permute-start | bytes 589832 | tf_op jit(solution)/shard_map/ppermute | solution.py:492
  8.0 3.8 %collective-permute-start.4 = (bf16[3,32,384]{2,1,0:T(8,128)(2,1)S(1)}, bf16[3,32,384]{2,1,0:T(8,128)(2,1)S(1)}, u32[]{:S(2)}, u32[]{:S(2)}) collective-permute-start(bf16[3,32,384]{2,1,0:T(8,128)(2,1)S(1)} %get-tuple-element.29), channel_id=1, source_target_pairs={{0,1},{1,2},{2,3},{3,4},{4,5},{5,6},{6,7},{7,8},{8,9},{9,10},{10,1... | collective-permute-start | bytes 221192 | tf_op jit(solution)/shard_map/ppermute | solution.py:466
  13.2 1.7 %copy-done.1 = bf16[3,3,3,192,192]{4,3,2,1,0:T(8,128)(2,1)S(1)} copy-done((bf16[3,3,3,192,192]{4,3,2,1,0:T(8,128)(2,1)S(1)}, bf16[3,3,3,192,192]{4,3,2,1,0:T(8,128)(2,1)}, u32[]{:S(2)}) %copy-start.1) | copy-done | bytes 1990680
  15.4 3.9 %collective-permute-done.4.above_ref = bf16[3,32,384]{2,1,0:T(8,128)(2,1)S(1)} collective-permute-done((bf16[3,32,384]{2,1,0:T(8,128)(2,1)S(1)}, bf16[3,32,384]{2,1,0:T(8,128)(2,1)S(1)}, u32[]{:S(2)}, u32[]{:S(2)}) %collective-permute-start.4) | collective-permute-done | bytes 73760 | tf_op jit(solution)/shard_map/ppermute | solution.py:466
  20.3 2.7 %shard_map.145 = (bf16[4,32,384]{2,1,0:T(8,128)(2,1)S(1)}, bf16[4,32,384]{2,1,0:T(8,128)(2,1)S(1)}, f32[8,192]{1,0:T(8,128)S(1)}) custom-call(bf16[2,4,32,384]{3,2,1,0:T(8,128)(2,1)S(1)} %collective-permute-done.1._.refs_1_, bf16[2,4,32,384]{3,2,1,0:T(8,128)(2,1)S(1)} %collective-permute-done.2.__.refs_2_, ...), custom_call_target="tpu_custom_call" | custom-call | flops 5500000256 | bytes 1024 | tf_op jit(solution)/shard_map/pallas_call | solution.py:452
  24.4 1.6 %collective-permute-start.8 = (bf16[2,5,32,384]{3,2,1,0:T(8,128)(2,1)S(1)}, bf16[2,5,32,384]{3,2,1,0:T(8,128)(2,1)S(1)}, u32[]{:S(2)}, u32[]{:S(2)}) collective-permute-start(bf16[2,5,32,384]{3,2,1,0:T(8,128)(2,1)S(1)} %shard_map.146.refs_5_.refs_0_), channel_id=1, source_target_pairs={{0,1},{1,0},{2,3},{3,2},{4,5},{5,4},{6,7},{7,6},{8,9},{9,8},{10,11... | collective-permute-start | bytes 737288 | tf_op jit(solution)/shard_map/ppermute | solution.py:492
  29.3 4.0 %collective-permute-done.8._.refs_1_ = bf16[2,5,32,384]{3,2,1,0:T(8,128)(2,1)S(1)} collective-permute-done((bf16[2,5,32,384]{3,2,1,0:T(8,128)(2,1)S(1)}, bf16[2,5,32,384]{3,2,1,0:T(8,128)(2,1)S(1)}, u32[]{:S(2)}, u32[]{:S(2)}) %collective-permute-start.8) | collective-permute-done | bytes 245792 | tf_op jit(solution)/shard_map/ppermute | solution.py:492
  33.3 3.4 %collective-permute-start.9 = (bf16[3,32,384]{2,1,0:T(8,128)(2,1)S(1)}, bf16[3,32,384]{2,1,0:T(8,128)(2,1)S(1)}, u32[]{:S(2)}, u32[]{:S(2)}) collective-permute-start(bf16[3,32,384]{2,1,0:T(8,128)(2,1)S(1)} %get-tuple-element.36), channel_id=1, source_target_pairs={{0,1},{1,2},{2,3},{3,4},{4,5},{5,6},{6,7},{7,8},{8,9},{9,10},{10,1... | collective-permute-start | bytes 221192 | tf_op jit(solution)/shard_map/ppermute | solution.py:466
  36.8 1.6 %collective-permute-start.10 = (bf16[3,32,384]{2,1,0:T(8,128)(2,1)S(1)}, bf16[3,32,384]{2,1,0:T(8,128)(2,1)S(1)}, u32[]{:S(2)}, u32[]{:S(2)}) collective-permute-start(bf16[3,32,384]{2,1,0:T(8,128)(2,1)S(1)} %get-tuple-element.37), channel_id=1, source_target_pairs={{1,0},{2,1},{3,2},{4,3},{5,4},{6,5},{7,6},{8,7},{9,8},{10,9},{11,1... | collective-permute-start | bytes 221192 | tf_op jit(solution)/shard_map/ppermute | solution.py:466
  38.3 1.5 %collective-permute-done.11.refs_2_ = bf16[2,5,32,384]{3,2,1,0:T(8,128)(2,1)S(1)} collective-permute-done((bf16[2,5,32,384]{3,2,1,0:T(8,128)(2,1)S(1)}, bf16[2,5,32,384]{3,2,1,0:T(8,128)(2,1)S(1)}, u32[]{:S(2)}, u32[]{:S(2)}) %collective-permute-start.11) | collective-permute-done | bytes 245792 | tf_op jit(solution)/shard_map/ppermute | solution.py:492
  39.8 5.5 %shard_map.150 = bf16[4,512,128]{2,1,0:T(8,128)(2,1)S(1)} custom-call(bf16[2,5,32,384]{3,2,1,0:T(8,128)(2,1)S(1)} %shard_map.146.refs_5_.refs_0_, bf16[2,5,32,384]{3,2,1,0:T(8,128)(2,1)S(1)} %collective-permute-done.8._.refs_1_, bf16[2,5,32,384]{3,2,1,0:T(8,128)(2,1)S(1)} %collective-permute-done.11.refs_2_, ...), custom_call_target="tpu_custom_call" | custom-call | flops 6600000000 | bytes 1024 | tf_op jit(solution)/shard_map/pallas_call | solution.py:452
  45.3 3.1 %collective-permute-start.13 = (bf16[512,128]{1,0:T(8,128)(2,1)S(1)}, bf16[512,128]{1,0:T(8,128)(2,1)S(1)}, u32[]{:S(2)}, u32[]{:S(2)}) collective-permute-start(bf16[512,128]{1,0:T(8,128)(2,1)S(1)} %get-tuple-element.50), channel_id=1, source_target_pairs={{0,4},{1,5},{2,6},{3,7},{4,8},{5,9},{6,10},{7,11},{8,12},{9,13},{1... | collective-permute-start | bytes 393224 | tf_op jit(solution)/shard_map/ppermute | solution.py:496
  48.4 2.1 %collective-permute-start.15 = (bf16[512,128]{1,0:T(8,128)(2,1)S(1)}, bf16[512,128]{1,0:T(8,128)(2,1)S(1)}, u32[]{:S(2)}, u32[]{:S(2)}) collective-permute-start(bf16[512,128]{1,0:T(8,128)(2,1)S(1)} %get-tuple-element.51), channel_id=1, source_target_pairs={{0,12},{1,13},{2,14},{3,15},{4,0},{5,1},{6,2},{7,3},{8,4},{9,5},{1... | collective-permute-start | bytes 393224 | tf_op jit(solution)/shard_map/ppermute | solution.py:496
  51.5 3.3 %shard_map.148 = (bf16[2,4,32,192]{3,2,1,0:T(8,128)(2,1)}, bf16[2,4,32,192]{3,2,1,0:T(8,128)(2,1)}, f32[8,192]{1,0:T(8,128)S(1)}) custom-call(bf16[4,32,384]{2,1,0:T(8,128)(2,1)S(1)} %get-tuple-element.34.keep_ref, bf16[4,32,384]{2,1,0:T(8,128)(2,1)S(1)} %get-tuple-element.35.give_ref, bf16[1,4,32,384]{3,2,1,0:T(8,128)(2,1)S(1)} %bitcast.19, ...), custom_call_target="tpu_custom_call" | custom-call | flops 6600000000 | bytes 1024 | tf_op jit(solution)/shard_map/pallas_call | solution.py:452
  55.4 5.9 %collective-permute-done.14 = bf16[512,128]{1,0:T(8,128)(2,1)S(1)} collective-permute-done((bf16[512,128]{1,0:T(8,128)(2,1)S(1)}, bf16[512,128]{1,0:T(8,128)(2,1)S(1)}, u32[]{:S(2)}, u32[]{:S(2)}) %collective-permute-start.14) | collective-permute-done | bytes 131104 | tf_op jit(solution)/shard_map/ppermute | solution.py:496
  61.5 2.3 %collective-permute-start.18 = (bf16[224,128]{1,0:T(8,128)(2,1)S(1)}, bf16[224,128]{1,0:T(8,128)(2,1)S(1)}, u32[]{:S(2)}, u32[]{:S(2)}) collective-permute-start(bf16[224,128]{1,0:T(8,128)(2,1)S(1)} %split.8.refs_0_), channel_id=1, source_target_pairs={{0,12},{1,13},{2,14},{3,15},{4,0},{5,1},{6,2},{7,3},{8,4},{9,5},{1... | collective-permute-start | bytes 172040 | tf_op jit(solution)/shard_map/ppermute | solution.py:496
  64.4 3.2 %collective-permute-start.28 = (bf16[304,128]{1,0:T(8,128)(2,1)S(1)}, bf16[304,128]{1,0:T(8,128)(2,1)S(1)}, u32[]{:S(2)}, u32[]{:S(2)}) collective-permute-start(bf16[304,128]{1,0:T(8,128)(2,1)S(1)} %pad_maximum_fusion.refs_0_), channel_id=1, source_target_pairs={{0,12},{1,13},{2,14},{3,15},{4,0},{5,1},{6,2},{7,3},{8,4},{9,5},{1... | collective-permute-start | bytes 233480 | tf_op jit(solution)/shard_map/ppermute | solution.py:496
  67.6 2.5 %collective-permute-done.17.refs_2_ = bf16[224,128]{1,0:T(8,128)(2,1)S(1)} collective-permute-done((bf16[224,128]{1,0:T(8,128)(2,1)S(1)}, bf16[224,128]{1,0:T(8,128)(2,1)S(1)}, u32[]{:S(2)}, u32[]{:S(2)}) %collective-permute-start.17) | collective-permute-done | bytes 57376 | tf_op jit(solution)/shard_map/ppermute | solution.py:496
  73.2 5.5 %collective-permute-done.27.refs_2_ = bf16[304,128]{1,0:T(8,128)(2,1)S(1)} collective-permute-done((bf16[304,128]{1,0:T(8,128)(2,1)S(1)}, bf16[304,128]{1,0:T(8,128)(2,1)S(1)}, u32[]{:S(2)}, u32[]{:S(2)}) %collective-permute-start.27) | collective-permute-done | bytes 77856 | tf_op jit(solution)/shard_map/ppermute | solution.py:496
  84.2 3.0 %collective-permute-done.19.refs_1_ = bf16[896,128]{1,0:T(8,128)(2,1)S(1)} collective-permute-done((bf16[896,128]{1,0:T(8,128)(2,1)S(1)}, bf16[896,128]{1,0:T(8,128)(2,1)S(1)}, u32[]{:S(2)}, u32[]{:S(2)}) %collective-permute-start.19) | collective-permute-done | bytes 229408 | tf_op jit(solution)/shard_map/ppermute | solution.py:492
  87.2 6.9 %collective-permute-done.31.refs_11_ = bf16[1168,128]{1,0:T(8,128)(2,1)S(1)} collective-permute-done((bf16[1168,128]{1,0:T(8,128)(2,1)S(1)}, bf16[1168,128]{1,0:T(8,128)(2,1)S(1)}, u32[]{:S(2)}, u32[]{:S(2)}) %collective-permute-start.31) | collective-permute-done | bytes 299040 | tf_op jit(solution)/shard_map/ppermute | solution.py:492
  94.1 2.8 %collective-permute-done.30.refs_10_ = bf16[1168,128]{1,0:T(8,128)(2,1)S(1)} collective-permute-done((bf16[1168,128]{1,0:T(8,128)(2,1)S(1)}, bf16[1168,128]{1,0:T(8,128)(2,1)S(1)}, u32[]{:S(2)}, u32[]{:S(2)}) %collective-permute-start.30) | collective-permute-done | bytes 299040 | tf_op jit(solution)/shard_map/ppermute | solution.py:492
  96.9 2.2 %collective-permute-done.29.refs_9_ = bf16[1168,128]{1,0:T(8,128)(2,1)S(1)} collective-permute-done((bf16[1168,128]{1,0:T(8,128)(2,1)S(1)}, bf16[1168,128]{1,0:T(8,128)(2,1)S(1)}, u32[]{:S(2)}, u32[]{:S(2)}) %collective-permute-start.29) | collective-permute-done | bytes 299040 | tf_op jit(solution)/shard_map/ppermute | solution.py:492
  101.4 2.9 %shard_map.153 = (bf16[27,192,192]{2,1,0:T(8,128)(2,1)}, bf16[27,192,192]{2,1,0:T(8,128)(2,1)}, bf16[1,192]{1,0:T(2,128)(2,1)S(1)}, bf16[1,192]{1,0:T(2,128)(2,1...) custom-call(bf16[896,128]{1,0:T(8,128)(2,1)S(1)} %shard_map.151.refs_0_, ...), custom_call_target="tpu_custom_call" | custom-call | flops 3300000000 | bytes 1024 | tf_op jit(solution)/shard_map/pallas_call | solution.py:452
  (94 shorter events, 26.1 us)
Async XLA Ops:
  3.5 16.8 %collective-permute-start.3 = (bf16[2,4,32,384]{3,2,1,0:T(8,128)(2,1)S(1)}, bf16[2,4,32,384]{3,2,1,0:T(8,128)(2,1)S(1)}, u32[]{:S(2)}, u32[]{:S(2)}) collective-permute-start(bf16[2,4,32,384]{3,2,1,0:T(8,128)(2,1)S(1)} %get-tuple-element.28.refs_0_), channel_id=1, source_target_pairs={{0,3},{1,2},{2,1},{3,0},{4,7},{5,6},{6,5},{7,4},{8,11},{9,10},{10,... | collective-permute-start | bytes 589832 | tf_op jit(solution)/shard_map/ppermute | solution.py:492
  7.4 12.9 %collective-permute-start.2 = (bf16[2,4,32,384]{3,2,1,0:T(8,128)(2,1)S(1)}, bf16[2,4,32,384]{3,2,1,0:T(8,128)(2,1)S(1)}, u32[]{:S(2)}, u32[]{:S(2)}) collective-permute-start(bf16[2,4,32,384]{3,2,1,0:T(8,128)(2,1)S(1)} %get-tuple-element.28.refs_0_), channel_id=1, source_target_pairs={{0,2},{1,3},{2,0},{3,1},{4,6},{5,7},{6,4},{7,5},{8,10},{9,11},{10,... | collective-permute-start | bytes 589832 | tf_op jit(solution)/shard_map/ppermute | solution.py:492
  7.9 12.4 %collective-permute-start.1 = (bf16[2,4,32,384]{3,2,1,0:T(8,128)(2,1)S(1)}, bf16[2,4,32,384]{3,2,1,0:T(8,128)(2,1)S(1)}, u32[]{:S(2)}, u32[]{:S(2)}) collective-permute-start(bf16[2,4,32,384]{3,2,1,0:T(8,128)(2,1)S(1)} %get-tuple-element.28.refs_0_), channel_id=1, source_target_pairs={{0,1},{1,0},{2,3},{3,2},{4,5},{5,4},{6,7},{7,6},{8,9},{9,8},{10,11... | collective-permute-start | bytes 589832 | tf_op jit(solution)/shard_map/ppermute | solution.py:492
  8.0 11.3 %collective-permute-start.4 = (bf16[3,32,384]{2,1,0:T(8,128)(2,1)S(1)}, bf16[3,32,384]{2,1,0:T(8,128)(2,1)S(1)}, u32[]{:S(2)}, u32[]{:S(2)}) collective-permute-start(bf16[3,32,384]{2,1,0:T(8,128)(2,1)S(1)} %get-tuple-element.29), channel_id=1, source_target_pairs={{0,1},{1,2},{2,3},{3,4},{4,5},{5,6},{6,7},{7,8},{8,9},{9,10},{10,1... | collective-permute-start | bytes 221192 | tf_op jit(solution)/shard_map/ppermute | solution.py:466
  11.8 8.4 %collective-permute-start.5 = (bf16[3,32,384]{2,1,0:T(8,128)(2,1)S(1)}, bf16[3,32,384]{2,1,0:T(8,128)(2,1)S(1)}, u32[]{:S(2)}, u32[]{:S(2)}) collective-permute-start(bf16[3,32,384]{2,1,0:T(8,128)(2,1)S(1)} %get-tuple-element.30), channel_id=1, source_target_pairs={{1,0},{2,1},{3,2},{4,3},{5,4},{6,5},{7,6},{8,7},{9,8},{10,9},{11,1... | collective-permute-start | bytes 221192 | tf_op jit(solution)/shard_map/ppermute | solution.py:466
  24.4 8.9 %collective-permute-start.8 = (bf16[2,5,32,384]{3,2,1,0:T(8,128)(2,1)S(1)}, bf16[2,5,32,384]{3,2,1,0:T(8,128)(2,1)S(1)}, u32[]{:S(2)}, u32[]{:S(2)}) collective-permute-start(bf16[2,5,32,384]{3,2,1,0:T(8,128)(2,1)S(1)} %shard_map.146.refs_5_.refs_0_), channel_id=1, source_target_pairs={{0,1},{1,0},{2,3},{3,2},{4,5},{5,4},{6,7},{7,6},{8,9},{9,8},{10,11... | collective-permute-start | bytes 737288 | tf_op jit(solution)/shard_map/ppermute | solution.py:492
  26.0 12.3 %collective-permute-start.12 = (bf16[2,5,32,384]{3,2,1,0:T(8,128)(2,1)S(1)}, bf16[2,5,32,384]{3,2,1,0:T(8,128)(2,1)S(1)}, u32[]{:S(2)}, u32[]{:S(2)}) collective-permute-start(bf16[2,5,32,384]{3,2,1,0:T(8,128)(2,1)S(1)} %shard_map.146.refs_5_.refs_0_), channel_id=1, source_target_pairs={{0,3},{1,2},{2,1},{3,0},{4,7},{5,6},{6,5},{7,4},{8,11},{9,10},{10,... | collective-permute-start | bytes 737288 | tf_op jit(solution)/shard_map/ppermute | solution.py:492
  26.7 13.1 %collective-permute-start.11 = (bf16[2,5,32,384]{3,2,1,0:T(8,128)(2,1)S(1)}, bf16[2,5,32,384]{3,2,1,0:T(8,128)(2,1)S(1)}, u32[]{:S(2)}, u32[]{:S(2)}) collective-permute-start(bf16[2,5,32,384]{3,2,1,0:T(8,128)(2,1)S(1)} %shard_map.146.refs_5_.refs_0_), channel_id=1, source_target_pairs={{0,2},{1,3},{2,0},{3,1},{4,6},{5,7},{6,4},{7,5},{8,10},{9,11},{10,... | collective-permute-start | bytes 737288 | tf_op jit(solution)/shard_map/ppermute | solution.py:492
  33.3 18.2 %collective-permute-start.9 = (bf16[3,32,384]{2,1,0:T(8,128)(2,1)S(1)}, bf16[3,32,384]{2,1,0:T(8,128)(2,1)S(1)}, u32[]{:S(2)}, u32[]{:S(2)}) collective-permute-start(bf16[3,32,384]{2,1,0:T(8,128)(2,1)S(1)} %get-tuple-element.36), channel_id=1, source_target_pairs={{0,1},{1,2},{2,3},{3,4},{4,5},{5,6},{6,7},{7,8},{8,9},{9,10},{10,1... | collective-permute-start | bytes 221192 | tf_op jit(solution)/shard_map/ppermute | solution.py:466
  36.8 14.7 %collective-permute-start.10 = (bf16[3,32,384]{2,1,0:T(8,128)(2,1)S(1)}, bf16[3,32,384]{2,1,0:T(8,128)(2,1)S(1)}, u32[]{:S(2)}, u32[]{:S(2)}) collective-permute-start(bf16[3,32,384]{2,1,0:T(8,128)(2,1)S(1)} %get-tuple-element.37), channel_id=1, source_target_pairs={{1,0},{2,1},{3,2},{4,3},{5,4},{6,5},{7,6},{8,7},{9,8},{10,9},{11,1... | collective-permute-start | bytes 221192 | tf_op jit(solution)/shard_map/ppermute | solution.py:466
  45.3 9.5 %collective-permute-start.13 = (bf16[512,128]{1,0:T(8,128)(2,1)S(1)}, bf16[512,128]{1,0:T(8,128)(2,1)S(1)}, u32[]{:S(2)}, u32[]{:S(2)}) collective-permute-start(bf16[512,128]{1,0:T(8,128)(2,1)S(1)} %get-tuple-element.50), channel_id=1, source_target_pairs={{0,4},{1,5},{2,6},{3,7},{4,8},{5,9},{6,10},{7,11},{8,12},{9,13},{1... | collective-permute-start | bytes 393224 | tf_op jit(solution)/shard_map/ppermute | solution.py:496
  50.5 10.8 %collective-permute-start.14 = (bf16[512,128]{1,0:T(8,128)(2,1)S(1)}, bf16[512,128]{1,0:T(8,128)(2,1)S(1)}, u32[]{:S(2)}, u32[]{:S(2)}) collective-permute-start(bf16[512,128]{1,0:T(8,128)(2,1)S(1)} %get-tuple-element.52), channel_id=1, source_target_pairs={{0,8},{1,9},{2,10},{3,11},{4,12},{5,13},{6,14},{7,15},{8,0},{9,1},... | collective-permute-start | bytes 393224 | tf_op jit(solution)/shard_map/ppermute | solution.py:496
  64.4 7.8 %collective-permute-start.28 = (bf16[304,128]{1,0:T(8,128)(2,1)S(1)}, bf16[304,128]{1,0:T(8,128)(2,1)S(1)}, u32[]{:S(2)}, u32[]{:S(2)}) collective-permute-start(bf16[304,128]{1,0:T(8,128)(2,1)S(1)} %pad_maximum_fusion.refs_0_), channel_id=1, source_target_pairs={{0,12},{1,13},{2,14},{3,15},{4,0},{5,1},{6,2},{7,3},{8,4},{9,5},{1... | collective-permute-start | bytes 233480 | tf_op jit(solution)/shard_map/ppermute | solution.py:496
  70.2 11.2 %collective-permute-start.22 = (bf16[896,128]{1,0:T(8,128)(2,1)S(1)}, bf16[896,128]{1,0:T(8,128)(2,1)S(1)}, u32[]{:S(2)}, u32[]{:S(2)}) collective-permute-start(bf16[896,128]{1,0:T(8,128)(2,1)S(1)} %shard_map.151.refs_0_), channel_id=1, source_target_pairs={{0,16},{16,0},{1,17},{17,1},{2,18},{18,2},{3,19},{19,3},{4,20},{20... | collective-permute-start | bytes 688136 | tf_op jit(solution)/shard_map/ppermute | solution.py:616
  70.3 12.0 %collective-permute-start.21 = (bf16[896,128]{1,0:T(8,128)(2,1)S(1)}, bf16[896,128]{1,0:T(8,128)(2,1)S(1)}, u32[]{:S(2)}, u32[]{:S(2)}) collective-permute-start(bf16[896,128]{1,0:T(8,128)(2,1)S(1)} %shard_map.151.refs_0_), channel_id=1, source_target_pairs={{0,3},{1,2},{2,1},{3,0},{4,7},{5,6},{6,5},{7,4},{8,11},{9,10},{10,... | collective-permute-start | bytes 688136 | tf_op jit(solution)/shard_map/ppermute | solution.py:492
  70.8 8.0 %collective-permute-start.27 = (bf16[304,128]{1,0:T(8,128)(2,1)S(1)}, bf16[304,128]{1,0:T(8,128)(2,1)S(1)}, u32[]{:S(2)}, u32[]{:S(2)}) collective-permute-start(bf16[304,128]{1,0:T(8,128)(2,1)S(1)} %pad_maximum_fusion.refs_0_), channel_id=1, source_target_pairs={{0,8},{1,9},{2,10},{3,11},{4,12},{5,13},{6,14},{7,15},{8,0},{9,1},... | collective-permute-start | bytes 233480 | tf_op jit(solution)/shard_map/ppermute | solution.py:496
  71.9 8.1 %collective-permute-start.26 = (bf16[304,128]{1,0:T(8,128)(2,1)S(1)}, bf16[304,128]{1,0:T(8,128)(2,1)S(1)}, u32[]{:S(2)}, u32[]{:S(2)}) collective-permute-start(bf16[304,128]{1,0:T(8,128)(2,1)S(1)} %pad_maximum_fusion.refs_0_), channel_id=1, source_target_pairs={{0,4},{1,5},{2,6},{3,7},{4,8},{5,9},{6,10},{7,11},{8,12},{9,13},{1... | collective-permute-start | bytes 233480 | tf_op jit(solution)/shard_map/ppermute | solution.py:496
  72.2 12.0 %collective-permute-start.20 = (bf16[896,128]{1,0:T(8,128)(2,1)S(1)}, bf16[896,128]{1,0:T(8,128)(2,1)S(1)}, u32[]{:S(2)}, u32[]{:S(2)}) collective-permute-start(bf16[896,128]{1,0:T(8,128)(2,1)S(1)} %shard_map.151.refs_0_), channel_id=1, source_target_pairs={{0,2},{1,3},{2,0},{3,1},{4,6},{5,7},{6,4},{7,5},{8,10},{9,11},{10,... | collective-permute-start | bytes 688136 | tf_op jit(solution)/shard_map/ppermute | solution.py:492
  78.7 8.5 %collective-permute-start.19 = (bf16[896,128]{1,0:T(8,128)(2,1)S(1)}, bf16[896,128]{1,0:T(8,128)(2,1)S(1)}, u32[]{:S(2)}, u32[]{:S(2)}) collective-permute-start(bf16[896,128]{1,0:T(8,128)(2,1)S(1)} %shard_map.151.refs_0_), channel_id=1, source_target_pairs={{0,1},{1,0},{2,3},{3,2},{4,5},{5,4},{6,7},{7,6},{8,9},{9,8},{10,11... | collective-permute-start | bytes 688136 | tf_op jit(solution)/shard_map/ppermute | solution.py:492
  80.0 14.1 %collective-permute-start.31 = (bf16[1168,128]{1,0:T(8,128)(2,1)S(1)}, bf16[1168,128]{1,0:T(8,128)(2,1)S(1)}, u32[]{:S(2)}, u32[]{:S(2)}) collective-permute-start(bf16[1168,128]{1,0:T(8,128)(2,1)S(1)} %shard_map.152.refs_8_), channel_id=1, source_target_pairs={{0,3},{1,2},{2,1},{3,0},{4,7},{5,6},{6,5},{7,4},{8,11},{9,10},{10,... | collective-permute-start | bytes 897032 | tf_op jit(solution)/shard_map/ppermute | solution.py:492
  81.4 15.6 %collective-permute-start.30 = (bf16[1168,128]{1,0:T(8,128)(2,1)S(1)}, bf16[1168,128]{1,0:T(8,128)(2,1)S(1)}, u32[]{:S(2)}, u32[]{:S(2)}) collective-permute-start(bf16[1168,128]{1,0:T(8,128)(2,1)S(1)} %shard_map.152.refs_8_), channel_id=1, source_target_pairs={{0,2},{1,3},{2,0},{3,1},{4,6},{5,7},{6,4},{7,5},{8,10},{9,11},{10,... | collective-permute-start | bytes 897032 | tf_op jit(solution)/shard_map/ppermute | solution.py:492
  82.3 16.8 %collective-permute-start.29 = (bf16[1168,128]{1,0:T(8,128)(2,1)S(1)}, bf16[1168,128]{1,0:T(8,128)(2,1)S(1)}, u32[]{:S(2)}, u32[]{:S(2)}) collective-permute-start(bf16[1168,128]{1,0:T(8,128)(2,1)S(1)} %shard_map.152.refs_8_), channel_id=1, source_target_pairs={{0,1},{1,0},{2,3},{3,2},{4,5},{5,4},{6,7},{7,6},{8,9},{9,8},{10,11... | collective-permute-start | bytes 897032 | tf_op jit(solution)/shard_map/ppermute | solution.py:492
  84.2 14.9 %collective-permute-start.32 = (bf16[1168,128]{1,0:T(8,128)(2,1)S(1)}, bf16[1168,128]{1,0:T(8,128)(2,1)S(1)}, u32[]{:S(2)}, u32[]{:S(2)}) collective-permute-start(bf16[1168,128]{1,0:T(8,128)(2,1)S(1)} %shard_map.152.refs_8_), channel_id=1, source_target_pairs={{0,16},{16,0},{1,17},{17,1},{2,18},{18,2},{3,19},{19,3},{4,20},{20... | collective-permute-start | bytes 897032 | tf_op jit(solution)/shard_map/ppermute | solution.py:616
  87.2 12.5 %collective-permute-start.25 = (bf16[896,128]{1,0:T(8,128)(2,1)S(1)}, bf16[896,128]{1,0:T(8,128)(2,1)S(1)}, u32[]{:S(2)}, u32[]{:S(2)}) collective-permute-start(bf16[896,128]{1,0:T(8,128)(2,1)S(1)} %collective-permute-done.21.refs_3_), channel_id=1, source_target_pairs={{0,16},{16,0},{1,17},{17,1},{2,18},{18,2},{3,19},{19,3},{4,20},{20... | collective-permute-start | bytes 688136 | tf_op jit(solution)/shard_map/ppermute | solution.py:616
  (22 other events, 156.3 us)

commit v12 on v9

--- a/solution.py
+++ b/solution.py
@@ -411,7 +411,6 @@
 def unpack_kernel(taps, held, *refs):
     pieces = refs[:8]
     outs, stage, sems = refs[8 + 2 * held : 10 + 2 * held], refs[-2], refs[-1]
-    more = refs[10 + 2 * held : -2]
     first, count = taps
     chans = stage.shape[1]
     half = chans // 2
@@ -435,12 +434,6 @@
                 copy = pltpu.make_async_copy(stage.at[slot], outs[which].at[tap], sems.at[slot])
                 pl.when(good)(copy.start)
                 made.append((good, copy))
-    if more:
-        sums = functools.reduce(lambda a, b: a + b, [src[src.shape[0] - 16 :].astype(f32) for src in pieces])
-        sums = sums[:8] + sums[8:]
-        for i in range(4):
-            row = jnp.concatenate([sums[2 * i : 2 * i + 1], sums[2 * i + 1 : 2 * i + 2, : chans - 128]], axis=1)
-            more[0][i : i + 1] = row.astype(bf16)
     for good, copy in made:
         pl.when(good)(copy.wait)
 
@@ -450,12 +443,12 @@
 in_hbm = pl.BlockSpec(memory_space=pltpu.HBM)
 
 
-def call(kernel, outs, args, us, mib, scratch=(), free=(), hbm=(), out_specs=None, **kw):
+def call(kernel, outs, args, us, mib, scratch=(), free=(), hbm=(), out_spec=vmem, **kw):
     return pl.pallas_call(
         kernel,
         out_shape=outs,
         in_specs=[in_hbm if i in hbm else anywhere if i in free else vmem for i in range(len(args))],
-        out_specs=out_specs or [vmem] * len(outs),
+        out_specs=[out_spec] * len(outs),
         scratch_shapes=list(scratch),
         compiler_params=pltpu.CompilerParams(vmem_limit_bytes=mib * 2**20),
         cost_estimate=pl.CostEstimate(flops=int(us * 1.1e9), bytes_accessed=1024, transcendentals=0),
@@ -586,8 +579,10 @@
         [window, window],
     )
 
-    small = jnp.concatenate([sums_one[:3], sums_two[:1]])
-    small = jnp.pad(small, ((0, 0), (0, -chans % 128))).reshape(-1, 128)
+    small = jnp.concatenate([sums_one[:3], sums_two[:1]]).reshape(-1, 128)
+    used = small.shape[0]
+    count = -(-used // 8) * 8
+    small = jnp.pad(small, ((0, count - used), (0, 0)))
 
     hop = 2
     while hop < tm:
@@ -616,20 +611,24 @@
             three = plane_move(send, 3)
         got = [send, one, two, three]
         others = [lax.ppermute(g, "tm", swap) for g in got]
+        if last:
+            small = total_of([v[planes * size :] for v in got + others])
+            small = (small[:count] + small[count:])[:used]
         held = len(grads) > 0
         grads = call(
             functools.partial(unpack_kernel, taps, held),
-            (gradient, gradient) + (jax.ShapeDtypeStruct((4, chans), bf16),) * last,
+            (gradient, gradient),
             (*got, *others, *grads),
             2,
             12,
             [pltpu.VMEM((8 * taps[1], chans, chans), bf16), pltpu.SemaphoreType.DMA((8 * taps[1],))],
             free=(8, 9) if held else (),
-            out_specs=[anywhere, anywhere] + [vmem] * last,
+            out_spec=anywhere,
             input_output_aliases={8: 0, 9: 1} if held else {},
         )
-    grad_one, grad_two, small = grads
+    grad_one, grad_two = grads
     shape = weight_one.shape
+    small = small.reshape(4, chans).astype(bf16)
     return (
         block_out,
         grad_input,

time: 104 us -> 99.3 us (0.955)
  waiting for transfers between devices: 42.8 us -> 34.4 us
  starting transfers between devices: 39.3 us -> 42.8 us
    ppermute x12, waiting for transfers between devices: 23.5 us -> 18.7 us  [plane_move(): return lax.ppermute(value, 'height', [(i, i ^ d) for i in range(height)])]
    ppermute x9, waiting for transfers between devices: 11.8 us -> 9.43 us  [column_move(): return lax.ppermute(value, 'height', pairs)]
    ppermute x12, starting transfers between devices: 13.5 us -> 15.3 us  [plane_move(): return lax.ppermute(value, 'height', [(i, i ^ d) for i in range(height)])]
    ppermute x9, starting transfers between devices: 13.5 us -> 15.1 us  [column_move(): return lax.ppermute(value, 'height', pairs)]
    ppermute x4, waiting for transfers between devices: 4.81 us -> 3.61 us  [moved(): lax.ppermute(value, axis, [(i, i + by) for i in range(size) if 0 <= i + b...]
  transfers between devices with their start and end apart: 36 -> 36, of which waited for: 16 -> 17; matrix products, arithmetic and copies ran while one was open for 0% -> 0% of each run, Pallas kernels for 12% -> 12%
where the time goes in v12:
time: 99.3 us; the launch traced here: 99.1 us
  starting transfers between devices  42.8 us (43%)
  waiting for transfers between devices  34.4 us (35%)
  Pallas kernels  16.9 us (17%)
  local copies, waits for them, and re-layouts  2.55 us (3%)
  other arithmetic  1.26 us (1%)
  between operations  1.19 us (1%)
    ppermute x12, waiting for transfers between devices, plane_move(): return lax.ppermute(value, 'height', [(i, i ^ d) for i in range(height)])  18.7 us
    pallas_call x12, Pallas kernels, call(): pl.pallas_call(kernel, out_shape=outs, in_specs=[in_hbm if i in hbm else...  16.9 us
    ppermute x12, starting transfers between devices, plane_move(): return lax.ppermute(value, 'height', [(i, i ^ d) for i in range(height)])  15.3 us
    ppermute x9, starting transfers between devices, column_move(): return lax.ppermute(value, 'height', pairs)  15.1 us
    ppermute x4, starting transfers between devices, moved(): lax.ppermute(value, axis, [(i, i + by) for i in range(size) if 0 <= i + b...  10.7 us
    ppermute x9, waiting for transfers between devices, column_move(): return lax.ppermute(value, 'height', pairs)  9.43 us
    ppermute x4, waiting for transfers between devices, moved(): lax.ppermute(value, axis, [(i, i + by) for i in range(size) if 0 <= i + b...  3.61 us
  transfers between devices with their start and end apart: 36, of which 17 were waited for; matrix products, arithmetic and copies ran while one was open for 0% of the time, Pallas kernels for 12%

profile of v12, /device:TPU:0, one launch (start us, length us, event | category | flops | bytes accessed | tf_op | source)
XLA Modules:
  0.0 99.1 jit_solution(1525997168500391144)
XLA Ops:
  3.5 2.9 %collective-permute-start.1 = (bf16[2,4,32,384]{3,2,1,0:T(8,128)(2,1)S(1)}, bf16[2,4,32,384]{3,2,1,0:T(8,128)(2,1)S(1)}, u32[]{:S(2)}, u32[]{:S(2)}) collective-permute-start(bf16[2,4,32,384]{3,2,1,0:T(8,128)(2,1)S(1)} %get-tuple-element.26.refs_0_), channel_id=1, source_target_pairs={{0,1},{1,0},{2,3},{3,2},{4,5},{5,4},{6,7},{7,6},{8,9},{9,8},{10,11... | collective-permute-start | bytes 589832 | tf_op jit(solution)/shard_map/ppermute | solution.py:487
  6.4 1.5 %collective-permute-start.2 = (bf16[2,4,32,384]{3,2,1,0:T(8,128)(2,1)S(1)}, bf16[2,4,32,384]{3,2,1,0:T(8,128)(2,1)S(1)}, u32[]{:S(2)}, u32[]{:S(2)}) collective-permute-start(bf16[2,4,32,384]{3,2,1,0:T(8,128)(2,1)S(1)} %get-tuple-element.26.refs_0_), channel_id=1, source_target_pairs={{0,2},{1,3},{2,0},{3,1},{4,6},{5,7},{6,4},{7,5},{8,10},{9,11},{10,... | collective-permute-start | bytes 589832 | tf_op jit(solution)/shard_map/ppermute | solution.py:487
  7.9 3.8 %collective-permute-start.4 = (bf16[3,32,384]{2,1,0:T(8,128)(2,1)S(1)}, bf16[3,32,384]{2,1,0:T(8,128)(2,1)S(1)}, u32[]{:S(2)}, u32[]{:S(2)}) collective-permute-start(bf16[3,32,384]{2,1,0:T(8,128)(2,1)S(1)} %get-tuple-element.27), channel_id=1, source_target_pairs={{0,1},{1,2},{2,3},{3,4},{4,5},{5,6},{6,7},{7,8},{8,9},{9,10},{10,1... | collective-permute-start | bytes 221192 | tf_op jit(solution)/shard_map/ppermute | solution.py:461
  13.2 1.7 %copy-done.1 = bf16[3,3,3,192,192]{4,3,2,1,0:T(8,128)(2,1)S(1)} copy-done((bf16[3,3,3,192,192]{4,3,2,1,0:T(8,128)(2,1)S(1)}, bf16[3,3,3,192,192]{4,3,2,1,0:T(8,128)(2,1)}, u32[]{:S(2)}) %copy-start.1) | copy-done | bytes 1990680
  15.4 2.1 %collective-permute-done.4.above_ref = bf16[3,32,384]{2,1,0:T(8,128)(2,1)S(1)} collective-permute-done((bf16[3,32,384]{2,1,0:T(8,128)(2,1)S(1)}, bf16[3,32,384]{2,1,0:T(8,128)(2,1)S(1)}, u32[]{:S(2)}, u32[]{:S(2)}) %collective-permute-start.4) | collective-permute-done | bytes 73760 | tf_op jit(solution)/shard_map/ppermute | solution.py:461
  17.5 1.5 %collective-permute-done.5.below_ref = bf16[3,32,384]{2,1,0:T(8,128)(2,1)S(1)} collective-permute-done((bf16[3,32,384]{2,1,0:T(8,128)(2,1)S(1)}, bf16[3,32,384]{2,1,0:T(8,128)(2,1)S(1)}, u32[]{:S(2)}, u32[]{:S(2)}) %collective-permute-start.5) | collective-permute-done | bytes 73760 | tf_op jit(solution)/shard_map/ppermute | solution.py:461
  19.1 2.7 %shard_map.145 = (bf16[4,32,384]{2,1,0:T(8,128)(2,1)S(1)}, bf16[4,32,384]{2,1,0:T(8,128)(2,1)S(1)}, f32[8,192]{1,0:T(8,128)S(1)}) custom-call(bf16[2,4,32,384]{3,2,1,0:T(8,128)(2,1)S(1)} %collective-permute-done.1._.refs_1_, bf16[2,4,32,384]{3,2,1,0:T(8,128)(2,1)S(1)} %collective-permute-done.2.__.refs_2_, ...), custom_call_target="tpu_custom_call" | custom-call | flops 5500000256 | bytes 1024 | tf_op jit(solution)/shard_map/pallas_call | solution.py:447
  23.2 2.7 %collective-permute-start.8 = (bf16[2,5,32,384]{3,2,1,0:T(8,128)(2,1)S(1)}, bf16[2,5,32,384]{3,2,1,0:T(8,128)(2,1)S(1)}, u32[]{:S(2)}, u32[]{:S(2)}) collective-permute-start(bf16[2,5,32,384]{3,2,1,0:T(8,128)(2,1)S(1)} %shard_map.146.refs_5_.refs_0_), channel_id=1, source_target_pairs={{0,1},{1,0},{2,3},{3,2},{4,5},{5,4},{6,7},{7,6},{8,9},{9,8},{10,11... | collective-permute-start | bytes 737288 | tf_op jit(solution)/shard_map/ppermute | solution.py:487
  28.8 3.9 %collective-permute-done.8._.refs_1_ = bf16[2,5,32,384]{3,2,1,0:T(8,128)(2,1)S(1)} collective-permute-done((bf16[2,5,32,384]{3,2,1,0:T(8,128)(2,1)S(1)}, bf16[2,5,32,384]{3,2,1,0:T(8,128)(2,1)S(1)}, u32[]{:S(2)}, u32[]{:S(2)}) %collective-permute-start.8) | collective-permute-done | bytes 245792 | tf_op jit(solution)/shard_map/ppermute | solution.py:487
  32.7 4.0 %collective-permute-start.9 = (bf16[3,32,384]{2,1,0:T(8,128)(2,1)S(1)}, bf16[3,32,384]{2,1,0:T(8,128)(2,1)S(1)}, u32[]{:S(2)}, u32[]{:S(2)}) collective-permute-start(bf16[3,32,384]{2,1,0:T(8,128)(2,1)S(1)} %get-tuple-element.34), channel_id=1, source_target_pairs={{0,1},{1,2},{2,3},{3,4},{4,5},{5,6},{6,7},{7,8},{8,9},{9,10},{10,1... | collective-permute-start | bytes 221192 | tf_op jit(solution)/shard_map/ppermute | solution.py:461
  36.7 1.6 %collective-permute-start.10 = (bf16[3,32,384]{2,1,0:T(8,128)(2,1)S(1)}, bf16[3,32,384]{2,1,0:T(8,128)(2,1)S(1)}, u32[]{:S(2)}, u32[]{:S(2)}) collective-permute-start(bf16[3,32,384]{2,1,0:T(8,128)(2,1)S(1)} %get-tuple-element.35), channel_id=1, source_target_pairs={{1,0},{2,1},{3,2},{4,3},{5,4},{6,5},{7,6},{8,7},{9,8},{10,9},{11,1... | collective-permute-start | bytes 221192 | tf_op jit(solution)/shard_map/ppermute | solution.py:461
  39.2 5.5 %shard_map.150 = bf16[4,512,128]{2,1,0:T(8,128)(2,1)S(1)} custom-call(bf16[2,5,32,384]{3,2,1,0:T(8,128)(2,1)S(1)} %shard_map.146.refs_5_.refs_0_, bf16[2,5,32,384]{3,2,1,0:T(8,128)(2,1)S(1)} %collective-permute-done.8._.refs_1_, bf16[2,5,32,384]{3,2,1,0:T(8,128)(2,1)S(1)} %collective-permute-done.11.refs_2_, ...), custom_call_target="tpu_custom_call" | custom-call | flops 6600000000 | bytes 1024 | tf_op jit(solution)/shard_map/pallas_call | solution.py:447
  44.7 5.1 %collective-permute-start.15 = (bf16[512,128]{1,0:T(8,128)(2,1)S(1)}, bf16[512,128]{1,0:T(8,128)(2,1)S(1)}, u32[]{:S(2)}, u32[]{:S(2)}) collective-permute-start(bf16[512,128]{1,0:T(8,128)(2,1)S(1)} %get-tuple-element.49), channel_id=1, source_target_pairs={{0,12},{1,13},{2,14},{3,15},{4,0},{5,1},{6,2},{7,3},{8,4},{9,5},{1... | collective-permute-start | bytes 393224 | tf_op jit(solution)/shard_map/ppermute | solution.py:491
  50.9 3.3 %shard_map.148 = (bf16[2,4,32,192]{3,2,1,0:T(8,128)(2,1)}, bf16[2,4,32,192]{3,2,1,0:T(8,128)(2,1)}, f32[8,192]{1,0:T(8,128)S(1)}) custom-call(bf16[4,32,384]{2,1,0:T(8,128)(2,1)S(1)} %get-tuple-element.32.keep_ref, bf16[4,32,384]{2,1,0:T(8,128)(2,1)S(1)} %get-tuple-element.33.give_ref, bf16[1,4,32,384]{3,2,1,0:T(8,128)(2,1)S(1)} %bitcast.20, ...), custom_call_target="tpu_custom_call" | custom-call | flops 6600000000 | bytes 1024 | tf_op jit(solution)/shard_map/pallas_call | solution.py:447
  54.3 6.4 %collective-permute-done.14 = bf16[512,128]{1,0:T(8,128)(2,1)S(1)} collective-permute-done((bf16[512,128]{1,0:T(8,128)(2,1)S(1)}, bf16[512,128]{1,0:T(8,128)(2,1)S(1)}, u32[]{:S(2)}, u32[]{:S(2)}) %collective-permute-start.14) | collective-permute-done | bytes 131104 | tf_op jit(solution)/shard_map/ppermute | solution.py:491
  61.5 2.0 %collective-permute-start.27 = (bf16[224,128]{1,0:T(8,128)(2,1)S(1)}, bf16[224,128]{1,0:T(8,128)(2,1)S(1)}, u32[]{:S(2)}, u32[]{:S(2)}) collective-permute-start(bf16[224,128]{1,0:T(8,128)(2,1)S(1)} %split.9.refs_0_), channel_id=1, source_target_pairs={{0,8},{1,9},{2,10},{3,11},{4,12},{5,13},{6,14},{7,15},{8,0},{9,1},... | collective-permute-start | bytes 172040 | tf_op jit(solution)/shard_map/ppermute | solution.py:491
  63.5 2.8 %collective-permute-start.28 = (bf16[224,128]{1,0:T(8,128)(2,1)S(1)}, bf16[224,128]{1,0:T(8,128)(2,1)S(1)}, u32[]{:S(2)}, u32[]{:S(2)}) collective-permute-start(bf16[224,128]{1,0:T(8,128)(2,1)S(1)} %split.9.refs_0_), channel_id=1, source_target_pairs={{0,12},{1,13},{2,14},{3,15},{4,0},{5,1},{6,2},{7,3},{8,4},{9,5},{1... | collective-permute-start | bytes 172040 | tf_op jit(solution)/shard_map/ppermute | solution.py:491
  67.4 2.8 %collective-permute-start.18 = (bf16[304,128]{1,0:T(8,128)(2,1)S(1)}, bf16[304,128]{1,0:T(8,128)(2,1)S(1)}, u32[]{:S(2)}, u32[]{:S(2)}) collective-permute-start(bf16[304,128]{1,0:T(8,128)(2,1)S(1)} %pad_maximum_fusion.refs_0_), channel_id=1, source_target_pairs={{0,12},{1,13},{2,14},{3,15},{4,0},{5,1},{6,2},{7,3},{8,4},{9,5},{1... | collective-permute-start | bytes 233480 | tf_op jit(solution)/shard_map/ppermute | solution.py:491
  75.3 2.8 %collective-permute-done.29.refs_1_ = bf16[896,128]{1,0:T(8,128)(2,1)S(1)} collective-permute-done((bf16[896,128]{1,0:T(8,128)(2,1)S(1)}, bf16[896,128]{1,0:T(8,128)(2,1)S(1)}, u32[]{:S(2)}, u32[]{:S(2)}) %collective-permute-start.29) | collective-permute-done | bytes 229408 | tf_op jit(solution)/shard_map/ppermute | solution.py:487
  79.3 3.1 %collective-permute-start.21 = (bf16[1168,128]{1,0:T(8,128)(2,1)S(1)}, bf16[1168,128]{1,0:T(8,128)(2,1)S(1)}, u32[]{:S(2)}, u32[]{:S(2)}) collective-permute-start(bf16[1168,128]{1,0:T(8,128)(2,1)S(1)} %shard_map.151.refs_0_), channel_id=1, source_target_pairs={{0,3},{1,2},{2,1},{3,0},{4,7},{5,6},{6,5},{7,4},{8,11},{9,10},{10,... | collective-permute-start | bytes 897032 | tf_op jit(solution)/shard_map/ppermute | solution.py:487
  84.2 4.9 %collective-permute-done.19.refs_1_ = bf16[1168,128]{1,0:T(8,128)(2,1)S(1)} collective-permute-done((bf16[1168,128]{1,0:T(8,128)(2,1)S(1)}, bf16[1168,128]{1,0:T(8,128)(2,1)S(1)}, u32[]{:S(2)}, u32[]{:S(2)}) %collective-permute-start.19) | collective-permute-done | bytes 299040 | tf_op jit(solution)/shard_map/ppermute | solution.py:487
  90.2 3.8 %collective-permute-done.21.refs_3_ = bf16[1168,128]{1,0:T(8,128)(2,1)S(1)} collective-permute-done((bf16[1168,128]{1,0:T(8,128)(2,1)S(1)}, bf16[1168,128]{1,0:T(8,128)(2,1)S(1)}, u32[]{:S(2)}, u32[]{:S(2)}) %collective-permute-start.21) | collective-permute-done | bytes 299040 | tf_op jit(solution)/shard_map/ppermute | solution.py:487
  94.5 1.7 %shard_map.153 = (bf16[27,192,192]{2,1,0:T(8,128)(2,1)}, bf16[27,192,192]{2,1,0:T(8,128)(2,1)}) custom-call(bf16[896,128]{1,0:T(8,128)(2,1)S(1)} %shard_map.152.refs_0_, bf16[896,128]{1,0:T(8,128)(2,1)S(1)} %collective-permute-done.29.refs_1_, bf16[896,128]{1,0:T(8,128)(2,1)S(1)} %collective-permute-done.30.refs_2_, ...), custom_call_target="tpu_custom_call" | custom-call | flops 2200000000 | bytes 1024 | tf_op jit(solution)/shard_map/pallas_call | solution.py:447
  97.0 1.9 %shard_map.154 = (bf16[27,192,192]{2,1,0:T(8,128)(2,1)}, bf16[27,192,192]{2,1,0:T(8,128)(2,1)}) custom-call(bf16[1168,128]{1,0:T(8,128)(2,1)S(1)} %shard_map.151.refs_0_, bf16[1168,128]{1,0:T(8,128)(2,1)S(1)} %collective-permute-done.19.refs_1_, bf16[1168,128]{1,0:T(8,128)(2,1)S(1)} %collective-permute-done.20.refs_2_, ...), custom_call_target="tpu_custom_call", output_to_operand_aliasing={{0}: (8, {}), {1}: (9, {})} | custom-call | flops 2200000000 | bytes 1024 | tf_op jit(solution)/shard_map/pallas_call | solution.py:447
  (96 shorter events, 23.4 us)
Async XLA Ops:
  3.5 15.6 %collective-permute-start.1 = (bf16[2,4,32,384]{3,2,1,0:T(8,128)(2,1)S(1)}, bf16[2,4,32,384]{3,2,1,0:T(8,128)(2,1)S(1)}, u32[]{:S(2)}, u32[]{:S(2)}) collective-permute-start(bf16[2,4,32,384]{3,2,1,0:T(8,128)(2,1)S(1)} %get-tuple-element.26.refs_0_), channel_id=1, source_target_pairs={{0,1},{1,0},{2,3},{3,2},{4,5},{5,4},{6,7},{7,6},{8,9},{9,8},{10,11... | collective-permute-start | bytes 589832 | tf_op jit(solution)/shard_map/ppermute | solution.py:487
  6.4 12.6 %collective-permute-start.2 = (bf16[2,4,32,384]{3,2,1,0:T(8,128)(2,1)S(1)}, bf16[2,4,32,384]{3,2,1,0:T(8,128)(2,1)S(1)}, u32[]{:S(2)}, u32[]{:S(2)}) collective-permute-start(bf16[2,4,32,384]{3,2,1,0:T(8,128)(2,1)S(1)} %get-tuple-element.26.refs_0_), channel_id=1, source_target_pairs={{0,2},{1,3},{2,0},{3,1},{4,6},{5,7},{6,4},{7,5},{8,10},{9,11},{10,... | collective-permute-start | bytes 589832 | tf_op jit(solution)/shard_map/ppermute | solution.py:487
  7.9 11.1 %collective-permute-start.3 = (bf16[2,4,32,384]{3,2,1,0:T(8,128)(2,1)S(1)}, bf16[2,4,32,384]{3,2,1,0:T(8,128)(2,1)S(1)}, u32[]{:S(2)}, u32[]{:S(2)}) collective-permute-start(bf16[2,4,32,384]{3,2,1,0:T(8,128)(2,1)S(1)} %get-tuple-element.26.refs_0_), channel_id=1, source_target_pairs={{0,3},{1,2},{2,1},{3,0},{4,7},{5,6},{6,5},{7,4},{8,11},{9,10},{10,... | collective-permute-start | bytes 589832 | tf_op jit(solution)/shard_map/ppermute | solution.py:487
  7.9 9.6 %collective-permute-start.4 = (bf16[3,32,384]{2,1,0:T(8,128)(2,1)S(1)}, bf16[3,32,384]{2,1,0:T(8,128)(2,1)S(1)}, u32[]{:S(2)}, u32[]{:S(2)}) collective-permute-start(bf16[3,32,384]{2,1,0:T(8,128)(2,1)S(1)} %get-tuple-element.27), channel_id=1, source_target_pairs={{0,1},{1,2},{2,3},{3,4},{4,5},{5,6},{6,7},{7,8},{8,9},{9,10},{10,1... | collective-permute-start | bytes 221192 | tf_op jit(solution)/shard_map/ppermute | solution.py:461
  23.2 9.5 %collective-permute-start.8 = (bf16[2,5,32,384]{3,2,1,0:T(8,128)(2,1)S(1)}, bf16[2,5,32,384]{3,2,1,0:T(8,128)(2,1)S(1)}, u32[]{:S(2)}, u32[]{:S(2)}) collective-permute-start(bf16[2,5,32,384]{3,2,1,0:T(8,128)(2,1)S(1)} %shard_map.146.refs_5_.refs_0_), channel_id=1, source_target_pairs={{0,1},{1,0},{2,3},{3,2},{4,5},{5,4},{6,7},{7,6},{8,9},{9,8},{10,11... | collective-permute-start | bytes 737288 | tf_op jit(solution)/shard_map/ppermute | solution.py:487
  25.9 13.3 %collective-permute-start.11 = (bf16[2,5,32,384]{3,2,1,0:T(8,128)(2,1)S(1)}, bf16[2,5,32,384]{3,2,1,0:T(8,128)(2,1)S(1)}, u32[]{:S(2)}, u32[]{:S(2)}) collective-permute-start(bf16[2,5,32,384]{3,2,1,0:T(8,128)(2,1)S(1)} %shard_map.146.refs_5_.refs_0_), channel_id=1, source_target_pairs={{0,2},{1,3},{2,0},{3,1},{4,6},{5,7},{6,4},{7,5},{8,10},{9,11},{10,... | collective-permute-start | bytes 737288 | tf_op jit(solution)/shard_map/ppermute | solution.py:487
  27.1 12.1 %collective-permute-start.12 = (bf16[2,5,32,384]{3,2,1,0:T(8,128)(2,1)S(1)}, bf16[2,5,32,384]{3,2,1,0:T(8,128)(2,1)S(1)}, u32[]{:S(2)}, u32[]{:S(2)}) collective-permute-start(bf16[2,5,32,384]{3,2,1,0:T(8,128)(2,1)S(1)} %shard_map.146.refs_5_.refs_0_), channel_id=1, source_target_pairs={{0,3},{1,2},{2,1},{3,0},{4,7},{5,6},{6,5},{7,4},{8,11},{9,10},{10,... | collective-permute-start | bytes 737288 | tf_op jit(solution)/shard_map/ppermute | solution.py:487
  32.7 18.2 %collective-permute-start.9 = (bf16[3,32,384]{2,1,0:T(8,128)(2,1)S(1)}, bf16[3,32,384]{2,1,0:T(8,128)(2,1)S(1)}, u32[]{:S(2)}, u32[]{:S(2)}) collective-permute-start(bf16[3,32,384]{2,1,0:T(8,128)(2,1)S(1)} %get-tuple-element.34), channel_id=1, source_target_pairs={{0,1},{1,2},{2,3},{3,4},{4,5},{5,6},{6,7},{7,8},{8,9},{9,10},{10,1... | collective-permute-start | bytes 221192 | tf_op jit(solution)/shard_map/ppermute | solution.py:461
  36.7 14.2 %collective-permute-start.10 = (bf16[3,32,384]{2,1,0:T(8,128)(2,1)S(1)}, bf16[3,32,384]{2,1,0:T(8,128)(2,1)S(1)}, u32[]{:S(2)}, u32[]{:S(2)}) collective-permute-start(bf16[3,32,384]{2,1,0:T(8,128)(2,1)S(1)} %get-tuple-element.35), channel_id=1, source_target_pairs={{1,0},{2,1},{3,2},{4,3},{5,4},{6,5},{7,6},{8,7},{9,8},{10,9},{11,1... | collective-permute-start | bytes 221192 | tf_op jit(solution)/shard_map/ppermute | solution.py:461
  44.7 9.6 %collective-permute-start.15 = (bf16[512,128]{1,0:T(8,128)(2,1)S(1)}, bf16[512,128]{1,0:T(8,128)(2,1)S(1)}, u32[]{:S(2)}, u32[]{:S(2)}) collective-permute-start(bf16[512,128]{1,0:T(8,128)(2,1)S(1)} %get-tuple-element.49), channel_id=1, source_target_pairs={{0,12},{1,13},{2,14},{3,15},{4,0},{5,1},{6,2},{7,3},{8,4},{9,5},{1... | collective-permute-start | bytes 393224 | tf_op jit(solution)/shard_map/ppermute | solution.py:491
  49.8 10.8 %collective-permute-start.14 = (bf16[512,128]{1,0:T(8,128)(2,1)S(1)}, bf16[512,128]{1,0:T(8,128)(2,1)S(1)}, u32[]{:S(2)}, u32[]{:S(2)}) collective-permute-start(bf16[512,128]{1,0:T(8,128)(2,1)S(1)} %get-tuple-element.50), channel_id=1, source_target_pairs={{0,8},{1,9},{2,10},{3,11},{4,12},{5,13},{6,14},{7,15},{8,0},{9,1},... | collective-permute-start | bytes 393224 | tf_op jit(solution)/shard_map/ppermute | solution.py:491
  49.9 10.8 %collective-permute-start.13 = (bf16[512,128]{1,0:T(8,128)(2,1)S(1)}, bf16[512,128]{1,0:T(8,128)(2,1)S(1)}, u32[]{:S(2)}, u32[]{:S(2)}) collective-permute-start(bf16[512,128]{1,0:T(8,128)(2,1)S(1)} %get-tuple-element.48), channel_id=1, source_target_pairs={{0,4},{1,5},{2,6},{3,7},{4,8},{5,9},{6,10},{7,11},{8,12},{9,13},{1... | collective-permute-start | bytes 393224 | tf_op jit(solution)/shard_map/ppermute | solution.py:491
  61.5 8.7 %collective-permute-start.27 = (bf16[224,128]{1,0:T(8,128)(2,1)S(1)}, bf16[224,128]{1,0:T(8,128)(2,1)S(1)}, u32[]{:S(2)}, u32[]{:S(2)}) collective-permute-start(bf16[224,128]{1,0:T(8,128)(2,1)S(1)} %split.9.refs_0_), channel_id=1, source_target_pairs={{0,8},{1,9},{2,10},{3,11},{4,12},{5,13},{6,14},{7,15},{8,0},{9,1},... | collective-permute-start | bytes 172040 | tf_op jit(solution)/shard_map/ppermute | solution.py:491
  66.4 8.8 %collective-permute-start.17 = (bf16[304,128]{1,0:T(8,128)(2,1)S(1)}, bf16[304,128]{1,0:T(8,128)(2,1)S(1)}, u32[]{:S(2)}, u32[]{:S(2)}) collective-permute-start(bf16[304,128]{1,0:T(8,128)(2,1)S(1)} %pad_maximum_fusion.refs_0_), channel_id=1, source_target_pairs={{0,8},{1,9},{2,10},{3,11},{4,12},{5,13},{6,14},{7,15},{8,0},{9,1},... | collective-permute-start | bytes 233480 | tf_op jit(solution)/shard_map/ppermute | solution.py:491
  67.4 7.8 %collective-permute-start.18 = (bf16[304,128]{1,0:T(8,128)(2,1)S(1)}, bf16[304,128]{1,0:T(8,128)(2,1)S(1)}, u32[]{:S(2)}, u32[]{:S(2)}) collective-permute-start(bf16[304,128]{1,0:T(8,128)(2,1)S(1)} %pad_maximum_fusion.refs_0_), channel_id=1, source_target_pairs={{0,12},{1,13},{2,14},{3,15},{4,0},{5,1},{6,2},{7,3},{8,4},{9,5},{1... | collective-permute-start | bytes 233480 | tf_op jit(solution)/shard_map/ppermute | solution.py:491
  70.3 7.8 %collective-permute-start.29 = (bf16[896,128]{1,0:T(8,128)(2,1)S(1)}, bf16[896,128]{1,0:T(8,128)(2,1)S(1)}, u32[]{:S(2)}, u32[]{:S(2)}) collective-permute-start(bf16[896,128]{1,0:T(8,128)(2,1)S(1)} %shard_map.152.refs_0_), channel_id=1, source_target_pairs={{0,1},{1,0},{2,3},{3,2},{4,5},{5,4},{6,7},{7,6},{8,9},{9,8},{10,11... | collective-permute-start | bytes 688136 | tf_op jit(solution)/shard_map/ppermute | solution.py:487
  70.4 8.9 %collective-permute-start.30 = (bf16[896,128]{1,0:T(8,128)(2,1)S(1)}, bf16[896,128]{1,0:T(8,128)(2,1)S(1)}, u32[]{:S(2)}, u32[]{:S(2)}) collective-permute-start(bf16[896,128]{1,0:T(8,128)(2,1)S(1)} %shard_map.152.refs_0_), channel_id=1, source_target_pairs={{0,2},{1,3},{2,0},{3,1},{4,6},{5,7},{6,4},{7,5},{8,10},{9,11},{10,... | collective-permute-start | bytes 688136 | tf_op jit(solution)/shard_map/ppermute | solution.py:487
  72.7 10.9 %collective-permute-start.31 = (bf16[896,128]{1,0:T(8,128)(2,1)S(1)}, bf16[896,128]{1,0:T(8,128)(2,1)S(1)}, u32[]{:S(2)}, u32[]{:S(2)}) collective-permute-start(bf16[896,128]{1,0:T(8,128)(2,1)S(1)} %shard_map.152.refs_0_), channel_id=1, source_target_pairs={{0,3},{1,2},{2,1},{3,0},{4,7},{5,6},{6,5},{7,4},{8,11},{9,10},{10,... | collective-permute-start | bytes 688136 | tf_op jit(solution)/shard_map/ppermute | solution.py:487
  75.2 8.5 %collective-permute-start.32 = (bf16[896,128]{1,0:T(8,128)(2,1)S(1)}, bf16[896,128]{1,0:T(8,128)(2,1)S(1)}, u32[]{:S(2)}, u32[]{:S(2)}) collective-permute-start(bf16[896,128]{1,0:T(8,128)(2,1)S(1)} %shard_map.152.refs_0_), channel_id=1, source_target_pairs={{0,16},{16,0},{1,17},{17,1},{2,18},{18,2},{3,19},{19,3},{4,20},{20... | collective-permute-start | bytes 688136 | tf_op jit(solution)/shard_map/ppermute | solution.py:613
  75.2 13.9 %collective-permute-start.19 = (bf16[1168,128]{1,0:T(8,128)(2,1)S(1)}, bf16[1168,128]{1,0:T(8,128)(2,1)S(1)}, u32[]{:S(2)}, u32[]{:S(2)}) collective-permute-start(bf16[1168,128]{1,0:T(8,128)(2,1)S(1)} %shard_map.151.refs_0_), channel_id=1, source_target_pairs={{0,1},{1,0},{2,3},{3,2},{4,5},{5,4},{6,7},{7,6},{8,9},{9,8},{10,11... | collective-permute-start | bytes 897032 | tf_op jit(solution)/shard_map/ppermute | solution.py:487
  78.1 12.0 %collective-permute-start.20 = (bf16[1168,128]{1,0:T(8,128)(2,1)S(1)}, bf16[1168,128]{1,0:T(8,128)(2,1)S(1)}, u32[]{:S(2)}, u32[]{:S(2)}) collective-permute-start(bf16[1168,128]{1,0:T(8,128)(2,1)S(1)} %shard_map.151.refs_0_), channel_id=1, source_target_pairs={{0,2},{1,3},{2,0},{3,1},{4,6},{5,7},{6,4},{7,5},{8,10},{9,11},{10,... | collective-permute-start | bytes 897032 | tf_op jit(solution)/shard_map/ppermute | solution.py:487
  79.3 14.6 %collective-permute-start.21 = (bf16[1168,128]{1,0:T(8,128)(2,1)S(1)}, bf16[1168,128]{1,0:T(8,128)(2,1)S(1)}, u32[]{:S(2)}, u32[]{:S(2)}) collective-permute-start(bf16[1168,128]{1,0:T(8,128)(2,1)S(1)} %shard_map.151.refs_0_), channel_id=1, source_target_pairs={{0,3},{1,2},{2,1},{3,0},{4,7},{5,6},{6,5},{7,4},{8,11},{9,10},{10,... | collective-permute-start | bytes 897032 | tf_op jit(solution)/shard_map/ppermute | solution.py:487
  83.6 10.3 %collective-permute-start.33 = (bf16[896,128]{1,0:T(8,128)(2,1)S(1)}, bf16[896,128]{1,0:T(8,128)(2,1)S(1)}, u32[]{:S(2)}, u32[]{:S(2)}) collective-permute-start(bf16[896,128]{1,0:T(8,128)(2,1)S(1)} %collective-permute-done.29.refs_1_), channel_id=1, source_target_pairs={{0,16},{16,0},{1,17},{17,1},{2,18},{18,2},{3,19},{19,3},{4,20},{20... | collective-permute-start | bytes 688136 | tf_op jit(solution)/shard_map/ppermute | solution.py:613
  83.6 10.8 %collective-permute-start.34 = (bf16[896,128]{1,0:T(8,128)(2,1)S(1)}, bf16[896,128]{1,0:T(8,128)(2,1)S(1)}, u32[]{:S(2)}, u32[]{:S(2)}) collective-permute-start(bf16[896,128]{1,0:T(8,128)(2,1)S(1)} %collective-permute-done.30.refs_2_), channel_id=1, source_target_pairs={{0,16},{16,0},{1,17},{17,1},{2,18},{18,2},{3,19},{19,3},{4,20},{20... | collective-permute-start | bytes 688136 | tf_op jit(solution)/shard_map/ppermute | solution.py:613
  (22 other events, 154.3 us)
